TPU v7x, 32 devices: a whole 2x2x4 slice. The times are simulated.
32 devices in a mesh: groups: 2 (over y), tp: 4 (over x, core), req: 4 (over z).
Axes of the slice: x: 2, y: 2, z: 4, core: 2. Of those that a mesh axis runs over, the one named last changes fastest.
Arguments:
- queries: bfloat16 [32, 8192], P(('groups', 'tp', 'req')), parts along dimension 0, may hold values from -6 to 6
- new_kv: bfloat16 [32, 1024], P(('groups', 'tp', 'req')), parts along dimension 0, may hold values from -8 to 8
- cache_pool: bfloat16 [8, 4, 6, 4, 128, 256], P(('groups', 'tp'), 'req'), parts along dimension 0, may hold values from -210 to 210
- page_slot: int32 [8, 4, 7], P(('groups', 'tp')), parts along dimension 0, may hold values from 0 to 5, as said below
- page_owner: int32 [8, 4, 7], P(('groups', 'tp')), parts along dimension 0, may hold values from 0 to 3, as said below
- context_len: int32 [8, 4], P(('groups', 'tp')), parts along dimension 0, may hold values from 1 to 896, as said below
- out_weight: bfloat16 [8192, 16384], P('tp', 'req'), may hold values from -0.0625 to 0.0625
Outputs:
- mixed: bfloat16 [32, 16384], P(('groups', 'tp'), 'req'), parts along dimension 0
There are 2 independent parts, one for each index of `groups`. A program takes and returns all parts, laid end to end along the dimension named above; an argument that names none is the same for every part. Nothing has to cross between parts.
Inputs may be any that keep to these rules, and one draw needn't show every extreme that they name: `page_owner`: the pool holding page j: a request's first pages are held by its own device, each later live page by a different other device; entries past the live pages name the request's own device; in each column some request has a page on every other device. `page_slot`: the page's slot in that pool; no slot holds two live pages. `context_len`: a request has ceil(length / 128) live pages; in each column some request is exactly 896 tokens long.
All inputs are finite; a program needn't handle non-finite values.
Results may differ from a plain program's by a relative error of at most 0.0051.
Values may be sent and summed in bfloat16 or wider, within the bound.
No kernel may reach another device: no remote copies, remote signals or barrier semaphores. Data moves between devices by JAX's collectives and lax.ppermute only.
A program may use at most 64 MiB of HBM per device.

v0:
```python
import math

import jax
import jax.numpy as jnp
from jax import lax
from jax.sharding import PartitionSpec as P

very_negative = -1e30


def page_parts(grouped, page_data, valid_mask):
    head_dim = grouped.shape[-1]
    key_part = page_data[..., :head_dim]
    values = page_data[..., head_dim:]
    scores = jnp.einsum(
        "phgd,phid->phgi", grouped, key_part, preferred_element_type=jnp.float32
    ) / math.sqrt(head_dim)
    token_mask = valid_mask[:, None, None, :]
    masked = jnp.where(token_mask, scores, very_negative)
    page_max = jnp.max(masked, axis=-1)
    weights = jnp.where(token_mask, jnp.exp(masked - page_max[..., None]), 0.0)
    page_total = jnp.sum(weights, axis=-1)
    page_sum = jnp.einsum(
        "phgi,phid->phgd", weights.astype(jnp.bfloat16), values, preferred_element_type=jnp.float32
    )
    return (page_max, page_total, page_sum)


def combine(page_max, page_total, page_sum, self_score, self_value):
    top_score = jnp.maximum(jnp.max(page_max, axis=0), self_score)
    factor = jnp.exp(page_max - top_score)
    own_factor = jnp.exp(self_score - top_score)
    numerator = (
        jnp.sum(factor[..., None] * page_sum, axis=0)
        + own_factor[..., None] * self_value[:, None, :]
    )
    denominator = jnp.sum(factor * page_total, axis=0) + own_factor
    return numerator / denominator[..., None]


def on_device(queries, new_kv, cache_pool, page_slot, page_owner, context_len, out_weight):
    req_count = lax.axis_size("req")
    this_index = lax.axis_index("req")
    pool_pages = cache_pool[0, 0]
    kv_heads = pool_pages.shape[1]
    page_len = pool_pages.shape[2]
    head_dim = pool_pages.shape[3] // 2
    slot_table = page_slot[0]
    owner_table = page_owner[0]
    lengths = context_len[0]
    table_width = slot_table.shape[1]
    grouped = queries[0].reshape(kv_heads, -1, head_dim)
    fresh_kv = new_kv[0].reshape(2, kv_heads, head_dim)
    entry_ids = jnp.arange(table_width, dtype=jnp.int32)
    token_ids = jnp.arange(page_len, dtype=jnp.int32)
    position = entry_ids[:, None] * page_len + token_ids[None, :]
    my_slots = slot_table[this_index]
    my_owners = owner_table[this_index]
    my_length = lengths[this_index]
    valid_mask = position < my_length
    peer_ids = jnp.arange(req_count, dtype=jnp.int32)
    counts = (lengths + page_len - 1) // page_len
    held_mask = (
        (owner_table == this_index)
        & (peer_ids[:, None] != this_index)
        & (entry_ids[None, :] < counts[:, None])
    )
    held_any = jnp.any(held_mask, axis=1)
    held_int = held_mask.astype(jnp.int32)
    held_slot = jnp.sum(held_int * slot_table, axis=1)
    held_pages = pool_pages[held_slot]
    spread = jnp.broadcast_to(grouped, (table_width,) + grouped.shape)
    outgoing = jnp.where(held_any[:, None, None, None], held_pages, jnp.zeros_like(held_pages))
    incoming = lax.all_to_all(outgoing, "req", split_axis=0, concat_axis=0, tiled=True)
    candidates = jnp.concatenate([pool_pages, incoming], axis=0)
    pick_index = jnp.where(my_owners == this_index, my_slots, pool_pages.shape[0] + my_owners)
    page_max, page_total, page_sum = page_parts(spread, candidates[pick_index], valid_mask)
    self_score = jnp.einsum(
        "hgd,hd->hg", grouped, fresh_kv[0], preferred_element_type=jnp.float32
    ) / math.sqrt(head_dim)
    attention = combine(page_max, page_total, page_sum, self_score, fresh_kv[1].astype(jnp.float32))
    attention = attention.astype(jnp.bfloat16).reshape(1, -1)
    head_rows = lax.all_to_all(attention, "tp", split_axis=1, concat_axis=0, tiled=True)
    partial_value = jnp.dot(
        lax.all_gather(head_rows, "req", axis=0, tiled=True),
        out_weight,
        preferred_element_type=jnp.float32,
    )
    partial_value = partial_value.reshape(req_count, -1, partial_value.shape[1])
    summed = lax.psum_scatter(partial_value, "tp", scatter_dimension=1, tiled=True)
    return summed.reshape(req_count, -1).astype(jnp.bfloat16)


def solution(mesh):
    placed = (
        P(("groups", "tp", "req"), None),
        P(("groups", "tp", "req"), None),
        P(("groups", "tp"), "req", None, None, None, None),
        P(("groups", "tp"), None, None),
        P(("groups", "tp"), None, None),
        P(("groups", "tp"), None),
        P("tp", "req"),
    )
    return jax.shard_map(
        on_device, mesh=mesh, in_specs=placed, out_specs=P(("groups", "tp"), "req"), check_vma=False
    )
```

profile of v0, /device:TPU:0, one launch (start us, length us, event | category | flops | bytes accessed | tf_op | source)
XLA Modules:
  0.0 90.2 jit_solution(10990809749500815336)
XLA Ops:
  0.0 0.0 copy-start
  0.0 0.7 and_select_fusion
  0.7 0.9 fusion.25
  1.6 0.8 fusion.18
  2.4 2.0 %gather_fusion = bf16[4,4,128,256]{3,2,1,0:T(8,128)(2,1)S(1)} fusion(bf16[6,4,128,256]{3,2,1,0:T(8,128)(2,1)} %bitcast.46, s32[1024]{0:T(1024)S(1)} %pad_clamp_fusion.1), kind=kCustom, calls=%fused_computation | custom fusion | bytes 2097168 | tf_op jit(solution)/shard_map/gather | solution.py:71
  4.4 0.0 copy-start.3
  4.4 0.0 copy-start.2
  4.4 1.2 %broadcast_select_fusion = bf16[4,4,128,256]{3,2,1,0:T(8,128)(2,1)} fusion(bf16[4,4,128,256]{3,2,1,0:T(8,128)(2,1)S(1)} %gather_fusion, pred[4]{0:T(512)(128)(4,1)S(1)} %get-tuple-element.11), kind=kLoop, calls=%fused_computation.8 | loop fusion | flops 524288 | bytes 2097156 | tf_op jit(solution)/shard_map/jit(_where)/select_n | solution.py:73
  5.6 6.3 %all-to-all-start = ((bf16[4,4,128,256]{3,2,1,0:T(8,128)(2,1)}), bf16[4,4,128,256]{3,2,1,0:T(8,128)(2,1)}, u32[]{:S(2)}, u32[]{:S(2)}) async-start(bf16[4,4,128,256]{3,2,1,0:T(8,128)(2,1)} %broadcast_select_fusion), calls=%async_computation | async-start | bytes 2097152 | tf_op jit(solution)/shard_map/all_to_all | solution.py:74
  11.9 0.0 copy-done.3
  11.9 0.6 constant_dynamic-slice_fusion.2
  12.5 0.0 copy-done
  12.5 0.1 reduce.1
  12.6 0.7 fusion.22
  13.3 0.7 add_compare_fusion
  14.0 0.0 copy-done.2
  14.0 0.1 fusion.16
  14.2 23.6 %all-to-all-done = bf16[4,4,128,256]{3,2,1,0:T(8,128)(2,1)} async-done(((bf16[4,4,128,256]{3,2,1,0:T(8,128)(2,1)}), bf16[4,4,128,256]{3,2,1,0:T(8,128)(2,1)}, u32[]{:S(2)}, u32[]{:S(2)}) %all-to-all-start) | async-done | bytes 1048608 | tf_op jit(solution)/shard_map/all_to_all | solution.py:74
  37.7 2.0 %pad_maximum_fusion = bf16[10,4,128,256]{3,2,1,0:T(8,128)(2,1)S(1)} fusion(bf16[4,4,128,256]{3,2,1,0:T(8,128)(2,1)} %all-to-all-done, bf16[6,4,128,256]{3,2,1,0:T(8,128)(2,1)} %bitcast.47), kind=kLoop, calls=%fused_computation.2 | loop fusion | flops 1310720 | bytes 5242880 | tf_op jit(solution)/shard_map/concatenate | solution.py:75
  39.7 1.9 %gather_fusion.1 = bf16[7,4,128,256]{3,2,1,0:T(8,128)(2,1)} fusion(bf16[10,4,128,256]{3,2,1,0:T(8,128)(2,1)S(1)} %pad_maximum_fusion, s32[1024]{0:T(1024)S(1)} %pad_clamp_fusion), kind=kCustom, calls=%fused_computation.1 | custom fusion | bytes 3670044 | tf_op jit(solution)/shard_map/gather | solution.py:77
  41.7 0.0 copy-start.1
  41.7 0.0 copy-start.4
  41.7 2.0 %fusion.27 = (f32[7,4,16]{2,1,0:T(4,128)S(1)}, f32[7,4,16,128]{3,2,1,0:T(8,128)S(1)}) fusion(bf16[4,16,128]{2,1,0:T(8,128)(2,1)S(1)} %bitcast.51, bf16[7,4,128,256]{3,2,1,0:T(8,128)(2,1)} %gather_fusion.1, pred[7,128]{1,0:T(8,128)(4,1)S(1)} %add_compare_fusion), kind=kOutput, calls=%fused_computation.58 | convolution fusion | flops 14851648 | bytes 1165952 | tf_op jit(solution)/shard_map/phgd,phid->phgi/dot_general | solution.py:15
  43.6 0.3 fusion.5
  44.0 0.0 copy-done.1
  44.0 0.4 fusion.2
  44.4 0.1 divide_convert_fusion
  44.5 0.5 broadcast.191
  45.0 0.7 reduce.2
  45.8 0.6 reshape.221
  46.4 3.3 %all-to-all-start.1 = ((bf16[4,2,1024]{2,1,0:T(2,128)(2,1)}), bf16[4,2,1024]{2,1,0:T(2,128)(2,1)S(1)}, u32[]{:S(2)}, u32[]{:S(2)}) async-start(bf16[4,2,1024]{2,1,0:T(2,128)(2,1)} %reshape.221), calls=%async_computation.1 | async-start | bytes 32768 | tf_op jit(solution)/shard_map/all_to_all | solution.py:83
  49.7 0.0 copy-done.4
  49.7 0.7 dynamic-slice.3
  50.3 3.1 %all-to-all-done.1 = bf16[4,2,1024]{2,1,0:T(2,128)(2,1)S(1)} async-done(((bf16[4,2,1024]{2,1,0:T(2,128)(2,1)}), bf16[4,2,1024]{2,1,0:T(2,128)(2,1)S(1)}, u32[]{:S(2)}, u32[]{:S(2)}) %all-to-all-start.1) | async-done | bytes 16416 | tf_op jit(solution)/shard_map/all_to_all | solution.py:83
  53.5 13.5 %all-gather = bf16[1,16,2048]{2,0,1:T(2,128)(2,1)S(1)} all-gather(bf16[1,4,2048]{2,0,1:T(2,128)(2,1)S(1)} %bitcast.48), channel_id=2, replica_groups=mesh['groups'=2,'tp'=4,'req'=4] {'req'}, dimensions={1}, use_global_device_ids=true | all-gather | bytes 81920 | tf_op jit(solution)/shard_map/all_gather | solution.py:85
  67.0 8.1 %fusion.11 = f32[16,4096]{1,0:T(8,128)S(1)} fusion(bf16[2048,4096]{1,0:T(8,128)(2,1)} %param.13, bf16[1,16,2048]{2,0,1:T(2,128)(2,1)S(1)} %all-gather), kind=kOutput, calls=%fused_computation.17 | convolution fusion | flops 268435456 | bytes 17104896 | tf_op jit(solution)/shard_map/dot_general | solution.py:84
  75.1 0.1 reshape.197
  75.2 0.2 copy.11
  75.4 13.5 %all-reduce.2 = bf16[4,4,4096]{2,0,1:T(4,128)(2,1)S(1)} all-reduce(f32[4,4,4096]{2,0,1:T(4,128)S(1)} %copy.11), channel_id=3, replica_groups=mesh['groups'=2,'tp'=4,'req'=4] {'tp'}, use_global_device_ids=true, to_apply=%region_7.8.clone | all-reduce | flops 65536 | bytes 393216
  88.9 1.3 %fusion.15 = bf16[4,4096]{1,0:T(4,128)(2,1)} fusion(bf16[4,4,4096]{2,0,1:T(4,128)(2,1)S(1)} %all-reduce.2, u32[]{:T(128)} %bitcast.15), kind=kLoop, calls=%fused_computation.22 | loop fusion | bytes 65540 | tf_op jit(solution)/shard_map/convert_element_type | solution.py:91
  (11 shorter events, 0.1 us)
Async XLA Ops:
  0.0 12.5 %copy-start = (bf16[1,8192]{1,0:T(2,128)(2,1)S(1)}, bf16[1,8192]{1,0:T(2,128)(2,1)}, u32[]{:S(2)}) copy-start(bf16[1,8192]{1,0:T(2,128)(2,1)} %param.7) | copy-start | bytes 49156
  4.4 7.5 %copy-start.3 = (s32[1,4]{1,0:T(1,128)S(1)}, s32[1,4]{1,0:T(1,128)}, u32[]{:S(2)}) copy-start(s32[1,4]{1,0:T(1,128)} %param.12) | copy-start | bytes 52
  4.4 9.6 %copy-start.2 = (bf16[1,1024]{1,0:T(2,128)(2,1)S(1)}, bf16[1,1024]{1,0:T(2,128)(2,1)}, u32[]{:S(2)}) copy-start(bf16[1,1024]{1,0:T(2,128)(2,1)} %param.8) | copy-start | bytes 6148
  5.6 32.1 %all-to-all-start = ((bf16[4,4,128,256]{3,2,1,0:T(8,128)(2,1)}), bf16[4,4,128,256]{3,2,1,0:T(8,128)(2,1)}, u32[]{:S(2)}, u32[]{:S(2)}) async-start(bf16[4,4,128,256]{3,2,1,0:T(8,128)(2,1)} %broadcast_select_fusion), calls=%async_computation | async-start | bytes 2097152 | tf_op jit(solution)/shard_map/all_to_all | solution.py:74
  41.7 2.3 %copy-start.1 = (bf16[7,4,128,256]{3,2,1,0:T(8,128)(2,1)S(1)}, bf16[7,4,128,256]{3,2,1,0:T(8,128)(2,1)}, u32[]{:S(2)}) copy-start(bf16[7,4,128,256]{3,2,1,0:T(8,128)(2,1)} %gather_fusion.1) | copy-start | bytes 5505028
  41.7 8.0 %copy-start.4 = (u32[32]{0:T(128)S(1)}, u32[32]{0:T(128)}, u32[]{:S(2)}) copy-start(u32[32]{0:T(128)} %constant.63) | copy-start | bytes 388
  46.4 7.1 %all-to-all-start.1 = ((bf16[4,2,1024]{2,1,0:T(2,128)(2,1)}), bf16[4,2,1024]{2,1,0:T(2,128)(2,1)S(1)}, u32[]{:S(2)}, u32[]{:S(2)}) async-start(bf16[4,2,1024]{2,1,0:T(2,128)(2,1)} %reshape.221), calls=%async_computation.1 | async-start | bytes 32768 | tf_op jit(solution)/shard_map/all_to_all | solution.py:83
where the time goes:
time: 90.8 us; the launch traced here: 90.2 us
  blocking collectives  27 us (30%)
  waiting for transfers between devices  26.7 us (29%)
  matrix products  10.6 us (12%)
  starting transfers between devices  9.57 us (11%)
  other arithmetic  8.19 us (9%)
  local copies, waits for them, and re-layouts  7.97 us (9%)
    all_to_all x1, waiting for transfers between devices, on_device(): lax.all_to_all(outgoing, 'req', split_axis=0, concat_axis=0, tiled=True)  23.6 us
    all_gather x1, blocking collectives, on_device(): lax.all_gather(head_rows, 'req', axis=0, tiled=True)  13.5 us
    unnamed x1, blocking collectives  13.5 us
    dot_general x1, matrix products, on_device(): jnp.dot(lax.all_gather(head_rows, 'req', axis=0, tiled=True), out_weight,...  8.06 us
    all_to_all x1, starting transfers between devices, on_device(): lax.all_to_all(outgoing, 'req', split_axis=0, concat_axis=0, tiled=True)  6.32 us
    all_to_all x1, starting transfers between devices, on_device(): lax.all_to_all(attention, 'tp', split_axis=1, concat_axis=0, tiled=True)  3.25 us
    all_to_all x1, waiting for transfers between devices, on_device(): lax.all_to_all(attention, 'tp', split_axis=1, concat_axis=0, tiled=True)  3.14 us
    gather x1, local copies, waits for them, and re-layouts, on_device(): held_pages = pool_pages[held_slot]  2.02 us
  transfers between devices with their start and end apart: 2, of which 2 were waited for; matrix products, arithmetic and copies ran while one was open for 3% of the time, Pallas kernels for 0%

commit v1 on v0

v1 whole, which is shorter than its diff:
```python
import functools
import math

import jax
import jax.numpy as jnp
from jax import lax
from jax.experimental import pallas as pl
from jax.experimental.pallas import tpu as pltpu
from jax.sharding import PartitionSpec as P

very_negative = -1e30
MIB = 1 << 20


def swap(x, axis, offset):
    count = lax.axis_size(axis)
    return lax.ppermute(x, axis, [(i, i ^ offset) for i in range(count)])


def round_up(value, step):
    return -(-value // step) * step


def attend_kernel(n_req, n_tp, *refs):
    q_refs = refs[:n_req]
    kv_ref, slot_ref, owner_ref, len_ref, pool_ref = refs[n_req : n_req + 5]
    out_refs = refs[n_req + 5 : n_req + 5 + n_tp]
    q_all, request_of, page_of, acc_all = refs[n_req + 5 + n_tp :]
    pool, kv_heads, page_len, width = pool_ref.shape
    head_dim = width // 2
    heads = q_refs[0].shape[0]
    group = heads // kv_heads
    chunk = heads // n_tp
    entries = slot_ref.shape[2]
    me = lax.axis_index("req")
    my_tp = lax.axis_index("tp")
    scale = 1.0 / math.sqrt(head_dim)

    for s in range(pool + 1):
        request_of[s] = -1
        page_of[s] = 0

    def enter(n, carry):
        length = len_ref[0, n]
        for j in range(entries):
            held = (owner_ref[0, n, j] == me) & (j * page_len < length)
            s = jnp.where(held, slot_ref[0, n, j], pool)
            request_of[s] = n
            page_of[s] = j
        return carry

    lax.fori_loop(0, n_req, enter, 0)

    for d in range(n_req):
        q_all[d] = q_refs[d][...]
    acc_all[...] = jnp.zeros_like(acc_all)
    token = lax.broadcasted_iota(jnp.int32, (group, page_len), 1)
    lane = lax.broadcasted_iota(jnp.int32, (heads, 128), 1)
    stat = jnp.full((heads, 128), very_negative, jnp.float32)

    own_q = q_all[0].astype(jnp.float32)
    new_k = jnp.concatenate(
        [jnp.broadcast_to(kv_ref[0:1, h * head_dim : (h + 1) * head_dim], (group, head_dim)) for h in range(kv_heads)], axis=0
    ).astype(jnp.float32)
    base = kv_heads * head_dim
    new_v = jnp.concatenate(
        [
            jnp.broadcast_to(kv_ref[0:1, base + h * head_dim : base + (h + 1) * head_dim], (group, head_dim))
            for h in range(kv_heads)
        ],
        axis=0,
    ).astype(jnp.float32)
    self_score = jnp.sum(own_q * new_k, axis=1, keepdims=True) * scale

    own_max, own_total, own_sum = [], [], []
    for s in range(pool):
        n = request_of[s]
        live = (n >= 0) & (s >= 0)
        nn = jnp.maximum(n, 0)
        valid = jnp.where(live, len_ref[0, nn] - page_of[s] * page_len, 0)
        mask = token < valid
        q = q_all[jnp.where(live, nn ^ me, 0)]
        maxes, totals, sums = [], [], []
        for h in range(kv_heads):
            scores = lax.dot_general(
                q[h * group : (h + 1) * group],
                pool_ref[s, h, :, :head_dim],
                (((1,), (1,)), ((), ())),
                preferred_element_type=jnp.float32,
            )
            masked = jnp.where(mask, scores * scale, very_negative)
            top = jnp.max(masked, axis=1, keepdims=True)
            weights = jnp.where(mask, jnp.exp(masked - top), 0.0)
            maxes.append(top)
            totals.append(jnp.sum(weights, axis=1, keepdims=True))
            sums.append(
                jnp.dot(
                    weights.astype(jnp.bfloat16), pool_ref[s, h, :, head_dim:], preferred_element_type=jnp.float32
                )
            )
        page_max = jnp.concatenate(maxes, axis=0)
        page_total = jnp.concatenate(totals, axis=0)
        page_sum = jnp.concatenate(sums, axis=0)
        other = live & (n != me)
        target = jnp.where(other, nn, me)
        safe_total = jnp.where(page_total > 0.0, page_total, 1.0)
        result = page_sum / safe_total
        logsum = page_max + jnp.log(safe_total)
        for c in range(n_tp):
            acc_all[c, target] = result[c * chunk : (c + 1) * chunk]
        stat = jnp.where(lane == target, logsum, stat)
        mine = live & (n == me)
        own_max.append(jnp.where(mine, page_max, very_negative))
        own_total.append(jnp.where(mine, page_total, 0.0))
        own_sum.append(page_sum)

    top = self_score
    for page_max in own_max:
        top = jnp.maximum(top, page_max)
    factor = jnp.exp(self_score - top)
    total = factor
    numerator = factor * new_v
    for page_max, page_total, page_sum in zip(own_max, own_total, own_sum):
        factor = jnp.exp(page_max - top)
        total = total + factor * page_total
        factor = jnp.where(page_total > 0.0, factor, 0.0)
        numerator = numerator + factor * page_sum
    result = numerator / total
    logsum = top + jnp.log(total)
    for c in range(n_tp):
        acc_all[c, me] = result[c * chunk : (c + 1) * chunk]
    stat = jnp.where(lane == me, logsum, stat)

    padded = stat
    if heads < 128:
        padded = jnp.concatenate([stat, jnp.zeros((128 - heads, 128), jnp.float32)], axis=0)
    turned = padded.T[: round_up(n_req, 8)]
    rows = n_req * chunk
    stat_rows = out_refs[0].shape[0] - rows
    high = turned.astype(jnp.bfloat16).astype(jnp.float32)
    rest = turned - high
    middle = rest.astype(jnp.bfloat16).astype(jnp.float32)
    low = rest - middle
    split = jnp.concatenate([high, middle, low], axis=0)
    if split.shape[0] < stat_rows:
        split = jnp.concatenate([split, jnp.zeros((stat_rows - split.shape[0], 128), jnp.float32)], axis=0)
    for d in range(n_tp):
        c = my_tp ^ d
        out_refs[d][:rows] = acc_all[c].reshape(rows, 128).astype(jnp.bfloat16)
        turned_to = pltpu.roll(split, (128 - c * chunk) % 128, 1)
        out_refs[d][rows:] = turned_to.astype(jnp.bfloat16)


def attend(q_list, new_kv, page_slot, page_owner, context_len, pool, n_req, n_tp):
    heads, head_dim = q_list[0].shape
    chunk = heads // n_tp
    rows = n_req * chunk
    stat_rows = round_up(3 * round_up(n_req, 8), 16)
    smem = pl.BlockSpec(memory_space=pltpu.SMEM)
    vmem = pl.BlockSpec(memory_space=pltpu.VMEM)
    slots = pool.shape[0]
    flops = 4 * pool.size // 2 * heads // pool.shape[1]
    return pl.pallas_call(
        functools.partial(attend_kernel, n_req, n_tp),
        out_shape=[jax.ShapeDtypeStruct((rows + stat_rows, head_dim), jnp.bfloat16)] * n_tp,
        in_specs=[vmem] * (n_req + 1) + [smem] * 3 + [vmem],
        out_specs=[vmem] * n_tp,
        scratch_shapes=[
            pltpu.VMEM((n_req, heads, head_dim), jnp.bfloat16),
            pltpu.SMEM((slots + 1,), jnp.int32),
            pltpu.SMEM((slots + 1,), jnp.int32),
            pltpu.VMEM((n_tp, n_req, chunk, head_dim), jnp.float32),
        ],
        compiler_params=pltpu.CompilerParams(vmem_limit_bytes=16 * MIB),
        cost_estimate=pl.CostEstimate(flops=flops, bytes_accessed=pool.size * 2, transcendentals=0),
        name="attend",
    )(*q_list, new_kv, page_slot, page_owner, context_len, pool)


def project_kernel(n_req, n_tp, chunk, *refs):
    part_refs = refs[:n_req]
    weight_ref = refs[n_req]
    out_refs = refs[n_req + 1 : n_req + 1 + n_tp]
    wide, logs, attention, sums = refs[n_req + 1 + n_tp :]
    rows = n_req * chunk
    step = round_up(n_req, 8)
    total_rows = n_tp * n_req
    depth, columns = weight_ref.shape
    my_tp = lax.axis_index("tp")
    for r in range(n_req):
        for c in range(n_tp):
            col = my_tp ^ c
            wide[r, pl.ds(pl.multiple_of(col * rows, 8), rows)] = part_refs[r][c, :rows].astype(jnp.float32)
            tail = part_refs[r][c, rows:].astype(jnp.float32)
            value = tail[:step] + tail[step : 2 * step] + tail[2 * step : 3 * step]
            logs[r, pl.ds(col * n_req, n_req)] = value[:n_req]
    values = [logs[r] for r in range(n_req)]
    top = functools.reduce(jnp.maximum, values)
    factors = [jnp.exp(v - top) for v in values]
    total = functools.reduce(jnp.add, factors)
    factors = [f / total for f in factors]
    for h in range(chunk):
        block = None
        for r in range(n_req):
            term = wide[r, pl.ds(h, total_rows, stride=chunk)] * factors[r][:, h : h + 1]
            block = term if block is None else block + term
        attention[:, h * 128 : (h + 1) * 128] = block.astype(jnp.bfloat16)
    tile = min(columns, 512)

    @pl.loop(0, columns // tile)
    def _(t):
        at = pl.ds(pl.multiple_of(t * tile, tile), tile)
        product = jnp.dot(attention[...], weight_ref[:, at], preferred_element_type=jnp.float32)
        for c in range(n_tp):
            sums[c, :, at] = product[c * n_req : (c + 1) * n_req]

    for d in range(n_tp):
        out_refs[d][...] = sums[my_tp ^ d].astype(out_refs[d].dtype)


def project(parts, out_weight, n_req, n_tp, chunk):
    depth, columns = out_weight.shape
    rows = n_req * chunk
    vmem = pl.BlockSpec(memory_space=pltpu.VMEM)
    own = jax.ShapeDtypeStruct((n_req, columns), jnp.float32)
    sent = jax.ShapeDtypeStruct((n_req, columns), jnp.bfloat16)
    total_rows = n_tp * n_req
    return pl.pallas_call(
        functools.partial(project_kernel, n_req, n_tp, chunk),
        out_shape=[own] + [sent] * (n_tp - 1),
        in_specs=[vmem] * (n_req + 1),
        out_specs=[vmem] * n_tp,
        scratch_shapes=[
            pltpu.VMEM((n_req, n_tp * rows, 128), jnp.float32),
            pltpu.VMEM((n_req, total_rows, 128), jnp.float32),
            pltpu.VMEM((total_rows, depth), jnp.bfloat16),
            pltpu.VMEM((n_tp, n_req, columns), jnp.float32),
        ],
        compiler_params=pltpu.CompilerParams(vmem_limit_bytes=32 * MIB),
        cost_estimate=pl.CostEstimate(
            flops=2 * total_rows * depth * columns, bytes_accessed=out_weight.size * 2, transcendentals=0
        ),
        name="project",
    )(*parts, out_weight)


def on_device(queries, new_kv, cache_pool, page_slot, page_owner, context_len, out_weight):
    n_req = lax.axis_size("req")
    n_tp = lax.axis_size("tp")
    pool = cache_pool[0, 0]
    head_dim = pool.shape[3] // 2
    q = queries.reshape(-1, head_dim)
    chunk = q.shape[0] // n_tp
    q_list = [q] + [swap(q, "req", d) for d in range(1, n_req)]
    pieces = attend(q_list, new_kv, page_slot, page_owner, context_len, pool, n_req, n_tp)
    arrived = jnp.stack([pieces[0]] + [swap(pieces[d], "tp", d) for d in range(1, n_tp)])
    parts = [arrived] + [swap(arrived, "req", d) for d in range(1, n_req)]
    sums = project(parts, out_weight, n_req, n_tp, chunk)
    total = sums[0]
    for d in range(1, n_tp):
        total = total + swap(sums[d], "tp", d).astype(jnp.float32)
    return total.astype(jnp.bfloat16)


def solution(mesh):
    placed = (
        P(("groups", "tp", "req"), None),
        P(("groups", "tp", "req"), None),
        P(("groups", "tp"), "req", None, None, None, None),
        P(("groups", "tp"), None, None),
        P(("groups", "tp"), None, None),
        P(("groups", "tp"), None),
        P("tp", "req"),
    )
    return jax.shard_map(
        on_device, mesh=mesh, in_specs=placed, out_specs=P(("groups", "tp"), "req"), check_vma=False
    )
```

time: 90.8 us -> 52.6 us (0.58)
  blocking collectives: 27 us -> 0 us
  matrix products: 10.6 us -> 0 us
  Pallas kernels: 0 us -> 10.1 us
  waiting for transfers between devices: 26.7 us -> 16.7 us
  other arithmetic: 8.19 us -> 1.51 us
  starting transfers between devices: 9.57 us -> 14.1 us
  local copies, waits for them, and re-layouts: 7.97 us -> 9.88 us
    all_to_all x2 -> x0, waiting for transfers between devices: 26.7 us -> none  [the longest x1 23.6 us: on_device(): lax.all_to_all(outgoing, 'req', split_axis=0, concat_axis=0, tiled=True)]
    ppermute x0 -> x12, waiting for transfers between devices: none -> 16.7 us  [swap(): return lax.ppermute(x, axis, [(i, i ^ offset) for i in range(count)])]
    ppermute x0 -> x12, starting transfers between devices: none -> 14.1 us  [swap(): return lax.ppermute(x, axis, [(i, i ^ offset) for i in range(count)])]
    all_gather x1 -> x0, blocking collectives: 13.5 us -> none  [on_device(): lax.all_gather(head_rows, 'req', axis=0, tiled=True)]
    unnamed x1 -> x0, blocking collectives: 13.5 us -> none
    dot_general x4 -> x0, matrix products: 10.6 us -> none  [the longest x1 8.06 us: on_device(): jnp.dot(lax.all_gather(head_rows, 'req', axis=0, tiled=True), out_weight,...]
    pallas_call x0 -> x2, Pallas kernels: none -> 10.1 us  [the longest x1 6.66 us: attend(): pl.pallas_call(functools.partial(attend_kernel, n_req, n_tp), out_shape=[...]
    all_to_all x2 -> x0, starting transfers between devices: 9.57 us -> none  [the longest x1 6.32 us: on_device(): lax.all_to_all(outgoing, 'req', split_axis=0, concat_axis=0, tiled=True)]
  transfers between devices with their start and end apart: 2 -> 12, of which waited for: 2 -> 8; matrix products, arithmetic and copies ran while one was open for 3% -> 0% of each run, Pallas kernels for 0% -> 0%
where the time goes in v1:
time: 52.6 us; the launch traced here: 52.3 us
  waiting for transfers between devices  16.7 us (32%)
  starting transfers between devices  14.1 us (27%)
  Pallas kernels  10.1 us (19%)
  local copies, waits for them, and re-layouts  9.88 us (19%)
  other arithmetic  1.51 us (3%)
    ppermute x12, waiting for transfers between devices, swap(): return lax.ppermute(x, axis, [(i, i ^ offset) for i in range(count)])  16.7 us
    ppermute x12, starting transfers between devices, swap(): return lax.ppermute(x, axis, [(i, i ^ offset) for i in range(count)])  14.1 us
    unnamed x12, local copies, waits for them, and re-layouts  9.88 us
    pallas_call x1, Pallas kernels, attend(): pl.pallas_call(functools.partial(attend_kernel, n_req, n_tp), out_shape=[...  6.66 us
    pallas_call x1, Pallas kernels, project(): pl.pallas_call(functools.partial(project_kernel, n_req, n_tp, chunk), out...  3.44 us
  transfers between devices with their start and end apart: 12, of which 8 were waited for; matrix products, arithmetic and copies ran while one was open for 0% of the time, Pallas kernels for 0%

profile of v1, /device:TPU:0, one launch (start us, length us, event | category | flops | bytes accessed | tf_op | source)
XLA Modules:
  0.0 52.3 jit_solution(4970242768869633163)
XLA Ops:
  0.0 0.8 %reduce = bf16[8192]{0:T(1024)(128)(2,1)S(1)} reduce(bf16[1,8192]{1,0:T(2,128)(2,1)} %param.7, bf16[]{:T(256)} %constant.6), dimensions={0}, to_apply=%param.7.reduce_sub_computation | reduce | bytes 32770 | tf_op args[0]
  0.8 5.1 %collective-permute-start.2 = (bf16[64,128]{1,0:T(8,128)(2,1)S(1)}, bf16[64,128]{1,0:T(8,128)(2,1)S(1)}, u32[]{:S(2)}, u32[]{:S(2)}) collective-permute-start(bf16[64,128]{1,0:T(8,128)(2,1)S(1)} %bitcast.7), channel_id=1, source_target_pairs={{0,3},{1,2},{2,1},{3,0},{4,7},{5,6},{6,5},{7,4},{8,11},{9,10},{10,... | collective-permute-start | bytes 49160 | tf_op jit(solution)/shard_map/ppermute | solution.py:17
  6.0 0.0 collective-permute-start.1
  6.0 0.6 %collective-permute-start = (bf16[64,128]{1,0:T(8,128)(2,1)S(1)}, bf16[64,128]{1,0:T(8,128)(2,1)S(1)}, u32[]{:S(2)}, u32[]{:S(2)}) collective-permute-start(bf16[64,128]{1,0:T(8,128)(2,1)S(1)} %bitcast.9), channel_id=1, source_target_pairs={{0,1},{1,0},{2,3},{3,2},{4,5},{5,4},{6,7},{7,6},{8,9},{9,8},{10,11... | collective-permute-start | bytes 49160 | tf_op jit(solution)/shard_map/ppermute | solution.py:17
  6.6 1.1 %collective-permute-done.2.refs_3_ = bf16[64,128]{1,0:T(8,128)(2,1)S(1)} collective-permute-done((bf16[64,128]{1,0:T(8,128)(2,1)S(1)}, bf16[64,128]{1,0:T(8,128)(2,1)S(1)}, u32[]{:S(2)}, u32[]{:S(2)}) %collective-permute-start.2) | collective-permute-done | bytes 16416 | tf_op jit(solution)/shard_map/ppermute | solution.py:17
  7.7 2.9 %collective-permute-done.1.refs_2_ = bf16[64,128]{1,0:T(8,128)(2,1)S(1)} collective-permute-done((bf16[64,128]{1,0:T(8,128)(2,1)S(1)}, bf16[64,128]{1,0:T(8,128)(2,1)S(1)}, u32[]{:S(2)}, u32[]{:S(2)}) %collective-permute-start.1) | collective-permute-done | bytes 16416 | tf_op jit(solution)/shard_map/ppermute | solution.py:17
  10.6 0.0 collective-permute-done.refs_1_
  10.6 0.0 copy-start.1
  10.6 1.4 %copy-done.1 = bf16[1,1,6,4,128,256]{5,4,3,2,1,0:T(8,128)(2,1)S(1)} copy-done((bf16[1,1,6,4,128,256]{5,4,3,2,1,0:T(8,128)(2,1)S(1)}, bf16[1,1,6,4,128,256]{5,4,3,2,1,0:T(8,128)(2,1)}, u32[]{:S(2)}) %copy-start.1) | copy-done | bytes 1572888
  12.0 0.0 copy-start.2
  12.0 0.7 %copy-done.2 = bf16[1,1024]{1,0:T(2,128)(2,1)S(1)} copy-done((bf16[1,1024]{1,0:T(2,128)(2,1)S(1)}, bf16[1,1024]{1,0:T(2,128)(2,1)}, u32[]{:S(2)}) %copy-start.2) | copy-done | bytes 2072
  12.7 0.0 copy-start.3
  12.7 0.7 %copy-done.3 = s32[1,4,7]{2,1,0:T(4,128)S(1)} copy-done((s32[1,4,7]{2,1,0:T(4,128)S(1)}, s32[1,4,7]{2,1,0:T(4,128)}, u32[]{:S(2)}) %copy-start.3) | copy-done | bytes 136
  13.4 0.0 copy-start.4
  13.4 0.7 %copy-done.4 = s32[1,4,7]{2,1,0:T(4,128)S(1)} copy-done((s32[1,4,7]{2,1,0:T(4,128)S(1)}, s32[1,4,7]{2,1,0:T(4,128)}, u32[]{:S(2)}) %copy-start.4) | copy-done | bytes 136
  14.1 0.0 copy-start.5
  14.1 0.7 %copy-done.5 = s32[1,4]{1,0:T(1,128)S(1)} copy-done((s32[1,4]{1,0:T(1,128)S(1)}, s32[1,4]{1,0:T(1,128)}, u32[]{:S(2)}) %copy-start.5) | copy-done | bytes 40
  14.7 6.7 %attend.1 = (bf16[96,128]{1,0:T(8,128)(2,1)S(1)}, bf16[96,128]{1,0:T(8,128)(2,1)S(1)}, bf16[96,128]{1,0:T(8,128)(2,1)S(1)}, bf16[96,128]{1,0:T(8,128)(2,1)S(1)}) custom-call(bf16[64,128]{1,0:T(8,128)(2,1)S(1)} %bitcast.10, bf16[64,128]{1,0:T(8,128)(2,1)S(1)} %collective-permute-done.refs_1_, bf16[64,128]{1,0:T(8,128)(2,1)S(1)} %collective-permute-done.1.refs_2_, ...), custom_call_target="tpu_custom_call" | custom-call | flops 25165824 | bytes 1572864 | tf_op jit(solution)/shard_map/attend/pallas_call | solution.py:163
  21.4 0.1 collective-permute-start.3
  21.5 1.6 %collective-permute-start.4 = (bf16[96,128]{1,0:T(8,128)(2,1)S(1)}, bf16[96,128]{1,0:T(8,128)(2,1)S(1)}, u32[]{:S(2)}, u32[]{:S(2)}) collective-permute-start(bf16[96,128]{1,0:T(8,128)(2,1)S(1)} %get-tuple-element.15), channel_id=1, source_target_pairs={{0,8},{4,12},{8,0},{12,4},{1,9},{5,13},{9,1},{13,5},{2,10},{6,14},... | collective-permute-start | bytes 73736 | tf_op jit(solution)/shard_map/ppermute | solution.py:17
  23.0 0.3 collective-permute-start.5
  23.3 0.0 collective-permute-done.3
  23.3 2.0 %collective-permute-done.4 = bf16[96,128]{1,0:T(8,128)(2,1)S(1)} collective-permute-done((bf16[96,128]{1,0:T(8,128)(2,1)S(1)}, bf16[96,128]{1,0:T(8,128)(2,1)S(1)}, u32[]{:S(2)}, u32[]{:S(2)}) %collective-permute-start.4) | collective-permute-done | bytes 24608 | tf_op jit(solution)/shard_map/ppermute | solution.py:17
  25.4 0.9 %collective-permute-done.5 = bf16[96,128]{1,0:T(8,128)(2,1)S(1)} collective-permute-done((bf16[96,128]{1,0:T(8,128)(2,1)S(1)}, bf16[96,128]{1,0:T(8,128)(2,1)S(1)}, u32[]{:S(2)}, u32[]{:S(2)}) %collective-permute-start.5) | collective-permute-done | bytes 24608 | tf_op jit(solution)/shard_map/ppermute | solution.py:17
  26.3 1.5 %collective-permute-start.8 = (bf16[4,96,128]{2,1,0:T(8,128)(2,1)S(1)}, bf16[4,96,128]{2,1,0:T(8,128)(2,1)S(1)}, u32[]{:S(2)}, u32[]{:S(2)}) collective-permute-start(bf16[4,96,128]{2,1,0:T(8,128)(2,1)S(1)} %pad_maximum_fusion.refs_0_), channel_id=1, source_target_pairs={{0,3},{1,2},{2,1},{3,0},{4,7},{5,6},{6,5},{7,4},{8,11},{9,10},{10,... | collective-permute-start | bytes 294920 | tf_op jit(solution)/shard_map/ppermute | solution.py:17
  27.8 0.6 %collective-permute-start.7 = (bf16[4,96,128]{2,1,0:T(8,128)(2,1)S(1)}, bf16[4,96,128]{2,1,0:T(8,128)(2,1)S(1)}, u32[]{:S(2)}, u32[]{:S(2)}) collective-permute-start(bf16[4,96,128]{2,1,0:T(8,128)(2,1)S(1)} %pad_maximum_fusion.refs_0_), channel_id=1, source_target_pairs={{0,2},{1,3},{2,0},{3,1},{4,6},{5,7},{6,4},{7,5},{8,10},{9,11},{10,... | collective-permute-start | bytes 294920 | tf_op jit(solution)/shard_map/ppermute | solution.py:17
  28.5 2.3 %collective-permute-start.6 = (bf16[4,96,128]{2,1,0:T(8,128)(2,1)S(1)}, bf16[4,96,128]{2,1,0:T(8,128)(2,1)S(1)}, u32[]{:S(2)}, u32[]{:S(2)}) collective-permute-start(bf16[4,96,128]{2,1,0:T(8,128)(2,1)S(1)} %pad_maximum_fusion.refs_0_), channel_id=1, source_target_pairs={{0,1},{1,0},{2,3},{3,2},{4,5},{5,4},{6,7},{7,6},{8,9},{9,8},{10,11... | collective-permute-start | bytes 294920 | tf_op jit(solution)/shard_map/ppermute | solution.py:17
  30.8 3.2 %collective-permute-done.8.refs_3_ = bf16[4,96,128]{2,1,0:T(8,128)(2,1)S(1)} collective-permute-done((bf16[4,96,128]{2,1,0:T(8,128)(2,1)S(1)}, bf16[4,96,128]{2,1,0:T(8,128)(2,1)S(1)}, u32[]{:S(2)}, u32[]{:S(2)}) %collective-permute-start.8) | collective-permute-done | bytes 98336 | tf_op jit(solution)/shard_map/ppermute | solution.py:17
  33.9 3.9 %collective-permute-done.7.refs_2_ = bf16[4,96,128]{2,1,0:T(8,128)(2,1)S(1)} collective-permute-done((bf16[4,96,128]{2,1,0:T(8,128)(2,1)S(1)}, bf16[4,96,128]{2,1,0:T(8,128)(2,1)S(1)}, u32[]{:S(2)}, u32[]{:S(2)}) %collective-permute-start.7) | collective-permute-done | bytes 98336 | tf_op jit(solution)/shard_map/ppermute | solution.py:17
  37.8 0.0 collective-permute-done.6.refs_1_
  37.8 0.0 copy-start
  37.8 5.8 %copy-done = bf16[2048,4096]{1,0:T(8,128)(2,1)S(1)} copy-done((bf16[2048,4096]{1,0:T(8,128)(2,1)S(1)}, bf16[2048,4096]{1,0:T(8,128)(2,1)}, u32[]{:S(2)}) %copy-start) | copy-done | bytes 16777240
  43.6 3.4 %project.1 = (f32[4,4096]{1,0:T(4,128)S(1)}, bf16[4,4096]{1,0:T(4,128)(2,1)S(1)}, bf16[4,4096]{1,0:T(4,128)(2,1)S(1)}, bf16[4,4096]{1,0:T(4,128)(2,1)S(1)}) custom-call(bf16[4,96,128]{2,1,0:T(8,128)(2,1)S(1)} %pad_maximum_fusion.refs_0_, bf16[4,96,128]{2,1,0:T(8,128)(2,1)S(1)} %collective-permute-done.6.refs_1_, ...), custom_call_target="tpu_custom_call" | custom-call | flops 268435456 | bytes 16777216 | tf_op jit(solution)/shard_map/project/pallas_call | solution.py:228
  47.1 0.1 collective-permute-start.9
  47.1 0.8 %collective-permute-start.10 = (bf16[4,4096]{1,0:T(4,128)(2,1)S(1)}, bf16[4,4096]{1,0:T(4,128)(2,1)S(1)}, u32[]{:S(2)}, u32[]{:S(2)}) collective-permute-start(bf16[4,4096]{1,0:T(4,128)(2,1)S(1)} %get-tuple-element.19), channel_id=1, source_target_pairs={{0,8},{4,12},{8,0},{12,4},{1,9},{5,13},{9,1},{13,5},{2,10},{6,14},... | collective-permute-start | bytes 98312 | tf_op jit(solution)/shard_map/ppermute | solution.py:17
  47.9 1.0 %collective-permute-start.11 = (bf16[4,4096]{1,0:T(4,128)(2,1)S(1)}, bf16[4,4096]{1,0:T(4,128)(2,1)S(1)}, u32[]{:S(2)}, u32[]{:S(2)}) collective-permute-start(bf16[4,4096]{1,0:T(4,128)(2,1)S(1)} %get-tuple-element.20), channel_id=1, source_target_pairs={{0,12},{4,8},{8,4},{12,0},{1,13},{5,9},{9,5},{13,1},{2,14},{6,10},... | collective-permute-start | bytes 98312 | tf_op jit(solution)/shard_map/ppermute | solution.py:17
  49.0 0.0 collective-permute-done.9
  49.0 2.3 %collective-permute-done.10 = bf16[4,4096]{1,0:T(4,128)(2,1)S(1)} collective-permute-done((bf16[4,4096]{1,0:T(4,128)(2,1)S(1)}, bf16[4,4096]{1,0:T(4,128)(2,1)S(1)}, u32[]{:S(2)}, u32[]{:S(2)}) %collective-permute-start.10) | collective-permute-done | bytes 32800 | tf_op jit(solution)/shard_map/ppermute | solution.py:17
  51.3 0.3 collective-permute-done.11
  51.6 0.7 %add_convert_fusion = bf16[4,4096]{1,0:T(4,128)(2,1)} fusion(bf16[4,4096]{1,0:T(4,128)(2,1)S(1)} %collective-permute-done.11, bf16[4,4096]{1,0:T(4,128)(2,1)S(1)} %collective-permute-done.10, f32[4,4096]{1,0:T(4,128)S(1)} %get-tuple-element.17, bf16[4,4096]{1,0:T(4,128)(2,1)S(1)} %collective-permute-done.9), kind=kLoop, calls=%fused_computation.1 | loop fusion | flops 114688 | bytes 196608 | tf_op jit(solution)/shard_map/convert_element_type | solution.py:262
  (1 shorter events, 0.0 us)
Async XLA Ops:
  0.8 6.8 %collective-permute-start.2 = (bf16[64,128]{1,0:T(8,128)(2,1)S(1)}, bf16[64,128]{1,0:T(8,128)(2,1)S(1)}, u32[]{:S(2)}, u32[]{:S(2)}) collective-permute-start(bf16[64,128]{1,0:T(8,128)(2,1)S(1)} %bitcast.7), channel_id=1, source_target_pairs={{0,3},{1,2},{2,1},{3,0},{4,7},{5,6},{6,5},{7,4},{8,11},{9,10},{10,... | collective-permute-start | bytes 49160 | tf_op jit(solution)/shard_map/ppermute | solution.py:17
  6.0 4.6 %collective-permute-start.1 = (bf16[64,128]{1,0:T(8,128)(2,1)S(1)}, bf16[64,128]{1,0:T(8,128)(2,1)S(1)}, u32[]{:S(2)}, u32[]{:S(2)}) collective-permute-start(bf16[64,128]{1,0:T(8,128)(2,1)S(1)} %bitcast.8), channel_id=1, source_target_pairs={{0,2},{1,3},{2,0},{3,1},{4,6},{5,7},{6,4},{7,5},{8,10},{9,11},{10,... | collective-permute-start | bytes 49160 | tf_op jit(solution)/shard_map/ppermute | solution.py:17
  6.0 4.6 %collective-permute-start = (bf16[64,128]{1,0:T(8,128)(2,1)S(1)}, bf16[64,128]{1,0:T(8,128)(2,1)S(1)}, u32[]{:S(2)}, u32[]{:S(2)}) collective-permute-start(bf16[64,128]{1,0:T(8,128)(2,1)S(1)} %bitcast.9), channel_id=1, source_target_pairs={{0,1},{1,0},{2,3},{3,2},{4,5},{5,4},{6,7},{7,6},{8,9},{9,8},{10,11... | collective-permute-start | bytes 49160 | tf_op jit(solution)/shard_map/ppermute | solution.py:17
  10.6 1.4 %copy-start.1 = (bf16[1,1,6,4,128,256]{5,4,3,2,1,0:T(8,128)(2,1)S(1)}, bf16[1,1,6,4,128,256]{5,4,3,2,1,0:T(8,128)(2,1)}, u32[]{:S(2)}) copy-start(bf16[1,1,6,4,128,256]{5,4,3,2,1,0:T(8,128)(2,1)} %param.9) | copy-start | bytes 4718596
  12.0 0.7 %copy-start.2 = (bf16[1,1024]{1,0:T(2,128)(2,1)S(1)}, bf16[1,1024]{1,0:T(2,128)(2,1)}, u32[]{:S(2)}) copy-start(bf16[1,1024]{1,0:T(2,128)(2,1)} %refs_4_.2) | copy-start | bytes 6148
  12.7 0.7 %copy-start.3 = (s32[1,4,7]{2,1,0:T(4,128)S(1)}, s32[1,4,7]{2,1,0:T(4,128)}, u32[]{:S(2)}) copy-start(s32[1,4,7]{2,1,0:T(4,128)} %refs_5_.1) | copy-start | bytes 340
  13.4 0.7 %copy-start.4 = (s32[1,4,7]{2,1,0:T(4,128)S(1)}, s32[1,4,7]{2,1,0:T(4,128)}, u32[]{:S(2)}) copy-start(s32[1,4,7]{2,1,0:T(4,128)} %refs_6_.1) | copy-start | bytes 340
  14.1 0.7 %copy-start.5 = (s32[1,4]{1,0:T(1,128)S(1)}, s32[1,4]{1,0:T(1,128)}, u32[]{:S(2)}) copy-start(s32[1,4]{1,0:T(1,128)} %refs_7_.1) | copy-start | bytes 52
  21.4 1.9 %collective-permute-start.3 = (bf16[96,128]{1,0:T(8,128)(2,1)S(1)}, bf16[96,128]{1,0:T(8,128)(2,1)S(1)}, u32[]{:S(2)}, u32[]{:S(2)}) collective-permute-start(bf16[96,128]{1,0:T(8,128)(2,1)S(1)} %get-tuple-element.14), channel_id=1, source_target_pairs={{0,4},{4,0},{8,12},{12,8},{1,5},{5,1},{9,13},{13,9},{2,6},{6,2},{1... | collective-permute-start | bytes 73736 | tf_op jit(solution)/shard_map/ppermute | solution.py:17
  21.5 3.9 %collective-permute-start.4 = (bf16[96,128]{1,0:T(8,128)(2,1)S(1)}, bf16[96,128]{1,0:T(8,128)(2,1)S(1)}, u32[]{:S(2)}, u32[]{:S(2)}) collective-permute-start(bf16[96,128]{1,0:T(8,128)(2,1)S(1)} %get-tuple-element.15), channel_id=1, source_target_pairs={{0,8},{4,12},{8,0},{12,4},{1,9},{5,13},{9,1},{13,5},{2,10},{6,14},... | collective-permute-start | bytes 73736 | tf_op jit(solution)/shard_map/ppermute | solution.py:17
  23.0 3.3 %collective-permute-start.5 = (bf16[96,128]{1,0:T(8,128)(2,1)S(1)}, bf16[96,128]{1,0:T(8,128)(2,1)S(1)}, u32[]{:S(2)}, u32[]{:S(2)}) collective-permute-start(bf16[96,128]{1,0:T(8,128)(2,1)S(1)} %get-tuple-element.16), channel_id=1, source_target_pairs={{0,12},{4,8},{8,4},{12,0},{1,13},{5,9},{9,5},{13,1},{2,14},{6,10},... | collective-permute-start | bytes 73736 | tf_op jit(solution)/shard_map/ppermute | solution.py:17
  26.3 7.6 %collective-permute-start.8 = (bf16[4,96,128]{2,1,0:T(8,128)(2,1)S(1)}, bf16[4,96,128]{2,1,0:T(8,128)(2,1)S(1)}, u32[]{:S(2)}, u32[]{:S(2)}) collective-permute-start(bf16[4,96,128]{2,1,0:T(8,128)(2,1)S(1)} %pad_maximum_fusion.refs_0_), channel_id=1, source_target_pairs={{0,3},{1,2},{2,1},{3,0},{4,7},{5,6},{6,5},{7,4},{8,11},{9,10},{10,... | collective-permute-start | bytes 294920 | tf_op jit(solution)/shard_map/ppermute | solution.py:17
  27.8 10.0 %collective-permute-start.7 = (bf16[4,96,128]{2,1,0:T(8,128)(2,1)S(1)}, bf16[4,96,128]{2,1,0:T(8,128)(2,1)S(1)}, u32[]{:S(2)}, u32[]{:S(2)}) collective-permute-start(bf16[4,96,128]{2,1,0:T(8,128)(2,1)S(1)} %pad_maximum_fusion.refs_0_), channel_id=1, source_target_pairs={{0,2},{1,3},{2,0},{3,1},{4,6},{5,7},{6,4},{7,5},{8,10},{9,11},{10,... | collective-permute-start | bytes 294920 | tf_op jit(solution)/shard_map/ppermute | solution.py:17
  28.5 9.4 %collective-permute-start.6 = (bf16[4,96,128]{2,1,0:T(8,128)(2,1)S(1)}, bf16[4,96,128]{2,1,0:T(8,128)(2,1)S(1)}, u32[]{:S(2)}, u32[]{:S(2)}) collective-permute-start(bf16[4,96,128]{2,1,0:T(8,128)(2,1)S(1)} %pad_maximum_fusion.refs_0_), channel_id=1, source_target_pairs={{0,1},{1,0},{2,3},{3,2},{4,5},{5,4},{6,7},{7,6},{8,9},{9,8},{10,11... | collective-permute-start | bytes 294920 | tf_op jit(solution)/shard_map/ppermute | solution.py:17
  37.8 5.8 %copy-start = (bf16[2048,4096]{1,0:T(8,128)(2,1)S(1)}, bf16[2048,4096]{1,0:T(8,128)(2,1)}, u32[]{:S(2)}) copy-start(bf16[2048,4096]{1,0:T(8,128)(2,1)} %refs_4_.3) | copy-start | bytes 50331652
  47.1 1.9 %collective-permute-start.9 = (bf16[4,4096]{1,0:T(4,128)(2,1)S(1)}, bf16[4,4096]{1,0:T(4,128)(2,1)S(1)}, u32[]{:S(2)}, u32[]{:S(2)}) collective-permute-start(bf16[4,4096]{1,0:T(4,128)(2,1)S(1)} %get-tuple-element.18), channel_id=1, source_target_pairs={{0,4},{4,0},{8,12},{12,8},{1,5},{5,1},{9,13},{13,9},{2,6},{6,2},{1... | collective-permute-start | bytes 98312 | tf_op jit(solution)/shard_map/ppermute | solution.py:17
  47.1 4.2 %collective-permute-start.10 = (bf16[4,4096]{1,0:T(4,128)(2,1)S(1)}, bf16[4,4096]{1,0:T(4,128)(2,1)S(1)}, u32[]{:S(2)}, u32[]{:S(2)}) collective-permute-start(bf16[4,4096]{1,0:T(4,128)(2,1)S(1)} %get-tuple-element.19), channel_id=1, source_target_pairs={{0,8},{4,12},{8,0},{12,4},{1,9},{5,13},{9,1},{13,5},{2,10},{6,14},... | collective-permute-start | bytes 98312 | tf_op jit(solution)/shard_map/ppermute | solution.py:17
  47.9 3.7 %collective-permute-start.11 = (bf16[4,4096]{1,0:T(4,128)(2,1)S(1)}, bf16[4,4096]{1,0:T(4,128)(2,1)S(1)}, u32[]{:S(2)}, u32[]{:S(2)}) collective-permute-start(bf16[4,4096]{1,0:T(4,128)(2,1)S(1)} %get-tuple-element.20), channel_id=1, source_target_pairs={{0,12},{4,8},{8,4},{12,0},{1,13},{5,9},{9,5},{13,1},{2,14},{6,10},... | collective-permute-start | bytes 98312 | tf_op jit(solution)/shard_map/ppermute | solution.py:17

commit v2 on v1

v2 whole, which is shorter than its diff:
```python
import functools
import math

import jax
import jax.numpy as jnp
from jax import lax
from jax.experimental import pallas as pl
from jax.experimental.pallas import tpu as pltpu
from jax.sharding import PartitionSpec as P

very_negative = -1e30
MIB = 1 << 20


def swap(x, axis, offset):
    count = lax.axis_size(axis)
    return lax.ppermute(x, axis, [(i, i ^ offset) for i in range(count)])


def round_up(value, step):
    return -(-value // step) * step


def halves(x):
    return pltpu.roll(x, 64, 1)


def query_tiles(stacked, kv_heads):
    turned = stacked.astype(jnp.float32).T
    lane = lax.broadcasted_iota(jnp.int32, turned.shape, 1)
    group = 64 // kv_heads
    return [
        [
            jnp.where((lane >= a * 64 + h * group) & (lane < a * 64 + (h + 1) * group), turned, 0.0).astype(jnp.bfloat16)
            for a in range(2)
        ]
        for h in range(kv_heads)
    ]


def pair_scores(page_a, page_b, tiles, head_dim):
    total = None
    for h in range(len(tiles)):
        for a, page in enumerate((page_a, page_b)):
            part = jnp.dot(page[h, :, :head_dim], tiles[h][a], preferred_element_type=jnp.float32)
            total = part if total is None else total + part
    return total


def pair_softmax(scores, limit):
    token = lax.broadcasted_iota(jnp.int32, scores.shape, 0)
    mask = token < limit
    masked = jnp.where(mask, scores, very_negative)
    top = jnp.max(masked, axis=0, keepdims=True)
    weights = jnp.where(mask, jnp.exp(masked - top), 0.0)
    return top, jnp.sum(weights, axis=0, keepdims=True), weights


def pair_values(weights, page_a, page_b, head_dim):
    turned = weights.T.astype(jnp.bfloat16)
    kv_heads = page_a.shape[0]
    group = 64 // kv_heads
    blocks = []
    for a, page in enumerate((page_a, page_b)):
        for h in range(kv_heads):
            at = a * 64 + h * group
            blocks.append(
                jnp.dot(turned[at : at + group], page[h, :, head_dim:], preferred_element_type=jnp.float32)
            )
    return jnp.concatenate(blocks, axis=0)


def to_columns(rows):
    stacked = jnp.concatenate(rows + [jnp.zeros((128 - len(rows), 128), jnp.float32)], axis=0)
    return stacked.T


def own_kernel(n_req, own_pages, *refs):
    (q_ref, kv_hbm, slot_hbm, owner_hbm, len_hbm, pool_hbm) = refs[:6]
    acc_ref, log_ref, limit_ref, pages_ref = refs[6:10]
    kv, slots, owners, lens, pool, small_sem, pool_sem, page_sem = refs[10:]
    slot_count, kv_heads, page_len, width = pool_hbm.shape
    head_dim = width // 2
    entries = slot_hbm.shape[2]
    me = lax.axis_index("req")
    scale = 1.0 / math.sqrt(head_dim)
    small = [
        pltpu.make_async_copy(src, dst, small_sem.at[i])
        for i, (src, dst) in enumerate(((slot_hbm, slots), (owner_hbm, owners), (len_hbm, lens), (kv_hbm, kv)))
    ]
    for copy in small:
        copy.start()
    whole = pltpu.make_async_copy(pool_hbm, pool, pool_sem)
    whole.start()
    stacked = jnp.concatenate([q_ref[...], q_ref[...]], axis=0)
    tiles = query_tiles(stacked, kv_heads)
    for copy in small:
        copy.wait()

    fetched = []
    lane = lax.broadcasted_iota(jnp.int32, (1, 128), 1)
    limits = []
    for d in range(1, n_req):
        n = me ^ d
        length = lens[0, n]
        slot = jnp.int32(0)
        limit = jnp.int32(0)
        for j in range(entries):
            held = (owners[0, n, j] == me) & (j * page_len < length)
            slot = jnp.where(held, slots[0, n, j], slot)
            limit = jnp.where(held, length - j * page_len, limit)
        copy = pltpu.make_async_copy(pool_hbm.at[slot], pages_ref.at[d - 1], page_sem.at[d - 1])
        copy.start()
        fetched.append(copy)
        limits.append(limit)
    if len(limits) % 2:
        limits.append(jnp.int32(0))
    for p in range(len(limits) // 2):
        limit_ref[p : p + 1] = jnp.where(lane < 64, limits[2 * p], limits[2 * p + 1])

    my_length = lens[0, me]
    pages, valid = [], []
    for i in range(own_pages):
        held = (owners[0, me, i] == me) & (i * page_len < my_length)
        pages.append(pool.at[jnp.where(held, slots[0, me, i], 0)])
        valid.append(jnp.where(held, my_length - i * page_len, 0))
    if own_pages % 2:
        pages.append(pages[0])
        valid.append(jnp.int32(0))
    pairs = len(pages) // 2

    base = kv_heads * head_dim
    new_k = [kv[0:1, h * head_dim : (h + 1) * head_dim] for h in range(kv_heads)]
    self_score = None
    for h in range(kv_heads):
        both = tiles[h][0] + tiles[h][1]
        part = jnp.dot(jnp.broadcast_to(new_k[h], (16, head_dim)), both, preferred_element_type=jnp.float32)
        self_score = part if self_score is None else self_score + part
    self_score = self_score[0:1] * scale

    whole.wait()
    scores = [pair_scores(pages[2 * p], pages[2 * p + 1], tiles, head_dim) * scale for p in range(pairs)]
    tops, totals, sums = [], [], []
    for p in range(pairs):
        limit = jnp.where(lane < 64, valid[2 * p], valid[2 * p + 1])
        top, total, weights = pair_softmax(scores[p], limit)
        tops.append(top)
        totals.append(total)
        sums.append(pair_values(weights, pages[2 * p], pages[2 * p + 1], head_dim))
    top = functools.reduce(jnp.maximum, tops)
    top = jnp.maximum(jnp.maximum(top, halves(top)), self_score)
    factors = [jnp.exp(t - top) for t in tops]
    own_factor = jnp.exp(self_score - top)
    total = functools.reduce(jnp.add, [f * t for f, t in zip(factors, totals)])
    total = total + halves(total) + own_factor
    columns = to_columns([f / total for f in factors] + [own_factor / total])
    result = None
    for p in range(pairs):
        term = sums[p] * columns[:, p : p + 1]
        result = term if result is None else result + term
    group = 64 // kv_heads
    new_v = jnp.concatenate(
        [
            jnp.broadcast_to(kv[0:1, base + h * head_dim : base + (h + 1) * head_dim].astype(jnp.float32), (group, head_dim))
            for h in range(kv_heads)
        ],
        axis=0,
    )
    acc_ref[...] = result[:64] + result[64:] + columns[:64, pairs : pairs + 1] * new_v
    log_ref[...] = jnp.broadcast_to(top + jnp.log(total), log_ref.shape)
    for copy in fetched:
        copy.wait()


def own_attention(q, new_kv, page_slot, page_owner, context_len, pool, n_req):
    heads, head_dim = q.shape
    slots, kv_heads, page_len, width = pool.shape
    own_pages = min(slots, page_slot.shape[2])
    hbm = pl.BlockSpec(memory_space=pl.ANY)
    vmem = pl.BlockSpec(memory_space=pltpu.VMEM)
    pair_count = round_up(n_req - 1, 2) // 2
    page_bytes = pool.size * 2 // slots
    return pl.pallas_call(
        functools.partial(own_kernel, n_req, own_pages),
        out_shape=[
            jax.ShapeDtypeStruct((heads, head_dim), jnp.float32),
            jax.ShapeDtypeStruct((8, 128), jnp.float32),
            jax.ShapeDtypeStruct((round_up(pair_count, 8), 128), jnp.int32),
            jax.ShapeDtypeStruct((n_req - 1, kv_heads, page_len, width), pool.dtype),
        ],
        in_specs=[vmem] + [hbm] * 5,
        out_specs=[vmem] * 4,
        scratch_shapes=[
            pltpu.VMEM(new_kv.shape, new_kv.dtype),
            pltpu.SMEM(page_slot.shape, jnp.int32),
            pltpu.SMEM(page_owner.shape, jnp.int32),
            pltpu.SMEM(context_len.shape, jnp.int32),
            pltpu.VMEM(pool.shape, pool.dtype),
            pltpu.SemaphoreType.DMA((4,)),
            pltpu.SemaphoreType.DMA,
            pltpu.SemaphoreType.DMA((n_req - 1,)),
        ],
        compiler_params=pltpu.CompilerParams(vmem_limit_bytes=16 * MIB),
        cost_estimate=pl.CostEstimate(
            flops=4 * own_pages * page_len * heads * head_dim,
            bytes_accessed=page_bytes * (slots + n_req - 1) * 2,
            transcendentals=0,
        ),
        name="own_attention",
    )(q, new_kv, page_slot, page_owner, context_len, pool)


def stat_rows_of(n_req):
    return round_up(2 * n_req, 8)


def other_kernel(n_req, n_tp, *refs):
    q_refs = refs[: n_req - 1]
    acc_ref, log_ref, limit_ref, pages_ref = refs[n_req - 1 : n_req + 3]
    out_refs = refs[n_req + 3 : n_req + 3 + n_tp]
    results, logs, stats = refs[n_req + 3 + n_tp :]
    kv_heads, width = pages_ref.shape[1], pages_ref.shape[3]
    head_dim = width // 2
    heads = q_refs[0].shape[0]
    chunk = heads // n_tp
    my_tp = lax.axis_index("tp")
    scale = 1.0 / math.sqrt(head_dim)
    others = n_req - 1
    pairs = round_up(others, 2) // 2
    results[0] = acc_ref[...]
    logs[0:1] = log_ref[0:1]
    scores, members = [], []
    for p in range(pairs):
        a, b = 2 * p, min(2 * p + 1, others - 1)
        members.append((a, b))
        tiles = query_tiles(jnp.concatenate([q_refs[a][...], q_refs[b][...]], axis=0), kv_heads)
        scores.append(pair_scores(pages_ref.at[a], pages_ref.at[b], tiles, head_dim) * scale)
    sums, inverse, log_rows = [], [], []
    for p in range(pairs):
        a, b = members[p]
        top, total, weights = pair_softmax(scores[p], limit_ref[p : p + 1])
        sums.append(pair_values(weights, pages_ref.at[a], pages_ref.at[b], head_dim))
        total = jnp.where(total > 0.0, total, 1.0)
        inverse.append(1.0 / total)
        log_rows.append(top + jnp.log(total))
    columns = to_columns(inverse)
    for p in range(pairs):
        result = sums[p] * columns[:, p : p + 1]
        results[2 * p + 1] = result[:64]
        logs[2 * p + 1 : 2 * p + 2] = log_rows[p]
        if 2 * p + 1 < others:
            results[2 * p + 2] = result[64:]
            logs[2 * p + 2 : 2 * p + 3] = halves(log_rows[p])
    lane = lax.broadcasted_iota(jnp.int32, (n_req, 128), 1)
    value = logs[0:n_req]
    high = value.astype(jnp.bfloat16).astype(jnp.float32)
    rest = value - high
    middle = rest.astype(jnp.bfloat16).astype(jnp.float32)
    stats[...] = jnp.zeros_like(stats)
    stats[0:n_req] = jnp.where(lane < 64, high, halves(middle))
    stats[n_req : 2 * n_req] = jnp.where(lane < 64, rest - middle, 0.0)
    tail = stats[...].astype(jnp.bfloat16)
    rows = n_req * chunk
    for d in range(n_tp):
        at = pl.ds(pl.multiple_of((my_tp ^ d) * chunk, chunk), chunk)
        for k in range(n_req):
            out_refs[d][k * chunk : (k + 1) * chunk] = results[k, at].astype(jnp.bfloat16)
        out_refs[d][rows:] = tail


def other_attention(q_list, own, n_req, n_tp):
    heads, head_dim = q_list[0].shape
    chunk = heads // n_tp
    rows = n_req * chunk + stat_rows_of(n_req)
    vmem = pl.BlockSpec(memory_space=pltpu.VMEM)
    return pl.pallas_call(
        functools.partial(other_kernel, n_req, n_tp),
        out_shape=[jax.ShapeDtypeStruct((rows, head_dim), jnp.bfloat16)] * n_tp,
        in_specs=[vmem] * (n_req + 3),
        out_specs=[vmem] * n_tp,
        scratch_shapes=[
            pltpu.VMEM((n_req, heads, head_dim), jnp.float32),
            pltpu.VMEM((round_up(n_req, 8), 128), jnp.float32),
            pltpu.VMEM((stat_rows_of(n_req), 128), jnp.float32),
        ],
        compiler_params=pltpu.CompilerParams(vmem_limit_bytes=16 * MIB),
        cost_estimate=pl.CostEstimate(flops=2 * own[3].size * 16, bytes_accessed=own[3].size * 2, transcendentals=0),
        name="other_attention",
    )(*q_list, *own)


def load_kernel(after_ref, weight_hbm, out_ref, sems):
    depth = weight_hbm.shape[0]
    parts = sems.shape[0]
    step = depth // parts
    copies = [
        pltpu.make_async_copy(
            weight_hbm.at[pl.ds(i * step, step)], out_ref.at[pl.ds(i * step, step)], sems.at[i]
        )
        for i in range(parts)
    ]
    for copy in copies:
        copy.start()
    for copy in copies:
        copy.wait()


def load_weight(after, out_weight):
    return pl.pallas_call(
        load_kernel,
        out_shape=jax.ShapeDtypeStruct(out_weight.shape, out_weight.dtype),
        in_specs=[pl.BlockSpec(memory_space=pl.ANY)] * 2,
        out_specs=pl.BlockSpec(memory_space=pltpu.VMEM),
        scratch_shapes=[pltpu.SemaphoreType.DMA((8,))],
        compiler_params=pltpu.CompilerParams(vmem_limit_bytes=20 * MIB),
        cost_estimate=pl.CostEstimate(flops=0, bytes_accessed=out_weight.size * 4, transcendentals=0),
        name="load_weight",
    )(after, out_weight)


def project_kernel(n_req, n_tp, chunk, *refs):
    part_refs = refs[:n_req]
    weight_ref = refs[n_req]
    out_refs = refs[n_req + 1 : n_req + 1 + n_tp]
    wide, logs, attention, sums = refs[n_req + 1 + n_tp :]
    rows = n_req * chunk
    total_rows = n_tp * n_req
    columns = weight_ref.shape[1]
    my_tp = lax.axis_index("tp")
    me = lax.axis_index("req")
    for r in range(n_req):
        for c in range(n_tp):
            col = my_tp ^ c
            block = part_refs[r][c, :rows].astype(jnp.float32)
            tail = part_refs[r][c, rows:].astype(jnp.float32)
            value = (tail[:n_req] + halves(tail[:n_req])) + tail[n_req : 2 * n_req]
            for k in range(n_req):
                row = col * n_req + (me ^ r ^ k)
                wide[r, pl.ds(pl.multiple_of(row * chunk, chunk), chunk)] = block[k * chunk : (k + 1) * chunk]
                logs[r, pl.ds(row, 1)] = value[k : k + 1]
    shift = (128 - my_tp * chunk) % 128
    values = [pltpu.roll(logs[r], shift, 1) for r in range(n_req)]
    top = functools.reduce(jnp.maximum, values)
    factors = [jnp.exp(v - top) for v in values]
    total = functools.reduce(jnp.add, factors)
    factors = [f / total for f in factors]
    for h in range(chunk):
        block = None
        for r in range(n_req):
            term = wide[r, pl.ds(h, total_rows, stride=chunk)] * factors[r][:, h : h + 1]
            block = term if block is None else block + term
        attention[:, h * 128 : (h + 1) * 128] = block.astype(jnp.bfloat16)
    tile = min(columns, 512)

    @pl.loop(0, columns // tile)
    def _(t):
        at = pl.ds(pl.multiple_of(t * tile, tile), tile)
        product = jnp.dot(attention[...], weight_ref[:, at], preferred_element_type=jnp.float32)
        for c in range(n_tp):
            sums[c, :, at] = product[c * n_req : (c + 1) * n_req]

    for d in range(n_tp):
        out_refs[d][...] = sums[my_tp ^ d].astype(out_refs[d].dtype)


def project(parts, out_weight, n_req, n_tp, chunk):
    depth, columns = out_weight.shape
    rows = n_req * chunk
    vmem = pl.BlockSpec(memory_space=pltpu.VMEM)
    own = jax.ShapeDtypeStruct((n_req, columns), jnp.float32)
    sent = jax.ShapeDtypeStruct((n_req, columns), jnp.bfloat16)
    total_rows = n_tp * n_req
    return pl.pallas_call(
        functools.partial(project_kernel, n_req, n_tp, chunk),
        out_shape=[own] + [sent] * (n_tp - 1),
        in_specs=[vmem] * (n_req + 1),
        out_specs=[vmem] * n_tp,
        scratch_shapes=[
            pltpu.VMEM((n_req, n_tp * rows, 128), jnp.float32),
            pltpu.VMEM((n_req, total_rows, 128), jnp.float32),
            pltpu.VMEM((total_rows, depth), jnp.bfloat16),
            pltpu.VMEM((n_tp, n_req, columns), jnp.float32),
        ],
        compiler_params=pltpu.CompilerParams(vmem_limit_bytes=24 * MIB),
        cost_estimate=pl.CostEstimate(
            flops=2 * total_rows * depth * columns, bytes_accessed=out_weight.size * 2, transcendentals=0
        ),
        name="project",
    )(*parts, out_weight)


def on_device(queries, new_kv, cache_pool, page_slot, page_owner, context_len, out_weight):
    n_req = lax.axis_size("req")
    n_tp = lax.axis_size("tp")
    pool = cache_pool[0, 0]
    head_dim = pool.shape[3] // 2
    q = queries.reshape(-1, head_dim)
    chunk = q.shape[0] // n_tp
    q_list = [swap(q, "req", d) for d in range(1, n_req)]
    own = own_attention(q, new_kv, page_slot, page_owner, context_len, pool, n_req)
    pieces = other_attention(q_list, own, n_req, n_tp)
    arrived = jnp.stack([pieces[0]] + [swap(pieces[d], "tp", d) for d in range(1, n_tp)])
    parts = [arrived] + [swap(arrived, "req", d) for d in range(1, n_req)]
    weight = load_weight(arrived, out_weight)
    sums = project(parts, weight, n_req, n_tp, chunk)
    total = sums[0]
    for d in range(1, n_tp):
        total = total + swap(sums[d], "tp", d).astype(jnp.float32)
    return total.astype(jnp.bfloat16)


def solution(mesh):
    placed = (
        P(("groups", "tp", "req"), None),
        P(("groups", "tp", "req"), None),
        P(("groups", "tp"), "req", None, None, None, None),
        P(("groups", "tp"), None, None),
        P(("groups", "tp"), None, None),
        P(("groups", "tp"), None),
        P("tp", "req"),
    )
    return jax.shard_map(
        on_device, mesh=mesh, in_specs=placed, out_specs=P(("groups", "tp"), "req"), check_vma=False
    )
```

time: 52.6 us -> 38.8 us (0.74)
  waiting for transfers between devices: 16.7 us -> 5.52 us
  Pallas kernels: 10.1 us -> 7.33 us
    ppermute x12, waiting for transfers between devices: 16.7 us -> 5.52 us  [swap(): return lax.ppermute(x, axis, [(i, i ^ offset) for i in range(count)])]
    pallas_call x1 -> x3, Pallas kernels: 6.66 us -> 3.74 us  [the longest x1 1.82 us: own_attention(): pl.pallas_call(functools.partial(own_kernel, n_req, own_pages), out_shape...]
  transfers between devices with their start and end apart: 12 -> 12, of which waited for: 8 -> 3; matrix products, arithmetic and copies ran while one was open for 0% -> 0% of each run, Pallas kernels for 0% -> 8%
where the time goes in v2:
time: 38.8 us; the launch traced here: 38.4 us
  starting transfers between devices  14.1 us (36%)
  local copies, waits for them, and re-layouts  9.88 us (25%)
  Pallas kernels  7.33 us (19%)
  waiting for transfers between devices  5.52 us (14%)
  other arithmetic  1.51 us (4%)
    ppermute x12, starting transfers between devices, swap(): return lax.ppermute(x, axis, [(i, i ^ offset) for i in range(count)])  14.1 us
    unnamed x12, local copies, waits for them, and re-layouts  9.88 us
    ppermute x12, waiting for transfers between devices, swap(): return lax.ppermute(x, axis, [(i, i ^ offset) for i in range(count)])  5.52 us
    pallas_call x1, Pallas kernels, project(): pl.pallas_call(functools.partial(project_kernel, n_req, n_tp, chunk), out...  3.59 us
    pallas_call x1, Pallas kernels, own_attention(): pl.pallas_call(functools.partial(own_kernel, n_req, own_pages), out_shape...  1.82 us
    pallas_call x1, Pallas kernels, load_weight(): pl.pallas_call(load_kernel, out_shape=jax.ShapeDtypeStruct(out_weight.sha...  1.2 us
    unnamed x1, other arithmetic  0.85 us
  transfers between devices with their start and end apart: 12, of which 3 were waited for; matrix products, arithmetic and copies ran while one was open for 0% of the time, Pallas kernels for 8%

profile of v2, /device:TPU:0, one launch (start us, length us, event | category | flops | bytes accessed | tf_op | source)
XLA Modules:
  0.0 38.4 jit_solution(911225156723485935)
XLA Ops:
  0.0 0.8 %reduce = bf16[8192]{0:T(1024)(128)(2,1)S(1)} reduce(bf16[1,8192]{1,0:T(2,128)(2,1)} %param.7, bf16[]{:T(256)} %constant.6), dimensions={0}, to_apply=%param.7.reduce_sub_computation | reduce | bytes 32770 | tf_op args[0]
  0.8 5.1 %collective-permute-start.2 = (bf16[64,128]{1,0:T(8,128)(2,1)S(1)}, bf16[64,128]{1,0:T(8,128)(2,1)S(1)}, u32[]{:S(2)}, u32[]{:S(2)}) collective-permute-start(bf16[64,128]{1,0:T(8,128)(2,1)S(1)} %bitcast.7), channel_id=1, source_target_pairs={{0,3},{1,2},{2,1},{3,0},{4,7},{5,6},{6,5},{7,4},{8,11},{9,10},{10,... | collective-permute-start | bytes 49160 | tf_op jit(solution)/shard_map/ppermute | solution.py:17
  6.0 0.0 collective-permute-start.1
  6.0 0.6 %collective-permute-start = (bf16[64,128]{1,0:T(8,128)(2,1)S(1)}, bf16[64,128]{1,0:T(8,128)(2,1)S(1)}, u32[]{:S(2)}, u32[]{:S(2)}) collective-permute-start(bf16[64,128]{1,0:T(8,128)(2,1)S(1)} %bitcast.9), channel_id=1, source_target_pairs={{0,1},{1,0},{2,3},{3,2},{4,5},{5,4},{6,7},{7,6},{8,9},{9,8},{10,11... | collective-permute-start | bytes 49160 | tf_op jit(solution)/shard_map/ppermute | solution.py:17
  6.6 0.0 copy-start.1
  6.6 1.4 %copy-done.1 = bf16[1,1,6,4,128,256]{5,4,3,2,1,0:T(8,128)(2,1)S(1)} copy-done((bf16[1,1,6,4,128,256]{5,4,3,2,1,0:T(8,128)(2,1)S(1)}, bf16[1,1,6,4,128,256]{5,4,3,2,1,0:T(8,128)(2,1)}, u32[]{:S(2)}) %copy-start.1) | copy-done | bytes 1572888
  8.0 0.0 copy-start.2
  8.0 0.7 %copy-done.2 = bf16[1,1024]{1,0:T(2,128)(2,1)S(1)} copy-done((bf16[1,1024]{1,0:T(2,128)(2,1)S(1)}, bf16[1,1024]{1,0:T(2,128)(2,1)}, u32[]{:S(2)}) %copy-start.2) | copy-done | bytes 2072
  8.7 0.0 copy-start.3
  8.7 0.7 %copy-done.3 = s32[1,4,7]{2,1,0:T(4,128)S(1)} copy-done((s32[1,4,7]{2,1,0:T(4,128)S(1)}, s32[1,4,7]{2,1,0:T(4,128)}, u32[]{:S(2)}) %copy-start.3) | copy-done | bytes 136
  9.4 0.0 copy-start.4
  9.4 0.7 %copy-done.4 = s32[1,4,7]{2,1,0:T(4,128)S(1)} copy-done((s32[1,4,7]{2,1,0:T(4,128)S(1)}, s32[1,4,7]{2,1,0:T(4,128)}, u32[]{:S(2)}) %copy-start.4) | copy-done | bytes 136
  10.1 0.0 copy-start.5
  10.1 0.7 %copy-done.5 = s32[1,4]{1,0:T(1,128)S(1)} copy-done((s32[1,4]{1,0:T(1,128)S(1)}, s32[1,4]{1,0:T(1,128)}, u32[]{:S(2)}) %copy-start.5) | copy-done | bytes 40
  10.7 1.8 %own_attention.1 = (f32[64,128]{1,0:T(8,128)S(1)}, f32[8,128]{1,0:T(8,128)S(1)}, s32[8,128]{1,0:T(8,128)S(1)}, bf16[3,4,128,256]{3,2,1,0:T(8,128)(2,1)S(1)}) custom-call(bf16[64,128]{1,0:T(8,128)(2,1)S(1)} %bitcast.10, bf16[1,1024]{1,0:T(2,128)(2,1)S(1)} %copy-done.2, s32[1,4,7]{2,1,0:T(4,128)S(1)} %copy-done.3, s32[1,4,7]{2,1,0:T(4,128)S(1)} %copy-done.4, ...), custom_call_target="tpu_custom_call" | custom-call | flops 25165824 | bytes 4718592 | tf_op jit(solution)/shard_map/own_attention/pallas_call | solution.py:183
  12.6 0.0 collective-permute-done.2.refs_2_
  12.6 0.0 collective-permute-done.1.refs_1_
  12.6 0.0 collective-permute-done.refs_0_
  12.6 0.7 %other_attention.1 = (bf16[72,128]{1,0:T(8,128)(2,1)S(1)}, bf16[72,128]{1,0:T(8,128)(2,1)S(1)}, bf16[72,128]{1,0:T(8,128)(2,1)S(1)}, bf16[72,128]{1,0:T(8,128)(2,1)S(1)}) custom-call(bf16[64,128]{1,0:T(8,128)(2,1)S(1)} %collective-permute-done.refs_0_, bf16[64,128]{1,0:T(8,128)(2,1)S(1)} %collective-permute-done.1.refs_1_, ...), custom_call_target="tpu_custom_call" | custom-call | flops 12582912 | bytes 786432 | tf_op jit(solution)/shard_map/other_attention/pallas_call | solution.py:276
  13.3 0.1 collective-permute-start.3
  13.4 1.7 %collective-permute-start.4 = (bf16[72,128]{1,0:T(8,128)(2,1)S(1)}, bf16[72,128]{1,0:T(8,128)(2,1)S(1)}, u32[]{:S(2)}, u32[]{:S(2)}) collective-permute-start(bf16[72,128]{1,0:T(8,128)(2,1)S(1)} %get-tuple-element.23), channel_id=1, source_target_pairs={{0,8},{4,12},{8,0},{12,4},{1,9},{5,13},{9,1},{13,5},{2,10},{6,14},... | collective-permute-start | bytes 55304 | tf_op jit(solution)/shard_map/ppermute | solution.py:17
  15.1 0.2 collective-permute-start.5
  15.2 0.0 collective-permute-done.3
  15.3 2.0 %collective-permute-done.4 = bf16[72,128]{1,0:T(8,128)(2,1)S(1)} collective-permute-done((bf16[72,128]{1,0:T(8,128)(2,1)S(1)}, bf16[72,128]{1,0:T(8,128)(2,1)S(1)}, u32[]{:S(2)}, u32[]{:S(2)}) %collective-permute-start.4) | collective-permute-done | bytes 18464 | tf_op jit(solution)/shard_map/ppermute | solution.py:17
  17.2 1.1 %collective-permute-done.5 = bf16[72,128]{1,0:T(8,128)(2,1)S(1)} collective-permute-done((bf16[72,128]{1,0:T(8,128)(2,1)S(1)}, bf16[72,128]{1,0:T(8,128)(2,1)S(1)}, u32[]{:S(2)}, u32[]{:S(2)}) %collective-permute-start.5) | collective-permute-done | bytes 18464 | tf_op jit(solution)/shard_map/ppermute | solution.py:17
  18.3 3.7 %collective-permute-start.8 = (bf16[4,72,128]{2,1,0:T(8,128)(2,1)S(1)}, bf16[4,72,128]{2,1,0:T(8,128)(2,1)S(1)}, u32[]{:S(2)}, u32[]{:S(2)}) collective-permute-start(bf16[4,72,128]{2,1,0:T(8,128)(2,1)S(1)} %pad_maximum_fusion.after_ref.refs_0_), channel_id=1, source_target_pairs={{0,3},{1,2},{2,1},{3,0},{4,7},{5,6},{6,5},{7,4},{8,11},{9,10},{10,... | collective-permute-start | bytes 221192 | tf_op jit(solution)/shard_map/ppermute | solution.py:17
  22.0 0.0 collective-permute-start.7
  22.0 0.8 %collective-permute-start.6 = (bf16[4,72,128]{2,1,0:T(8,128)(2,1)S(1)}, bf16[4,72,128]{2,1,0:T(8,128)(2,1)S(1)}, u32[]{:S(2)}, u32[]{:S(2)}) collective-permute-start(bf16[4,72,128]{2,1,0:T(8,128)(2,1)S(1)} %pad_maximum_fusion.after_ref.refs_0_), channel_id=1, source_target_pairs={{0,1},{1,0},{2,3},{3,2},{4,5},{5,4},{6,7},{7,6},{8,9},{9,8},{10,11... | collective-permute-start | bytes 221192 | tf_op jit(solution)/shard_map/ppermute | solution.py:17
  22.8 0.0 copy-start
  22.8 5.8 %copy-done = bf16[2048,4096]{1,0:T(8,128)(2,1)S(1)} copy-done((bf16[2048,4096]{1,0:T(8,128)(2,1)S(1)}, bf16[2048,4096]{1,0:T(8,128)(2,1)}, u32[]{:S(2)}) %copy-start) | copy-done | bytes 16777240
  28.5 1.2 %load_weight.1.refs_4_ = bf16[2048,4096]{1,0:T(8,128)(2,1)S(1)} custom-call(bf16[4,72,128]{2,1,0:T(8,128)(2,1)S(1)} %pad_maximum_fusion.after_ref.refs_0_, bf16[2048,4096]{1,0:T(8,128)(2,1)S(1)} %copy-done), custom_call_target="tpu_custom_call" | custom-call | bytes 33554432 | tf_op jit(solution)/shard_map/load_weight/pallas_call | solution.py:309
  29.7 0.0 collective-permute-done.8.refs_3_
  29.7 0.0 collective-permute-done.7.refs_2_
  29.8 0.0 collective-permute-done.6.refs_1_
  29.8 3.6 %project.1 = (f32[4,4096]{1,0:T(4,128)S(1)}, bf16[4,4096]{1,0:T(4,128)(2,1)S(1)}, bf16[4,4096]{1,0:T(4,128)(2,1)S(1)}, bf16[4,4096]{1,0:T(4,128)(2,1)S(1)}) custom-call(bf16[4,72,128]{2,1,0:T(8,128)(2,1)S(1)} %pad_maximum_fusion.after_ref.refs_0_, bf16[4,72,128]{2,1,0:T(8,128)(2,1)S(1)} %collective-permute-done.6.refs_1_, ...), custom_call_target="tpu_custom_call" | custom-call | flops 268435456 | bytes 16777216 | tf_op jit(solution)/shard_map/project/pallas_call | solution.py:373
  33.4 0.1 collective-permute-start.9
  33.4 0.6 %collective-permute-start.10 = (bf16[4,4096]{1,0:T(4,128)(2,1)S(1)}, bf16[4,4096]{1,0:T(4,128)(2,1)S(1)}, u32[]{:S(2)}, u32[]{:S(2)}) collective-permute-start(bf16[4,4096]{1,0:T(4,128)(2,1)S(1)} %get-tuple-element.27), channel_id=1, source_target_pairs={{0,8},{4,12},{8,0},{12,4},{1,9},{5,13},{9,1},{13,5},{2,10},{6,14},... | collective-permute-start | bytes 98312 | tf_op jit(solution)/shard_map/ppermute | solution.py:17
  34.1 1.2 %collective-permute-start.11 = (bf16[4,4096]{1,0:T(4,128)(2,1)S(1)}, bf16[4,4096]{1,0:T(4,128)(2,1)S(1)}, u32[]{:S(2)}, u32[]{:S(2)}) collective-permute-start(bf16[4,4096]{1,0:T(4,128)(2,1)S(1)} %get-tuple-element.28), channel_id=1, source_target_pairs={{0,12},{4,8},{8,4},{12,0},{1,13},{5,9},{9,5},{13,1},{2,14},{6,10},... | collective-permute-start | bytes 98312 | tf_op jit(solution)/shard_map/ppermute | solution.py:17
  35.3 0.0 collective-permute-done.9
  35.3 2.5 %collective-permute-done.10 = bf16[4,4096]{1,0:T(4,128)(2,1)S(1)} collective-permute-done((bf16[4,4096]{1,0:T(4,128)(2,1)S(1)}, bf16[4,4096]{1,0:T(4,128)(2,1)S(1)}, u32[]{:S(2)}, u32[]{:S(2)}) %collective-permute-start.10) | collective-permute-done | bytes 32800 | tf_op jit(solution)/shard_map/ppermute | solution.py:17
  37.8 0.0 collective-permute-done.11
  37.8 0.7 %add_convert_fusion = bf16[4,4096]{1,0:T(4,128)(2,1)} fusion(bf16[4,4096]{1,0:T(4,128)(2,1)S(1)} %collective-permute-done.11, bf16[4,4096]{1,0:T(4,128)(2,1)S(1)} %collective-permute-done.10, f32[4,4096]{1,0:T(4,128)S(1)} %get-tuple-element.25, bf16[4,4096]{1,0:T(4,128)(2,1)S(1)} %collective-permute-done.9), kind=kLoop, calls=%fused_computation.1 | loop fusion | flops 114688 | bytes 196608 | tf_op jit(solution)/shard_map/convert_element_type | solution.py:409
  (1 shorter events, 0.0 us)
Async XLA Ops:
  0.8 11.7 %collective-permute-start.2 = (bf16[64,128]{1,0:T(8,128)(2,1)S(1)}, bf16[64,128]{1,0:T(8,128)(2,1)S(1)}, u32[]{:S(2)}, u32[]{:S(2)}) collective-permute-start(bf16[64,128]{1,0:T(8,128)(2,1)S(1)} %bitcast.7), channel_id=1, source_target_pairs={{0,3},{1,2},{2,1},{3,0},{4,7},{5,6},{6,5},{7,4},{8,11},{9,10},{10,... | collective-permute-start | bytes 49160 | tf_op jit(solution)/shard_map/ppermute | solution.py:17
  6.0 6.6 %collective-permute-start.1 = (bf16[64,128]{1,0:T(8,128)(2,1)S(1)}, bf16[64,128]{1,0:T(8,128)(2,1)S(1)}, u32[]{:S(2)}, u32[]{:S(2)}) collective-permute-start(bf16[64,128]{1,0:T(8,128)(2,1)S(1)} %bitcast.8), channel_id=1, source_target_pairs={{0,2},{1,3},{2,0},{3,1},{4,6},{5,7},{6,4},{7,5},{8,10},{9,11},{10,... | collective-permute-start | bytes 49160 | tf_op jit(solution)/shard_map/ppermute | solution.py:17
  6.0 6.6 %collective-permute-start = (bf16[64,128]{1,0:T(8,128)(2,1)S(1)}, bf16[64,128]{1,0:T(8,128)(2,1)S(1)}, u32[]{:S(2)}, u32[]{:S(2)}) collective-permute-start(bf16[64,128]{1,0:T(8,128)(2,1)S(1)} %bitcast.9), channel_id=1, source_target_pairs={{0,1},{1,0},{2,3},{3,2},{4,5},{5,4},{6,7},{7,6},{8,9},{9,8},{10,11... | collective-permute-start | bytes 49160 | tf_op jit(solution)/shard_map/ppermute | solution.py:17
  6.6 1.4 %copy-start.1 = (bf16[1,1,6,4,128,256]{5,4,3,2,1,0:T(8,128)(2,1)S(1)}, bf16[1,1,6,4,128,256]{5,4,3,2,1,0:T(8,128)(2,1)}, u32[]{:S(2)}) copy-start(bf16[1,1,6,4,128,256]{5,4,3,2,1,0:T(8,128)(2,1)} %param.9) | copy-start | bytes 4718596
  8.0 0.7 %copy-start.2 = (bf16[1,1024]{1,0:T(2,128)(2,1)S(1)}, bf16[1,1024]{1,0:T(2,128)(2,1)}, u32[]{:S(2)}) copy-start(bf16[1,1024]{1,0:T(2,128)(2,1)} %refs_1_.1) | copy-start | bytes 6148
  8.7 0.7 %copy-start.3 = (s32[1,4,7]{2,1,0:T(4,128)S(1)}, s32[1,4,7]{2,1,0:T(4,128)}, u32[]{:S(2)}) copy-start(s32[1,4,7]{2,1,0:T(4,128)} %refs_2_.1) | copy-start | bytes 340
  9.4 0.7 %copy-start.4 = (s32[1,4,7]{2,1,0:T(4,128)S(1)}, s32[1,4,7]{2,1,0:T(4,128)}, u32[]{:S(2)}) copy-start(s32[1,4,7]{2,1,0:T(4,128)} %refs_3_.1) | copy-start | bytes 340
  10.1 0.7 %copy-start.5 = (s32[1,4]{1,0:T(1,128)S(1)}, s32[1,4]{1,0:T(1,128)}, u32[]{:S(2)}) copy-start(s32[1,4]{1,0:T(1,128)} %refs_4_.1) | copy-start | bytes 52
  13.3 1.9 %collective-permute-start.3 = (bf16[72,128]{1,0:T(8,128)(2,1)S(1)}, bf16[72,128]{1,0:T(8,128)(2,1)S(1)}, u32[]{:S(2)}, u32[]{:S(2)}) collective-permute-start(bf16[72,128]{1,0:T(8,128)(2,1)S(1)} %get-tuple-element.22), channel_id=1, source_target_pairs={{0,4},{4,0},{8,12},{12,8},{1,5},{5,1},{9,13},{13,9},{2,6},{6,2},{1... | collective-permute-start | bytes 55304 | tf_op jit(solution)/shard_map/ppermute | solution.py:17
  13.4 3.8 %collective-permute-start.4 = (bf16[72,128]{1,0:T(8,128)(2,1)S(1)}, bf16[72,128]{1,0:T(8,128)(2,1)S(1)}, u32[]{:S(2)}, u32[]{:S(2)}) collective-permute-start(bf16[72,128]{1,0:T(8,128)(2,1)S(1)} %get-tuple-element.23), channel_id=1, source_target_pairs={{0,8},{4,12},{8,0},{12,4},{1,9},{5,13},{9,1},{13,5},{2,10},{6,14},... | collective-permute-start | bytes 55304 | tf_op jit(solution)/shard_map/ppermute | solution.py:17
  15.1 3.2 %collective-permute-start.5 = (bf16[72,128]{1,0:T(8,128)(2,1)S(1)}, bf16[72,128]{1,0:T(8,128)(2,1)S(1)}, u32[]{:S(2)}, u32[]{:S(2)}) collective-permute-start(bf16[72,128]{1,0:T(8,128)(2,1)S(1)} %get-tuple-element.24), channel_id=1, source_target_pairs={{0,12},{4,8},{8,4},{12,0},{1,13},{5,9},{9,5},{13,1},{2,14},{6,10},... | collective-permute-start | bytes 55304 | tf_op jit(solution)/shard_map/ppermute | solution.py:17
  18.3 11.4 %collective-permute-start.8 = (bf16[4,72,128]{2,1,0:T(8,128)(2,1)S(1)}, bf16[4,72,128]{2,1,0:T(8,128)(2,1)S(1)}, u32[]{:S(2)}, u32[]{:S(2)}) collective-permute-start(bf16[4,72,128]{2,1,0:T(8,128)(2,1)S(1)} %pad_maximum_fusion.after_ref.refs_0_), channel_id=1, source_target_pairs={{0,3},{1,2},{2,1},{3,0},{4,7},{5,6},{6,5},{7,4},{8,11},{9,10},{10,... | collective-permute-start | bytes 221192 | tf_op jit(solution)/shard_map/ppermute | solution.py:17
  22.0 7.8 %collective-permute-start.7 = (bf16[4,72,128]{2,1,0:T(8,128)(2,1)S(1)}, bf16[4,72,128]{2,1,0:T(8,128)(2,1)S(1)}, u32[]{:S(2)}, u32[]{:S(2)}) collective-permute-start(bf16[4,72,128]{2,1,0:T(8,128)(2,1)S(1)} %pad_maximum_fusion.after_ref.refs_0_), channel_id=1, source_target_pairs={{0,2},{1,3},{2,0},{3,1},{4,6},{5,7},{6,4},{7,5},{8,10},{9,11},{10,... | collective-permute-start | bytes 221192 | tf_op jit(solution)/shard_map/ppermute | solution.py:17
  22.0 7.8 %collective-permute-start.6 = (bf16[4,72,128]{2,1,0:T(8,128)(2,1)S(1)}, bf16[4,72,128]{2,1,0:T(8,128)(2,1)S(1)}, u32[]{:S(2)}, u32[]{:S(2)}) collective-permute-start(bf16[4,72,128]{2,1,0:T(8,128)(2,1)S(1)} %pad_maximum_fusion.after_ref.refs_0_), channel_id=1, source_target_pairs={{0,1},{1,0},{2,3},{3,2},{4,5},{5,4},{6,7},{7,6},{8,9},{9,8},{10,11... | collective-permute-start | bytes 221192 | tf_op jit(solution)/shard_map/ppermute | solution.py:17
  22.8 5.8 %copy-start = (bf16[2048,4096]{1,0:T(8,128)(2,1)S(1)}, bf16[2048,4096]{1,0:T(8,128)(2,1)}, u32[]{:S(2)}) copy-start(bf16[2048,4096]{1,0:T(8,128)(2,1)} %weight_hbm.1) | copy-start | bytes 50331652
  33.4 1.9 %collective-permute-start.9 = (bf16[4,4096]{1,0:T(4,128)(2,1)S(1)}, bf16[4,4096]{1,0:T(4,128)(2,1)S(1)}, u32[]{:S(2)}, u32[]{:S(2)}) collective-permute-start(bf16[4,4096]{1,0:T(4,128)(2,1)S(1)} %get-tuple-element.26), channel_id=1, source_target_pairs={{0,4},{4,0},{8,12},{12,8},{1,5},{5,1},{9,13},{13,9},{2,6},{6,2},{1... | collective-permute-start | bytes 98312 | tf_op jit(solution)/shard_map/ppermute | solution.py:17
  33.4 4.3 %collective-permute-start.10 = (bf16[4,4096]{1,0:T(4,128)(2,1)S(1)}, bf16[4,4096]{1,0:T(4,128)(2,1)S(1)}, u32[]{:S(2)}, u32[]{:S(2)}) collective-permute-start(bf16[4,4096]{1,0:T(4,128)(2,1)S(1)} %get-tuple-element.27), channel_id=1, source_target_pairs={{0,8},{4,12},{8,0},{12,4},{1,9},{5,13},{9,1},{13,5},{2,10},{6,14},... | collective-permute-start | bytes 98312 | tf_op jit(solution)/shard_map/ppermute | solution.py:17
  34.1 3.7 %collective-permute-start.11 = (bf16[4,4096]{1,0:T(4,128)(2,1)S(1)}, bf16[4,4096]{1,0:T(4,128)(2,1)S(1)}, u32[]{:S(2)}, u32[]{:S(2)}) collective-permute-start(bf16[4,4096]{1,0:T(4,128)(2,1)S(1)} %get-tuple-element.28), channel_id=1, source_target_pairs={{0,12},{4,8},{8,4},{12,0},{1,13},{5,9},{9,5},{13,1},{2,14},{6,10},... | collective-permute-start | bytes 98312 | tf_op jit(solution)/shard_map/ppermute | solution.py:17

commit v3 on v2

--- a/solution.py
+++ b/solution.py
@@ -17,6 +17,10 @@
     return lax.ppermute(x, axis, [(i, i ^ offset) for i in range(count)])
 
 
+def in_hbm(x):
+    return pltpu.with_memory_space_constraint(x, pltpu.HBM)
+
+
 def round_up(value, step):
     return -(-value // step) * step
 
@@ -25,8 +29,14 @@
     return pltpu.roll(x, 64, 1)
 
 
+def lay_rows(target, start, q_ref):
+    head_dim = target.shape[1]
+    for h in range(64):
+        target[start + h : start + h + 1] = q_ref[0:1, h * head_dim : (h + 1) * head_dim].astype(jnp.float32)
+
+
 def query_tiles(stacked, kv_heads):
-    turned = stacked.astype(jnp.float32).T
+    turned = stacked.T
     lane = lax.broadcasted_iota(jnp.int32, turned.shape, 1)
     group = 64 // kv_heads
     return [
@@ -76,9 +86,9 @@
 
 
 def own_kernel(n_req, own_pages, *refs):
-    (q_ref, kv_hbm, slot_hbm, owner_hbm, len_hbm, pool_hbm) = refs[:6]
+    (q_hbm, kv_hbm, slot_hbm, owner_hbm, len_hbm, pool_hbm) = refs[:6]
     acc_ref, log_ref, limit_ref, pages_ref = refs[6:10]
-    kv, slots, owners, lens, pool, small_sem, pool_sem, page_sem = refs[10:]
+    q_row, q_heads, kv, slots, owners, lens, pool, small_sem, pool_sem, page_sem = refs[10:]
     slot_count, kv_heads, page_len, width = pool_hbm.shape
     head_dim = width // 2
     entries = slot_hbm.shape[2]
@@ -86,14 +96,14 @@
     scale = 1.0 / math.sqrt(head_dim)
     small = [
         pltpu.make_async_copy(src, dst, small_sem.at[i])
-        for i, (src, dst) in enumerate(((slot_hbm, slots), (owner_hbm, owners), (len_hbm, lens), (kv_hbm, kv)))
+        for i, (src, dst) in enumerate(
+            ((slot_hbm, slots), (owner_hbm, owners), (len_hbm, lens), (kv_hbm, kv), (q_hbm, q_row))
+        )
     ]
     for copy in small:
         copy.start()
     whole = pltpu.make_async_copy(pool_hbm, pool, pool_sem)
     whole.start()
-    stacked = jnp.concatenate([q_ref[...], q_ref[...]], axis=0)
-    tiles = query_tiles(stacked, kv_heads)
     for copy in small:
         copy.wait()
 
@@ -118,6 +128,9 @@
     for p in range(len(limits) // 2):
         limit_ref[p : p + 1] = jnp.where(lane < 64, limits[2 * p], limits[2 * p + 1])
 
+    lay_rows(q_heads, 0, q_row)
+    q_heads[64:] = q_heads[:64]
+    tiles = query_tiles(q_heads[...], kv_heads)
     my_length = lens[0, me]
     pages, valid = [], []
     for i in range(own_pages):
@@ -173,10 +186,11 @@
 
 
 def own_attention(q, new_kv, page_slot, page_owner, context_len, pool, n_req):
-    heads, head_dim = q.shape
     slots, kv_heads, page_len, width = pool.shape
+    head_dim = width // 2
+    heads = q.shape[1] // head_dim
     own_pages = min(slots, page_slot.shape[2])
-    hbm = pl.BlockSpec(memory_space=pl.ANY)
+    hbm = pl.BlockSpec(memory_space=pltpu.HBM)
     vmem = pl.BlockSpec(memory_space=pltpu.VMEM)
     pair_count = round_up(n_req - 1, 2) // 2
     page_bytes = pool.size * 2 // slots
@@ -188,15 +202,17 @@
             jax.ShapeDtypeStruct((round_up(pair_count, 8), 128), jnp.int32),
             jax.ShapeDtypeStruct((n_req - 1, kv_heads, page_len, width), pool.dtype),
         ],
-        in_specs=[vmem] + [hbm] * 5,
+        in_specs=[hbm] * 6,
         out_specs=[vmem] * 4,
         scratch_shapes=[
+            pltpu.VMEM(q.shape, q.dtype),
+            pltpu.VMEM((128, head_dim), jnp.float32),
             pltpu.VMEM(new_kv.shape, new_kv.dtype),
             pltpu.SMEM(page_slot.shape, jnp.int32),
             pltpu.SMEM(page_owner.shape, jnp.int32),
             pltpu.SMEM(context_len.shape, jnp.int32),
             pltpu.VMEM(pool.shape, pool.dtype),
-            pltpu.SemaphoreType.DMA((4,)),
+            pltpu.SemaphoreType.DMA((5,)),
             pltpu.SemaphoreType.DMA,
             pltpu.SemaphoreType.DMA((n_req - 1,)),
         ],
@@ -207,7 +223,7 @@
             transcendentals=0,
         ),
         name="own_attention",
-    )(q, new_kv, page_slot, page_owner, context_len, pool)
+    )(*(in_hbm(x) for x in (q, new_kv, page_slot, page_owner, context_len, pool)))
 
 
 def stat_rows_of(n_req):
@@ -218,10 +234,10 @@
     q_refs = refs[: n_req - 1]
     acc_ref, log_ref, limit_ref, pages_ref = refs[n_req - 1 : n_req + 3]
     out_refs = refs[n_req + 3 : n_req + 3 + n_tp]
-    results, logs, stats = refs[n_req + 3 + n_tp :]
+    results, logs, stats, q_heads = refs[n_req + 3 + n_tp :]
     kv_heads, width = pages_ref.shape[1], pages_ref.shape[3]
     head_dim = width // 2
-    heads = q_refs[0].shape[0]
+    heads = results.shape[1]
     chunk = heads // n_tp
     my_tp = lax.axis_index("tp")
     scale = 1.0 / math.sqrt(head_dim)
@@ -233,7 +249,9 @@
     for p in range(pairs):
         a, b = 2 * p, min(2 * p + 1, others - 1)
         members.append((a, b))
-        tiles = query_tiles(jnp.concatenate([q_refs[a][...], q_refs[b][...]], axis=0), kv_heads)
+        lay_rows(q_heads.at[p], 0, q_refs[a])
+        lay_rows(q_heads.at[p], 64, q_refs[b])
+        tiles = query_tiles(q_heads[p], kv_heads)
         scores.append(pair_scores(pages_ref.at[a], pages_ref.at[b], tiles, head_dim) * scale)
     sums, inverse, log_rows = [], [], []
     for p in range(pairs):
@@ -269,7 +287,7 @@
 
 
 def other_attention(q_list, own, n_req, n_tp):
-    heads, head_dim = q_list[0].shape
+    heads, head_dim = own[0].shape
     chunk = heads // n_tp
     rows = n_req * chunk + stat_rows_of(n_req)
     vmem = pl.BlockSpec(memory_space=pltpu.VMEM)
@@ -282,6 +300,7 @@
             pltpu.VMEM((n_req, heads, head_dim), jnp.float32),
             pltpu.VMEM((round_up(n_req, 8), 128), jnp.float32),
             pltpu.VMEM((stat_rows_of(n_req), 128), jnp.float32),
+            pltpu.VMEM((round_up(n_req - 1, 2) // 2, 128, head_dim), jnp.float32),
         ],
         compiler_params=pltpu.CompilerParams(vmem_limit_bytes=16 * MIB),
         cost_estimate=pl.CostEstimate(flops=2 * own[3].size * 16, bytes_accessed=own[3].size * 2, transcendentals=0),
@@ -289,13 +308,12 @@
     )(*q_list, *own)
 
 
-def load_kernel(after_ref, weight_hbm, out_ref, sems):
-    depth = weight_hbm.shape[0]
+def load_kernel(first, after_ref, weight_hbm, out_ref, sems):
     parts = sems.shape[0]
-    step = depth // parts
+    step = out_ref.shape[0] // parts
     copies = [
         pltpu.make_async_copy(
-            weight_hbm.at[pl.ds(i * step, step)], out_ref.at[pl.ds(i * step, step)], sems.at[i]
+            weight_hbm.at[pl.ds(first + i * step, step)], out_ref.at[pl.ds(i * step, step)], sems.at[i]
         )
         for i in range(parts)
     ]
@@ -305,27 +323,29 @@
         copy.wait()
 
 
-def load_weight(after, out_weight):
+def load_weight(after, out_weight, first, rows):
+    columns = out_weight.shape[1]
     return pl.pallas_call(
-        load_kernel,
-        out_shape=jax.ShapeDtypeStruct(out_weight.shape, out_weight.dtype),
-        in_specs=[pl.BlockSpec(memory_space=pl.ANY)] * 2,
+        functools.partial(load_kernel, first),
+        out_shape=jax.ShapeDtypeStruct((rows, columns), out_weight.dtype),
+        in_specs=[pl.BlockSpec(memory_space=pl.ANY), pl.BlockSpec(memory_space=pltpu.HBM)],
         out_specs=pl.BlockSpec(memory_space=pltpu.VMEM),
-        scratch_shapes=[pltpu.SemaphoreType.DMA((8,))],
+        scratch_shapes=[pltpu.SemaphoreType.DMA((4,))],
         compiler_params=pltpu.CompilerParams(vmem_limit_bytes=20 * MIB),
-        cost_estimate=pl.CostEstimate(flops=0, bytes_accessed=out_weight.size * 4, transcendentals=0),
+        cost_estimate=pl.CostEstimate(flops=0, bytes_accessed=rows * columns * 4, transcendentals=0),
         name="load_weight",
-    )(after, out_weight)
+    )(after, in_hbm(out_weight))
 
 
 def project_kernel(n_req, n_tp, chunk, *refs):
     part_refs = refs[:n_req]
-    weight_ref = refs[n_req]
-    out_refs = refs[n_req + 1 : n_req + 1 + n_tp]
-    wide, logs, attention, sums = refs[n_req + 1 + n_tp :]
+    weight_refs = refs[n_req : n_req + 2]
+    out_refs = refs[n_req + 2 : n_req + 2 + n_tp]
+    wide, logs, attention, sums = refs[n_req + 2 + n_tp :]
     rows = n_req * chunk
     total_rows = n_tp * n_req
-    columns = weight_ref.shape[1]
+    split = weight_refs[0].shape[0]
+    columns = weight_refs[0].shape[1]
     my_tp = lax.axis_index("tp")
     me = lax.axis_index("req")
     for r in range(n_req):
@@ -355,7 +375,8 @@
     @pl.loop(0, columns // tile)
     def _(t):
         at = pl.ds(pl.multiple_of(t * tile, tile), tile)
-        product = jnp.dot(attention[...], weight_ref[:, at], preferred_element_type=jnp.float32)
+        product = jnp.dot(attention[:, :split], weight_refs[0][:, at], preferred_element_type=jnp.float32)
+        product += jnp.dot(attention[:, split:], weight_refs[1][:, at], preferred_element_type=jnp.float32)
         for c in range(n_tp):
             sums[c, :, at] = product[c * n_req : (c + 1) * n_req]
 
@@ -363,8 +384,9 @@
         out_refs[d][...] = sums[my_tp ^ d].astype(out_refs[d].dtype)
 
 
-def project(parts, out_weight, n_req, n_tp, chunk):
-    depth, columns = out_weight.shape
+def project(parts, weights, n_req, n_tp, chunk):
+    depth = sum(w.shape[0] for w in weights)
+    columns = weights[0].shape[1]
     rows = n_req * chunk
     vmem = pl.BlockSpec(memory_space=pltpu.VMEM)
     own = jax.ShapeDtypeStruct((n_req, columns), jnp.float32)
@@ -373,7 +395,7 @@
     return pl.pallas_call(
         functools.partial(project_kernel, n_req, n_tp, chunk),
         out_shape=[own] + [sent] * (n_tp - 1),
-        in_specs=[vmem] * (n_req + 1),
+        in_specs=[vmem] * (n_req + 2),
         out_specs=[vmem] * n_tp,
         scratch_shapes=[
             pltpu.VMEM((n_req, n_tp * rows, 128), jnp.float32),
@@ -383,10 +405,10 @@
         ],
         compiler_params=pltpu.CompilerParams(vmem_limit_bytes=24 * MIB),
         cost_estimate=pl.CostEstimate(
-            flops=2 * total_rows * depth * columns, bytes_accessed=out_weight.size * 2, transcendentals=0
+            flops=2 * total_rows * depth * columns, bytes_accessed=depth * columns * 2, transcendentals=0
         ),
         name="project",
-    )(*parts, out_weight)
+    )(*parts, *weights)
 
 
 def on_device(queries, new_kv, cache_pool, page_slot, page_owner, context_len, out_weight):
@@ -394,15 +416,17 @@
     n_tp = lax.axis_size("tp")
     pool = cache_pool[0, 0]
     head_dim = pool.shape[3] // 2
-    q = queries.reshape(-1, head_dim)
-    chunk = q.shape[0] // n_tp
-    q_list = [swap(q, "req", d) for d in range(1, n_req)]
-    own = own_attention(q, new_kv, page_slot, page_owner, context_len, pool, n_req)
+    chunk = queries.shape[1] // head_dim // n_tp
+    q_list = [swap(queries, "req", d) for d in range(1, n_req)]
+    own = own_attention(queries, new_kv, page_slot, page_owner, context_len, pool, n_req)
     pieces = other_attention(q_list, own, n_req, n_tp)
+    depth = out_weight.shape[0]
+    early = depth * 3 // 8
+    first = load_weight(pieces[0], out_weight, 0, early)
     arrived = jnp.stack([pieces[0]] + [swap(pieces[d], "tp", d) for d in range(1, n_tp)])
     parts = [arrived] + [swap(arrived, "req", d) for d in range(1, n_req)]
-    weight = load_weight(arrived, out_weight)
-    sums = project(parts, weight, n_req, n_tp, chunk)
+    second = load_weight(arrived, out_weight, early, depth - early)
+    sums = project(parts, (first, second), n_req, n_tp, chunk)
     total = sums[0]
     for d in range(1, n_tp):
         total = total + swap(sums[d], "tp", d).astype(jnp.float32)

time: 38.8 us -> 37.6 us (0.969)
  local copies, waits for them, and re-layouts: 9.88 us -> 0 us
  Pallas kernels: 7.33 us -> 13.7 us
  waiting for transfers between devices: 5.52 us -> 9.03 us
  other arithmetic: 1.51 us -> 0.67 us
    unnamed x12 -> x0, local copies, waits for them, and re-layouts: 9.88 us -> none
    pallas_call x1 -> x2, Pallas kernels: 1.2 us -> 6.97 us  [load_weight(): pl.pallas_call(functools.partial(load_kernel, first), out_shape=jax.Shape...]
    ppermute x12, waiting for transfers between devices: 5.52 us -> 9.03 us  [swap(): return lax.ppermute(x, axis, [(i, i ^ offset) for i in range(count)])]
    unnamed x1 -> x0, other arithmetic: 0.85 us -> none
    pallas_call x1, Pallas kernels: 1.82 us -> 2.39 us  [own_attention(): pl.pallas_call(functools.partial(own_kernel, n_req, own_pages), out_shape...]
  transfers between devices with their start and end apart: 12 -> 12, of which waited for: 3 -> 6; matrix products, arithmetic and copies ran while one was open for 0% -> 0% of each run, Pallas kernels for 8% -> 25%
where the time goes in v3:
time: 37.6 us; the launch traced here: 37.4 us
  starting transfers between devices  13.9 us (37%)
  Pallas kernels  13.7 us (36%)
  waiting for transfers between devices  9.03 us (24%)
  other arithmetic  0.67 us (2%)
    ppermute x12, starting transfers between devices, swap(): return lax.ppermute(x, axis, [(i, i ^ offset) for i in range(count)])  13.9 us
    ppermute x12, waiting for transfers between devices, swap(): return lax.ppermute(x, axis, [(i, i ^ offset) for i in range(count)])  9.03 us
    pallas_call x2, Pallas kernels, load_weight(): pl.pallas_call(functools.partial(load_kernel, first), out_shape=jax.Shape...  6.97 us
    pallas_call x1, Pallas kernels, project(): pl.pallas_call(functools.partial(project_kernel, n_req, n_tp, chunk), out...  3.59 us
    pallas_call x1, Pallas kernels, own_attention(): pl.pallas_call(functools.partial(own_kernel, n_req, own_pages), out_shape...  2.39 us
    pallas_call x1, Pallas kernels, other_attention(): pl.pallas_call(functools.partial(other_kernel, n_req, n_tp), out_shape=[j...  0.77 us
  transfers between devices with their start and end apart: 12, of which 6 were waited for; matrix products, arithmetic and copies ran while one was open for 0% of the time, Pallas kernels for 25%

profile of v3, /device:TPU:0, one launch (start us, length us, event | category | flops | bytes accessed | tf_op | source)
XLA Modules:
  0.0 37.4 jit_solution(1208563185940286794)
XLA Ops:
  0.0 4.0 %collective-permute-start.1 = (bf16[1,8192]{1,0:T(2,128)(2,1)}, bf16[1,8192]{1,0:T(2,128)(2,1)S(1)}, u32[]{:S(2)}, u32[]{:S(2)}) collective-permute-start(bf16[1,8192]{1,0:T(2,128)(2,1)} %refs_0_.1), channel_id=1, source_target_pairs={{0,2},{1,3},{2,0},{3,1},{4,6},{5,7},{6,4},{7,5},{8,10},{9,11},{10,... | collective-permute-start | bytes 49160 | tf_op jit(solution)/shard_map/ppermute | solution.py:17
  4.0 1.6 %collective-permute-start = (bf16[1,8192]{1,0:T(2,128)(2,1)}, bf16[1,8192]{1,0:T(2,128)(2,1)S(1)}, u32[]{:S(2)}, u32[]{:S(2)}) collective-permute-start(bf16[1,8192]{1,0:T(2,128)(2,1)} %refs_0_.1), channel_id=1, source_target_pairs={{0,1},{1,0},{2,3},{3,2},{4,5},{5,4},{6,7},{7,6},{8,9},{9,8},{10,11... | collective-permute-start | bytes 49160 | tf_op jit(solution)/shard_map/ppermute | solution.py:17
  5.6 0.0 collective-permute-start.2
  5.6 2.4 %own_attention.1 = (f32[64,128]{1,0:T(8,128)S(1)}, f32[8,128]{1,0:T(8,128)S(1)}, s32[8,128]{1,0:T(8,128)S(1)}, bf16[3,4,128,256]{3,2,1,0:T(8,128)(2,1)S(1)}) custom-call(bf16[1,8192]{1,0:T(2,128)(2,1)} %refs_0_.1, bf16[1,1024]{1,0:T(2,128)(2,1)} %refs_1_.1, s32[1,4,7]{2,1,0:T(4,128)} %refs_2_.1, s32[1,4,7]{2,1,0:T(4,128)} %refs_3_.1, s32[1,4]{1,0:T(1,128)} %refs_4_.1, ...), custom_call_target="tpu_custom_call" | custom-call | flops 25165824 | bytes 4718592 | tf_op jit(solution)/shard_map/own_attention/pallas_call | solution.py:197
  8.0 0.0 collective-permute-done.1.refs_1_
  8.0 0.1 collective-permute-done.refs_0_
  8.2 3.4 %collective-permute-done.2.refs_2_ = bf16[1,8192]{1,0:T(2,128)(2,1)S(1)} collective-permute-done((bf16[1,8192]{1,0:T(2,128)(2,1)}, bf16[1,8192]{1,0:T(2,128)(2,1)S(1)}, u32[]{:S(2)}, u32[]{:S(2)}) %collective-permute-start.2) | collective-permute-done | bytes 16416 | tf_op jit(solution)/shard_map/ppermute | solution.py:17
  11.5 0.8 %other_attention.1 = (bf16[72,128]{1,0:T(8,128)(2,1)S(1)}, bf16[72,128]{1,0:T(8,128)(2,1)S(1)}, bf16[72,128]{1,0:T(8,128)(2,1)S(1)}, bf16[72,128]{1,0:T(8,128)(2,1)S(1)}) custom-call(bf16[1,8192]{1,0:T(2,128)(2,1)S(1)} %collective-permute-done.refs_0_, bf16[1,8192]{1,0:T(2,128)(2,1)S(1)} %collective-permute-done.1.refs_1_, ...), custom_call_target="tpu_custom_call" | custom-call | flops 12582912 | bytes 786432 | tf_op jit(solution)/shard_map/other_attention/pallas_call | solution.py:294
  12.3 0.1 collective-permute-start.3
  12.4 1.6 %collective-permute-start.4 = (bf16[72,128]{1,0:T(8,128)(2,1)S(1)}, bf16[72,128]{1,0:T(8,128)(2,1)S(1)}, u32[]{:S(2)}, u32[]{:S(2)}) collective-permute-start(bf16[72,128]{1,0:T(8,128)(2,1)S(1)} %get-tuple-element.23), channel_id=1, source_target_pairs={{0,8},{4,12},{8,0},{12,4},{1,9},{5,13},{9,1},{13,5},{2,10},{6,14},... | collective-permute-start | bytes 55304 | tf_op jit(solution)/shard_map/ppermute | solution.py:17
  13.9 0.3 collective-permute-start.5
  14.3 0.0 collective-permute-done.3
  14.3 2.0 %collective-permute-done.4 = bf16[72,128]{1,0:T(8,128)(2,1)S(1)} collective-permute-done((bf16[72,128]{1,0:T(8,128)(2,1)S(1)}, bf16[72,128]{1,0:T(8,128)(2,1)S(1)}, u32[]{:S(2)}, u32[]{:S(2)}) %collective-permute-start.4) | collective-permute-done | bytes 18464 | tf_op jit(solution)/shard_map/ppermute | solution.py:17
  16.2 0.9 %collective-permute-done.5 = bf16[72,128]{1,0:T(8,128)(2,1)S(1)} collective-permute-done((bf16[72,128]{1,0:T(8,128)(2,1)S(1)}, bf16[72,128]{1,0:T(8,128)(2,1)S(1)}, u32[]{:S(2)}, u32[]{:S(2)}) %collective-permute-start.5) | collective-permute-done | bytes 18464 | tf_op jit(solution)/shard_map/ppermute | solution.py:17
  17.1 0.4 %collective-permute-start.8 = (bf16[4,72,128]{2,1,0:T(8,128)(2,1)S(1)}, bf16[4,72,128]{2,1,0:T(8,128)(2,1)S(1)}, u32[]{:S(2)}, u32[]{:S(2)}) collective-permute-start(bf16[4,72,128]{2,1,0:T(8,128)(2,1)S(1)} %pad_maximum_fusion.after_ref.refs_0_), channel_id=1, source_target_pairs={{0,3},{1,2},{2,1},{3,0},{4,7},{5,6},{6,5},{7,4},{8,11},{9,10},{10,... | collective-permute-start | bytes 221192 | tf_op jit(solution)/shard_map/ppermute | solution.py:17
  17.6 0.1 collective-permute-start.7
  17.7 3.9 %collective-permute-start.6 = (bf16[4,72,128]{2,1,0:T(8,128)(2,1)S(1)}, bf16[4,72,128]{2,1,0:T(8,128)(2,1)S(1)}, u32[]{:S(2)}, u32[]{:S(2)}) collective-permute-start(bf16[4,72,128]{2,1,0:T(8,128)(2,1)S(1)} %pad_maximum_fusion.after_ref.refs_0_), channel_id=1, source_target_pairs={{0,1},{1,0},{2,3},{3,2},{4,5},{5,4},{6,7},{7,6},{8,9},{9,8},{10,11... | collective-permute-start | bytes 221192 | tf_op jit(solution)/shard_map/ppermute | solution.py:17
  21.6 2.9 %load_weight.2.refs_4_ = bf16[768,4096]{1,0:T(8,128)(2,1)S(1)} custom-call(bf16[72,128]{1,0:T(8,128)(2,1)S(1)} %get-tuple-element.21.after_ref, bf16[2048,4096]{1,0:T(8,128)(2,1)} %weight_hbm.3), custom_call_target="tpu_custom_call" | custom-call | bytes 12582912 | tf_op jit(solution)/shard_map/load_weight/pallas_call | solution.py:328
  24.5 4.1 %load_weight.3.refs_5_ = bf16[1280,4096]{1,0:T(8,128)(2,1)S(1)} custom-call(bf16[4,72,128]{2,1,0:T(8,128)(2,1)S(1)} %pad_maximum_fusion.after_ref.refs_0_, bf16[2048,4096]{1,0:T(8,128)(2,1)} %weight_hbm.3), custom_call_target="tpu_custom_call" | custom-call | bytes 20971520 | tf_op jit(solution)/shard_map/load_weight/pallas_call | solution.py:328
  28.6 0.0 collective-permute-done.8.refs_3_
  28.6 0.0 collective-permute-done.7.refs_2_
  28.6 0.0 collective-permute-done.6.refs_1_
  28.6 3.6 %project.1 = (f32[4,4096]{1,0:T(4,128)S(1)}, bf16[4,4096]{1,0:T(4,128)(2,1)S(1)}, bf16[4,4096]{1,0:T(4,128)(2,1)S(1)}, bf16[4,4096]{1,0:T(4,128)(2,1)S(1)}) custom-call(bf16[4,72,128]{2,1,0:T(8,128)(2,1)S(1)} %pad_maximum_fusion.after_ref.refs_0_, bf16[4,72,128]{2,1,0:T(8,128)(2,1)S(1)} %collective-permute-done.6.refs_1_, ...), custom_call_target="tpu_custom_call" | custom-call | flops 268435456 | bytes 16777216 | tf_op jit(solution)/shard_map/project/pallas_call | solution.py:395
  32.2 0.1 collective-permute-start.9
  32.3 0.8 %collective-permute-start.10 = (bf16[4,4096]{1,0:T(4,128)(2,1)S(1)}, bf16[4,4096]{1,0:T(4,128)(2,1)S(1)}, u32[]{:S(2)}, u32[]{:S(2)}) collective-permute-start(bf16[4,4096]{1,0:T(4,128)(2,1)S(1)} %get-tuple-element.27), channel_id=1, source_target_pairs={{0,8},{4,12},{8,0},{12,4},{1,9},{5,13},{9,1},{13,5},{2,10},{6,14},... | collective-permute-start | bytes 98312 | tf_op jit(solution)/shard_map/ppermute | solution.py:17
  33.1 1.1 %collective-permute-start.11 = (bf16[4,4096]{1,0:T(4,128)(2,1)S(1)}, bf16[4,4096]{1,0:T(4,128)(2,1)S(1)}, u32[]{:S(2)}, u32[]{:S(2)}) collective-permute-start(bf16[4,4096]{1,0:T(4,128)(2,1)S(1)} %get-tuple-element.28), channel_id=1, source_target_pairs={{0,12},{4,8},{8,4},{12,0},{1,13},{5,9},{9,5},{13,1},{2,14},{6,10},... | collective-permute-start | bytes 98312 | tf_op jit(solution)/shard_map/ppermute | solution.py:17
  34.2 0.0 collective-permute-done.9
  34.2 2.3 %collective-permute-done.10 = bf16[4,4096]{1,0:T(4,128)(2,1)S(1)} collective-permute-done((bf16[4,4096]{1,0:T(4,128)(2,1)S(1)}, bf16[4,4096]{1,0:T(4,128)(2,1)S(1)}, u32[]{:S(2)}, u32[]{:S(2)}) %collective-permute-start.10) | collective-permute-done | bytes 32800 | tf_op jit(solution)/shard_map/ppermute | solution.py:17
  36.5 0.3 collective-permute-done.11
  36.8 0.7 %add_convert_fusion = bf16[4,4096]{1,0:T(4,128)(2,1)} fusion(bf16[4,4096]{1,0:T(4,128)(2,1)S(1)} %collective-permute-done.11, bf16[4,4096]{1,0:T(4,128)(2,1)S(1)} %collective-permute-done.10, f32[4,4096]{1,0:T(4,128)S(1)} %get-tuple-element.25, bf16[4,4096]{1,0:T(4,128)(2,1)S(1)} %collective-permute-done.9), kind=kLoop, calls=%fused_computation.1 | loop fusion | flops 114688 | bytes 196608 | tf_op jit(solution)/shard_map/convert_element_type | solution.py:433
  (1 shorter events, 0.0 us)
Async XLA Ops:
  0.0 8.0 %collective-permute-start.1 = (bf16[1,8192]{1,0:T(2,128)(2,1)}, bf16[1,8192]{1,0:T(2,128)(2,1)S(1)}, u32[]{:S(2)}, u32[]{:S(2)}) collective-permute-start(bf16[1,8192]{1,0:T(2,128)(2,1)} %refs_0_.1), channel_id=1, source_target_pairs={{0,2},{1,3},{2,0},{3,1},{4,6},{5,7},{6,4},{7,5},{8,10},{9,11},{10,... | collective-permute-start | bytes 49160 | tf_op jit(solution)/shard_map/ppermute | solution.py:17
  4.0 4.1 %collective-permute-start = (bf16[1,8192]{1,0:T(2,128)(2,1)}, bf16[1,8192]{1,0:T(2,128)(2,1)S(1)}, u32[]{:S(2)}, u32[]{:S(2)}) collective-permute-start(bf16[1,8192]{1,0:T(2,128)(2,1)} %refs_0_.1), channel_id=1, source_target_pairs={{0,1},{1,0},{2,3},{3,2},{4,5},{5,4},{6,7},{7,6},{8,9},{9,8},{10,11... | collective-permute-start | bytes 49160 | tf_op jit(solution)/shard_map/ppermute | solution.py:17
  5.6 5.9 %collective-permute-start.2 = (bf16[1,8192]{1,0:T(2,128)(2,1)}, bf16[1,8192]{1,0:T(2,128)(2,1)S(1)}, u32[]{:S(2)}, u32[]{:S(2)}) collective-permute-start(bf16[1,8192]{1,0:T(2,128)(2,1)} %refs_0_.1), channel_id=1, source_target_pairs={{0,3},{1,2},{2,1},{3,0},{4,7},{5,6},{6,5},{7,4},{8,11},{9,10},{10,... | collective-permute-start | bytes 49160 | tf_op jit(solution)/shard_map/ppermute | solution.py:17
  12.3 1.9 %collective-permute-start.3 = (bf16[72,128]{1,0:T(8,128)(2,1)S(1)}, bf16[72,128]{1,0:T(8,128)(2,1)S(1)}, u32[]{:S(2)}, u32[]{:S(2)}) collective-permute-start(bf16[72,128]{1,0:T(8,128)(2,1)S(1)} %get-tuple-element.22), channel_id=1, source_target_pairs={{0,4},{4,0},{8,12},{12,8},{1,5},{5,1},{9,13},{13,9},{2,6},{6,2},{1... | collective-permute-start | bytes 55304 | tf_op jit(solution)/shard_map/ppermute | solution.py:17
  12.4 3.8 %collective-permute-start.4 = (bf16[72,128]{1,0:T(8,128)(2,1)S(1)}, bf16[72,128]{1,0:T(8,128)(2,1)S(1)}, u32[]{:S(2)}, u32[]{:S(2)}) collective-permute-start(bf16[72,128]{1,0:T(8,128)(2,1)S(1)} %get-tuple-element.23), channel_id=1, source_target_pairs={{0,8},{4,12},{8,0},{12,4},{1,9},{5,13},{9,1},{13,5},{2,10},{6,14},... | collective-permute-start | bytes 55304 | tf_op jit(solution)/shard_map/ppermute | solution.py:17
  13.9 3.2 %collective-permute-start.5 = (bf16[72,128]{1,0:T(8,128)(2,1)S(1)}, bf16[72,128]{1,0:T(8,128)(2,1)S(1)}, u32[]{:S(2)}, u32[]{:S(2)}) collective-permute-start(bf16[72,128]{1,0:T(8,128)(2,1)S(1)} %get-tuple-element.24), channel_id=1, source_target_pairs={{0,12},{4,8},{8,4},{12,0},{1,13},{5,9},{9,5},{13,1},{2,14},{6,10},... | collective-permute-start | bytes 55304 | tf_op jit(solution)/shard_map/ppermute | solution.py:17
  17.1 11.4 %collective-permute-start.8 = (bf16[4,72,128]{2,1,0:T(8,128)(2,1)S(1)}, bf16[4,72,128]{2,1,0:T(8,128)(2,1)S(1)}, u32[]{:S(2)}, u32[]{:S(2)}) collective-permute-start(bf16[4,72,128]{2,1,0:T(8,128)(2,1)S(1)} %pad_maximum_fusion.after_ref.refs_0_), channel_id=1, source_target_pairs={{0,3},{1,2},{2,1},{3,0},{4,7},{5,6},{6,5},{7,4},{8,11},{9,10},{10,... | collective-permute-start | bytes 221192 | tf_op jit(solution)/shard_map/ppermute | solution.py:17
  17.6 11.0 %collective-permute-start.7 = (bf16[4,72,128]{2,1,0:T(8,128)(2,1)S(1)}, bf16[4,72,128]{2,1,0:T(8,128)(2,1)S(1)}, u32[]{:S(2)}, u32[]{:S(2)}) collective-permute-start(bf16[4,72,128]{2,1,0:T(8,128)(2,1)S(1)} %pad_maximum_fusion.after_ref.refs_0_), channel_id=1, source_target_pairs={{0,2},{1,3},{2,0},{3,1},{4,6},{5,7},{6,4},{7,5},{8,10},{9,11},{10,... | collective-permute-start | bytes 221192 | tf_op jit(solution)/shard_map/ppermute | solution.py:17
  17.7 10.9 %collective-permute-start.6 = (bf16[4,72,128]{2,1,0:T(8,128)(2,1)S(1)}, bf16[4,72,128]{2,1,0:T(8,128)(2,1)S(1)}, u32[]{:S(2)}, u32[]{:S(2)}) collective-permute-start(bf16[4,72,128]{2,1,0:T(8,128)(2,1)S(1)} %pad_maximum_fusion.after_ref.refs_0_), channel_id=1, source_target_pairs={{0,1},{1,0},{2,3},{3,2},{4,5},{5,4},{6,7},{7,6},{8,9},{9,8},{10,11... | collective-permute-start | bytes 221192 | tf_op jit(solution)/shard_map/ppermute | solution.py:17
  32.2 1.9 %collective-permute-start.9 = (bf16[4,4096]{1,0:T(4,128)(2,1)S(1)}, bf16[4,4096]{1,0:T(4,128)(2,1)S(1)}, u32[]{:S(2)}, u32[]{:S(2)}) collective-permute-start(bf16[4,4096]{1,0:T(4,128)(2,1)S(1)} %get-tuple-element.26), channel_id=1, source_target_pairs={{0,4},{4,0},{8,12},{12,8},{1,5},{5,1},{9,13},{13,9},{2,6},{6,2},{1... | collective-permute-start | bytes 98312 | tf_op jit(solution)/shard_map/ppermute | solution.py:17
  32.3 4.2 %collective-permute-start.10 = (bf16[4,4096]{1,0:T(4,128)(2,1)S(1)}, bf16[4,4096]{1,0:T(4,128)(2,1)S(1)}, u32[]{:S(2)}, u32[]{:S(2)}) collective-permute-start(bf16[4,4096]{1,0:T(4,128)(2,1)S(1)} %get-tuple-element.27), channel_id=1, source_target_pairs={{0,8},{4,12},{8,0},{12,4},{1,9},{5,13},{9,1},{13,5},{2,10},{6,14},... | collective-permute-start | bytes 98312 | tf_op jit(solution)/shard_map/ppermute | solution.py:17
  33.1 3.7 %collective-permute-start.11 = (bf16[4,4096]{1,0:T(4,128)(2,1)S(1)}, bf16[4,4096]{1,0:T(4,128)(2,1)S(1)}, u32[]{:S(2)}, u32[]{:S(2)}) collective-permute-start(bf16[4,4096]{1,0:T(4,128)(2,1)S(1)} %get-tuple-element.28), channel_id=1, source_target_pairs={{0,12},{4,8},{8,4},{12,0},{1,13},{5,9},{9,5},{13,1},{2,14},{6,10},... | collective-permute-start | bytes 98312 | tf_op jit(solution)/shard_map/ppermute | solution.py:17

commit v4 on v3

--- a/solution.py
+++ b/solution.py
@@ -233,8 +233,8 @@
 def other_kernel(n_req, n_tp, *refs):
     q_refs = refs[: n_req - 1]
     acc_ref, log_ref, limit_ref, pages_ref = refs[n_req - 1 : n_req + 3]
-    out_refs = refs[n_req + 3 : n_req + 3 + n_tp]
-    results, logs, stats, q_heads = refs[n_req + 3 + n_tp :]
+    out_refs = refs[n_req + 3 : n_req + 5]
+    results, logs, stats, q_heads = refs[n_req + 5 :]
     kv_heads, width = pages_ref.shape[1], pages_ref.shape[3]
     head_dim = width // 2
     heads = results.shape[1]
@@ -282,8 +282,8 @@
     for d in range(n_tp):
         at = pl.ds(pl.multiple_of((my_tp ^ d) * chunk, chunk), chunk)
         for k in range(n_req):
-            out_refs[d][k * chunk : (k + 1) * chunk] = results[k, at].astype(jnp.bfloat16)
-        out_refs[d][rows:] = tail
+            out_refs[d % 2][d // 2, k * chunk : (k + 1) * chunk] = results[k, at].astype(jnp.bfloat16)
+        out_refs[d % 2][d // 2, rows:] = tail
 
 
 def other_attention(q_list, own, n_req, n_tp):
@@ -293,9 +293,9 @@
     vmem = pl.BlockSpec(memory_space=pltpu.VMEM)
     return pl.pallas_call(
         functools.partial(other_kernel, n_req, n_tp),
-        out_shape=[jax.ShapeDtypeStruct((rows, head_dim), jnp.bfloat16)] * n_tp,
+        out_shape=[jax.ShapeDtypeStruct((n_tp // 2, rows, head_dim), jnp.bfloat16)] * 2,
         in_specs=[vmem] * (n_req + 3),
-        out_specs=[vmem] * n_tp,
+        out_specs=[vmem] * 2,
         scratch_shapes=[
             pltpu.VMEM((n_req, heads, head_dim), jnp.float32),
             pltpu.VMEM((round_up(n_req, 8), 128), jnp.float32),
@@ -308,25 +308,29 @@
     )(*q_list, *own)
 
 
-def load_kernel(first, after_ref, weight_hbm, out_ref, sems):
+def row_copies(source, first, target, sems):
     parts = sems.shape[0]
-    step = out_ref.shape[0] // parts
-    copies = [
+    step = target.shape[0] // parts
+    return [
         pltpu.make_async_copy(
-            weight_hbm.at[pl.ds(first + i * step, step)], out_ref.at[pl.ds(i * step, step)], sems.at[i]
+            source.at[pl.ds(first + i * step, step)], target.at[pl.ds(i * step, step)], sems.at[i]
         )
         for i in range(parts)
     ]
+
+
+def load_kernel(after_ref, weight_hbm, out_ref, sems):
+    copies = row_copies(weight_hbm, 0, out_ref, sems)
     for copy in copies:
         copy.start()
     for copy in copies:
         copy.wait()
 
 
-def load_weight(after, out_weight, first, rows):
+def load_weight(after, out_weight, rows):
     columns = out_weight.shape[1]
     return pl.pallas_call(
-        functools.partial(load_kernel, first),
+        load_kernel,
         out_shape=jax.ShapeDtypeStruct((rows, columns), out_weight.dtype),
         in_specs=[pl.BlockSpec(memory_space=pl.ANY), pl.BlockSpec(memory_space=pltpu.HBM)],
         out_specs=pl.BlockSpec(memory_space=pltpu.VMEM),
@@ -339,15 +343,17 @@
 
 def project_kernel(n_req, n_tp, chunk, *refs):
     part_refs = refs[:n_req]
-    weight_refs = refs[n_req : n_req + 2]
-    out_refs = refs[n_req + 2 : n_req + 2 + n_tp]
-    wide, logs, attention, sums = refs[n_req + 2 + n_tp :]
+    first_ref, weight_hbm = refs[n_req : n_req + 2]
+    kept_ref, sent_ref = refs[n_req + 2 : n_req + 4]
+    wide, logs, attention, second, sums, sems = refs[n_req + 4 :]
     rows = n_req * chunk
     total_rows = n_tp * n_req
-    split = weight_refs[0].shape[0]
-    columns = weight_refs[0].shape[1]
+    early, columns = first_ref.shape
     my_tp = lax.axis_index("tp")
     me = lax.axis_index("req")
+    copies = row_copies(weight_hbm, early, second, sems)
+    for copy in copies:
+        copy.start()
     for r in range(n_req):
         for c in range(n_tp):
             col = my_tp ^ c
@@ -375,40 +381,52 @@
     @pl.loop(0, columns // tile)
     def _(t):
         at = pl.ds(pl.multiple_of(t * tile, tile), tile)
-        product = jnp.dot(attention[:, :split], weight_refs[0][:, at], preferred_element_type=jnp.float32)
-        product += jnp.dot(attention[:, split:], weight_refs[1][:, at], preferred_element_type=jnp.float32)
+        product = jnp.dot(attention[:, :early], first_ref[:, at], preferred_element_type=jnp.float32)
         for c in range(n_tp):
             sums[c, :, at] = product[c * n_req : (c + 1) * n_req]
 
+    for copy in copies:
+        copy.wait()
+
+    @pl.loop(0, columns // tile)
+    def _(t):
+        at = pl.ds(pl.multiple_of(t * tile, tile), tile)
+        product = jnp.dot(attention[:, early:], second[:, at], preferred_element_type=jnp.float32)
+        for c in range(n_tp):
+            sums[c, :, at] += product[c * n_req : (c + 1) * n_req]
+
     for d in range(n_tp):
-        out_refs[d][...] = sums[my_tp ^ d].astype(out_refs[d].dtype)
-
-
-def project(parts, weights, n_req, n_tp, chunk):
-    depth = sum(w.shape[0] for w in weights)
-    columns = weights[0].shape[1]
+        target = (kept_ref, sent_ref)[d % 2]
+        target[d // 2] = sums[my_tp ^ d].astype(target.dtype)
+
+
+def project(parts, first, out_weight, n_req, n_tp, chunk):
+    depth, columns = out_weight.shape
     rows = n_req * chunk
     vmem = pl.BlockSpec(memory_space=pltpu.VMEM)
-    own = jax.ShapeDtypeStruct((n_req, columns), jnp.float32)
-    sent = jax.ShapeDtypeStruct((n_req, columns), jnp.bfloat16)
     total_rows = n_tp * n_req
     return pl.pallas_call(
         functools.partial(project_kernel, n_req, n_tp, chunk),
-        out_shape=[own] + [sent] * (n_tp - 1),
-        in_specs=[vmem] * (n_req + 2),
-        out_specs=[vmem] * n_tp,
+        out_shape=[
+            jax.ShapeDtypeStruct((n_tp // 2, n_req, columns), jnp.float32),
+            jax.ShapeDtypeStruct((n_tp // 2, n_req, columns), jnp.bfloat16),
+        ],
+        in_specs=[vmem] * (n_req + 1) + [pl.BlockSpec(memory_space=pltpu.HBM)],
+        out_specs=[vmem] * 2,
         scratch_shapes=[
             pltpu.VMEM((n_req, n_tp * rows, 128), jnp.float32),
             pltpu.VMEM((n_req, total_rows, 128), jnp.float32),
             pltpu.VMEM((total_rows, depth), jnp.bfloat16),
+            pltpu.VMEM((depth - first.shape[0], columns), jnp.bfloat16),
             pltpu.VMEM((n_tp, n_req, columns), jnp.float32),
+            pltpu.SemaphoreType.DMA((4,)),
         ],
         compiler_params=pltpu.CompilerParams(vmem_limit_bytes=24 * MIB),
         cost_estimate=pl.CostEstimate(
             flops=2 * total_rows * depth * columns, bytes_accessed=depth * columns * 2, transcendentals=0
         ),
         name="project",
-    )(*parts, *weights)
+    )(*parts, first, in_hbm(out_weight))
 
 
 def on_device(queries, new_kv, cache_pool, page_slot, page_owner, context_len, out_weight):
@@ -419,17 +437,21 @@
     chunk = queries.shape[1] // head_dim // n_tp
     q_list = [swap(queries, "req", d) for d in range(1, n_req)]
     own = own_attention(queries, new_kv, page_slot, page_owner, context_len, pool, n_req)
-    pieces = other_attention(q_list, own, n_req, n_tp)
+    even, odd = other_attention(q_list, own, n_req, n_tp)
+    beside = swap(odd, "tp", 1)
+    arrived = [even[0], beside[0]]
+    for e in range(1, n_tp // 2):
+        pair = swap(jnp.stack([even[e], beside[e]]), "tp", 2 * e)
+        arrived += [pair[0], pair[1]]
+    arrived = jnp.stack(arrived)
+    parts = [arrived] + [swap(arrived, "req", d) for d in range(1, n_req)]
     depth = out_weight.shape[0]
-    early = depth * 3 // 8
-    first = load_weight(pieces[0], out_weight, 0, early)
-    arrived = jnp.stack([pieces[0]] + [swap(pieces[d], "tp", d) for d in range(1, n_tp)])
-    parts = [arrived] + [swap(arrived, "req", d) for d in range(1, n_req)]
-    second = load_weight(arrived, out_weight, early, depth - early)
-    sums = project(parts, (first, second), n_req, n_tp, chunk)
-    total = sums[0]
-    for d in range(1, n_tp):
-        total = total + swap(sums[d], "tp", d).astype(jnp.float32)
+    first = load_weight(arrived, out_weight, depth * 5 // 8)
+    kept, sent = project(parts, first, out_weight, n_req, n_tp, chunk)
+    both = kept + swap(sent, "tp", 1).astype(jnp.float32)
+    total = both[0]
+    for e in range(1, n_tp // 2):
+        total = total + swap(both[e].astype(jnp.bfloat16), "tp", 2 * e).astype(jnp.float32)
     return total.astype(jnp.bfloat16)
 
 

time: 37.6 us -> 37.3 us (level)
  waiting for transfers between devices: 9.03 us -> 10.8 us
  Pallas kernels: 13.7 us -> 12.1 us
  starting transfers between devices: 13.9 us -> 13.3 us
    pallas_call x2 -> x1, Pallas kernels: 6.97 us -> 4.1 us  [load_weight(): pl.pallas_call(load_kernel, out_shape=jax.ShapeDtypeStruct((rows, columns...]
    ppermute x12 -> x10, waiting for transfers between devices: 9.03 us -> 10.8 us  [swap(): return lax.ppermute(x, axis, [(i, i ^ offset) for i in range(count)])]
    pallas_call x1, Pallas kernels: 3.59 us -> 4.88 us  [project(): pl.pallas_call(functools.partial(project_kernel, n_req, n_tp, chunk), out...]
    ppermute x12 -> x10, starting transfers between devices: 13.9 us -> 13.3 us  [swap(): return lax.ppermute(x, axis, [(i, i ^ offset) for i in range(count)])]
  transfers between devices with their start and end apart: 12 -> 10, of which waited for: 6 -> 6; matrix products, arithmetic and copies ran while one was open for 0% -> 0% of each run, Pallas kernels for 25% -> 17%
where the time goes in v4:
time: 37.3 us; the launch traced here: 37.1 us
  starting transfers between devices  13.3 us (36%)
  Pallas kernels  12.1 us (32%)
  waiting for transfers between devices  10.8 us (29%)
  other arithmetic  0.67 us (2%)
    ppermute x10, starting transfers between devices, swap(): return lax.ppermute(x, axis, [(i, i ^ offset) for i in range(count)])  13.3 us
    ppermute x10, waiting for transfers between devices, swap(): return lax.ppermute(x, axis, [(i, i ^ offset) for i in range(count)])  10.8 us
    pallas_call x1, Pallas kernels, project(): pl.pallas_call(functools.partial(project_kernel, n_req, n_tp, chunk), out...  4.88 us
    pallas_call x1, Pallas kernels, load_weight(): pl.pallas_call(load_kernel, out_shape=jax.ShapeDtypeStruct((rows, columns...  4.1 us
    pallas_call x1, Pallas kernels, own_attention(): pl.pallas_call(functools.partial(own_kernel, n_req, own_pages), out_shape...  2.39 us
    pallas_call x1, Pallas kernels, other_attention(): pl.pallas_call(functools.partial(other_kernel, n_req, n_tp), out_shape=[j...  0.77 us
  transfers between devices with their start and end apart: 10, of which 6 were waited for; matrix products, arithmetic and copies ran while one was open for 0% of the time, Pallas kernels for 17%

profile of v4, /device:TPU:0, one launch (start us, length us, event | category | flops | bytes accessed | tf_op | source)
XLA Modules:
  0.0 37.1 jit_solution(14791104296326829673)
XLA Ops:
  0.0 4.0 %collective-permute-start.1 = (bf16[1,8192]{1,0:T(2,128)(2,1)}, bf16[1,8192]{1,0:T(2,128)(2,1)S(1)}, u32[]{:S(2)}, u32[]{:S(2)}) collective-permute-start(bf16[1,8192]{1,0:T(2,128)(2,1)} %refs_0_.1), channel_id=1, source_target_pairs={{0,2},{1,3},{2,0},{3,1},{4,6},{5,7},{6,4},{7,5},{8,10},{9,11},{10,... | collective-permute-start | bytes 49160 | tf_op jit(solution)/shard_map/ppermute | solution.py:17
  4.0 1.6 %collective-permute-start = (bf16[1,8192]{1,0:T(2,128)(2,1)}, bf16[1,8192]{1,0:T(2,128)(2,1)S(1)}, u32[]{:S(2)}, u32[]{:S(2)}) collective-permute-start(bf16[1,8192]{1,0:T(2,128)(2,1)} %refs_0_.1), channel_id=1, source_target_pairs={{0,1},{1,0},{2,3},{3,2},{4,5},{5,4},{6,7},{7,6},{8,9},{9,8},{10,11... | collective-permute-start | bytes 49160 | tf_op jit(solution)/shard_map/ppermute | solution.py:17
  5.6 0.0 collective-permute-start.2
  5.6 2.4 %own_attention.1 = (f32[64,128]{1,0:T(8,128)S(1)}, f32[8,128]{1,0:T(8,128)S(1)}, s32[8,128]{1,0:T(8,128)S(1)}, bf16[3,4,128,256]{3,2,1,0:T(8,128)(2,1)S(1)}) custom-call(bf16[1,8192]{1,0:T(2,128)(2,1)} %refs_0_.1, bf16[1,1024]{1,0:T(2,128)(2,1)} %refs_1_.1, s32[1,4,7]{2,1,0:T(4,128)} %refs_2_.1, s32[1,4,7]{2,1,0:T(4,128)} %refs_3_.1, s32[1,4]{1,0:T(1,128)} %refs_4_.1, ...), custom_call_target="tpu_custom_call" | custom-call | flops 25165824 | bytes 4718592 | tf_op jit(solution)/shard_map/own_attention/pallas_call | solution.py:197
  8.0 0.0 collective-permute-done.1.refs_1_
  8.0 0.1 collective-permute-done.refs_0_
  8.2 3.4 %collective-permute-done.2.refs_2_ = bf16[1,8192]{1,0:T(2,128)(2,1)S(1)} collective-permute-done((bf16[1,8192]{1,0:T(2,128)(2,1)}, bf16[1,8192]{1,0:T(2,128)(2,1)S(1)}, u32[]{:S(2)}, u32[]{:S(2)}) %collective-permute-start.2) | collective-permute-done | bytes 16416 | tf_op jit(solution)/shard_map/ppermute | solution.py:17
  11.5 0.8 %other_attention.1 = (bf16[2,72,128]{2,1,0:T(8,128)(2,1)S(1)}, bf16[2,72,128]{2,1,0:T(8,128)(2,1)S(1)}) custom-call(bf16[1,8192]{1,0:T(2,128)(2,1)S(1)} %collective-permute-done.refs_0_, bf16[1,8192]{1,0:T(2,128)(2,1)S(1)} %collective-permute-done.1.refs_1_, bf16[1,8192]{1,0:T(2,128)(2,1)S(1)} %collective-permute-done.2.refs_2_, ...), custom_call_target="tpu_custom_call" | custom-call | flops 12582912 | bytes 786432 | tf_op jit(solution)/shard_map/other_attention/pallas_call | solution.py:294
  12.3 0.1 collective-permute-start.3
  12.4 1.2 %collective-permute-done.3 = bf16[2,72,128]{2,1,0:T(8,128)(2,1)S(1)} collective-permute-done((bf16[2,72,128]{2,1,0:T(8,128)(2,1)S(1)}, bf16[2,72,128]{2,1,0:T(8,128)(2,1)S(1)}, u32[]{:S(2)}, u32[]{:S(2)}) %collective-permute-start.3) | collective-permute-done | bytes 36896 | tf_op jit(solution)/shard_map/ppermute | solution.py:17
  13.6 1.6 %collective-permute-start.4 = (bf16[2,72,128]{2,1,0:T(8,128)(2,1)S(1)}, bf16[2,72,128]{2,1,0:T(8,128)(2,1)S(1)}, u32[]{:S(2)}, u32[]{:S(2)}) collective-permute-start(bf16[2,72,128]{2,1,0:T(8,128)(2,1)S(1)} %pad_maximum_fusion.1), channel_id=1, source_target_pairs={{0,8},{4,12},{8,0},{12,4},{1,9},{5,13},{9,1},{13,5},{2,10},{6,14},... | collective-permute-start | bytes 110600 | tf_op jit(solution)/shard_map/ppermute | solution.py:17
  15.2 2.5 %collective-permute-done.4 = bf16[2,72,128]{2,1,0:T(8,128)(2,1)S(1)} collective-permute-done((bf16[2,72,128]{2,1,0:T(8,128)(2,1)S(1)}, bf16[2,72,128]{2,1,0:T(8,128)(2,1)S(1)}, u32[]{:S(2)}, u32[]{:S(2)}) %collective-permute-start.4) | collective-permute-done | bytes 36896 | tf_op jit(solution)/shard_map/ppermute | solution.py:17
  17.6 0.4 %collective-permute-start.7 = (bf16[4,72,128]{2,1,0:T(8,128)(2,1)S(1)}, bf16[4,72,128]{2,1,0:T(8,128)(2,1)S(1)}, u32[]{:S(2)}, u32[]{:S(2)}) collective-permute-start(bf16[4,72,128]{2,1,0:T(8,128)(2,1)S(1)} %pad_maximum_fusion.after_ref.refs_0_), channel_id=1, source_target_pairs={{0,3},{1,2},{2,1},{3,0},{4,7},{5,6},{6,5},{7,4},{8,11},{9,10},{10,... | collective-permute-start | bytes 221192 | tf_op jit(solution)/shard_map/ppermute | solution.py:17
  18.1 0.1 collective-permute-start.6
  18.2 3.9 %collective-permute-start.5 = (bf16[4,72,128]{2,1,0:T(8,128)(2,1)S(1)}, bf16[4,72,128]{2,1,0:T(8,128)(2,1)S(1)}, u32[]{:S(2)}, u32[]{:S(2)}) collective-permute-start(bf16[4,72,128]{2,1,0:T(8,128)(2,1)S(1)} %pad_maximum_fusion.after_ref.refs_0_), channel_id=1, source_target_pairs={{0,1},{1,0},{2,3},{3,2},{4,5},{5,4},{6,7},{7,6},{8,9},{9,8},{10,11... | collective-permute-start | bytes 221192 | tf_op jit(solution)/shard_map/ppermute | solution.py:17
  22.1 4.1 %load_weight.1.refs_4_ = bf16[1280,4096]{1,0:T(8,128)(2,1)S(1)} custom-call(bf16[4,72,128]{2,1,0:T(8,128)(2,1)S(1)} %pad_maximum_fusion.after_ref.refs_0_, bf16[2048,4096]{1,0:T(8,128)(2,1)} %refs_5_.1), custom_call_target="tpu_custom_call" | custom-call | bytes 20971520 | tf_op jit(solution)/shard_map/load_weight/pallas_call | solution.py:332
  26.2 0.0 collective-permute-done.7.refs_3_
  26.2 0.0 collective-permute-done.6.refs_2_
  26.2 0.0 collective-permute-done.5.refs_1_
  26.2 4.9 %project.1 = (f32[2,4,4096]{2,1,0:T(4,128)S(1)}, bf16[2,4,4096]{2,1,0:T(4,128)(2,1)S(1)}) custom-call(bf16[4,72,128]{2,1,0:T(8,128)(2,1)S(1)} %pad_maximum_fusion.after_ref.refs_0_, bf16[4,72,128]{2,1,0:T(8,128)(2,1)S(1)} %collective-permute-done.5.refs_1_, bf16[4,72,128]{2,1,0:T(8,128)(2,1)S(1)} %collective-permute-done.6.refs_2_, ...), custom_call_target="tpu_custom_call" | custom-call | flops 268435456 | bytes 16777216 | tf_op jit(solution)/shard_map/project/pallas_call | solution.py:408
  31.1 0.1 collective-permute-start.8
  31.2 1.2 %collective-permute-done.8 = bf16[2,4,4096]{2,1,0:T(4,128)(2,1)S(1)} collective-permute-done((bf16[2,4,4096]{2,1,0:T(4,128)(2,1)S(1)}, bf16[2,4,4096]{2,1,0:T(4,128)(2,1)S(1)}, u32[]{:S(2)}, u32[]{:S(2)}) %collective-permute-start.8) | collective-permute-done | bytes 65568 | tf_op jit(solution)/shard_map/ppermute | solution.py:17
  32.5 1.6 %collective-permute-start.9 = (bf16[4,4096]{1,0:T(4,128)(2,1)S(1)}, bf16[4,4096]{1,0:T(4,128)(2,1)S(1)}, u32[]{:S(2)}, u32[]{:S(2)}) collective-permute-start(bf16[4,4096]{1,0:T(4,128)(2,1)S(1)} %fusion.2), channel_id=1, source_target_pairs={{0,8},{4,12},{8,0},{12,4},{1,9},{5,13},{9,1},{13,5},{2,10},{6,14},... | collective-permute-start | bytes 98312 | tf_op jit(solution)/shard_map/ppermute | solution.py:17
  34.0 2.4 %collective-permute-done.9 = bf16[4,4096]{1,0:T(4,128)(2,1)S(1)} collective-permute-done((bf16[4,4096]{1,0:T(4,128)(2,1)S(1)}, bf16[4,4096]{1,0:T(4,128)(2,1)S(1)}, u32[]{:S(2)}, u32[]{:S(2)}) %collective-permute-start.9) | collective-permute-done | bytes 32800 | tf_op jit(solution)/shard_map/ppermute | solution.py:17
  36.5 0.6 %fusion.1 = bf16[4,4096]{1,0:T(4,128)(2,1)} fusion(f32[2,4,4096]{2,1,0:T(4,128)S(1)} %bitcast.15, bf16[4,4096]{1,0:T(4,128)(2,1)S(1)} %collective-permute-done.9), kind=kLoop, calls=%fused_computation.5 | loop fusion | flops 49152 | bytes 131072 | tf_op jit(solution)/shard_map/convert_element_type | solution.py:455
  (6 shorter events, 0.1 us)
Async XLA Ops:
  0.0 8.0 %collective-permute-start.1 = (bf16[1,8192]{1,0:T(2,128)(2,1)}, bf16[1,8192]{1,0:T(2,128)(2,1)S(1)}, u32[]{:S(2)}, u32[]{:S(2)}) collective-permute-start(bf16[1,8192]{1,0:T(2,128)(2,1)} %refs_0_.1), channel_id=1, source_target_pairs={{0,2},{1,3},{2,0},{3,1},{4,6},{5,7},{6,4},{7,5},{8,10},{9,11},{10,... | collective-permute-start | bytes 49160 | tf_op jit(solution)/shard_map/ppermute | solution.py:17
  4.0 4.1 %collective-permute-start = (bf16[1,8192]{1,0:T(2,128)(2,1)}, bf16[1,8192]{1,0:T(2,128)(2,1)S(1)}, u32[]{:S(2)}, u32[]{:S(2)}) collective-permute-start(bf16[1,8192]{1,0:T(2,128)(2,1)} %refs_0_.1), channel_id=1, source_target_pairs={{0,1},{1,0},{2,3},{3,2},{4,5},{5,4},{6,7},{7,6},{8,9},{9,8},{10,11... | collective-permute-start | bytes 49160 | tf_op jit(solution)/shard_map/ppermute | solution.py:17
  5.6 5.9 %collective-permute-start.2 = (bf16[1,8192]{1,0:T(2,128)(2,1)}, bf16[1,8192]{1,0:T(2,128)(2,1)S(1)}, u32[]{:S(2)}, u32[]{:S(2)}) collective-permute-start(bf16[1,8192]{1,0:T(2,128)(2,1)} %refs_0_.1), channel_id=1, source_target_pairs={{0,3},{1,2},{2,1},{3,0},{4,7},{5,6},{6,5},{7,4},{8,11},{9,10},{10,... | collective-permute-start | bytes 49160 | tf_op jit(solution)/shard_map/ppermute | solution.py:17
  12.3 1.3 %collective-permute-start.3 = (bf16[2,72,128]{2,1,0:T(8,128)(2,1)S(1)}, bf16[2,72,128]{2,1,0:T(8,128)(2,1)S(1)}, u32[]{:S(2)}, u32[]{:S(2)}) collective-permute-start(bf16[2,72,128]{2,1,0:T(8,128)(2,1)S(1)} %get-tuple-element.18), channel_id=1, source_target_pairs={{0,4},{4,0},{8,12},{12,8},{1,5},{5,1},{9,13},{13,9},{2,6},{6,2},{1... | collective-permute-start | bytes 110600 | tf_op jit(solution)/shard_map/ppermute | solution.py:17
  13.6 4.0 %collective-permute-start.4 = (bf16[2,72,128]{2,1,0:T(8,128)(2,1)S(1)}, bf16[2,72,128]{2,1,0:T(8,128)(2,1)S(1)}, u32[]{:S(2)}, u32[]{:S(2)}) collective-permute-start(bf16[2,72,128]{2,1,0:T(8,128)(2,1)S(1)} %pad_maximum_fusion.1), channel_id=1, source_target_pairs={{0,8},{4,12},{8,0},{12,4},{1,9},{5,13},{9,1},{13,5},{2,10},{6,14},... | collective-permute-start | bytes 110600 | tf_op jit(solution)/shard_map/ppermute | solution.py:17
  17.6 8.6 %collective-permute-start.7 = (bf16[4,72,128]{2,1,0:T(8,128)(2,1)S(1)}, bf16[4,72,128]{2,1,0:T(8,128)(2,1)S(1)}, u32[]{:S(2)}, u32[]{:S(2)}) collective-permute-start(bf16[4,72,128]{2,1,0:T(8,128)(2,1)S(1)} %pad_maximum_fusion.after_ref.refs_0_), channel_id=1, source_target_pairs={{0,3},{1,2},{2,1},{3,0},{4,7},{5,6},{6,5},{7,4},{8,11},{9,10},{10,... | collective-permute-start | bytes 221192 | tf_op jit(solution)/shard_map/ppermute | solution.py:17
  18.1 8.2 %collective-permute-start.6 = (bf16[4,72,128]{2,1,0:T(8,128)(2,1)S(1)}, bf16[4,72,128]{2,1,0:T(8,128)(2,1)S(1)}, u32[]{:S(2)}, u32[]{:S(2)}) collective-permute-start(bf16[4,72,128]{2,1,0:T(8,128)(2,1)S(1)} %pad_maximum_fusion.after_ref.refs_0_), channel_id=1, source_target_pairs={{0,2},{1,3},{2,0},{3,1},{4,6},{5,7},{6,4},{7,5},{8,10},{9,11},{10,... | collective-permute-start | bytes 221192 | tf_op jit(solution)/shard_map/ppermute | solution.py:17
  18.2 8.0 %collective-permute-start.5 = (bf16[4,72,128]{2,1,0:T(8,128)(2,1)S(1)}, bf16[4,72,128]{2,1,0:T(8,128)(2,1)S(1)}, u32[]{:S(2)}, u32[]{:S(2)}) collective-permute-start(bf16[4,72,128]{2,1,0:T(8,128)(2,1)S(1)} %pad_maximum_fusion.after_ref.refs_0_), channel_id=1, source_target_pairs={{0,1},{1,0},{2,3},{3,2},{4,5},{5,4},{6,7},{7,6},{8,9},{9,8},{10,11... | collective-permute-start | bytes 221192 | tf_op jit(solution)/shard_map/ppermute | solution.py:17
  31.1 1.3 %collective-permute-start.8 = (bf16[2,4,4096]{2,1,0:T(4,128)(2,1)S(1)}, bf16[2,4,4096]{2,1,0:T(4,128)(2,1)S(1)}, u32[]{:S(2)}, u32[]{:S(2)}) collective-permute-start(bf16[2,4,4096]{2,1,0:T(4,128)(2,1)S(1)} %get-tuple-element.20), channel_id=1, source_target_pairs={{0,4},{4,0},{8,12},{12,8},{1,5},{5,1},{9,13},{13,9},{2,6},{6,2},{1... | collective-permute-start | bytes 196616 | tf_op jit(solution)/shard_map/ppermute | solution.py:17
  32.5 4.0 %collective-permute-start.9 = (bf16[4,4096]{1,0:T(4,128)(2,1)S(1)}, bf16[4,4096]{1,0:T(4,128)(2,1)S(1)}, u32[]{:S(2)}, u32[]{:S(2)}) collective-permute-start(bf16[4,4096]{1,0:T(4,128)(2,1)S(1)} %fusion.2), channel_id=1, source_target_pairs={{0,8},{4,12},{8,0},{12,4},{1,9},{5,13},{9,1},{13,5},{2,10},{6,14},... | collective-permute-start | bytes 98312 | tf_op jit(solution)/shard_map/ppermute | solution.py:17

commit v5 on v3

--- a/solution.py
+++ b/solution.py
@@ -29,10 +29,12 @@
     return pltpu.roll(x, 64, 1)
 
 
-def lay_rows(target, start, q_ref):
-    head_dim = target.shape[1]
+def lay_rows(places, q_ref):
+    head_dim = places[0][0].shape[1]
     for h in range(64):
-        target[start + h : start + h + 1] = q_ref[0:1, h * head_dim : (h + 1) * head_dim].astype(jnp.float32)
+        block = q_ref[:, h * head_dim : (h + 1) * head_dim].astype(jnp.float32)
+        for i, (target, start) in enumerate(places):
+            target[start + h : start + h + 1] = block[i : i + 1]
 
 
 def query_tiles(stacked, kv_heads):
@@ -87,8 +89,8 @@
 
 def own_kernel(n_req, own_pages, *refs):
     (q_hbm, kv_hbm, slot_hbm, owner_hbm, len_hbm, pool_hbm) = refs[:6]
-    acc_ref, log_ref, limit_ref, pages_ref = refs[6:10]
-    q_row, q_heads, kv, slots, owners, lens, pool, small_sem, pool_sem, page_sem = refs[10:]
+    acc_ref, log_ref, limit_ref, pages_ref = refs[7:11]
+    q_row, q_heads, kv, slots, owners, lens, pool, small_sem, pool_sem, page_sem = refs[11:]
     slot_count, kv_heads, page_len, width = pool_hbm.shape
     head_dim = width // 2
     entries = slot_hbm.shape[2]
@@ -128,7 +130,7 @@
     for p in range(len(limits) // 2):
         limit_ref[p : p + 1] = jnp.where(lane < 64, limits[2 * p], limits[2 * p + 1])
 
-    lay_rows(q_heads, 0, q_row)
+    lay_rows([(q_heads, 0)], q_row)
     q_heads[64:] = q_heads[:64]
     tiles = query_tiles(q_heads[...], kv_heads)
     my_length = lens[0, me]
@@ -185,7 +187,7 @@
         copy.wait()
 
 
-def own_attention(q, new_kv, page_slot, page_owner, context_len, pool, n_req):
+def own_attention(q, new_kv, page_slot, page_owner, context_len, pool, after, n_req):
     slots, kv_heads, page_len, width = pool.shape
     head_dim = width // 2
     heads = q.shape[1] // head_dim
@@ -202,7 +204,7 @@
             jax.ShapeDtypeStruct((round_up(pair_count, 8), 128), jnp.int32),
             jax.ShapeDtypeStruct((n_req - 1, kv_heads, page_len, width), pool.dtype),
         ],
-        in_specs=[hbm] * 6,
+        in_specs=[hbm] * 6 + [pl.BlockSpec(memory_space=pl.ANY)],
         out_specs=[vmem] * 4,
         scratch_shapes=[
             pltpu.VMEM(q.shape, q.dtype),
@@ -223,7 +225,7 @@
             transcendentals=0,
         ),
         name="own_attention",
-    )(*(in_hbm(x) for x in (q, new_kv, page_slot, page_owner, context_len, pool)))
+    )(*(in_hbm(x) for x in (q, new_kv, page_slot, page_owner, context_len, pool)), after)
 
 
 def stat_rows_of(n_req):
@@ -231,10 +233,10 @@
 
 
 def other_kernel(n_req, n_tp, *refs):
-    q_refs = refs[: n_req - 1]
-    acc_ref, log_ref, limit_ref, pages_ref = refs[n_req - 1 : n_req + 3]
-    out_refs = refs[n_req + 3 : n_req + 3 + n_tp]
-    results, logs, stats, q_heads = refs[n_req + 3 + n_tp :]
+    count = n_req.bit_length() - 1
+    acc_ref, log_ref, limit_ref, pages_ref = refs[count : count + 4]
+    out_refs = refs[count + 4 : count + 4 + n_tp]
+    results, logs, stats, q_heads = refs[count + 4 + n_tp :]
     kv_heads, width = pages_ref.shape[1], pages_ref.shape[3]
     head_dim = width // 2
     heads = results.shape[1]
@@ -245,12 +247,14 @@
     pairs = round_up(others, 2) // 2
     results[0] = acc_ref[...]
     logs[0:1] = log_ref[0:1]
+    for k in range(count):
+        lay_rows([(q_heads.at[(d - 1) // 2], (d - 1) % 2 * 64) for d in range(1 << k, 2 << k)], refs[k])
+    if others % 2:
+        q_heads[pairs - 1, 64:] = q_heads[pairs - 1, :64]
     scores, members = [], []
     for p in range(pairs):
         a, b = 2 * p, min(2 * p + 1, others - 1)
         members.append((a, b))
-        lay_rows(q_heads.at[p], 0, q_refs[a])
-        lay_rows(q_heads.at[p], 64, q_refs[b])
         tiles = query_tiles(q_heads[p], kv_heads)
         scores.append(pair_scores(pages_ref.at[a], pages_ref.at[b], tiles, head_dim) * scale)
     sums, inverse, log_rows = [], [], []
@@ -294,7 +298,7 @@
     return pl.pallas_call(
         functools.partial(other_kernel, n_req, n_tp),
         out_shape=[jax.ShapeDtypeStruct((rows, head_dim), jnp.bfloat16)] * n_tp,
-        in_specs=[vmem] * (n_req + 3),
+        in_specs=[vmem] * (len(q_list) + 4),
         out_specs=[vmem] * n_tp,
         scratch_shapes=[
             pltpu.VMEM((n_req, heads, head_dim), jnp.float32),
@@ -308,33 +312,42 @@
     )(*q_list, *own)
 
 
-def load_kernel(first, after_ref, weight_hbm, out_ref, sems):
+def row_copies(source, first, target, sems):
     parts = sems.shape[0]
-    step = out_ref.shape[0] // parts
-    copies = [
+    step = target.shape[0] // parts
+    return [
         pltpu.make_async_copy(
-            weight_hbm.at[pl.ds(first + i * step, step)], out_ref.at[pl.ds(i * step, step)], sems.at[i]
+            source.at[pl.ds(first + i * step, step)], target.at[pl.ds(i * step, step)], sems.at[i]
         )
         for i in range(parts)
     ]
+
+
+def load_kernel(first, piece_ref, weight_hbm, out_ref, same_ref, sems):
+    copies = row_copies(weight_hbm, first, out_ref, sems)
     for copy in copies:
         copy.start()
+    same_ref[...] = piece_ref[...]
     for copy in copies:
         copy.wait()
 
 
-def load_weight(after, out_weight, first, rows):
+def load_weight(piece, out_weight, first, rows):
     columns = out_weight.shape[1]
+    vmem = pl.BlockSpec(memory_space=pltpu.VMEM)
     return pl.pallas_call(
         functools.partial(load_kernel, first),
-        out_shape=jax.ShapeDtypeStruct((rows, columns), out_weight.dtype),
-        in_specs=[pl.BlockSpec(memory_space=pl.ANY), pl.BlockSpec(memory_space=pltpu.HBM)],
-        out_specs=pl.BlockSpec(memory_space=pltpu.VMEM),
+        out_shape=[
+            jax.ShapeDtypeStruct((rows, columns), out_weight.dtype),
+            jax.ShapeDtypeStruct(piece.shape, piece.dtype),
+        ],
+        in_specs=[vmem, pl.BlockSpec(memory_space=pltpu.HBM)],
+        out_specs=[vmem] * 2,
         scratch_shapes=[pltpu.SemaphoreType.DMA((4,))],
         compiler_params=pltpu.CompilerParams(vmem_limit_bytes=20 * MIB),
         cost_estimate=pl.CostEstimate(flops=0, bytes_accessed=rows * columns * 4, transcendentals=0),
         name="load_weight",
-    )(after, in_hbm(out_weight))
+    )(piece, in_hbm(out_weight))
 
 
 def project_kernel(n_req, n_tp, chunk, *refs):
@@ -344,8 +357,7 @@
     wide, logs, attention, sums = refs[n_req + 2 + n_tp :]
     rows = n_req * chunk
     total_rows = n_tp * n_req
-    split = weight_refs[0].shape[0]
-    columns = weight_refs[0].shape[1]
+    split, columns = weight_refs[0].shape
     my_tp = lax.axis_index("tp")
     me = lax.axis_index("req")
     for r in range(n_req):
@@ -417,16 +429,20 @@
     pool = cache_pool[0, 0]
     head_dim = pool.shape[3] // 2
     chunk = queries.shape[1] // head_dim // n_tp
-    q_list = [swap(queries, "req", d) for d in range(1, n_req)]
-    own = own_attention(queries, new_kv, page_slot, page_owner, context_len, pool, n_req)
+    held, q_list = queries, []
+    for k in range(n_req.bit_length() - 1):
+        q_list.append(swap(held, "req", 1 << k))
+        held = jnp.concatenate([held, q_list[-1]], axis=0)
+    own = own_attention(queries, new_kv, page_slot, page_owner, context_len, pool, q_list[0], n_req)
     pieces = other_attention(q_list, own, n_req, n_tp)
     depth = out_weight.shape[0]
-    early = depth * 3 // 8
-    first = load_weight(pieces[0], out_weight, 0, early)
-    arrived = jnp.stack([pieces[0]] + [swap(pieces[d], "tp", d) for d in range(1, n_tp)])
-    parts = [arrived] + [swap(arrived, "req", d) for d in range(1, n_req)]
-    second = load_weight(arrived, out_weight, early, depth - early)
-    sums = project(parts, (first, second), n_req, n_tp, chunk)
+    early = depth * 5 // 16
+    swapped = [swap(pieces[d], "tp", d) for d in range(1, n_tp)]
+    first, mine = load_weight(pieces[0], out_weight, 0, early)
+    arrived = jnp.stack([mine] + swapped)
+    parts = [swap(arrived, "req", d) for d in range(1, n_req)]
+    second, mine = load_weight(arrived, out_weight, early, depth - early)
+    sums = project([mine] + parts, (first, second), n_req, n_tp, chunk)
     total = sums[0]
     for d in range(1, n_tp):
         total = total + swap(sums[d], "tp", d).astype(jnp.float32)

time: 37.6 us -> 36.6 us (0.973)
  waiting for transfers between devices: 9.03 us -> 6.64 us
  other arithmetic: 0.67 us -> 1.5 us
  starting transfers between devices: 13.9 us -> 14.4 us
    ppermute x12 -> x11, waiting for transfers between devices: 9.03 us -> 6.64 us  [swap(): return lax.ppermute(x, axis, [(i, i ^ offset) for i in range(count)])]
    concatenate x0 -> x1, other arithmetic: none -> 0.83 us  [on_device(): held = jnp.concatenate([held, q_list[-1]], axis=0)]
    ppermute x12 -> x11, starting transfers between devices: 13.9 us -> 14.4 us  [swap(): return lax.ppermute(x, axis, [(i, i ^ offset) for i in range(count)])]
  transfers between devices with their start and end apart: 12 -> 11, of which waited for: 6 -> 5; matrix products, arithmetic and copies ran while one was open for 0% -> 0% of each run, Pallas kernels for 25% -> 26%
where the time goes in v5:
time: 36.6 us; the launch traced here: 36.4 us
  starting transfers between devices  14.4 us (39%)
  Pallas kernels  13.7 us (37%)
  waiting for transfers between devices  6.64 us (18%)
  other arithmetic  1.5 us (4%)
    ppermute x11, starting transfers between devices, swap(): return lax.ppermute(x, axis, [(i, i ^ offset) for i in range(count)])  14.4 us
    pallas_call x2, Pallas kernels, load_weight(): pl.pallas_call(functools.partial(load_kernel, first), out_shape=[jax.Shap...  6.93 us
    ppermute x11, waiting for transfers between devices, swap(): return lax.ppermute(x, axis, [(i, i ^ offset) for i in range(count)])  6.64 us
    pallas_call x1, Pallas kernels, project(): pl.pallas_call(functools.partial(project_kernel, n_req, n_tp, chunk), out...  3.6 us
    pallas_call x1, Pallas kernels, own_attention(): pl.pallas_call(functools.partial(own_kernel, n_req, own_pages), out_shape...  2.39 us
    concatenate x1, other arithmetic, on_device(): held = jnp.concatenate([held, q_list[-1]], axis=0)  0.83 us
    pallas_call x1, Pallas kernels, other_attention(): pl.pallas_call(functools.partial(other_kernel, n_req, n_tp), out_shape=[j...  0.76 us
  transfers between devices with their start and end apart: 11, of which 5 were waited for; matrix products, arithmetic and copies ran while one was open for 0% of the time, Pallas kernels for 26%

profile of v5, /device:TPU:0, one launch (start us, length us, event | category | flops | bytes accessed | tf_op | source)
XLA Modules:
  0.0 36.4 jit_solution(10622992047031288447)
XLA Ops:
  0.0 3.0 %collective-permute-start = (bf16[1,8192]{1,0:T(2,128)(2,1)}, bf16[1,8192]{1,0:T(2,128)(2,1)S(1)}, u32[]{:S(2)}, u32[]{:S(2)}) collective-permute-start(bf16[1,8192]{1,0:T(2,128)(2,1)} %refs_0_.1), channel_id=1, source_target_pairs={{0,1},{1,0},{2,3},{3,2},{4,5},{5,4},{6,7},{7,6},{8,9},{9,8},{10,11... | collective-permute-start | bytes 49160 | tf_op jit(solution)/shard_map/ppermute | solution.py:17
  3.0 2.1 %collective-permute-done.refs_6_.refs_0_ = bf16[1,8192]{1,0:T(2,128)(2,1)S(1)} collective-permute-done((bf16[1,8192]{1,0:T(2,128)(2,1)}, bf16[1,8192]{1,0:T(2,128)(2,1)S(1)}, u32[]{:S(2)}, u32[]{:S(2)}) %collective-permute-start) | collective-permute-done | bytes 16416 | tf_op jit(solution)/shard_map/ppermute | solution.py:17
  5.1 0.8 %pad_maximum_fusion.1 = bf16[2,8192]{1,0:T(2,128)(2,1)S(1)} fusion(bf16[1,8192]{1,0:T(2,128)(2,1)S(1)} %collective-permute-done.refs_6_.refs_0_, bf16[1,8192]{1,0:T(2,128)(2,1)} %refs_0_.1), kind=kLoop, calls=%fused_computation.2 | loop fusion | flops 65536 | bytes 65536 | tf_op jit(solution)/shard_map/concatenate | solution.py:435
  6.0 3.1 %collective-permute-start.1 = (bf16[2,8192]{1,0:T(2,128)(2,1)S(1)}, bf16[2,8192]{1,0:T(2,128)(2,1)S(1)}, u32[]{:S(2)}, u32[]{:S(2)}) collective-permute-start(bf16[2,8192]{1,0:T(2,128)(2,1)S(1)} %pad_maximum_fusion.1), channel_id=1, source_target_pairs={{0,2},{1,3},{2,0},{3,1},{4,6},{5,7},{6,4},{7,5},{8,10},{9,11},{10,... | collective-permute-start | bytes 98312 | tf_op jit(solution)/shard_map/ppermute | solution.py:17
  9.1 2.4 %own_attention.1 = (f32[64,128]{1,0:T(8,128)S(1)}, f32[8,128]{1,0:T(8,128)S(1)}, s32[8,128]{1,0:T(8,128)S(1)}, bf16[3,4,128,256]{3,2,1,0:T(8,128)(2,1)S(1)}) custom-call(bf16[1,8192]{1,0:T(2,128)(2,1)} %refs_0_.1, bf16[1,1024]{1,0:T(2,128)(2,1)} %refs_1_.1, s32[1,4,7]{2,1,0:T(4,128)} %refs_2_.1, s32[1,4,7]{2,1,0:T(4,128)} %refs_3_.1, s32[1,4]{1,0:T(1,128)} %refs_4_.1, ...), custom_call_target="tpu_custom_call" | custom-call | flops 25165824 | bytes 4718592 | tf_op jit(solution)/shard_map/own_attention/pallas_call | solution.py:199
  11.5 0.0 collective-permute-done.1.refs_1_
  11.5 0.8 %other_attention.1 = (bf16[72,128]{1,0:T(8,128)(2,1)S(1)}, bf16[72,128]{1,0:T(8,128)(2,1)S(1)}, bf16[72,128]{1,0:T(8,128)(2,1)S(1)}, bf16[72,128]{1,0:T(8,128)(2,1)S(1)}) custom-call(bf16[1,8192]{1,0:T(2,128)(2,1)S(1)} %collective-permute-done.refs_6_.refs_0_, bf16[2,8192]{1,0:T(2,128)(2,1)S(1)} %collective-permute-done.1.refs_1_, ...), custom_call_target="tpu_custom_call" | custom-call | flops 12582912 | bytes 786432 | tf_op jit(solution)/shard_map/other_attention/pallas_call | solution.py:298
  12.2 0.1 collective-permute-start.2
  12.3 1.6 %collective-permute-start.3 = (bf16[72,128]{1,0:T(8,128)(2,1)S(1)}, bf16[72,128]{1,0:T(8,128)(2,1)S(1)}, u32[]{:S(2)}, u32[]{:S(2)}) collective-permute-start(bf16[72,128]{1,0:T(8,128)(2,1)S(1)} %get-tuple-element.28), channel_id=1, source_target_pairs={{0,8},{4,12},{8,0},{12,4},{1,9},{5,13},{9,1},{13,5},{2,10},{6,14},... | collective-permute-start | bytes 55304 | tf_op jit(solution)/shard_map/ppermute | solution.py:17
  13.9 0.3 collective-permute-start.4
  14.2 2.5 %load_weight.2 = (bf16[640,4096]{1,0:T(8,128)(2,1)S(1)}, bf16[72,128]{1,0:T(8,128)(2,1)S(1)}) custom-call(bf16[72,128]{1,0:T(8,128)(2,1)S(1)} %get-tuple-element.25.piece_ref, bf16[2048,4096]{1,0:T(8,128)(2,1)} %weight_hbm.3), custom_call_target="tpu_custom_call" | custom-call | bytes 10485760 | tf_op jit(solution)/shard_map/load_weight/pallas_call | solution.py:338
  16.7 0.0 collective-permute-done.2
  16.7 0.0 collective-permute-done.3
  16.7 0.3 collective-permute-done.4
  17.1 3.7 %collective-permute-start.7 = (bf16[4,72,128]{2,1,0:T(8,128)(2,1)S(1)}, bf16[4,72,128]{2,1,0:T(8,128)(2,1)S(1)}, u32[]{:S(2)}, u32[]{:S(2)}) collective-permute-start(bf16[4,72,128]{2,1,0:T(8,128)(2,1)S(1)} %pad_maximum_fusion.piece_ref), channel_id=1, source_target_pairs={{0,3},{1,2},{2,1},{3,0},{4,7},{5,6},{6,5},{7,4},{8,11},{9,10},{10,... | collective-permute-start | bytes 221192 | tf_op jit(solution)/shard_map/ppermute | solution.py:17
  20.8 0.0 collective-permute-start.6
  20.8 0.7 %collective-permute-start.5 = (bf16[4,72,128]{2,1,0:T(8,128)(2,1)S(1)}, bf16[4,72,128]{2,1,0:T(8,128)(2,1)S(1)}, u32[]{:S(2)}, u32[]{:S(2)}) collective-permute-start(bf16[4,72,128]{2,1,0:T(8,128)(2,1)S(1)} %pad_maximum_fusion.piece_ref), channel_id=1, source_target_pairs={{0,1},{1,0},{2,3},{3,2},{4,5},{5,4},{6,7},{7,6},{8,9},{9,8},{10,11... | collective-permute-start | bytes 221192 | tf_op jit(solution)/shard_map/ppermute | solution.py:17
  21.5 4.4 %load_weight.3 = (bf16[1408,4096]{1,0:T(8,128)(2,1)S(1)}, bf16[4,72,128]{2,1,0:T(8,128)(2,1)S(1)}) custom-call(bf16[4,72,128]{2,1,0:T(8,128)(2,1)S(1)} %pad_maximum_fusion.piece_ref, bf16[2048,4096]{1,0:T(8,128)(2,1)} %weight_hbm.3), custom_call_target="tpu_custom_call" | custom-call | bytes 23068672 | tf_op jit(solution)/shard_map/load_weight/pallas_call | solution.py:338
  25.9 0.0 collective-permute-done.7.refs_3_
  25.9 1.3 %collective-permute-done.6.refs_2_ = bf16[4,72,128]{2,1,0:T(8,128)(2,1)S(1)} collective-permute-done((bf16[4,72,128]{2,1,0:T(8,128)(2,1)S(1)}, bf16[4,72,128]{2,1,0:T(8,128)(2,1)S(1)}, u32[]{:S(2)}, u32[]{:S(2)}) %collective-permute-start.6) | collective-permute-done | bytes 73760 | tf_op jit(solution)/shard_map/ppermute | solution.py:17
  27.2 0.0 collective-permute-done.5.refs_1_
  27.2 3.6 %project.1 = (f32[4,4096]{1,0:T(4,128)S(1)}, bf16[4,4096]{1,0:T(4,128)(2,1)S(1)}, bf16[4,4096]{1,0:T(4,128)(2,1)S(1)}, bf16[4,4096]{1,0:T(4,128)(2,1)S(1)}) custom-call(bf16[4,72,128]{2,1,0:T(8,128)(2,1)S(1)} %get-tuple-element.30.refs_0_, bf16[4,72,128]{2,1,0:T(8,128)(2,1)S(1)} %collective-permute-done.5.refs_1_, ...), custom_call_target="tpu_custom_call" | custom-call | flops 268435456 | bytes 16777216 | tf_op jit(solution)/shard_map/project/pallas_call | solution.py:407
  30.9 0.1 collective-permute-start.8
  30.9 1.4 %collective-permute-start.9 = (bf16[4,4096]{1,0:T(4,128)(2,1)S(1)}, bf16[4,4096]{1,0:T(4,128)(2,1)S(1)}, u32[]{:S(2)}, u32[]{:S(2)}) collective-permute-start(bf16[4,4096]{1,0:T(4,128)(2,1)S(1)} %get-tuple-element.35), channel_id=1, source_target_pairs={{0,8},{4,12},{8,0},{12,4},{1,9},{5,13},{9,1},{13,5},{2,10},{6,14},... | collective-permute-start | bytes 98312 | tf_op jit(solution)/shard_map/ppermute | solution.py:17
  32.4 0.4 %collective-permute-start.10 = (bf16[4,4096]{1,0:T(4,128)(2,1)S(1)}, bf16[4,4096]{1,0:T(4,128)(2,1)S(1)}, u32[]{:S(2)}, u32[]{:S(2)}) collective-permute-start(bf16[4,4096]{1,0:T(4,128)(2,1)S(1)} %get-tuple-element.36), channel_id=1, source_target_pairs={{0,12},{4,8},{8,4},{12,0},{1,13},{5,9},{9,5},{13,1},{2,14},{6,10},... | collective-permute-start | bytes 98312 | tf_op jit(solution)/shard_map/ppermute | solution.py:17
  32.8 0.0 collective-permute-done.8
  32.8 2.1 %collective-permute-done.9 = bf16[4,4096]{1,0:T(4,128)(2,1)S(1)} collective-permute-done((bf16[4,4096]{1,0:T(4,128)(2,1)S(1)}, bf16[4,4096]{1,0:T(4,128)(2,1)S(1)}, u32[]{:S(2)}, u32[]{:S(2)}) %collective-permute-start.9) | collective-permute-done | bytes 32800 | tf_op jit(solution)/shard_map/ppermute | solution.py:17
  34.9 0.8 %collective-permute-done.10 = bf16[4,4096]{1,0:T(4,128)(2,1)S(1)} collective-permute-done((bf16[4,4096]{1,0:T(4,128)(2,1)S(1)}, bf16[4,4096]{1,0:T(4,128)(2,1)S(1)}, u32[]{:S(2)}, u32[]{:S(2)}) %collective-permute-start.10) | collective-permute-done | bytes 32800 | tf_op jit(solution)/shard_map/ppermute | solution.py:17
  35.7 0.7 %add_convert_fusion = bf16[4,4096]{1,0:T(4,128)(2,1)} fusion(bf16[4,4096]{1,0:T(4,128)(2,1)S(1)} %collective-permute-done.10, bf16[4,4096]{1,0:T(4,128)(2,1)S(1)} %collective-permute-done.9, f32[4,4096]{1,0:T(4,128)S(1)} %get-tuple-element.33, bf16[4,4096]{1,0:T(4,128)(2,1)S(1)} %collective-permute-done.8), kind=kLoop, calls=%fused_computation.1 | loop fusion | flops 114688 | bytes 196608 | tf_op jit(solution)/shard_map/convert_element_type | solution.py:449
  (1 shorter events, 0.0 us)
Async XLA Ops:
  0.0 5.1 %collective-permute-start = (bf16[1,8192]{1,0:T(2,128)(2,1)}, bf16[1,8192]{1,0:T(2,128)(2,1)S(1)}, u32[]{:S(2)}, u32[]{:S(2)}) collective-permute-start(bf16[1,8192]{1,0:T(2,128)(2,1)} %refs_0_.1), channel_id=1, source_target_pairs={{0,1},{1,0},{2,3},{3,2},{4,5},{5,4},{6,7},{7,6},{8,9},{9,8},{10,11... | collective-permute-start | bytes 49160 | tf_op jit(solution)/shard_map/ppermute | solution.py:17
  6.0 5.5 %collective-permute-start.1 = (bf16[2,8192]{1,0:T(2,128)(2,1)S(1)}, bf16[2,8192]{1,0:T(2,128)(2,1)S(1)}, u32[]{:S(2)}, u32[]{:S(2)}) collective-permute-start(bf16[2,8192]{1,0:T(2,128)(2,1)S(1)} %pad_maximum_fusion.1), channel_id=1, source_target_pairs={{0,2},{1,3},{2,0},{3,1},{4,6},{5,7},{6,4},{7,5},{8,10},{9,11},{10,... | collective-permute-start | bytes 98312 | tf_op jit(solution)/shard_map/ppermute | solution.py:17
  12.2 4.5 %collective-permute-start.2 = (bf16[72,128]{1,0:T(8,128)(2,1)S(1)}, bf16[72,128]{1,0:T(8,128)(2,1)S(1)}, u32[]{:S(2)}, u32[]{:S(2)}) collective-permute-start(bf16[72,128]{1,0:T(8,128)(2,1)S(1)} %get-tuple-element.27), channel_id=1, source_target_pairs={{0,4},{4,0},{8,12},{12,8},{1,5},{5,1},{9,13},{13,9},{2,6},{6,2},{1... | collective-permute-start | bytes 55304 | tf_op jit(solution)/shard_map/ppermute | solution.py:17
  12.3 4.4 %collective-permute-start.3 = (bf16[72,128]{1,0:T(8,128)(2,1)S(1)}, bf16[72,128]{1,0:T(8,128)(2,1)S(1)}, u32[]{:S(2)}, u32[]{:S(2)}) collective-permute-start(bf16[72,128]{1,0:T(8,128)(2,1)S(1)} %get-tuple-element.28), channel_id=1, source_target_pairs={{0,8},{4,12},{8,0},{12,4},{1,9},{5,13},{9,1},{13,5},{2,10},{6,14},... | collective-permute-start | bytes 55304 | tf_op jit(solution)/shard_map/ppermute | solution.py:17
  13.9 3.2 %collective-permute-start.4 = (bf16[72,128]{1,0:T(8,128)(2,1)S(1)}, bf16[72,128]{1,0:T(8,128)(2,1)S(1)}, u32[]{:S(2)}, u32[]{:S(2)}) collective-permute-start(bf16[72,128]{1,0:T(8,128)(2,1)S(1)} %get-tuple-element.29), channel_id=1, source_target_pairs={{0,12},{4,8},{8,4},{12,0},{1,13},{5,9},{9,5},{13,1},{2,14},{6,10},... | collective-permute-start | bytes 55304 | tf_op jit(solution)/shard_map/ppermute | solution.py:17
  17.1 8.9 %collective-permute-start.7 = (bf16[4,72,128]{2,1,0:T(8,128)(2,1)S(1)}, bf16[4,72,128]{2,1,0:T(8,128)(2,1)S(1)}, u32[]{:S(2)}, u32[]{:S(2)}) collective-permute-start(bf16[4,72,128]{2,1,0:T(8,128)(2,1)S(1)} %pad_maximum_fusion.piece_ref), channel_id=1, source_target_pairs={{0,3},{1,2},{2,1},{3,0},{4,7},{5,6},{6,5},{7,4},{8,11},{9,10},{10,... | collective-permute-start | bytes 221192 | tf_op jit(solution)/shard_map/ppermute | solution.py:17
  20.8 6.5 %collective-permute-start.6 = (bf16[4,72,128]{2,1,0:T(8,128)(2,1)S(1)}, bf16[4,72,128]{2,1,0:T(8,128)(2,1)S(1)}, u32[]{:S(2)}, u32[]{:S(2)}) collective-permute-start(bf16[4,72,128]{2,1,0:T(8,128)(2,1)S(1)} %pad_maximum_fusion.piece_ref), channel_id=1, source_target_pairs={{0,2},{1,3},{2,0},{3,1},{4,6},{5,7},{6,4},{7,5},{8,10},{9,11},{10,... | collective-permute-start | bytes 221192 | tf_op jit(solution)/shard_map/ppermute | solution.py:17
  20.8 6.5 %collective-permute-start.5 = (bf16[4,72,128]{2,1,0:T(8,128)(2,1)S(1)}, bf16[4,72,128]{2,1,0:T(8,128)(2,1)S(1)}, u32[]{:S(2)}, u32[]{:S(2)}) collective-permute-start(bf16[4,72,128]{2,1,0:T(8,128)(2,1)S(1)} %pad_maximum_fusion.piece_ref), channel_id=1, source_target_pairs={{0,1},{1,0},{2,3},{3,2},{4,5},{5,4},{6,7},{7,6},{8,9},{9,8},{10,11... | collective-permute-start | bytes 221192 | tf_op jit(solution)/shard_map/ppermute | solution.py:17
  30.9 1.9 %collective-permute-start.8 = (bf16[4,4096]{1,0:T(4,128)(2,1)S(1)}, bf16[4,4096]{1,0:T(4,128)(2,1)S(1)}, u32[]{:S(2)}, u32[]{:S(2)}) collective-permute-start(bf16[4,4096]{1,0:T(4,128)(2,1)S(1)} %get-tuple-element.34), channel_id=1, source_target_pairs={{0,4},{4,0},{8,12},{12,8},{1,5},{5,1},{9,13},{13,9},{2,6},{6,2},{1... | collective-permute-start | bytes 98312 | tf_op jit(solution)/shard_map/ppermute | solution.py:17
  30.9 4.0 %collective-permute-start.9 = (bf16[4,4096]{1,0:T(4,128)(2,1)S(1)}, bf16[4,4096]{1,0:T(4,128)(2,1)S(1)}, u32[]{:S(2)}, u32[]{:S(2)}) collective-permute-start(bf16[4,4096]{1,0:T(4,128)(2,1)S(1)} %get-tuple-element.35), channel_id=1, source_target_pairs={{0,8},{4,12},{8,0},{12,4},{1,9},{5,13},{9,1},{13,5},{2,10},{6,14},... | collective-permute-start | bytes 98312 | tf_op jit(solution)/shard_map/ppermute | solution.py:17
  32.4 3.3 %collective-permute-start.10 = (bf16[4,4096]{1,0:T(4,128)(2,1)S(1)}, bf16[4,4096]{1,0:T(4,128)(2,1)S(1)}, u32[]{:S(2)}, u32[]{:S(2)}) collective-permute-start(bf16[4,4096]{1,0:T(4,128)(2,1)S(1)} %get-tuple-element.36), channel_id=1, source_target_pairs={{0,12},{4,8},{8,4},{12,0},{1,13},{5,9},{9,5},{13,1},{2,14},{6,10},... | collective-permute-start | bytes 98312 | tf_op jit(solution)/shard_map/ppermute | solution.py:17

commit v6 on v5

--- a/solution.py
+++ b/solution.py
@@ -29,16 +29,8 @@
     return pltpu.roll(x, 64, 1)
 
 
-def lay_rows(places, q_ref):
-    head_dim = places[0][0].shape[1]
-    for h in range(64):
-        block = q_ref[:, h * head_dim : (h + 1) * head_dim].astype(jnp.float32)
-        for i, (target, start) in enumerate(places):
-            target[start + h : start + h + 1] = block[i : i + 1]
-
-
 def query_tiles(stacked, kv_heads):
-    turned = stacked.T
+    turned = stacked.astype(jnp.float32).T
     lane = lax.broadcasted_iota(jnp.int32, turned.shape, 1)
     group = 64 // kv_heads
     return [
@@ -88,9 +80,9 @@
 
 
 def own_kernel(n_req, own_pages, *refs):
-    (q_hbm, kv_hbm, slot_hbm, owner_hbm, len_hbm, pool_hbm) = refs[:6]
-    acc_ref, log_ref, limit_ref, pages_ref = refs[7:11]
-    q_row, q_heads, kv, slots, owners, lens, pool, small_sem, pool_sem, page_sem = refs[11:]
+    q_ref, kv_hbm, slot_hbm, owner_hbm, len_hbm, pool_hbm = refs[:6]
+    acc_ref, log_ref, limit_ref, pages_ref = refs[6:10]
+    kv, slots, owners, lens, pool, small_sem, pool_sem, page_sem = refs[10:]
     slot_count, kv_heads, page_len, width = pool_hbm.shape
     head_dim = width // 2
     entries = slot_hbm.shape[2]
@@ -99,13 +91,14 @@
     small = [
         pltpu.make_async_copy(src, dst, small_sem.at[i])
         for i, (src, dst) in enumerate(
-            ((slot_hbm, slots), (owner_hbm, owners), (len_hbm, lens), (kv_hbm, kv), (q_hbm, q_row))
+            ((slot_hbm, slots), (owner_hbm, owners), (len_hbm, lens), (kv_hbm, kv))
         )
     ]
     for copy in small:
         copy.start()
     whole = pltpu.make_async_copy(pool_hbm, pool, pool_sem)
     whole.start()
+    tiles = query_tiles(jnp.concatenate([q_ref[...], q_ref[...]], axis=0), kv_heads)
     for copy in small:
         copy.wait()
 
@@ -130,9 +123,6 @@
     for p in range(len(limits) // 2):
         limit_ref[p : p + 1] = jnp.where(lane < 64, limits[2 * p], limits[2 * p + 1])
 
-    lay_rows([(q_heads, 0)], q_row)
-    q_heads[64:] = q_heads[:64]
-    tiles = query_tiles(q_heads[...], kv_heads)
     my_length = lens[0, me]
     pages, valid = [], []
     for i in range(own_pages):
@@ -187,10 +177,10 @@
         copy.wait()
 
 
-def own_attention(q, new_kv, page_slot, page_owner, context_len, pool, after, n_req):
+def own_attention(q, new_kv, page_slot, page_owner, context_len, pool, n_req):
     slots, kv_heads, page_len, width = pool.shape
     head_dim = width // 2
-    heads = q.shape[1] // head_dim
+    heads = q.shape[0]
     own_pages = min(slots, page_slot.shape[2])
     hbm = pl.BlockSpec(memory_space=pltpu.HBM)
     vmem = pl.BlockSpec(memory_space=pltpu.VMEM)
@@ -204,17 +194,15 @@
             jax.ShapeDtypeStruct((round_up(pair_count, 8), 128), jnp.int32),
             jax.ShapeDtypeStruct((n_req - 1, kv_heads, page_len, width), pool.dtype),
         ],
-        in_specs=[hbm] * 6 + [pl.BlockSpec(memory_space=pl.ANY)],
+        in_specs=[vmem] + [hbm] * 5,
         out_specs=[vmem] * 4,
         scratch_shapes=[
-            pltpu.VMEM(q.shape, q.dtype),
-            pltpu.VMEM((128, head_dim), jnp.float32),
             pltpu.VMEM(new_kv.shape, new_kv.dtype),
             pltpu.SMEM(page_slot.shape, jnp.int32),
             pltpu.SMEM(page_owner.shape, jnp.int32),
             pltpu.SMEM(context_len.shape, jnp.int32),
             pltpu.VMEM(pool.shape, pool.dtype),
-            pltpu.SemaphoreType.DMA((5,)),
+            pltpu.SemaphoreType.DMA((4,)),
             pltpu.SemaphoreType.DMA,
             pltpu.SemaphoreType.DMA((n_req - 1,)),
         ],
@@ -225,37 +213,34 @@
             transcendentals=0,
         ),
         name="own_attention",
-    )(*(in_hbm(x) for x in (q, new_kv, page_slot, page_owner, context_len, pool)), after)
-
-
-def stat_rows_of(n_req):
-    return round_up(2 * n_req, 8)
+    )(q, *(in_hbm(x) for x in (new_kv, page_slot, page_owner, context_len, pool)))
 
 
 def other_kernel(n_req, n_tp, *refs):
-    count = n_req.bit_length() - 1
-    acc_ref, log_ref, limit_ref, pages_ref = refs[count : count + 4]
-    out_refs = refs[count + 4 : count + 4 + n_tp]
-    results, logs, stats, q_heads = refs[count + 4 + n_tp :]
+    q_refs = refs[: n_req - 1]
+    acc_ref, log_ref, limit_ref, pages_ref = refs[n_req - 1 : n_req + 3]
+    out_refs = refs[n_req + 3 : n_req + 3 + n_tp]
+    results, logs = refs[n_req + 3 + n_tp :]
     kv_heads, width = pages_ref.shape[1], pages_ref.shape[3]
     head_dim = width // 2
-    heads = results.shape[1]
-    chunk = heads // n_tp
+    chunk = 64 // n_tp
     my_tp = lax.axis_index("tp")
+    me = lax.axis_index("req")
     scale = 1.0 / math.sqrt(head_dim)
     others = n_req - 1
     pairs = round_up(others, 2) // 2
-    results[0] = acc_ref[...]
-    logs[0:1] = log_ref[0:1]
-    for k in range(count):
-        lay_rows([(q_heads.at[(d - 1) // 2], (d - 1) % 2 * 64) for d in range(1 << k, 2 << k)], refs[k])
-    if others % 2:
-        q_heads[pairs - 1, 64:] = q_heads[pairs - 1, :64]
+
+    def keep(d, result, log_row):
+        n = me ^ d
+        results[pl.ds(pl.multiple_of(n * 64, 64), 64)] = result
+        logs[pl.ds(n, 1)] = log_row
+
+    logs[...] = jnp.zeros_like(logs)
     scores, members = [], []
     for p in range(pairs):
         a, b = 2 * p, min(2 * p + 1, others - 1)
         members.append((a, b))
-        tiles = query_tiles(q_heads[p], kv_heads)
+        tiles = query_tiles(jnp.concatenate([q_refs[a][...], q_refs[b][...]], axis=0), kv_heads)
         scores.append(pair_scores(pages_ref.at[a], pages_ref.at[b], tiles, head_dim) * scale)
     sums, inverse, log_rows = [], [], []
     for p in range(pairs):
@@ -266,45 +251,43 @@
         inverse.append(1.0 / total)
         log_rows.append(top + jnp.log(total))
     columns = to_columns(inverse)
+    keep(0, acc_ref[...], log_ref[0:1])
     for p in range(pairs):
         result = sums[p] * columns[:, p : p + 1]
-        results[2 * p + 1] = result[:64]
-        logs[2 * p + 1 : 2 * p + 2] = log_rows[p]
+        keep(2 * p + 1, result[:64], log_rows[p])
         if 2 * p + 1 < others:
-            results[2 * p + 2] = result[64:]
-            logs[2 * p + 2 : 2 * p + 3] = halves(log_rows[p])
-    lane = lax.broadcasted_iota(jnp.int32, (n_req, 128), 1)
-    value = logs[0:n_req]
+            keep(2 * p + 2, result[64:], halves(log_rows[p]))
+
+    value = logs[...]
+    lane = lax.broadcasted_iota(jnp.int32, value.shape, 1)
     high = value.astype(jnp.bfloat16).astype(jnp.float32)
     rest = value - high
     middle = rest.astype(jnp.bfloat16).astype(jnp.float32)
-    stats[...] = jnp.zeros_like(stats)
-    stats[0:n_req] = jnp.where(lane < 64, high, halves(middle))
-    stats[n_req : 2 * n_req] = jnp.where(lane < 64, rest - middle, 0.0)
-    tail = stats[...].astype(jnp.bfloat16)
-    rows = n_req * chunk
+    low = rest - middle
     for d in range(n_tp):
-        at = pl.ds(pl.multiple_of((my_tp ^ d) * chunk, chunk), chunk)
-        for k in range(n_req):
-            out_refs[d][k * chunk : (k + 1) * chunk] = results[k, at].astype(jnp.bfloat16)
-        out_refs[d][rows:] = tail
+        first = (my_tp ^ d) * chunk
+        for h in range(chunk):
+            rows = results[pl.ds(first + h, n_req, stride=64)]
+            out_refs[d][:, h * head_dim : (h + 1) * head_dim] = rows.astype(jnp.bfloat16)
+        shift = 128 - first
+        stats = jnp.where(lane < chunk, pltpu.roll(high, shift % 128, 1), 0.0)
+        stats = jnp.where((lane >= chunk) & (lane < 2 * chunk), pltpu.roll(middle, (shift + chunk) % 128, 1), stats)
+        stats = jnp.where((lane >= 2 * chunk) & (lane < 3 * chunk), pltpu.roll(low, (shift + 2 * chunk) % 128, 1), stats)
+        out_refs[d][:, chunk * head_dim :] = stats[:n_req].astype(jnp.bfloat16)
 
 
 def other_attention(q_list, own, n_req, n_tp):
     heads, head_dim = own[0].shape
     chunk = heads // n_tp
-    rows = n_req * chunk + stat_rows_of(n_req)
     vmem = pl.BlockSpec(memory_space=pltpu.VMEM)
     return pl.pallas_call(
         functools.partial(other_kernel, n_req, n_tp),
-        out_shape=[jax.ShapeDtypeStruct((rows, head_dim), jnp.bfloat16)] * n_tp,
-        in_specs=[vmem] * (len(q_list) + 4),
+        out_shape=[jax.ShapeDtypeStruct((n_req, chunk * head_dim + 128), jnp.bfloat16)] * n_tp,
+        in_specs=[vmem] * (n_req + 3),
         out_specs=[vmem] * n_tp,
         scratch_shapes=[
-            pltpu.VMEM((n_req, heads, head_dim), jnp.float32),
+            pltpu.VMEM((n_req * heads, head_dim), jnp.float32),
             pltpu.VMEM((round_up(n_req, 8), 128), jnp.float32),
-            pltpu.VMEM((stat_rows_of(n_req), 128), jnp.float32),
-            pltpu.VMEM((round_up(n_req - 1, 2) // 2, 128, head_dim), jnp.float32),
         ],
         compiler_params=pltpu.CompilerParams(vmem_limit_bytes=16 * MIB),
         cost_estimate=pl.CostEstimate(flops=2 * own[3].size * 16, bytes_accessed=own[3].size * 2, transcendentals=0),
@@ -350,74 +333,53 @@
     )(piece, in_hbm(out_weight))
 
 
-def project_kernel(n_req, n_tp, chunk, *refs):
+def project_kernel(n_req, n_tp, *refs):
     part_refs = refs[:n_req]
     weight_refs = refs[n_req : n_req + 2]
     out_refs = refs[n_req + 2 : n_req + 2 + n_tp]
-    wide, logs, attention, sums = refs[n_req + 2 + n_tp :]
-    rows = n_req * chunk
-    total_rows = n_tp * n_req
+    attention = refs[n_req + 2 + n_tp]
     split, columns = weight_refs[0].shape
-    my_tp = lax.axis_index("tp")
-    me = lax.axis_index("req")
-    for r in range(n_req):
-        for c in range(n_tp):
-            col = my_tp ^ c
-            block = part_refs[r][c, :rows].astype(jnp.float32)
-            tail = part_refs[r][c, rows:].astype(jnp.float32)
-            value = (tail[:n_req] + halves(tail[:n_req])) + tail[n_req : 2 * n_req]
-            for k in range(n_req):
-                row = col * n_req + (me ^ r ^ k)
-                wide[r, pl.ds(pl.multiple_of(row * chunk, chunk), chunk)] = block[k * chunk : (k + 1) * chunk]
-                logs[r, pl.ds(row, 1)] = value[k : k + 1]
-    shift = (128 - my_tp * chunk) % 128
-    values = [pltpu.roll(logs[r], shift, 1) for r in range(n_req)]
+    depth = attention.shape[1]
+    chunk = depth // 128
+    values = []
+    for part in part_refs:
+        stats = part[:, depth:].astype(jnp.float32)
+        values.append(stats + pltpu.roll(stats, 128 - chunk, 1) + pltpu.roll(stats, 128 - 2 * chunk, 1))
     top = functools.reduce(jnp.maximum, values)
     factors = [jnp.exp(v - top) for v in values]
     total = functools.reduce(jnp.add, factors)
     factors = [f / total for f in factors]
     for h in range(chunk):
-        block = None
-        for r in range(n_req):
-            term = wide[r, pl.ds(h, total_rows, stride=chunk)] * factors[r][:, h : h + 1]
-            block = term if block is None else block + term
-        attention[:, h * 128 : (h + 1) * 128] = block.astype(jnp.bfloat16)
-    tile = min(columns, 512)
+        at = slice(h * 128, (h + 1) * 128)
+        terms = [part[:, at].astype(jnp.float32) * f[:, h : h + 1] for part, f in zip(part_refs, factors)]
+        attention[:, at] = functools.reduce(jnp.add, terms).astype(jnp.bfloat16)
+    tile = min(columns, 1024)
 
     @pl.loop(0, columns // tile)
     def _(t):
         at = pl.ds(pl.multiple_of(t * tile, tile), tile)
         product = jnp.dot(attention[:, :split], weight_refs[0][:, at], preferred_element_type=jnp.float32)
         product += jnp.dot(attention[:, split:], weight_refs[1][:, at], preferred_element_type=jnp.float32)
-        for c in range(n_tp):
-            sums[c, :, at] = product[c * n_req : (c + 1) * n_req]
-
-    for d in range(n_tp):
-        out_refs[d][...] = sums[my_tp ^ d].astype(out_refs[d].dtype)
-
-
-def project(parts, weights, n_req, n_tp, chunk):
+        for d in range(n_tp):
+            out_refs[d][:, at] = product[d * n_req : (d + 1) * n_req].astype(out_refs[d].dtype)
+
+
+def project(parts, weights, n_req, n_tp):
     depth = sum(w.shape[0] for w in weights)
     columns = weights[0].shape[1]
-    rows = n_req * chunk
     vmem = pl.BlockSpec(memory_space=pltpu.VMEM)
     own = jax.ShapeDtypeStruct((n_req, columns), jnp.float32)
     sent = jax.ShapeDtypeStruct((n_req, columns), jnp.bfloat16)
-    total_rows = n_tp * n_req
+    rows = n_tp * n_req
     return pl.pallas_call(
-        functools.partial(project_kernel, n_req, n_tp, chunk),
+        functools.partial(project_kernel, n_req, n_tp),
         out_shape=[own] + [sent] * (n_tp - 1),
         in_specs=[vmem] * (n_req + 2),
         out_specs=[vmem] * n_tp,
-        scratch_shapes=[
-            pltpu.VMEM((n_req, n_tp * rows, 128), jnp.float32),
-            pltpu.VMEM((n_req, total_rows, 128), jnp.float32),
-            pltpu.VMEM((total_rows, depth), jnp.bfloat16),
-            pltpu.VMEM((n_tp, n_req, columns), jnp.float32),
-        ],
-        compiler_params=pltpu.CompilerParams(vmem_limit_bytes=24 * MIB),
+        scratch_shapes=[pltpu.VMEM((rows, depth), jnp.bfloat16)],
+        compiler_params=pltpu.CompilerParams(vmem_limit_bytes=16 * MIB),
         cost_estimate=pl.CostEstimate(
-            flops=2 * total_rows * depth * columns, bytes_accessed=depth * columns * 2, transcendentals=0
+            flops=2 * rows * depth * columns, bytes_accessed=depth * columns * 2, transcendentals=0
         ),
         name="project",
     )(*parts, *weights)
@@ -428,21 +390,18 @@
     n_tp = lax.axis_size("tp")
     pool = cache_pool[0, 0]
     head_dim = pool.shape[3] // 2
-    chunk = queries.shape[1] // head_dim // n_tp
-    held, q_list = queries, []
-    for k in range(n_req.bit_length() - 1):
-        q_list.append(swap(held, "req", 1 << k))
-        held = jnp.concatenate([held, q_list[-1]], axis=0)
-    own = own_attention(queries, new_kv, page_slot, page_owner, context_len, pool, q_list[0], n_req)
+    q = queries.reshape(-1, head_dim)
+    q_list = [swap(q, "req", d) for d in range(1, n_req)]
+    own = own_attention(q, new_kv, page_slot, page_owner, context_len, pool, n_req)
     pieces = other_attention(q_list, own, n_req, n_tp)
     depth = out_weight.shape[0]
     early = depth * 5 // 16
     swapped = [swap(pieces[d], "tp", d) for d in range(1, n_tp)]
     first, mine = load_weight(pieces[0], out_weight, 0, early)
-    arrived = jnp.stack([mine] + swapped)
+    arrived = jnp.concatenate([mine] + swapped, axis=0)
     parts = [swap(arrived, "req", d) for d in range(1, n_req)]
     second, mine = load_weight(arrived, out_weight, early, depth - early)
-    sums = project([mine] + parts, (first, second), n_req, n_tp, chunk)
+    sums = project([mine] + parts, (first, second), n_req, n_tp)
     total = sums[0]
     for d in range(1, n_tp):
         total = total + swap(sums[d], "tp", d).astype(jnp.float32)

time: 36.6 us -> 34 us (0.929)
  waiting for transfers between devices: 6.64 us -> 5.11 us
  Pallas kernels: 13.7 us -> 13 us
  starting transfers between devices: 14.4 us -> 14 us
    ppermute x11 -> x12, waiting for transfers between devices: 6.64 us -> 5.11 us  [swap(): return lax.ppermute(x, axis, [(i, i ^ offset) for i in range(count)])]
    unnamed x0 -> x1, other arithmetic: none -> 0.85 us
    concatenate x1, other arithmetic: 0.83 us -> 0.05 us  [on_device(): arrived = jnp.concatenate([mine] + swapped, axis=0)]
    pallas_call x1, Pallas kernels: 3.6 us -> 2.97 us  [project(): pl.pallas_call(functools.partial(project_kernel, n_req, n_tp), out_shape=...]
    ppermute x11 -> x12, starting transfers between devices: 14.4 us -> 14 us  [swap(): return lax.ppermute(x, axis, [(i, i ^ offset) for i in range(count)])]
  transfers between devices with their start and end apart: 11 -> 12, of which waited for: 5 -> 5; matrix products, arithmetic and copies ran while one was open for 0% -> 0% of each run, Pallas kernels for 26% -> 27%
where the time goes in v6:
time: 34 us; the launch traced here: 33.8 us
  starting transfers between devices  14 us (41%)
  Pallas kernels  13 us (38%)
  waiting for transfers between devices  5.11 us (15%)
  other arithmetic  1.55 us (5%)
    ppermute x12, starting transfers between devices, swap(): return lax.ppermute(x, axis, [(i, i ^ offset) for i in range(count)])  14 us
    pallas_call x2, Pallas kernels, load_weight(): pl.pallas_call(functools.partial(load_kernel, first), out_shape=[jax.Shap...  6.93 us
    ppermute x12, waiting for transfers between devices, swap(): return lax.ppermute(x, axis, [(i, i ^ offset) for i in range(count)])  5.11 us
    pallas_call x1, Pallas kernels, project(): pl.pallas_call(functools.partial(project_kernel, n_req, n_tp), out_shape=...  2.97 us
    pallas_call x1, Pallas kernels, own_attention(): pl.pallas_call(functools.partial(own_kernel, n_req, own_pages), out_shape...  2.36 us
    unnamed x1, other arithmetic  0.85 us
    pallas_call x1, Pallas kernels, other_attention(): pl.pallas_call(functools.partial(other_kernel, n_req, n_tp), out_shape=[j...  0.79 us
  transfers between devices with their start and end apart: 12, of which 5 were waited for; matrix products, arithmetic and copies ran while one was open for 0% of the time, Pallas kernels for 27%

profile of v6, /device:TPU:0, one launch (start us, length us, event | category | flops | bytes accessed | tf_op | source)
XLA Modules:
  0.0 33.8 jit_solution(2187969050754629149)
XLA Ops:
  0.0 0.8 %reduce = bf16[8192]{0:T(1024)(128)(2,1)S(1)} reduce(bf16[1,8192]{1,0:T(2,128)(2,1)} %param.7, bf16[]{:T(256)} %constant.6), dimensions={0}, to_apply=%param.7.reduce_sub_computation | reduce | bytes 32770 | tf_op args[0]
  0.8 5.1 %collective-permute-start.2 = (bf16[64,128]{1,0:T(8,128)(2,1)S(1)}, bf16[64,128]{1,0:T(8,128)(2,1)S(1)}, u32[]{:S(2)}, u32[]{:S(2)}) collective-permute-start(bf16[64,128]{1,0:T(8,128)(2,1)S(1)} %bitcast.2), channel_id=1, source_target_pairs={{0,3},{1,2},{2,1},{3,0},{4,7},{5,6},{6,5},{7,4},{8,11},{9,10},{10,... | collective-permute-start | bytes 49160 | tf_op jit(solution)/shard_map/ppermute | solution.py:17
  6.0 0.0 collective-permute-start.1
  6.0 0.6 %collective-permute-start = (bf16[64,128]{1,0:T(8,128)(2,1)S(1)}, bf16[64,128]{1,0:T(8,128)(2,1)S(1)}, u32[]{:S(2)}, u32[]{:S(2)}) collective-permute-start(bf16[64,128]{1,0:T(8,128)(2,1)S(1)} %bitcast.4), channel_id=1, source_target_pairs={{0,1},{1,0},{2,3},{3,2},{4,5},{5,4},{6,7},{7,6},{8,9},{9,8},{10,11... | collective-permute-start | bytes 49160 | tf_op jit(solution)/shard_map/ppermute | solution.py:17
  6.6 2.4 %own_attention.1 = (f32[64,128]{1,0:T(8,128)S(1)}, f32[8,128]{1,0:T(8,128)S(1)}, s32[8,128]{1,0:T(8,128)S(1)}, bf16[3,4,128,256]{3,2,1,0:T(8,128)(2,1)S(1)}) custom-call(bf16[64,128]{1,0:T(8,128)(2,1)S(1)} %bitcast.5, bf16[1,1024]{1,0:T(2,128)(2,1)} %refs_1_.1, s32[1,4,7]{2,1,0:T(4,128)} %refs_2_.1, s32[1,4,7]{2,1,0:T(4,128)} %refs_3_.1, s32[1,4]{1,0:T(1,128)} %refs_4_.1, ...), custom_call_target="tpu_custom_call" | custom-call | flops 25165824 | bytes 4718592 | tf_op jit(solution)/shard_map/own_attention/pallas_call | solution.py:189
  9.0 0.0 collective-permute-done.2.refs_2_
  9.0 1.6 %collective-permute-done.1.refs_1_ = bf16[64,128]{1,0:T(8,128)(2,1)S(1)} collective-permute-done((bf16[64,128]{1,0:T(8,128)(2,1)S(1)}, bf16[64,128]{1,0:T(8,128)(2,1)S(1)}, u32[]{:S(2)}, u32[]{:S(2)}) %collective-permute-start.1) | collective-permute-done | bytes 16416 | tf_op jit(solution)/shard_map/ppermute | solution.py:17
  10.6 0.0 collective-permute-done.refs_0_
  10.6 0.8 %other_attention.1 = (bf16[4,2176]{1,0:T(4,128)(2,1)S(1)}, bf16[4,2176]{1,0:T(4,128)(2,1)S(1)}, bf16[4,2176]{1,0:T(4,128)(2,1)S(1)}, bf16[4,2176]{1,0:T(4,128)(2,1)S(1)}) custom-call(bf16[64,128]{1,0:T(8,128)(2,1)S(1)} %collective-permute-done.refs_0_, bf16[64,128]{1,0:T(8,128)(2,1)S(1)} %collective-permute-done.1.refs_1_, ...), custom_call_target="tpu_custom_call" | custom-call | flops 12582912 | bytes 786432 | tf_op jit(solution)/shard_map/other_attention/pallas_call | solution.py:283
  11.4 0.1 collective-permute-start.3
  11.5 1.6 %collective-permute-start.4 = (bf16[4,2176]{1,0:T(4,128)(2,1)S(1)}, bf16[4,2176]{1,0:T(4,128)(2,1)S(1)}, u32[]{:S(2)}, u32[]{:S(2)}) collective-permute-start(bf16[4,2176]{1,0:T(4,128)(2,1)S(1)} %get-tuple-element.28), channel_id=1, source_target_pairs={{0,8},{4,12},{8,0},{12,4},{1,9},{5,13},{9,1},{13,5},{2,10},{6,14},... | collective-permute-start | bytes 52232 | tf_op jit(solution)/shard_map/ppermute | solution.py:17
  13.0 0.3 collective-permute-start.5
  13.3 2.5 %load_weight.2 = (bf16[640,4096]{1,0:T(8,128)(2,1)S(1)}, bf16[4,2176]{1,0:T(4,128)(2,1)S(1)}) custom-call(bf16[4,2176]{1,0:T(4,128)(2,1)S(1)} %get-tuple-element.25.piece_ref, bf16[2048,4096]{1,0:T(8,128)(2,1)} %weight_hbm.3), custom_call_target="tpu_custom_call" | custom-call | bytes 10485760 | tf_op jit(solution)/shard_map/load_weight/pallas_call | solution.py:321
  15.9 0.0 collective-permute-done.3
  15.9 0.0 collective-permute-done.4
  15.9 0.3 collective-permute-done.5
  16.3 2.2 %collective-permute-start.8 = (bf16[16,2176]{1,0:T(8,128)(2,1)S(1)}, bf16[16,2176]{1,0:T(8,128)(2,1)S(1)}, u32[]{:S(2)}, u32[]{:S(2)}) collective-permute-start(bf16[16,2176]{1,0:T(8,128)(2,1)S(1)} %pad_maximum_fusion.piece_ref), channel_id=1, source_target_pairs={{0,3},{1,2},{2,1},{3,0},{4,7},{5,6},{6,5},{7,4},{8,11},{9,10},{10,... | collective-permute-start | bytes 208904 | tf_op jit(solution)/shard_map/ppermute | solution.py:17
  18.5 0.0 collective-permute-start.7
  18.5 2.2 %collective-permute-start.6 = (bf16[16,2176]{1,0:T(8,128)(2,1)S(1)}, bf16[16,2176]{1,0:T(8,128)(2,1)S(1)}, u32[]{:S(2)}, u32[]{:S(2)}) collective-permute-start(bf16[16,2176]{1,0:T(8,128)(2,1)S(1)} %pad_maximum_fusion.piece_ref), channel_id=1, source_target_pairs={{0,1},{1,0},{2,3},{3,2},{4,5},{5,4},{6,7},{7,6},{8,9},{9,8},{10,11... | collective-permute-start | bytes 208904 | tf_op jit(solution)/shard_map/ppermute | solution.py:17
  20.7 4.4 %load_weight.3 = (bf16[1408,4096]{1,0:T(8,128)(2,1)S(1)}, bf16[16,2176]{1,0:T(8,128)(2,1)S(1)}) custom-call(bf16[16,2176]{1,0:T(8,128)(2,1)S(1)} %pad_maximum_fusion.piece_ref, bf16[2048,4096]{1,0:T(8,128)(2,1)} %weight_hbm.3), custom_call_target="tpu_custom_call" | custom-call | bytes 23068672 | tf_op jit(solution)/shard_map/load_weight/pallas_call | solution.py:321
  25.1 0.0 collective-permute-done.8.refs_3_
  25.1 0.3 collective-permute-done.7.refs_2_
  25.4 0.0 collective-permute-done.6.refs_1_
  25.4 3.0 %project.1 = (f32[4,4096]{1,0:T(4,128)S(1)}, bf16[4,4096]{1,0:T(4,128)(2,1)S(1)}, bf16[4,4096]{1,0:T(4,128)(2,1)S(1)}, bf16[4,4096]{1,0:T(4,128)(2,1)S(1)}) custom-call(bf16[16,2176]{1,0:T(8,128)(2,1)S(1)} %get-tuple-element.30.refs_0_, bf16[16,2176]{1,0:T(8,128)(2,1)S(1)} %collective-permute-done.6.refs_1_, ...), custom_call_target="tpu_custom_call" | custom-call | flops 268435456 | bytes 16777216 | tf_op jit(solution)/shard_map/project/pallas_call | solution.py:374
  28.4 0.0 collective-permute-start.9
  28.4 1.4 %collective-permute-start.10 = (bf16[4,4096]{1,0:T(4,128)(2,1)S(1)}, bf16[4,4096]{1,0:T(4,128)(2,1)S(1)}, u32[]{:S(2)}, u32[]{:S(2)}) collective-permute-start(bf16[4,4096]{1,0:T(4,128)(2,1)S(1)} %get-tuple-element.35), channel_id=1, source_target_pairs={{0,8},{4,12},{8,0},{12,4},{1,9},{5,13},{9,1},{13,5},{2,10},{6,14},... | collective-permute-start | bytes 98312 | tf_op jit(solution)/shard_map/ppermute | solution.py:17
  29.8 0.5 %collective-permute-start.11 = (bf16[4,4096]{1,0:T(4,128)(2,1)S(1)}, bf16[4,4096]{1,0:T(4,128)(2,1)S(1)}, u32[]{:S(2)}, u32[]{:S(2)}) collective-permute-start(bf16[4,4096]{1,0:T(4,128)(2,1)S(1)} %get-tuple-element.36), channel_id=1, source_target_pairs={{0,12},{4,8},{8,4},{12,0},{1,13},{5,9},{9,5},{13,1},{2,14},{6,10},... | collective-permute-start | bytes 98312 | tf_op jit(solution)/shard_map/ppermute | solution.py:17
  30.3 0.0 collective-permute-done.9
  30.3 2.1 %collective-permute-done.10 = bf16[4,4096]{1,0:T(4,128)(2,1)S(1)} collective-permute-done((bf16[4,4096]{1,0:T(4,128)(2,1)S(1)}, bf16[4,4096]{1,0:T(4,128)(2,1)S(1)}, u32[]{:S(2)}, u32[]{:S(2)}) %collective-permute-start.10) | collective-permute-done | bytes 32800 | tf_op jit(solution)/shard_map/ppermute | solution.py:17
  32.4 0.8 %collective-permute-done.11 = bf16[4,4096]{1,0:T(4,128)(2,1)S(1)} collective-permute-done((bf16[4,4096]{1,0:T(4,128)(2,1)S(1)}, bf16[4,4096]{1,0:T(4,128)(2,1)S(1)}, u32[]{:S(2)}, u32[]{:S(2)}) %collective-permute-start.11) | collective-permute-done | bytes 32800 | tf_op jit(solution)/shard_map/ppermute | solution.py:17
  33.1 0.7 %add_convert_fusion = bf16[4,4096]{1,0:T(4,128)(2,1)} fusion(bf16[4,4096]{1,0:T(4,128)(2,1)S(1)} %collective-permute-done.11, bf16[4,4096]{1,0:T(4,128)(2,1)S(1)} %collective-permute-done.10, f32[4,4096]{1,0:T(4,128)S(1)} %get-tuple-element.33, bf16[4,4096]{1,0:T(4,128)(2,1)S(1)} %collective-permute-done.9), kind=kLoop, calls=%fused_computation.1 | loop fusion | flops 114688 | bytes 196608 | tf_op jit(solution)/shard_map/convert_element_type | solution.py:408
  (1 shorter events, 0.0 us)
Async XLA Ops:
  0.8 8.1 %collective-permute-start.2 = (bf16[64,128]{1,0:T(8,128)(2,1)S(1)}, bf16[64,128]{1,0:T(8,128)(2,1)S(1)}, u32[]{:S(2)}, u32[]{:S(2)}) collective-permute-start(bf16[64,128]{1,0:T(8,128)(2,1)S(1)} %bitcast.2), channel_id=1, source_target_pairs={{0,3},{1,2},{2,1},{3,0},{4,7},{5,6},{6,5},{7,4},{8,11},{9,10},{10,... | collective-permute-start | bytes 49160 | tf_op jit(solution)/shard_map/ppermute | solution.py:17
  6.0 4.6 %collective-permute-start.1 = (bf16[64,128]{1,0:T(8,128)(2,1)S(1)}, bf16[64,128]{1,0:T(8,128)(2,1)S(1)}, u32[]{:S(2)}, u32[]{:S(2)}) collective-permute-start(bf16[64,128]{1,0:T(8,128)(2,1)S(1)} %bitcast.3), channel_id=1, source_target_pairs={{0,2},{1,3},{2,0},{3,1},{4,6},{5,7},{6,4},{7,5},{8,10},{9,11},{10,... | collective-permute-start | bytes 49160 | tf_op jit(solution)/shard_map/ppermute | solution.py:17
  6.0 4.6 %collective-permute-start = (bf16[64,128]{1,0:T(8,128)(2,1)S(1)}, bf16[64,128]{1,0:T(8,128)(2,1)S(1)}, u32[]{:S(2)}, u32[]{:S(2)}) collective-permute-start(bf16[64,128]{1,0:T(8,128)(2,1)S(1)} %bitcast.4), channel_id=1, source_target_pairs={{0,1},{1,0},{2,3},{3,2},{4,5},{5,4},{6,7},{7,6},{8,9},{9,8},{10,11... | collective-permute-start | bytes 49160 | tf_op jit(solution)/shard_map/ppermute | solution.py:17
  11.4 4.5 %collective-permute-start.3 = (bf16[4,2176]{1,0:T(4,128)(2,1)S(1)}, bf16[4,2176]{1,0:T(4,128)(2,1)S(1)}, u32[]{:S(2)}, u32[]{:S(2)}) collective-permute-start(bf16[4,2176]{1,0:T(4,128)(2,1)S(1)} %get-tuple-element.27), channel_id=1, source_target_pairs={{0,4},{4,0},{8,12},{12,8},{1,5},{5,1},{9,13},{13,9},{2,6},{6,2},{1... | collective-permute-start | bytes 52232 | tf_op jit(solution)/shard_map/ppermute | solution.py:17
  11.5 4.4 %collective-permute-start.4 = (bf16[4,2176]{1,0:T(4,128)(2,1)S(1)}, bf16[4,2176]{1,0:T(4,128)(2,1)S(1)}, u32[]{:S(2)}, u32[]{:S(2)}) collective-permute-start(bf16[4,2176]{1,0:T(4,128)(2,1)S(1)} %get-tuple-element.28), channel_id=1, source_target_pairs={{0,8},{4,12},{8,0},{12,4},{1,9},{5,13},{9,1},{13,5},{2,10},{6,14},... | collective-permute-start | bytes 52232 | tf_op jit(solution)/shard_map/ppermute | solution.py:17
  13.0 3.2 %collective-permute-start.5 = (bf16[4,2176]{1,0:T(4,128)(2,1)S(1)}, bf16[4,2176]{1,0:T(4,128)(2,1)S(1)}, u32[]{:S(2)}, u32[]{:S(2)}) collective-permute-start(bf16[4,2176]{1,0:T(4,128)(2,1)S(1)} %get-tuple-element.29), channel_id=1, source_target_pairs={{0,12},{4,8},{8,4},{12,0},{1,13},{5,9},{9,5},{13,1},{2,14},{6,10},... | collective-permute-start | bytes 52232 | tf_op jit(solution)/shard_map/ppermute | solution.py:17
  16.3 8.9 %collective-permute-start.8 = (bf16[16,2176]{1,0:T(8,128)(2,1)S(1)}, bf16[16,2176]{1,0:T(8,128)(2,1)S(1)}, u32[]{:S(2)}, u32[]{:S(2)}) collective-permute-start(bf16[16,2176]{1,0:T(8,128)(2,1)S(1)} %pad_maximum_fusion.piece_ref), channel_id=1, source_target_pairs={{0,3},{1,2},{2,1},{3,0},{4,7},{5,6},{6,5},{7,4},{8,11},{9,10},{10,... | collective-permute-start | bytes 208904 | tf_op jit(solution)/shard_map/ppermute | solution.py:17
  18.5 6.9 %collective-permute-start.7 = (bf16[16,2176]{1,0:T(8,128)(2,1)S(1)}, bf16[16,2176]{1,0:T(8,128)(2,1)S(1)}, u32[]{:S(2)}, u32[]{:S(2)}) collective-permute-start(bf16[16,2176]{1,0:T(8,128)(2,1)S(1)} %pad_maximum_fusion.piece_ref), channel_id=1, source_target_pairs={{0,2},{1,3},{2,0},{3,1},{4,6},{5,7},{6,4},{7,5},{8,10},{9,11},{10,... | collective-permute-start | bytes 208904 | tf_op jit(solution)/shard_map/ppermute | solution.py:17
  18.5 6.9 %collective-permute-start.6 = (bf16[16,2176]{1,0:T(8,128)(2,1)S(1)}, bf16[16,2176]{1,0:T(8,128)(2,1)S(1)}, u32[]{:S(2)}, u32[]{:S(2)}) collective-permute-start(bf16[16,2176]{1,0:T(8,128)(2,1)S(1)} %pad_maximum_fusion.piece_ref), channel_id=1, source_target_pairs={{0,1},{1,0},{2,3},{3,2},{4,5},{5,4},{6,7},{7,6},{8,9},{9,8},{10,11... | collective-permute-start | bytes 208904 | tf_op jit(solution)/shard_map/ppermute | solution.py:17
  28.4 1.9 %collective-permute-start.9 = (bf16[4,4096]{1,0:T(4,128)(2,1)S(1)}, bf16[4,4096]{1,0:T(4,128)(2,1)S(1)}, u32[]{:S(2)}, u32[]{:S(2)}) collective-permute-start(bf16[4,4096]{1,0:T(4,128)(2,1)S(1)} %get-tuple-element.34), channel_id=1, source_target_pairs={{0,4},{4,0},{8,12},{12,8},{1,5},{5,1},{9,13},{13,9},{2,6},{6,2},{1... | collective-permute-start | bytes 98312 | tf_op jit(solution)/shard_map/ppermute | solution.py:17
  28.4 4.0 %collective-permute-start.10 = (bf16[4,4096]{1,0:T(4,128)(2,1)S(1)}, bf16[4,4096]{1,0:T(4,128)(2,1)S(1)}, u32[]{:S(2)}, u32[]{:S(2)}) collective-permute-start(bf16[4,4096]{1,0:T(4,128)(2,1)S(1)} %get-tuple-element.35), channel_id=1, source_target_pairs={{0,8},{4,12},{8,0},{12,4},{1,9},{5,13},{9,1},{13,5},{2,10},{6,14},... | collective-permute-start | bytes 98312 | tf_op jit(solution)/shard_map/ppermute | solution.py:17
  29.8 3.3 %collective-permute-start.11 = (bf16[4,4096]{1,0:T(4,128)(2,1)S(1)}, bf16[4,4096]{1,0:T(4,128)(2,1)S(1)}, u32[]{:S(2)}, u32[]{:S(2)}) collective-permute-start(bf16[4,4096]{1,0:T(4,128)(2,1)S(1)} %get-tuple-element.36), channel_id=1, source_target_pairs={{0,12},{4,8},{8,4},{12,0},{1,13},{5,9},{9,5},{13,1},{2,14},{6,10},... | collective-permute-start | bytes 98312 | tf_op jit(solution)/shard_map/ppermute | solution.py:17

commit v7 on v6

--- a/solution.py
+++ b/solution.py
@@ -15,6 +15,10 @@
 def swap(x, axis, offset):
     count = lax.axis_size(axis)
     return lax.ppermute(x, axis, [(i, i ^ offset) for i in range(count)])
+
+
+def near_last(count):
+    return list(range(2, count)) + [1]
 
 
 def in_hbm(x):
@@ -217,7 +221,8 @@
 
 
 def other_kernel(n_req, n_tp, *refs):
-    q_refs = refs[: n_req - 1]
+    q_of = dict(zip(reversed(near_last(n_req)), refs[: n_req - 1]))
+    q_refs = [q_of[d] for d in range(1, n_req)]
     acc_ref, log_ref, limit_ref, pages_ref = refs[n_req - 1 : n_req + 3]
     out_refs = refs[n_req + 3 : n_req + 3 + n_tp]
     results, logs = refs[n_req + 3 + n_tp :]
@@ -353,15 +358,15 @@
         at = slice(h * 128, (h + 1) * 128)
         terms = [part[:, at].astype(jnp.float32) * f[:, h : h + 1] for part, f in zip(part_refs, factors)]
         attention[:, at] = functools.reduce(jnp.add, terms).astype(jnp.bfloat16)
-    tile = min(columns, 1024)
+    tile = min(columns, 2048)
 
     @pl.loop(0, columns // tile)
     def _(t):
         at = pl.ds(pl.multiple_of(t * tile, tile), tile)
         product = jnp.dot(attention[:, :split], weight_refs[0][:, at], preferred_element_type=jnp.float32)
         product += jnp.dot(attention[:, split:], weight_refs[1][:, at], preferred_element_type=jnp.float32)
-        for d in range(n_tp):
-            out_refs[d][:, at] = product[d * n_req : (d + 1) * n_req].astype(out_refs[d].dtype)
+        for i, d in enumerate([0] + near_last(n_tp)):
+            out_refs[d][:, at] = product[i * n_req : (i + 1) * n_req].astype(out_refs[d].dtype)
 
 
 def project(parts, weights, n_req, n_tp):
@@ -391,19 +396,19 @@
     pool = cache_pool[0, 0]
     head_dim = pool.shape[3] // 2
     q = queries.reshape(-1, head_dim)
-    q_list = [swap(q, "req", d) for d in range(1, n_req)]
+    q_list = [swap(q, "req", d) for d in reversed(near_last(n_req))]
     own = own_attention(q, new_kv, page_slot, page_owner, context_len, pool, n_req)
     pieces = other_attention(q_list, own, n_req, n_tp)
     depth = out_weight.shape[0]
     early = depth * 5 // 16
-    swapped = [swap(pieces[d], "tp", d) for d in range(1, n_tp)]
+    swapped = [swap(pieces[d], "tp", d) for d in near_last(n_tp)]
     first, mine = load_weight(pieces[0], out_weight, 0, early)
     arrived = jnp.concatenate([mine] + swapped, axis=0)
-    parts = [swap(arrived, "req", d) for d in range(1, n_req)]
+    parts = [swap(arrived, "req", d) for d in reversed(near_last(n_req))]
     second, mine = load_weight(arrived, out_weight, early, depth - early)
     sums = project([mine] + parts, (first, second), n_req, n_tp)
     total = sums[0]
-    for d in range(1, n_tp):
+    for d in near_last(n_tp):
         total = total + swap(sums[d], "tp", d).astype(jnp.float32)
     return total.astype(jnp.bfloat16)
 

time: 34 us -> 33.5 us (0.985)
  starting transfers between devices: 14 us -> 13.6 us
    ppermute x12, starting transfers between devices: 14 us -> 13.6 us  [swap(): return lax.ppermute(x, axis, [(i, i ^ offset) for i in range(count)])]
  transfers between devices with their start and end apart: 12 -> 12, of which waited for: 5 -> 4; matrix products, arithmetic and copies ran while one was open for 0% -> 0% of each run, Pallas kernels for 27% -> 28%
where the time goes in v7:
time: 33.5 us; the launch traced here: 33.3 us
  starting transfers between devices  13.6 us (41%)
  Pallas kernels  12.8 us (38%)
  waiting for transfers between devices  5.28 us (16%)
  other arithmetic  1.55 us (5%)
    ppermute x12, starting transfers between devices, swap(): return lax.ppermute(x, axis, [(i, i ^ offset) for i in range(count)])  13.6 us
    pallas_call x2, Pallas kernels, load_weight(): pl.pallas_call(functools.partial(load_kernel, first), out_shape=[jax.Shap...  6.93 us
    ppermute x12, waiting for transfers between devices, swap(): return lax.ppermute(x, axis, [(i, i ^ offset) for i in range(count)])  5.28 us
    pallas_call x1, Pallas kernels, project(): pl.pallas_call(functools.partial(project_kernel, n_req, n_tp), out_shape=...  2.73 us
    pallas_call x1, Pallas kernels, own_attention(): pl.pallas_call(functools.partial(own_kernel, n_req, own_pages), out_shape...  2.36 us
    unnamed x1, other arithmetic  0.85 us
    pallas_call x1, Pallas kernels, other_attention(): pl.pallas_call(functools.partial(other_kernel, n_req, n_tp), out_shape=[j...  0.79 us
  transfers between devices with their start and end apart: 12, of which 4 were waited for; matrix products, arithmetic and copies ran while one was open for 0% of the time, Pallas kernels for 28%

profile of v7, /device:TPU:0, one launch (start us, length us, event | category | flops | bytes accessed | tf_op | source)
XLA Modules:
  0.0 33.3 jit_solution(4668355855938195558)
XLA Ops:
  0.0 0.8 %reduce = bf16[8192]{0:T(1024)(128)(2,1)S(1)} reduce(bf16[1,8192]{1,0:T(2,128)(2,1)} %param.7, bf16[]{:T(256)} %constant.6), dimensions={0}, to_apply=%param.7.reduce_sub_computation | reduce | bytes 32770 | tf_op args[0]
  0.8 4.1 %collective-permute-start.2 = (bf16[64,128]{1,0:T(8,128)(2,1)S(1)}, bf16[64,128]{1,0:T(8,128)(2,1)S(1)}, u32[]{:S(2)}, u32[]{:S(2)}) collective-permute-start(bf16[64,128]{1,0:T(8,128)(2,1)S(1)} %bitcast.2), channel_id=1, source_target_pairs={{0,2},{1,3},{2,0},{3,1},{4,6},{5,7},{6,4},{7,5},{8,10},{9,11},{10,... | collective-permute-start | bytes 49160 | tf_op jit(solution)/shard_map/ppermute | solution.py:17
  5.0 1.3 %collective-permute-start.1 = (bf16[64,128]{1,0:T(8,128)(2,1)S(1)}, bf16[64,128]{1,0:T(8,128)(2,1)S(1)}, u32[]{:S(2)}, u32[]{:S(2)}) collective-permute-start(bf16[64,128]{1,0:T(8,128)(2,1)S(1)} %bitcast.3), channel_id=1, source_target_pairs={{0,3},{1,2},{2,1},{3,0},{4,7},{5,6},{6,5},{7,4},{8,11},{9,10},{10,... | collective-permute-start | bytes 49160 | tf_op jit(solution)/shard_map/ppermute | solution.py:17
  6.3 0.2 collective-permute-start
  6.5 2.4 %own_attention.1 = (f32[64,128]{1,0:T(8,128)S(1)}, f32[8,128]{1,0:T(8,128)S(1)}, s32[8,128]{1,0:T(8,128)S(1)}, bf16[3,4,128,256]{3,2,1,0:T(8,128)(2,1)S(1)}) custom-call(bf16[64,128]{1,0:T(8,128)(2,1)S(1)} %bitcast.5, bf16[1,1024]{1,0:T(2,128)(2,1)} %refs_1_.1, s32[1,4,7]{2,1,0:T(4,128)} %refs_2_.1, s32[1,4,7]{2,1,0:T(4,128)} %refs_3_.1, s32[1,4]{1,0:T(1,128)} %refs_4_.1, ...), custom_call_target="tpu_custom_call" | custom-call | flops 25165824 | bytes 4718592 | tf_op jit(solution)/shard_map/own_attention/pallas_call | solution.py:193
  8.9 0.0 collective-permute-done.2.refs_2_
  8.9 1.6 %collective-permute-done.1.refs_1_ = bf16[64,128]{1,0:T(8,128)(2,1)S(1)} collective-permute-done((bf16[64,128]{1,0:T(8,128)(2,1)S(1)}, bf16[64,128]{1,0:T(8,128)(2,1)S(1)}, u32[]{:S(2)}, u32[]{:S(2)}) %collective-permute-start.1) | collective-permute-done | bytes 16416 | tf_op jit(solution)/shard_map/ppermute | solution.py:17
  10.5 0.0 collective-permute-done.refs_0_
  10.5 0.8 %other_attention.1 = (bf16[4,2176]{1,0:T(4,128)(2,1)S(1)}, bf16[4,2176]{1,0:T(4,128)(2,1)S(1)}, bf16[4,2176]{1,0:T(4,128)(2,1)S(1)}, bf16[4,2176]{1,0:T(4,128)(2,1)S(1)}) custom-call(bf16[64,128]{1,0:T(8,128)(2,1)S(1)} %collective-permute-done.refs_0_, bf16[64,128]{1,0:T(8,128)(2,1)S(1)} %collective-permute-done.1.refs_1_, ...), custom_call_target="tpu_custom_call" | custom-call | flops 12582912 | bytes 786432 | tf_op jit(solution)/shard_map/other_attention/pallas_call | solution.py:288
  11.3 1.6 %collective-permute-start.3 = (bf16[4,2176]{1,0:T(4,128)(2,1)S(1)}, bf16[4,2176]{1,0:T(4,128)(2,1)S(1)}, u32[]{:S(2)}, u32[]{:S(2)}) collective-permute-start(bf16[4,2176]{1,0:T(4,128)(2,1)S(1)} %get-tuple-element.27), channel_id=1, source_target_pairs={{0,8},{4,12},{8,0},{12,4},{1,9},{5,13},{9,1},{13,5},{2,10},{6,14},... | collective-permute-start | bytes 52232 | tf_op jit(solution)/shard_map/ppermute | solution.py:17
  12.8 0.0 collective-permute-start.4
  12.8 0.7 %collective-permute-start.5 = (bf16[4,2176]{1,0:T(4,128)(2,1)S(1)}, bf16[4,2176]{1,0:T(4,128)(2,1)S(1)}, u32[]{:S(2)}, u32[]{:S(2)}) collective-permute-start(bf16[4,2176]{1,0:T(4,128)(2,1)S(1)} %get-tuple-element.29), channel_id=1, source_target_pairs={{0,4},{4,0},{8,12},{12,8},{1,5},{5,1},{9,13},{13,9},{2,6},{6,2},{1... | collective-permute-start | bytes 52232 | tf_op jit(solution)/shard_map/ppermute | solution.py:17
  13.5 2.5 %load_weight.2 = (bf16[640,4096]{1,0:T(8,128)(2,1)S(1)}, bf16[4,2176]{1,0:T(4,128)(2,1)S(1)}) custom-call(bf16[4,2176]{1,0:T(4,128)(2,1)S(1)} %get-tuple-element.25.piece_ref, bf16[2048,4096]{1,0:T(8,128)(2,1)} %weight_hbm.3), custom_call_target="tpu_custom_call" | custom-call | bytes 10485760 | tf_op jit(solution)/shard_map/load_weight/pallas_call | solution.py:326
  16.0 0.0 collective-permute-done.3
  16.0 0.0 collective-permute-done.4
  16.1 0.0 collective-permute-done.5
  16.1 1.3 %collective-permute-start.8 = (bf16[16,2176]{1,0:T(8,128)(2,1)S(1)}, bf16[16,2176]{1,0:T(8,128)(2,1)S(1)}, u32[]{:S(2)}, u32[]{:S(2)}) collective-permute-start(bf16[16,2176]{1,0:T(8,128)(2,1)S(1)} %pad_maximum_fusion.piece_ref), channel_id=1, source_target_pairs={{0,2},{1,3},{2,0},{3,1},{4,6},{5,7},{6,4},{7,5},{8,10},{9,11},{10,... | collective-permute-start | bytes 208904 | tf_op jit(solution)/shard_map/ppermute | solution.py:17
  17.4 1.3 %collective-permute-start.7 = (bf16[16,2176]{1,0:T(8,128)(2,1)S(1)}, bf16[16,2176]{1,0:T(8,128)(2,1)S(1)}, u32[]{:S(2)}, u32[]{:S(2)}) collective-permute-start(bf16[16,2176]{1,0:T(8,128)(2,1)S(1)} %pad_maximum_fusion.piece_ref), channel_id=1, source_target_pairs={{0,3},{1,2},{2,1},{3,0},{4,7},{5,6},{6,5},{7,4},{8,11},{9,10},{10,... | collective-permute-start | bytes 208904 | tf_op jit(solution)/shard_map/ppermute | solution.py:17
  18.8 0.9 %collective-permute-start.6 = (bf16[16,2176]{1,0:T(8,128)(2,1)S(1)}, bf16[16,2176]{1,0:T(8,128)(2,1)S(1)}, u32[]{:S(2)}, u32[]{:S(2)}) collective-permute-start(bf16[16,2176]{1,0:T(8,128)(2,1)S(1)} %pad_maximum_fusion.piece_ref), channel_id=1, source_target_pairs={{0,1},{1,0},{2,3},{3,2},{4,5},{5,4},{6,7},{7,6},{8,9},{9,8},{10,11... | collective-permute-start | bytes 208904 | tf_op jit(solution)/shard_map/ppermute | solution.py:17
  19.7 4.4 %load_weight.3 = (bf16[1408,4096]{1,0:T(8,128)(2,1)S(1)}, bf16[16,2176]{1,0:T(8,128)(2,1)S(1)}) custom-call(bf16[16,2176]{1,0:T(8,128)(2,1)S(1)} %pad_maximum_fusion.piece_ref, bf16[2048,4096]{1,0:T(8,128)(2,1)} %weight_hbm.3), custom_call_target="tpu_custom_call" | custom-call | bytes 23068672 | tf_op jit(solution)/shard_map/load_weight/pallas_call | solution.py:326
  24.1 0.0 collective-permute-done.8.refs_3_
  24.1 0.0 collective-permute-done.7.refs_2_
  24.1 1.0 %collective-permute-done.6.refs_1_ = bf16[16,2176]{1,0:T(8,128)(2,1)S(1)} collective-permute-done((bf16[16,2176]{1,0:T(8,128)(2,1)S(1)}, bf16[16,2176]{1,0:T(8,128)(2,1)S(1)}, u32[]{:S(2)}, u32[]{:S(2)}) %collective-permute-start.6) | collective-permute-done | bytes 69664 | tf_op jit(solution)/shard_map/ppermute | solution.py:17
  25.1 2.7 %project.1 = (f32[4,4096]{1,0:T(4,128)S(1)}, bf16[4,4096]{1,0:T(4,128)(2,1)S(1)}, bf16[4,4096]{1,0:T(4,128)(2,1)S(1)}, bf16[4,4096]{1,0:T(4,128)(2,1)S(1)}) custom-call(bf16[16,2176]{1,0:T(8,128)(2,1)S(1)} %get-tuple-element.30.refs_0_, bf16[16,2176]{1,0:T(8,128)(2,1)S(1)} %collective-permute-done.6.refs_1_, ...), custom_call_target="tpu_custom_call" | custom-call | flops 268435456 | bytes 16777216 | tf_op jit(solution)/shard_map/project/pallas_call | solution.py:379
  27.8 1.5 %collective-permute-start.9 = (bf16[4,4096]{1,0:T(4,128)(2,1)S(1)}, bf16[4,4096]{1,0:T(4,128)(2,1)S(1)}, u32[]{:S(2)}, u32[]{:S(2)}) collective-permute-start(bf16[4,4096]{1,0:T(4,128)(2,1)S(1)} %get-tuple-element.34), channel_id=1, source_target_pairs={{0,8},{4,12},{8,0},{12,4},{1,9},{5,13},{9,1},{13,5},{2,10},{6,14},... | collective-permute-start | bytes 98312 | tf_op jit(solution)/shard_map/ppermute | solution.py:17
  29.3 0.0 collective-permute-start.10
  29.3 0.6 %collective-permute-start.11 = (bf16[4,4096]{1,0:T(4,128)(2,1)S(1)}, bf16[4,4096]{1,0:T(4,128)(2,1)S(1)}, u32[]{:S(2)}, u32[]{:S(2)}) collective-permute-start(bf16[4,4096]{1,0:T(4,128)(2,1)S(1)} %get-tuple-element.36), channel_id=1, source_target_pairs={{0,4},{4,0},{8,12},{12,8},{1,5},{5,1},{9,13},{13,9},{2,6},{6,2},{1... | collective-permute-start | bytes 98312 | tf_op jit(solution)/shard_map/ppermute | solution.py:17
  30.0 1.8 %collective-permute-done.9 = bf16[4,4096]{1,0:T(4,128)(2,1)S(1)} collective-permute-done((bf16[4,4096]{1,0:T(4,128)(2,1)S(1)}, bf16[4,4096]{1,0:T(4,128)(2,1)S(1)}, u32[]{:S(2)}, u32[]{:S(2)}) %collective-permute-start.9) | collective-permute-done | bytes 32800 | tf_op jit(solution)/shard_map/ppermute | solution.py:17
  31.7 0.9 %collective-permute-done.10 = bf16[4,4096]{1,0:T(4,128)(2,1)S(1)} collective-permute-done((bf16[4,4096]{1,0:T(4,128)(2,1)S(1)}, bf16[4,4096]{1,0:T(4,128)(2,1)S(1)}, u32[]{:S(2)}, u32[]{:S(2)}) %collective-permute-start.10) | collective-permute-done | bytes 32800 | tf_op jit(solution)/shard_map/ppermute | solution.py:17
  32.7 0.0 collective-permute-done.11
  32.7 0.7 %add_convert_fusion = bf16[4,4096]{1,0:T(4,128)(2,1)} fusion(bf16[4,4096]{1,0:T(4,128)(2,1)S(1)} %collective-permute-done.11, bf16[4,4096]{1,0:T(4,128)(2,1)S(1)} %collective-permute-done.10, f32[4,4096]{1,0:T(4,128)S(1)} %get-tuple-element.33, bf16[4,4096]{1,0:T(4,128)(2,1)S(1)} %collective-permute-done.9), kind=kLoop, calls=%fused_computation.1 | loop fusion | flops 114688 | bytes 196608 | tf_op jit(solution)/shard_map/convert_element_type | solution.py:413
  (1 shorter events, 0.0 us)
Async XLA Ops:
  0.8 8.1 %collective-permute-start.2 = (bf16[64,128]{1,0:T(8,128)(2,1)S(1)}, bf16[64,128]{1,0:T(8,128)(2,1)S(1)}, u32[]{:S(2)}, u32[]{:S(2)}) collective-permute-start(bf16[64,128]{1,0:T(8,128)(2,1)S(1)} %bitcast.2), channel_id=1, source_target_pairs={{0,2},{1,3},{2,0},{3,1},{4,6},{5,7},{6,4},{7,5},{8,10},{9,11},{10,... | collective-permute-start | bytes 49160 | tf_op jit(solution)/shard_map/ppermute | solution.py:17
  5.0 5.5 %collective-permute-start.1 = (bf16[64,128]{1,0:T(8,128)(2,1)S(1)}, bf16[64,128]{1,0:T(8,128)(2,1)S(1)}, u32[]{:S(2)}, u32[]{:S(2)}) collective-permute-start(bf16[64,128]{1,0:T(8,128)(2,1)S(1)} %bitcast.3), channel_id=1, source_target_pairs={{0,3},{1,2},{2,1},{3,0},{4,7},{5,6},{6,5},{7,4},{8,11},{9,10},{10,... | collective-permute-start | bytes 49160 | tf_op jit(solution)/shard_map/ppermute | solution.py:17
  6.3 4.2 %collective-permute-start = (bf16[64,128]{1,0:T(8,128)(2,1)S(1)}, bf16[64,128]{1,0:T(8,128)(2,1)S(1)}, u32[]{:S(2)}, u32[]{:S(2)}) collective-permute-start(bf16[64,128]{1,0:T(8,128)(2,1)S(1)} %bitcast.4), channel_id=1, source_target_pairs={{0,1},{1,0},{2,3},{3,2},{4,5},{5,4},{6,7},{7,6},{8,9},{9,8},{10,11... | collective-permute-start | bytes 49160 | tf_op jit(solution)/shard_map/ppermute | solution.py:17
  11.3 4.8 %collective-permute-start.3 = (bf16[4,2176]{1,0:T(4,128)(2,1)S(1)}, bf16[4,2176]{1,0:T(4,128)(2,1)S(1)}, u32[]{:S(2)}, u32[]{:S(2)}) collective-permute-start(bf16[4,2176]{1,0:T(4,128)(2,1)S(1)} %get-tuple-element.27), channel_id=1, source_target_pairs={{0,8},{4,12},{8,0},{12,4},{1,9},{5,13},{9,1},{13,5},{2,10},{6,14},... | collective-permute-start | bytes 52232 | tf_op jit(solution)/shard_map/ppermute | solution.py:17
  12.8 3.2 %collective-permute-start.4 = (bf16[4,2176]{1,0:T(4,128)(2,1)S(1)}, bf16[4,2176]{1,0:T(4,128)(2,1)S(1)}, u32[]{:S(2)}, u32[]{:S(2)}) collective-permute-start(bf16[4,2176]{1,0:T(4,128)(2,1)S(1)} %get-tuple-element.28), channel_id=1, source_target_pairs={{0,12},{4,8},{8,4},{12,0},{1,13},{5,9},{9,5},{13,1},{2,14},{6,10},... | collective-permute-start | bytes 52232 | tf_op jit(solution)/shard_map/ppermute | solution.py:17
  12.8 3.2 %collective-permute-start.5 = (bf16[4,2176]{1,0:T(4,128)(2,1)S(1)}, bf16[4,2176]{1,0:T(4,128)(2,1)S(1)}, u32[]{:S(2)}, u32[]{:S(2)}) collective-permute-start(bf16[4,2176]{1,0:T(4,128)(2,1)S(1)} %get-tuple-element.29), channel_id=1, source_target_pairs={{0,4},{4,0},{8,12},{12,8},{1,5},{5,1},{9,13},{13,9},{2,6},{6,2},{1... | collective-permute-start | bytes 52232 | tf_op jit(solution)/shard_map/ppermute | solution.py:17
  16.1 8.0 %collective-permute-start.8 = (bf16[16,2176]{1,0:T(8,128)(2,1)S(1)}, bf16[16,2176]{1,0:T(8,128)(2,1)S(1)}, u32[]{:S(2)}, u32[]{:S(2)}) collective-permute-start(bf16[16,2176]{1,0:T(8,128)(2,1)S(1)} %pad_maximum_fusion.piece_ref), channel_id=1, source_target_pairs={{0,2},{1,3},{2,0},{3,1},{4,6},{5,7},{6,4},{7,5},{8,10},{9,11},{10,... | collective-permute-start | bytes 208904 | tf_op jit(solution)/shard_map/ppermute | solution.py:17
  17.4 6.7 %collective-permute-start.7 = (bf16[16,2176]{1,0:T(8,128)(2,1)S(1)}, bf16[16,2176]{1,0:T(8,128)(2,1)S(1)}, u32[]{:S(2)}, u32[]{:S(2)}) collective-permute-start(bf16[16,2176]{1,0:T(8,128)(2,1)S(1)} %pad_maximum_fusion.piece_ref), channel_id=1, source_target_pairs={{0,3},{1,2},{2,1},{3,0},{4,7},{5,6},{6,5},{7,4},{8,11},{9,10},{10,... | collective-permute-start | bytes 208904 | tf_op jit(solution)/shard_map/ppermute | solution.py:17
  18.8 6.3 %collective-permute-start.6 = (bf16[16,2176]{1,0:T(8,128)(2,1)S(1)}, bf16[16,2176]{1,0:T(8,128)(2,1)S(1)}, u32[]{:S(2)}, u32[]{:S(2)}) collective-permute-start(bf16[16,2176]{1,0:T(8,128)(2,1)S(1)} %pad_maximum_fusion.piece_ref), channel_id=1, source_target_pairs={{0,1},{1,0},{2,3},{3,2},{4,5},{5,4},{6,7},{7,6},{8,9},{9,8},{10,11... | collective-permute-start | bytes 208904 | tf_op jit(solution)/shard_map/ppermute | solution.py:17
  27.8 3.9 %collective-permute-start.9 = (bf16[4,4096]{1,0:T(4,128)(2,1)S(1)}, bf16[4,4096]{1,0:T(4,128)(2,1)S(1)}, u32[]{:S(2)}, u32[]{:S(2)}) collective-permute-start(bf16[4,4096]{1,0:T(4,128)(2,1)S(1)} %get-tuple-element.34), channel_id=1, source_target_pairs={{0,8},{4,12},{8,0},{12,4},{1,9},{5,13},{9,1},{13,5},{2,10},{6,14},... | collective-permute-start | bytes 98312 | tf_op jit(solution)/shard_map/ppermute | solution.py:17
  29.3 3.3 %collective-permute-start.10 = (bf16[4,4096]{1,0:T(4,128)(2,1)S(1)}, bf16[4,4096]{1,0:T(4,128)(2,1)S(1)}, u32[]{:S(2)}, u32[]{:S(2)}) collective-permute-start(bf16[4,4096]{1,0:T(4,128)(2,1)S(1)} %get-tuple-element.35), channel_id=1, source_target_pairs={{0,12},{4,8},{8,4},{12,0},{1,13},{5,9},{9,5},{13,1},{2,14},{6,10},... | collective-permute-start | bytes 98312 | tf_op jit(solution)/shard_map/ppermute | solution.py:17
  29.3 3.3 %collective-permute-start.11 = (bf16[4,4096]{1,0:T(4,128)(2,1)S(1)}, bf16[4,4096]{1,0:T(4,128)(2,1)S(1)}, u32[]{:S(2)}, u32[]{:S(2)}) collective-permute-start(bf16[4,4096]{1,0:T(4,128)(2,1)S(1)} %get-tuple-element.36), channel_id=1, source_target_pairs={{0,4},{4,0},{8,12},{12,8},{1,5},{5,1},{9,13},{13,9},{2,6},{6,2},{1... | collective-permute-start | bytes 98312 | tf_op jit(solution)/shard_map/ppermute | solution.py:17

commit v8 on v7

--- a/solution.py
+++ b/solution.py
@@ -33,8 +33,14 @@
     return pltpu.roll(x, 64, 1)
 
 
+def lay_rows(target, start, q_ref):
+    head_dim = target.shape[1]
+    for h in range(64):
+        target[start + h : start + h + 1] = q_ref[0:1, h * head_dim : (h + 1) * head_dim].astype(jnp.float32)
+
+
 def query_tiles(stacked, kv_heads):
-    turned = stacked.astype(jnp.float32).T
+    turned = stacked.T
     lane = lax.broadcasted_iota(jnp.int32, turned.shape, 1)
     group = 64 // kv_heads
     return [
@@ -84,9 +90,9 @@
 
 
 def own_kernel(n_req, own_pages, *refs):
-    q_ref, kv_hbm, slot_hbm, owner_hbm, len_hbm, pool_hbm = refs[:6]
+    q_hbm, kv_hbm, slot_hbm, owner_hbm, len_hbm, pool_hbm = refs[:6]
     acc_ref, log_ref, limit_ref, pages_ref = refs[6:10]
-    kv, slots, owners, lens, pool, small_sem, pool_sem, page_sem = refs[10:]
+    q_row, q_heads, kv, slots, owners, lens, pool, small_sem, pool_sem, page_sem = refs[10:]
     slot_count, kv_heads, page_len, width = pool_hbm.shape
     head_dim = width // 2
     entries = slot_hbm.shape[2]
@@ -95,14 +101,13 @@
     small = [
         pltpu.make_async_copy(src, dst, small_sem.at[i])
         for i, (src, dst) in enumerate(
-            ((slot_hbm, slots), (owner_hbm, owners), (len_hbm, lens), (kv_hbm, kv))
+            ((slot_hbm, slots), (owner_hbm, owners), (len_hbm, lens), (kv_hbm, kv), (q_hbm, q_row))
         )
     ]
     for copy in small:
         copy.start()
     whole = pltpu.make_async_copy(pool_hbm, pool, pool_sem)
     whole.start()
-    tiles = query_tiles(jnp.concatenate([q_ref[...], q_ref[...]], axis=0), kv_heads)
     for copy in small:
         copy.wait()
 
@@ -127,6 +132,9 @@
     for p in range(len(limits) // 2):
         limit_ref[p : p + 1] = jnp.where(lane < 64, limits[2 * p], limits[2 * p + 1])
 
+    lay_rows(q_heads, 0, q_row)
+    q_heads[64:] = q_heads[:64]
+    tiles = query_tiles(q_heads[...], kv_heads)
     my_length = lens[0, me]
     pages, valid = [], []
     for i in range(own_pages):
@@ -184,7 +192,7 @@
 def own_attention(q, new_kv, page_slot, page_owner, context_len, pool, n_req):
     slots, kv_heads, page_len, width = pool.shape
     head_dim = width // 2
-    heads = q.shape[0]
+    heads = q.shape[1] // head_dim
     own_pages = min(slots, page_slot.shape[2])
     hbm = pl.BlockSpec(memory_space=pltpu.HBM)
     vmem = pl.BlockSpec(memory_space=pltpu.VMEM)
@@ -198,15 +206,17 @@
             jax.ShapeDtypeStruct((round_up(pair_count, 8), 128), jnp.int32),
             jax.ShapeDtypeStruct((n_req - 1, kv_heads, page_len, width), pool.dtype),
         ],
-        in_specs=[vmem] + [hbm] * 5,
+        in_specs=[hbm] * 6,
         out_specs=[vmem] * 4,
         scratch_shapes=[
+            pltpu.VMEM(q.shape, q.dtype),
+            pltpu.VMEM((128, head_dim), jnp.float32),
             pltpu.VMEM(new_kv.shape, new_kv.dtype),
             pltpu.SMEM(page_slot.shape, jnp.int32),
             pltpu.SMEM(page_owner.shape, jnp.int32),
             pltpu.SMEM(context_len.shape, jnp.int32),
             pltpu.VMEM(pool.shape, pool.dtype),
-            pltpu.SemaphoreType.DMA((4,)),
+            pltpu.SemaphoreType.DMA((5,)),
             pltpu.SemaphoreType.DMA,
             pltpu.SemaphoreType.DMA((n_req - 1,)),
         ],
@@ -217,15 +227,14 @@
             transcendentals=0,
         ),
         name="own_attention",
-    )(q, *(in_hbm(x) for x in (new_kv, page_slot, page_owner, context_len, pool)))
+    )(*(in_hbm(x) for x in (q, new_kv, page_slot, page_owner, context_len, pool)))
 
 
 def other_kernel(n_req, n_tp, *refs):
-    q_of = dict(zip(reversed(near_last(n_req)), refs[: n_req - 1]))
-    q_refs = [q_of[d] for d in range(1, n_req)]
+    q_refs = refs[: n_req - 1][::-1]
     acc_ref, log_ref, limit_ref, pages_ref = refs[n_req - 1 : n_req + 3]
     out_refs = refs[n_req + 3 : n_req + 3 + n_tp]
-    results, logs = refs[n_req + 3 + n_tp :]
+    results, logs, q_heads = refs[n_req + 3 + n_tp :]
     kv_heads, width = pages_ref.shape[1], pages_ref.shape[3]
     head_dim = width // 2
     chunk = 64 // n_tp
@@ -245,7 +254,9 @@
     for p in range(pairs):
         a, b = 2 * p, min(2 * p + 1, others - 1)
         members.append((a, b))
-        tiles = query_tiles(jnp.concatenate([q_refs[a][...], q_refs[b][...]], axis=0), kv_heads)
+        lay_rows(q_heads.at[p], 0, q_refs[a])
+        lay_rows(q_heads.at[p], 64, q_refs[b])
+        tiles = query_tiles(q_heads[p], kv_heads)
         scores.append(pair_scores(pages_ref.at[a], pages_ref.at[b], tiles, head_dim) * scale)
     sums, inverse, log_rows = [], [], []
     for p in range(pairs):
@@ -293,6 +304,7 @@
         scratch_shapes=[
             pltpu.VMEM((n_req * heads, head_dim), jnp.float32),
             pltpu.VMEM((round_up(n_req, 8), 128), jnp.float32),
+            pltpu.VMEM((round_up(n_req - 1, 2) // 2, 128, head_dim), jnp.float32),
         ],
         compiler_params=pltpu.CompilerParams(vmem_limit_bytes=16 * MIB),
         cost_estimate=pl.CostEstimate(flops=2 * own[3].size * 16, bytes_accessed=own[3].size * 2, transcendentals=0),
@@ -394,13 +406,11 @@
     n_req = lax.axis_size("req")
     n_tp = lax.axis_size("tp")
     pool = cache_pool[0, 0]
-    head_dim = pool.shape[3] // 2
-    q = queries.reshape(-1, head_dim)
-    q_list = [swap(q, "req", d) for d in reversed(near_last(n_req))]
-    own = own_attention(q, new_kv, page_slot, page_owner, context_len, pool, n_req)
+    q_list = [swap(queries, "req", d) for d in range(n_req - 1, 0, -1)]
+    own = own_attention(queries, new_kv, page_slot, page_owner, context_len, pool, n_req)
     pieces = other_attention(q_list, own, n_req, n_tp)
     depth = out_weight.shape[0]
-    early = depth * 5 // 16
+    early = depth // 4
     swapped = [swap(pieces[d], "tp", d) for d in near_last(n_tp)]
     first, mine = load_weight(pieces[0], out_weight, 0, early)
     arrived = jnp.concatenate([mine] + swapped, axis=0)

time: 33.5 us -> 32.7 us (0.976)
  other arithmetic: 1.55 us -> 0.7 us
    unnamed x1 -> x0, other arithmetic: 0.85 us -> none
  transfers between devices with their start and end apart: 12 -> 12, of which waited for: 4 -> 4; matrix products, arithmetic and copies ran while one was open for 0% -> 0% of each run, Pallas kernels for 28% -> 29%
where the time goes in v8:
time: 32.7 us; the launch traced here: 32.5 us
  starting transfers between devices  13.5 us (41%)
  Pallas kernels  12.8 us (39%)
  waiting for transfers between devices  5.33 us (16%)
  other arithmetic  0.7 us (2%)
    ppermute x12, starting transfers between devices, swap(): return lax.ppermute(x, axis, [(i, i ^ offset) for i in range(count)])  13.5 us
    pallas_call x2, Pallas kernels, load_weight(): pl.pallas_call(functools.partial(load_kernel, first), out_shape=[jax.Shap...  6.89 us
    ppermute x12, waiting for transfers between devices, swap(): return lax.ppermute(x, axis, [(i, i ^ offset) for i in range(count)])  5.33 us
    pallas_call x1, Pallas kernels, project(): pl.pallas_call(functools.partial(project_kernel, n_req, n_tp), out_shape=...  2.73 us
    pallas_call x1, Pallas kernels, own_attention(): pl.pallas_call(functools.partial(own_kernel, n_req, own_pages), out_shape...  2.39 us
    pallas_call x1, Pallas kernels, other_attention(): pl.pallas_call(functools.partial(other_kernel, n_req, n_tp), out_shape=[j...  0.84 us
  transfers between devices with their start and end apart: 12, of which 4 were waited for; matrix products, arithmetic and copies ran while one was open for 0% of the time, Pallas kernels for 29%

profile of v8, /device:TPU:0, one launch (start us, length us, event | category | flops | bytes accessed | tf_op | source)
XLA Modules:
  0.0 32.5 jit_solution(181376810134010774)
XLA Ops:
  0.0 4.0 %collective-permute-start.1 = (bf16[1,8192]{1,0:T(2,128)(2,1)}, bf16[1,8192]{1,0:T(2,128)(2,1)S(1)}, u32[]{:S(2)}, u32[]{:S(2)}) collective-permute-start(bf16[1,8192]{1,0:T(2,128)(2,1)} %refs_0_.1), channel_id=1, source_target_pairs={{0,2},{1,3},{2,0},{3,1},{4,6},{5,7},{6,4},{7,5},{8,10},{9,11},{10,... | collective-permute-start | bytes 49160 | tf_op jit(solution)/shard_map/ppermute | solution.py:17
  4.0 1.3 %collective-permute-start = (bf16[1,8192]{1,0:T(2,128)(2,1)}, bf16[1,8192]{1,0:T(2,128)(2,1)S(1)}, u32[]{:S(2)}, u32[]{:S(2)}) collective-permute-start(bf16[1,8192]{1,0:T(2,128)(2,1)} %refs_0_.1), channel_id=1, source_target_pairs={{0,3},{1,2},{2,1},{3,0},{4,7},{5,6},{6,5},{7,4},{8,11},{9,10},{10,... | collective-permute-start | bytes 49160 | tf_op jit(solution)/shard_map/ppermute | solution.py:17
  5.4 0.2 collective-permute-start.2
  5.6 2.4 %own_attention.1 = (f32[64,128]{1,0:T(8,128)S(1)}, f32[8,128]{1,0:T(8,128)S(1)}, s32[8,128]{1,0:T(8,128)S(1)}, bf16[3,4,128,256]{3,2,1,0:T(8,128)(2,1)S(1)}) custom-call(bf16[1,8192]{1,0:T(2,128)(2,1)} %refs_0_.1, bf16[1,1024]{1,0:T(2,128)(2,1)} %refs_1_.1, s32[1,4,7]{2,1,0:T(4,128)} %refs_2_.1, s32[1,4,7]{2,1,0:T(4,128)} %refs_3_.1, s32[1,4]{1,0:T(1,128)} %refs_4_.1, ...), custom_call_target="tpu_custom_call" | custom-call | flops 25165824 | bytes 4718592 | tf_op jit(solution)/shard_map/own_attention/pallas_call | solution.py:201
  8.0 0.0 collective-permute-done.1.refs_1_
  8.0 1.9 %collective-permute-done.refs_0_ = bf16[1,8192]{1,0:T(2,128)(2,1)S(1)} collective-permute-done((bf16[1,8192]{1,0:T(2,128)(2,1)}, bf16[1,8192]{1,0:T(2,128)(2,1)S(1)}, u32[]{:S(2)}, u32[]{:S(2)}) %collective-permute-start) | collective-permute-done | bytes 16416 | tf_op jit(solution)/shard_map/ppermute | solution.py:17
  10.0 0.0 collective-permute-done.2.refs_2_
  10.0 0.8 %other_attention.1 = (bf16[4,2176]{1,0:T(4,128)(2,1)S(1)}, bf16[4,2176]{1,0:T(4,128)(2,1)S(1)}, bf16[4,2176]{1,0:T(4,128)(2,1)S(1)}, bf16[4,2176]{1,0:T(4,128)(2,1)S(1)}) custom-call(bf16[1,8192]{1,0:T(2,128)(2,1)S(1)} %collective-permute-done.refs_0_, bf16[1,8192]{1,0:T(2,128)(2,1)S(1)} %collective-permute-done.1.refs_1_, ...), custom_call_target="tpu_custom_call" | custom-call | flops 12582912 | bytes 786432 | tf_op jit(solution)/shard_map/other_attention/pallas_call | solution.py:299
  10.8 1.6 %collective-permute-start.3 = (bf16[4,2176]{1,0:T(4,128)(2,1)S(1)}, bf16[4,2176]{1,0:T(4,128)(2,1)S(1)}, u32[]{:S(2)}, u32[]{:S(2)}) collective-permute-start(bf16[4,2176]{1,0:T(4,128)(2,1)S(1)} %get-tuple-element.27), channel_id=1, source_target_pairs={{0,8},{4,12},{8,0},{12,4},{1,9},{5,13},{9,1},{13,5},{2,10},{6,14},... | collective-permute-start | bytes 52232 | tf_op jit(solution)/shard_map/ppermute | solution.py:17
  12.4 0.0 collective-permute-start.4
  12.4 0.6 %collective-permute-start.5 = (bf16[4,2176]{1,0:T(4,128)(2,1)S(1)}, bf16[4,2176]{1,0:T(4,128)(2,1)S(1)}, u32[]{:S(2)}, u32[]{:S(2)}) collective-permute-start(bf16[4,2176]{1,0:T(4,128)(2,1)S(1)} %get-tuple-element.29), channel_id=1, source_target_pairs={{0,4},{4,0},{8,12},{12,8},{1,5},{5,1},{9,13},{13,9},{2,6},{6,2},{1... | collective-permute-start | bytes 52232 | tf_op jit(solution)/shard_map/ppermute | solution.py:17
  13.0 2.2 %load_weight.2 = (bf16[512,4096]{1,0:T(8,128)(2,1)S(1)}, bf16[4,2176]{1,0:T(4,128)(2,1)S(1)}) custom-call(bf16[4,2176]{1,0:T(4,128)(2,1)S(1)} %get-tuple-element.25.piece_ref, bf16[2048,4096]{1,0:T(8,128)(2,1)} %weight_hbm.3), custom_call_target="tpu_custom_call" | custom-call | bytes 8388608 | tf_op jit(solution)/shard_map/load_weight/pallas_call | solution.py:338
  15.2 0.0 collective-permute-done.3
  15.2 0.3 collective-permute-done.4
  15.5 0.0 collective-permute-done.5
  15.6 1.3 %collective-permute-start.8 = (bf16[16,2176]{1,0:T(8,128)(2,1)S(1)}, bf16[16,2176]{1,0:T(8,128)(2,1)S(1)}, u32[]{:S(2)}, u32[]{:S(2)}) collective-permute-start(bf16[16,2176]{1,0:T(8,128)(2,1)S(1)} %pad_maximum_fusion.piece_ref), channel_id=1, source_target_pairs={{0,2},{1,3},{2,0},{3,1},{4,6},{5,7},{6,4},{7,5},{8,10},{9,11},{10,... | collective-permute-start | bytes 208904 | tf_op jit(solution)/shard_map/ppermute | solution.py:17
  16.9 1.0 %collective-permute-start.7 = (bf16[16,2176]{1,0:T(8,128)(2,1)S(1)}, bf16[16,2176]{1,0:T(8,128)(2,1)S(1)}, u32[]{:S(2)}, u32[]{:S(2)}) collective-permute-start(bf16[16,2176]{1,0:T(8,128)(2,1)S(1)} %pad_maximum_fusion.piece_ref), channel_id=1, source_target_pairs={{0,3},{1,2},{2,1},{3,0},{4,7},{5,6},{6,5},{7,4},{8,11},{9,10},{10,... | collective-permute-start | bytes 208904 | tf_op jit(solution)/shard_map/ppermute | solution.py:17
  17.9 1.2 %collective-permute-start.6 = (bf16[16,2176]{1,0:T(8,128)(2,1)S(1)}, bf16[16,2176]{1,0:T(8,128)(2,1)S(1)}, u32[]{:S(2)}, u32[]{:S(2)}) collective-permute-start(bf16[16,2176]{1,0:T(8,128)(2,1)S(1)} %pad_maximum_fusion.piece_ref), channel_id=1, source_target_pairs={{0,1},{1,0},{2,3},{3,2},{4,5},{5,4},{6,7},{7,6},{8,9},{9,8},{10,11... | collective-permute-start | bytes 208904 | tf_op jit(solution)/shard_map/ppermute | solution.py:17
  19.2 4.7 %load_weight.3 = (bf16[1536,4096]{1,0:T(8,128)(2,1)S(1)}, bf16[16,2176]{1,0:T(8,128)(2,1)S(1)}) custom-call(bf16[16,2176]{1,0:T(8,128)(2,1)S(1)} %pad_maximum_fusion.piece_ref, bf16[2048,4096]{1,0:T(8,128)(2,1)} %weight_hbm.3), custom_call_target="tpu_custom_call" | custom-call | bytes 25165824 | tf_op jit(solution)/shard_map/load_weight/pallas_call | solution.py:338
  23.9 0.0 collective-permute-done.8.refs_3_
  23.9 0.0 collective-permute-done.7.refs_2_
  23.9 0.0 collective-permute-done.6.refs_1_
  23.9 2.7 %project.1 = (f32[4,4096]{1,0:T(4,128)S(1)}, bf16[4,4096]{1,0:T(4,128)(2,1)S(1)}, bf16[4,4096]{1,0:T(4,128)(2,1)S(1)}, bf16[4,4096]{1,0:T(4,128)(2,1)S(1)}) custom-call(bf16[16,2176]{1,0:T(8,128)(2,1)S(1)} %get-tuple-element.30.refs_0_, bf16[16,2176]{1,0:T(8,128)(2,1)S(1)} %collective-permute-done.6.refs_1_, ...), custom_call_target="tpu_custom_call" | custom-call | flops 268435456 | bytes 16777216 | tf_op jit(solution)/shard_map/project/pallas_call | solution.py:391
  26.6 1.7 %collective-permute-start.9 = (bf16[4,4096]{1,0:T(4,128)(2,1)S(1)}, bf16[4,4096]{1,0:T(4,128)(2,1)S(1)}, u32[]{:S(2)}, u32[]{:S(2)}) collective-permute-start(bf16[4,4096]{1,0:T(4,128)(2,1)S(1)} %get-tuple-element.34), channel_id=1, source_target_pairs={{0,8},{4,12},{8,0},{12,4},{1,9},{5,13},{9,1},{13,5},{2,10},{6,14},... | collective-permute-start | bytes 98312 | tf_op jit(solution)/shard_map/ppermute | solution.py:17
  28.4 0.0 collective-permute-start.10
  28.4 0.4 %collective-permute-start.11 = (bf16[4,4096]{1,0:T(4,128)(2,1)S(1)}, bf16[4,4096]{1,0:T(4,128)(2,1)S(1)}, u32[]{:S(2)}, u32[]{:S(2)}) collective-permute-start(bf16[4,4096]{1,0:T(4,128)(2,1)S(1)} %get-tuple-element.36), channel_id=1, source_target_pairs={{0,4},{4,0},{8,12},{12,8},{1,5},{5,1},{9,13},{13,9},{2,6},{6,2},{1... | collective-permute-start | bytes 98312 | tf_op jit(solution)/shard_map/ppermute | solution.py:17
  28.8 1.8 %collective-permute-done.9 = bf16[4,4096]{1,0:T(4,128)(2,1)S(1)} collective-permute-done((bf16[4,4096]{1,0:T(4,128)(2,1)S(1)}, bf16[4,4096]{1,0:T(4,128)(2,1)S(1)}, u32[]{:S(2)}, u32[]{:S(2)}) %collective-permute-start.9) | collective-permute-done | bytes 32800 | tf_op jit(solution)/shard_map/ppermute | solution.py:17
  30.5 1.3 %collective-permute-done.10 = bf16[4,4096]{1,0:T(4,128)(2,1)S(1)} collective-permute-done((bf16[4,4096]{1,0:T(4,128)(2,1)S(1)}, bf16[4,4096]{1,0:T(4,128)(2,1)S(1)}, u32[]{:S(2)}, u32[]{:S(2)}) %collective-permute-start.10) | collective-permute-done | bytes 32800 | tf_op jit(solution)/shard_map/ppermute | solution.py:17
  31.8 0.0 collective-permute-done.11
  31.8 0.7 %add_convert_fusion = bf16[4,4096]{1,0:T(4,128)(2,1)} fusion(bf16[4,4096]{1,0:T(4,128)(2,1)S(1)} %collective-permute-done.11, bf16[4,4096]{1,0:T(4,128)(2,1)S(1)} %collective-permute-done.10, f32[4,4096]{1,0:T(4,128)S(1)} %get-tuple-element.33, bf16[4,4096]{1,0:T(4,128)(2,1)S(1)} %collective-permute-done.9), kind=kLoop, calls=%fused_computation.1 | loop fusion | flops 114688 | bytes 196608 | tf_op jit(solution)/shard_map/convert_element_type | solution.py:423
  (1 shorter events, 0.0 us)
Async XLA Ops:
  0.0 8.0 %collective-permute-start.1 = (bf16[1,8192]{1,0:T(2,128)(2,1)}, bf16[1,8192]{1,0:T(2,128)(2,1)S(1)}, u32[]{:S(2)}, u32[]{:S(2)}) collective-permute-start(bf16[1,8192]{1,0:T(2,128)(2,1)} %refs_0_.1), channel_id=1, source_target_pairs={{0,2},{1,3},{2,0},{3,1},{4,6},{5,7},{6,4},{7,5},{8,10},{9,11},{10,... | collective-permute-start | bytes 49160 | tf_op jit(solution)/shard_map/ppermute | solution.py:17
  4.0 5.9 %collective-permute-start = (bf16[1,8192]{1,0:T(2,128)(2,1)}, bf16[1,8192]{1,0:T(2,128)(2,1)S(1)}, u32[]{:S(2)}, u32[]{:S(2)}) collective-permute-start(bf16[1,8192]{1,0:T(2,128)(2,1)} %refs_0_.1), channel_id=1, source_target_pairs={{0,3},{1,2},{2,1},{3,0},{4,7},{5,6},{6,5},{7,4},{8,11},{9,10},{10,... | collective-permute-start | bytes 49160 | tf_op jit(solution)/shard_map/ppermute | solution.py:17
  5.4 4.6 %collective-permute-start.2 = (bf16[1,8192]{1,0:T(2,128)(2,1)}, bf16[1,8192]{1,0:T(2,128)(2,1)S(1)}, u32[]{:S(2)}, u32[]{:S(2)}) collective-permute-start(bf16[1,8192]{1,0:T(2,128)(2,1)} %refs_0_.1), channel_id=1, source_target_pairs={{0,1},{1,0},{2,3},{3,2},{4,5},{5,4},{6,7},{7,6},{8,9},{9,8},{10,11... | collective-permute-start | bytes 49160 | tf_op jit(solution)/shard_map/ppermute | solution.py:17
  10.8 4.4 %collective-permute-start.3 = (bf16[4,2176]{1,0:T(4,128)(2,1)S(1)}, bf16[4,2176]{1,0:T(4,128)(2,1)S(1)}, u32[]{:S(2)}, u32[]{:S(2)}) collective-permute-start(bf16[4,2176]{1,0:T(4,128)(2,1)S(1)} %get-tuple-element.27), channel_id=1, source_target_pairs={{0,8},{4,12},{8,0},{12,4},{1,9},{5,13},{9,1},{13,5},{2,10},{6,14},... | collective-permute-start | bytes 52232 | tf_op jit(solution)/shard_map/ppermute | solution.py:17
  12.4 3.2 %collective-permute-start.4 = (bf16[4,2176]{1,0:T(4,128)(2,1)S(1)}, bf16[4,2176]{1,0:T(4,128)(2,1)S(1)}, u32[]{:S(2)}, u32[]{:S(2)}) collective-permute-start(bf16[4,2176]{1,0:T(4,128)(2,1)S(1)} %get-tuple-element.28), channel_id=1, source_target_pairs={{0,12},{4,8},{8,4},{12,0},{1,13},{5,9},{9,5},{13,1},{2,14},{6,10},... | collective-permute-start | bytes 52232 | tf_op jit(solution)/shard_map/ppermute | solution.py:17
  12.4 3.2 %collective-permute-start.5 = (bf16[4,2176]{1,0:T(4,128)(2,1)S(1)}, bf16[4,2176]{1,0:T(4,128)(2,1)S(1)}, u32[]{:S(2)}, u32[]{:S(2)}) collective-permute-start(bf16[4,2176]{1,0:T(4,128)(2,1)S(1)} %get-tuple-element.29), channel_id=1, source_target_pairs={{0,4},{4,0},{8,12},{12,8},{1,5},{5,1},{9,13},{13,9},{2,6},{6,2},{1... | collective-permute-start | bytes 52232 | tf_op jit(solution)/shard_map/ppermute | solution.py:17
  15.6 8.3 %collective-permute-start.8 = (bf16[16,2176]{1,0:T(8,128)(2,1)S(1)}, bf16[16,2176]{1,0:T(8,128)(2,1)S(1)}, u32[]{:S(2)}, u32[]{:S(2)}) collective-permute-start(bf16[16,2176]{1,0:T(8,128)(2,1)S(1)} %pad_maximum_fusion.piece_ref), channel_id=1, source_target_pairs={{0,2},{1,3},{2,0},{3,1},{4,6},{5,7},{6,4},{7,5},{8,10},{9,11},{10,... | collective-permute-start | bytes 208904 | tf_op jit(solution)/shard_map/ppermute | solution.py:17
  16.9 7.0 %collective-permute-start.7 = (bf16[16,2176]{1,0:T(8,128)(2,1)S(1)}, bf16[16,2176]{1,0:T(8,128)(2,1)S(1)}, u32[]{:S(2)}, u32[]{:S(2)}) collective-permute-start(bf16[16,2176]{1,0:T(8,128)(2,1)S(1)} %pad_maximum_fusion.piece_ref), channel_id=1, source_target_pairs={{0,3},{1,2},{2,1},{3,0},{4,7},{5,6},{6,5},{7,4},{8,11},{9,10},{10,... | collective-permute-start | bytes 208904 | tf_op jit(solution)/shard_map/ppermute | solution.py:17
  17.9 6.0 %collective-permute-start.6 = (bf16[16,2176]{1,0:T(8,128)(2,1)S(1)}, bf16[16,2176]{1,0:T(8,128)(2,1)S(1)}, u32[]{:S(2)}, u32[]{:S(2)}) collective-permute-start(bf16[16,2176]{1,0:T(8,128)(2,1)S(1)} %pad_maximum_fusion.piece_ref), channel_id=1, source_target_pairs={{0,1},{1,0},{2,3},{3,2},{4,5},{5,4},{6,7},{7,6},{8,9},{9,8},{10,11... | collective-permute-start | bytes 208904 | tf_op jit(solution)/shard_map/ppermute | solution.py:17
  26.6 3.9 %collective-permute-start.9 = (bf16[4,4096]{1,0:T(4,128)(2,1)S(1)}, bf16[4,4096]{1,0:T(4,128)(2,1)S(1)}, u32[]{:S(2)}, u32[]{:S(2)}) collective-permute-start(bf16[4,4096]{1,0:T(4,128)(2,1)S(1)} %get-tuple-element.34), channel_id=1, source_target_pairs={{0,8},{4,12},{8,0},{12,4},{1,9},{5,13},{9,1},{13,5},{2,10},{6,14},... | collective-permute-start | bytes 98312 | tf_op jit(solution)/shard_map/ppermute | solution.py:17
  28.4 3.5 %collective-permute-start.10 = (bf16[4,4096]{1,0:T(4,128)(2,1)S(1)}, bf16[4,4096]{1,0:T(4,128)(2,1)S(1)}, u32[]{:S(2)}, u32[]{:S(2)}) collective-permute-start(bf16[4,4096]{1,0:T(4,128)(2,1)S(1)} %get-tuple-element.35), channel_id=1, source_target_pairs={{0,12},{4,8},{8,4},{12,0},{1,13},{5,9},{9,5},{13,1},{2,14},{6,10},... | collective-permute-start | bytes 98312 | tf_op jit(solution)/shard_map/ppermute | solution.py:17
  28.4 3.5 %collective-permute-start.11 = (bf16[4,4096]{1,0:T(4,128)(2,1)S(1)}, bf16[4,4096]{1,0:T(4,128)(2,1)S(1)}, u32[]{:S(2)}, u32[]{:S(2)}) collective-permute-start(bf16[4,4096]{1,0:T(4,128)(2,1)S(1)} %get-tuple-element.36), channel_id=1, source_target_pairs={{0,4},{4,0},{8,12},{12,8},{1,5},{5,1},{9,13},{13,9},{2,6},{6,2},{1... | collective-permute-start | bytes 98312 | tf_op jit(solution)/shard_map/ppermute | solution.py:17

commit v9 on v8

--- a/solution.py
+++ b/solution.py
@@ -19,6 +19,10 @@
 
 def near_last(count):
     return list(range(2, count)) + [1]
+
+
+def query_order(count):
+    return [count - 1, 1] + list(range(2, count - 1))
 
 
 def in_hbm(x):
@@ -231,7 +235,8 @@
 
 
 def other_kernel(n_req, n_tp, *refs):
-    q_refs = refs[: n_req - 1][::-1]
+    q_of = dict(zip(query_order(n_req), refs[: n_req - 1]))
+    q_refs = [q_of[d] for d in range(1, n_req)]
     acc_ref, log_ref, limit_ref, pages_ref = refs[n_req - 1 : n_req + 3]
     out_refs = refs[n_req + 3 : n_req + 3 + n_tp]
     results, logs, q_heads = refs[n_req + 3 + n_tp :]
@@ -312,19 +317,20 @@
     )(*q_list, *own)
 
 
-def row_copies(source, first, target, sems):
+def row_copies(source, first, column, target, sems):
     parts = sems.shape[0]
     step = target.shape[0] // parts
+    columns = pl.ds(column, target.shape[1])
     return [
         pltpu.make_async_copy(
-            source.at[pl.ds(first + i * step, step)], target.at[pl.ds(i * step, step)], sems.at[i]
+            source.at[pl.ds(first + i * step, step), columns], target.at[pl.ds(i * step, step)], sems.at[i]
         )
         for i in range(parts)
     ]
 
 
 def load_kernel(first, piece_ref, weight_hbm, out_ref, same_ref, sems):
-    copies = row_copies(weight_hbm, first, out_ref, sems)
+    copies = row_copies(weight_hbm, first, 0, out_ref, sems)
     for copy in copies:
         copy.start()
     same_ref[...] = piece_ref[...]
@@ -332,8 +338,7 @@
         copy.wait()
 
 
-def load_weight(piece, out_weight, first, rows):
-    columns = out_weight.shape[1]
+def load_weight(piece, out_weight, first, rows, columns):
     vmem = pl.BlockSpec(memory_space=pltpu.VMEM)
     return pl.pallas_call(
         functools.partial(load_kernel, first),
@@ -352,10 +357,13 @@
 
 def project_kernel(n_req, n_tp, *refs):
     part_refs = refs[:n_req]
-    weight_refs = refs[n_req : n_req + 2]
-    out_refs = refs[n_req + 2 : n_req + 2 + n_tp]
-    attention = refs[n_req + 2 + n_tp]
-    split, columns = weight_refs[0].shape
+    upper, lower, weight_hbm = refs[n_req : n_req + 3]
+    out_refs = refs[n_req + 3 : n_req + 3 + n_tp]
+    attention, last, sems = refs[n_req + 3 + n_tp :]
+    split, columns = upper.shape
+    copies = row_copies(weight_hbm, 0, columns, last, sems)
+    for copy in copies:
+        copy.start()
     depth = attention.shape[1]
     chunk = depth // 128
     values = []
@@ -370,20 +378,26 @@
         at = slice(h * 128, (h + 1) * 128)
         terms = [part[:, at].astype(jnp.float32) * f[:, h : h + 1] for part, f in zip(part_refs, factors)]
         attention[:, at] = functools.reduce(jnp.add, terms).astype(jnp.bfloat16)
-    tile = min(columns, 2048)
-
-    @pl.loop(0, columns // tile)
-    def _(t):
-        at = pl.ds(pl.multiple_of(t * tile, tile), tile)
-        product = jnp.dot(attention[:, :split], weight_refs[0][:, at], preferred_element_type=jnp.float32)
-        product += jnp.dot(attention[:, split:], weight_refs[1][:, at], preferred_element_type=jnp.float32)
+
+    def put(product, at):
         for i, d in enumerate([0] + near_last(n_tp)):
             out_refs[d][:, at] = product[i * n_req : (i + 1) * n_req].astype(out_refs[d].dtype)
 
-
-def project(parts, weights, n_req, n_tp):
-    depth = sum(w.shape[0] for w in weights)
-    columns = weights[0].shape[1]
+    tile = columns // pl.cdiv(columns, 2048)
+    for t in range(0, columns, tile):
+        at = slice(t, t + tile)
+        product = jnp.dot(attention[:, :split], upper[:, at], preferred_element_type=jnp.float32)
+        product += jnp.dot(attention[:, split:], lower[:, at], preferred_element_type=jnp.float32)
+        put(product, at)
+    for copy in copies:
+        copy.wait()
+    product = jnp.dot(attention[...], last[...], preferred_element_type=jnp.float32)
+    put(product, slice(columns, columns + last.shape[1]))
+
+
+def project(parts, weights, out_weight, n_req, n_tp):
+    depth, columns = out_weight.shape
+    last = columns - weights[0].shape[1]
     vmem = pl.BlockSpec(memory_space=pltpu.VMEM)
     own = jax.ShapeDtypeStruct((n_req, columns), jnp.float32)
     sent = jax.ShapeDtypeStruct((n_req, columns), jnp.bfloat16)
@@ -391,32 +405,37 @@
     return pl.pallas_call(
         functools.partial(project_kernel, n_req, n_tp),
         out_shape=[own] + [sent] * (n_tp - 1),
-        in_specs=[vmem] * (n_req + 2),
+        in_specs=[vmem] * (n_req + 2) + [pl.BlockSpec(memory_space=pltpu.HBM)],
         out_specs=[vmem] * n_tp,
-        scratch_shapes=[pltpu.VMEM((rows, depth), jnp.bfloat16)],
+        scratch_shapes=[
+            pltpu.VMEM((rows, depth), jnp.bfloat16),
+            pltpu.VMEM((depth, last), jnp.bfloat16),
+            pltpu.SemaphoreType.DMA((2,)),
+        ],
         compiler_params=pltpu.CompilerParams(vmem_limit_bytes=16 * MIB),
         cost_estimate=pl.CostEstimate(
             flops=2 * rows * depth * columns, bytes_accessed=depth * columns * 2, transcendentals=0
         ),
         name="project",
-    )(*parts, *weights)
+    )(*parts, *weights, in_hbm(out_weight))
 
 
 def on_device(queries, new_kv, cache_pool, page_slot, page_owner, context_len, out_weight):
     n_req = lax.axis_size("req")
     n_tp = lax.axis_size("tp")
     pool = cache_pool[0, 0]
-    q_list = [swap(queries, "req", d) for d in range(n_req - 1, 0, -1)]
+    q_list = [swap(queries, "req", d) for d in query_order(n_req)]
     own = own_attention(queries, new_kv, page_slot, page_owner, context_len, pool, n_req)
     pieces = other_attention(q_list, own, n_req, n_tp)
-    depth = out_weight.shape[0]
+    depth, columns = out_weight.shape
     early = depth // 4
+    columns -= min(512, columns // 2)
     swapped = [swap(pieces[d], "tp", d) for d in near_last(n_tp)]
-    first, mine = load_weight(pieces[0], out_weight, 0, early)
+    first, mine = load_weight(pieces[0], out_weight, 0, early, columns)
     arrived = jnp.concatenate([mine] + swapped, axis=0)
     parts = [swap(arrived, "req", d) for d in reversed(near_last(n_req))]
-    second, mine = load_weight(arrived, out_weight, early, depth - early)
-    sums = project([mine] + parts, (first, second), n_req, n_tp)
+    second, mine = load_weight(arrived, out_weight, early, depth - early, columns)
+    sums = project([mine] + parts, (first, second), out_weight, n_req, n_tp)
     total = sums[0]
     for d in near_last(n_tp):
         total = total + swap(sums[d], "tp", d).astype(jnp.float32)

time: 32.7 us -> 33.4 us (1.021)
  waiting for transfers between devices: 5.33 us -> 6.73 us
  Pallas kernels: 12.8 us -> 12.1 us
    ppermute x12, waiting for transfers between devices: 5.33 us -> 6.73 us  [swap(): return lax.ppermute(x, axis, [(i, i ^ offset) for i in range(count)])]
    pallas_call x2, Pallas kernels: 6.89 us -> 6.29 us  [load_weight(): pl.pallas_call(functools.partial(load_kernel, first), out_shape=[jax.Shap...]
  transfers between devices with their start and end apart: 12 -> 12, of which waited for: 4 -> 7; matrix products, arithmetic and copies ran while one was open for 0% -> 0% of each run, Pallas kernels for 29% -> 26%
where the time goes in v9:
time: 33.4 us; the launch traced here: 33.2 us
  starting transfers between devices  13.6 us (41%)
  Pallas kernels  12.1 us (36%)
  waiting for transfers between devices  6.73 us (20%)
  other arithmetic  0.7 us (2%)
    ppermute x12, starting transfers between devices, swap(): return lax.ppermute(x, axis, [(i, i ^ offset) for i in range(count)])  13.6 us
    ppermute x12, waiting for transfers between devices, swap(): return lax.ppermute(x, axis, [(i, i ^ offset) for i in range(count)])  6.73 us
    pallas_call x2, Pallas kernels, load_weight(): pl.pallas_call(functools.partial(load_kernel, first), out_shape=[jax.Shap...  6.29 us
    pallas_call x1, Pallas kernels, project(): pl.pallas_call(functools.partial(project_kernel, n_req, n_tp), out_shape=...  2.61 us
    pallas_call x1, Pallas kernels, own_attention(): pl.pallas_call(functools.partial(own_kernel, n_req, own_pages), out_shape...  2.39 us
    pallas_call x1, Pallas kernels, other_attention(): pl.pallas_call(functools.partial(other_kernel, n_req, n_tp), out_shape=[j...  0.84 us
  transfers between devices with their start and end apart: 12, of which 7 were waited for; matrix products, arithmetic and copies ran while one was open for 0% of the time, Pallas kernels for 26%

profile of v9, /device:TPU:0, one launch (start us, length us, event | category | flops | bytes accessed | tf_op | source)
XLA Modules:
  0.0 33.2 jit_solution(9039895409339410293)
XLA Ops:
  0.0 3.0 %collective-permute-start.1 = (bf16[1,8192]{1,0:T(2,128)(2,1)}, bf16[1,8192]{1,0:T(2,128)(2,1)S(1)}, u32[]{:S(2)}, u32[]{:S(2)}) collective-permute-start(bf16[1,8192]{1,0:T(2,128)(2,1)} %refs_0_.1), channel_id=1, source_target_pairs={{0,1},{1,0},{2,3},{3,2},{4,5},{5,4},{6,7},{7,6},{8,9},{9,8},{10,11... | collective-permute-start | bytes 49160 | tf_op jit(solution)/shard_map/ppermute | solution.py:17
  3.0 2.5 %collective-permute-start = (bf16[1,8192]{1,0:T(2,128)(2,1)}, bf16[1,8192]{1,0:T(2,128)(2,1)S(1)}, u32[]{:S(2)}, u32[]{:S(2)}) collective-permute-start(bf16[1,8192]{1,0:T(2,128)(2,1)} %refs_0_.1), channel_id=1, source_target_pairs={{0,3},{1,2},{2,1},{3,0},{4,7},{5,6},{6,5},{7,4},{8,11},{9,10},{10,... | collective-permute-start | bytes 49160 | tf_op jit(solution)/shard_map/ppermute | solution.py:17
  5.5 0.1 collective-permute-start.2
  5.6 2.4 %own_attention.1 = (f32[64,128]{1,0:T(8,128)S(1)}, f32[8,128]{1,0:T(8,128)S(1)}, s32[8,128]{1,0:T(8,128)S(1)}, bf16[3,4,128,256]{3,2,1,0:T(8,128)(2,1)S(1)}) custom-call(bf16[1,8192]{1,0:T(2,128)(2,1)} %refs_0_.1, bf16[1,1024]{1,0:T(2,128)(2,1)} %refs_1_.1, s32[1,4,7]{2,1,0:T(4,128)} %refs_2_.1, s32[1,4,7]{2,1,0:T(4,128)} %refs_3_.1, s32[1,4]{1,0:T(1,128)} %refs_4_.1, ...), custom_call_target="tpu_custom_call" | custom-call | flops 25165824 | bytes 4718592 | tf_op jit(solution)/shard_map/own_attention/pallas_call | solution.py:205
  8.0 0.0 collective-permute-done.1.refs_1_
  8.0 1.4 %collective-permute-done.refs_0_ = bf16[1,8192]{1,0:T(2,128)(2,1)S(1)} collective-permute-done((bf16[1,8192]{1,0:T(2,128)(2,1)}, bf16[1,8192]{1,0:T(2,128)(2,1)S(1)}, u32[]{:S(2)}, u32[]{:S(2)}) %collective-permute-start) | collective-permute-done | bytes 16416 | tf_op jit(solution)/shard_map/ppermute | solution.py:17
  9.4 1.5 %collective-permute-done.2.refs_2_ = bf16[1,8192]{1,0:T(2,128)(2,1)S(1)} collective-permute-done((bf16[1,8192]{1,0:T(2,128)(2,1)}, bf16[1,8192]{1,0:T(2,128)(2,1)S(1)}, u32[]{:S(2)}, u32[]{:S(2)}) %collective-permute-start.2) | collective-permute-done | bytes 16416 | tf_op jit(solution)/shard_map/ppermute | solution.py:17
  10.9 0.8 %other_attention.1 = (bf16[4,2176]{1,0:T(4,128)(2,1)S(1)}, bf16[4,2176]{1,0:T(4,128)(2,1)S(1)}, bf16[4,2176]{1,0:T(4,128)(2,1)S(1)}, bf16[4,2176]{1,0:T(4,128)(2,1)S(1)}) custom-call(bf16[1,8192]{1,0:T(2,128)(2,1)S(1)} %collective-permute-done.refs_0_, bf16[1,8192]{1,0:T(2,128)(2,1)S(1)} %collective-permute-done.1.refs_1_, ...), custom_call_target="tpu_custom_call" | custom-call | flops 12582912 | bytes 786432 | tf_op jit(solution)/shard_map/other_attention/pallas_call | solution.py:304
  11.7 1.6 %collective-permute-start.3 = (bf16[4,2176]{1,0:T(4,128)(2,1)S(1)}, bf16[4,2176]{1,0:T(4,128)(2,1)S(1)}, u32[]{:S(2)}, u32[]{:S(2)}) collective-permute-start(bf16[4,2176]{1,0:T(4,128)(2,1)S(1)} %get-tuple-element.27), channel_id=1, source_target_pairs={{0,8},{4,12},{8,0},{12,4},{1,9},{5,13},{9,1},{13,5},{2,10},{6,14},... | collective-permute-start | bytes 52232 | tf_op jit(solution)/shard_map/ppermute | solution.py:17
  13.3 0.0 collective-permute-start.4
  13.3 0.6 %collective-permute-start.5 = (bf16[4,2176]{1,0:T(4,128)(2,1)S(1)}, bf16[4,2176]{1,0:T(4,128)(2,1)S(1)}, u32[]{:S(2)}, u32[]{:S(2)}) collective-permute-start(bf16[4,2176]{1,0:T(4,128)(2,1)S(1)} %get-tuple-element.29), channel_id=1, source_target_pairs={{0,4},{4,0},{8,12},{12,8},{1,5},{5,1},{9,13},{13,9},{2,6},{6,2},{1... | collective-permute-start | bytes 52232 | tf_op jit(solution)/shard_map/ppermute | solution.py:17
  13.9 2.0 %load_weight.2 = (bf16[512,3584]{1,0:T(8,128)(2,1)S(1)}, bf16[4,2176]{1,0:T(4,128)(2,1)S(1)}) custom-call(bf16[4,2176]{1,0:T(4,128)(2,1)S(1)} %get-tuple-element.25.piece_ref, bf16[2048,4096]{1,0:T(8,128)(2,1)} %refs_6_.1), custom_call_target="tpu_custom_call" | custom-call | bytes 7340032 | tf_op jit(solution)/shard_map/load_weight/pallas_call | solution.py:343
  16.0 0.0 collective-permute-done.3
  16.0 0.5 %collective-permute-done.4 = bf16[4,2176]{1,0:T(4,128)(2,1)S(1)} collective-permute-done((bf16[4,2176]{1,0:T(4,128)(2,1)S(1)}, bf16[4,2176]{1,0:T(4,128)(2,1)S(1)}, u32[]{:S(2)}, u32[]{:S(2)}) %collective-permute-start.4) | collective-permute-done | bytes 17440 | tf_op jit(solution)/shard_map/ppermute | solution.py:17
  16.5 0.0 collective-permute-done.5
  16.5 0.1 collective-permute-start.8
  16.6 2.8 %collective-permute-start.7 = (bf16[16,2176]{1,0:T(8,128)(2,1)S(1)}, bf16[16,2176]{1,0:T(8,128)(2,1)S(1)}, u32[]{:S(2)}, u32[]{:S(2)}) collective-permute-start(bf16[16,2176]{1,0:T(8,128)(2,1)S(1)} %pad_maximum_fusion.piece_ref), channel_id=1, source_target_pairs={{0,3},{1,2},{2,1},{3,0},{4,7},{5,6},{6,5},{7,4},{8,11},{9,10},{10,... | collective-permute-start | bytes 208904 | tf_op jit(solution)/shard_map/ppermute | solution.py:17
  19.4 0.7 %collective-permute-start.6 = (bf16[16,2176]{1,0:T(8,128)(2,1)S(1)}, bf16[16,2176]{1,0:T(8,128)(2,1)S(1)}, u32[]{:S(2)}, u32[]{:S(2)}) collective-permute-start(bf16[16,2176]{1,0:T(8,128)(2,1)S(1)} %pad_maximum_fusion.piece_ref), channel_id=1, source_target_pairs={{0,1},{1,0},{2,3},{3,2},{4,5},{5,4},{6,7},{7,6},{8,9},{9,8},{10,11... | collective-permute-start | bytes 208904 | tf_op jit(solution)/shard_map/ppermute | solution.py:17
  20.1 4.2 %load_weight.3 = (bf16[1536,3584]{1,0:T(8,128)(2,1)S(1)}, bf16[16,2176]{1,0:T(8,128)(2,1)S(1)}) custom-call(bf16[16,2176]{1,0:T(8,128)(2,1)S(1)} %pad_maximum_fusion.piece_ref, bf16[2048,4096]{1,0:T(8,128)(2,1)} %refs_6_.1), custom_call_target="tpu_custom_call" | custom-call | bytes 22020096 | tf_op jit(solution)/shard_map/load_weight/pallas_call | solution.py:343
  24.3 0.1 collective-permute-done.8.refs_3_
  24.4 0.0 collective-permute-done.7.refs_2_
  24.4 0.3 %collective-permute-done.6.refs_1_ = bf16[16,2176]{1,0:T(8,128)(2,1)S(1)} collective-permute-done((bf16[16,2176]{1,0:T(8,128)(2,1)S(1)}, bf16[16,2176]{1,0:T(8,128)(2,1)S(1)}, u32[]{:S(2)}, u32[]{:S(2)}) %collective-permute-start.6) | collective-permute-done | bytes 69664 | tf_op jit(solution)/shard_map/ppermute | solution.py:17
  24.7 2.6 %project.1 = (f32[4,4096]{1,0:T(4,128)S(1)}, bf16[4,4096]{1,0:T(4,128)(2,1)S(1)}, bf16[4,4096]{1,0:T(4,128)(2,1)S(1)}, bf16[4,4096]{1,0:T(4,128)(2,1)S(1)}) custom-call(bf16[16,2176]{1,0:T(8,128)(2,1)S(1)} %get-tuple-element.30.refs_0_, bf16[16,2176]{1,0:T(8,128)(2,1)S(1)} %collective-permute-done.6.refs_1_, ...), custom_call_target="tpu_custom_call" | custom-call | flops 268435456 | bytes 16777216 | tf_op jit(solution)/shard_map/project/pallas_call | solution.py:405
  27.4 1.8 %collective-permute-start.9 = (bf16[4,4096]{1,0:T(4,128)(2,1)S(1)}, bf16[4,4096]{1,0:T(4,128)(2,1)S(1)}, u32[]{:S(2)}, u32[]{:S(2)}) collective-permute-start(bf16[4,4096]{1,0:T(4,128)(2,1)S(1)} %get-tuple-element.34), channel_id=1, source_target_pairs={{0,8},{4,12},{8,0},{12,4},{1,9},{5,13},{9,1},{13,5},{2,10},{6,14},... | collective-permute-start | bytes 98312 | tf_op jit(solution)/shard_map/ppermute | solution.py:17
  29.2 0.0 collective-permute-start.10
  29.2 0.4 %collective-permute-start.11 = (bf16[4,4096]{1,0:T(4,128)(2,1)S(1)}, bf16[4,4096]{1,0:T(4,128)(2,1)S(1)}, u32[]{:S(2)}, u32[]{:S(2)}) collective-permute-start(bf16[4,4096]{1,0:T(4,128)(2,1)S(1)} %get-tuple-element.36), channel_id=1, source_target_pairs={{0,4},{4,0},{8,12},{12,8},{1,5},{5,1},{9,13},{13,9},{2,6},{6,2},{1... | collective-permute-start | bytes 98312 | tf_op jit(solution)/shard_map/ppermute | solution.py:17
  29.6 1.8 %collective-permute-done.9 = bf16[4,4096]{1,0:T(4,128)(2,1)S(1)} collective-permute-done((bf16[4,4096]{1,0:T(4,128)(2,1)S(1)}, bf16[4,4096]{1,0:T(4,128)(2,1)S(1)}, u32[]{:S(2)}, u32[]{:S(2)}) %collective-permute-start.9) | collective-permute-done | bytes 32800 | tf_op jit(solution)/shard_map/ppermute | solution.py:17
  31.3 1.2 %collective-permute-done.10 = bf16[4,4096]{1,0:T(4,128)(2,1)S(1)} collective-permute-done((bf16[4,4096]{1,0:T(4,128)(2,1)S(1)}, bf16[4,4096]{1,0:T(4,128)(2,1)S(1)}, u32[]{:S(2)}, u32[]{:S(2)}) %collective-permute-start.10) | collective-permute-done | bytes 32800 | tf_op jit(solution)/shard_map/ppermute | solution.py:17
  32.6 0.0 collective-permute-done.11
  32.6 0.7 %add_convert_fusion = bf16[4,4096]{1,0:T(4,128)(2,1)} fusion(bf16[4,4096]{1,0:T(4,128)(2,1)S(1)} %collective-permute-done.11, bf16[4,4096]{1,0:T(4,128)(2,1)S(1)} %collective-permute-done.10, f32[4,4096]{1,0:T(4,128)S(1)} %get-tuple-element.33, bf16[4,4096]{1,0:T(4,128)(2,1)S(1)} %collective-permute-done.9), kind=kLoop, calls=%fused_computation.1 | loop fusion | flops 114688 | bytes 196608 | tf_op jit(solution)/shard_map/convert_element_type | solution.py:442
  (1 shorter events, 0.0 us)
Async XLA Ops:
  0.0 8.0 %collective-permute-start.1 = (bf16[1,8192]{1,0:T(2,128)(2,1)}, bf16[1,8192]{1,0:T(2,128)(2,1)S(1)}, u32[]{:S(2)}, u32[]{:S(2)}) collective-permute-start(bf16[1,8192]{1,0:T(2,128)(2,1)} %refs_0_.1), channel_id=1, source_target_pairs={{0,1},{1,0},{2,3},{3,2},{4,5},{5,4},{6,7},{7,6},{8,9},{9,8},{10,11... | collective-permute-start | bytes 49160 | tf_op jit(solution)/shard_map/ppermute | solution.py:17
  3.0 6.4 %collective-permute-start = (bf16[1,8192]{1,0:T(2,128)(2,1)}, bf16[1,8192]{1,0:T(2,128)(2,1)S(1)}, u32[]{:S(2)}, u32[]{:S(2)}) collective-permute-start(bf16[1,8192]{1,0:T(2,128)(2,1)} %refs_0_.1), channel_id=1, source_target_pairs={{0,3},{1,2},{2,1},{3,0},{4,7},{5,6},{6,5},{7,4},{8,11},{9,10},{10,... | collective-permute-start | bytes 49160 | tf_op jit(solution)/shard_map/ppermute | solution.py:17
  5.5 5.4 %collective-permute-start.2 = (bf16[1,8192]{1,0:T(2,128)(2,1)}, bf16[1,8192]{1,0:T(2,128)(2,1)S(1)}, u32[]{:S(2)}, u32[]{:S(2)}) collective-permute-start(bf16[1,8192]{1,0:T(2,128)(2,1)} %refs_0_.1), channel_id=1, source_target_pairs={{0,2},{1,3},{2,0},{3,1},{4,6},{5,7},{6,4},{7,5},{8,10},{9,11},{10,... | collective-permute-start | bytes 49160 | tf_op jit(solution)/shard_map/ppermute | solution.py:17
  11.7 4.3 %collective-permute-start.3 = (bf16[4,2176]{1,0:T(4,128)(2,1)S(1)}, bf16[4,2176]{1,0:T(4,128)(2,1)S(1)}, u32[]{:S(2)}, u32[]{:S(2)}) collective-permute-start(bf16[4,2176]{1,0:T(4,128)(2,1)S(1)} %get-tuple-element.27), channel_id=1, source_target_pairs={{0,8},{4,12},{8,0},{12,4},{1,9},{5,13},{9,1},{13,5},{2,10},{6,14},... | collective-permute-start | bytes 52232 | tf_op jit(solution)/shard_map/ppermute | solution.py:17
  13.3 3.2 %collective-permute-start.4 = (bf16[4,2176]{1,0:T(4,128)(2,1)S(1)}, bf16[4,2176]{1,0:T(4,128)(2,1)S(1)}, u32[]{:S(2)}, u32[]{:S(2)}) collective-permute-start(bf16[4,2176]{1,0:T(4,128)(2,1)S(1)} %get-tuple-element.28), channel_id=1, source_target_pairs={{0,12},{4,8},{8,4},{12,0},{1,13},{5,9},{9,5},{13,1},{2,14},{6,10},... | collective-permute-start | bytes 52232 | tf_op jit(solution)/shard_map/ppermute | solution.py:17
  13.3 3.2 %collective-permute-start.5 = (bf16[4,2176]{1,0:T(4,128)(2,1)S(1)}, bf16[4,2176]{1,0:T(4,128)(2,1)S(1)}, u32[]{:S(2)}, u32[]{:S(2)}) collective-permute-start(bf16[4,2176]{1,0:T(4,128)(2,1)S(1)} %get-tuple-element.29), channel_id=1, source_target_pairs={{0,4},{4,0},{8,12},{12,8},{1,5},{5,1},{9,13},{13,9},{2,6},{6,2},{1... | collective-permute-start | bytes 52232 | tf_op jit(solution)/shard_map/ppermute | solution.py:17
  16.5 7.9 %collective-permute-start.8 = (bf16[16,2176]{1,0:T(8,128)(2,1)S(1)}, bf16[16,2176]{1,0:T(8,128)(2,1)S(1)}, u32[]{:S(2)}, u32[]{:S(2)}) collective-permute-start(bf16[16,2176]{1,0:T(8,128)(2,1)S(1)} %pad_maximum_fusion.piece_ref), channel_id=1, source_target_pairs={{0,2},{1,3},{2,0},{3,1},{4,6},{5,7},{6,4},{7,5},{8,10},{9,11},{10,... | collective-permute-start | bytes 208904 | tf_op jit(solution)/shard_map/ppermute | solution.py:17
  16.6 7.8 %collective-permute-start.7 = (bf16[16,2176]{1,0:T(8,128)(2,1)S(1)}, bf16[16,2176]{1,0:T(8,128)(2,1)S(1)}, u32[]{:S(2)}, u32[]{:S(2)}) collective-permute-start(bf16[16,2176]{1,0:T(8,128)(2,1)S(1)} %pad_maximum_fusion.piece_ref), channel_id=1, source_target_pairs={{0,3},{1,2},{2,1},{3,0},{4,7},{5,6},{6,5},{7,4},{8,11},{9,10},{10,... | collective-permute-start | bytes 208904 | tf_op jit(solution)/shard_map/ppermute | solution.py:17
  19.4 5.4 %collective-permute-start.6 = (bf16[16,2176]{1,0:T(8,128)(2,1)S(1)}, bf16[16,2176]{1,0:T(8,128)(2,1)S(1)}, u32[]{:S(2)}, u32[]{:S(2)}) collective-permute-start(bf16[16,2176]{1,0:T(8,128)(2,1)S(1)} %pad_maximum_fusion.piece_ref), channel_id=1, source_target_pairs={{0,1},{1,0},{2,3},{3,2},{4,5},{5,4},{6,7},{7,6},{8,9},{9,8},{10,11... | collective-permute-start | bytes 208904 | tf_op jit(solution)/shard_map/ppermute | solution.py:17
  27.4 4.0 %collective-permute-start.9 = (bf16[4,4096]{1,0:T(4,128)(2,1)S(1)}, bf16[4,4096]{1,0:T(4,128)(2,1)S(1)}, u32[]{:S(2)}, u32[]{:S(2)}) collective-permute-start(bf16[4,4096]{1,0:T(4,128)(2,1)S(1)} %get-tuple-element.34), channel_id=1, source_target_pairs={{0,8},{4,12},{8,0},{12,4},{1,9},{5,13},{9,1},{13,5},{2,10},{6,14},... | collective-permute-start | bytes 98312 | tf_op jit(solution)/shard_map/ppermute | solution.py:17
  29.2 3.3 %collective-permute-start.10 = (bf16[4,4096]{1,0:T(4,128)(2,1)S(1)}, bf16[4,4096]{1,0:T(4,128)(2,1)S(1)}, u32[]{:S(2)}, u32[]{:S(2)}) collective-permute-start(bf16[4,4096]{1,0:T(4,128)(2,1)S(1)} %get-tuple-element.35), channel_id=1, source_target_pairs={{0,12},{4,8},{8,4},{12,0},{1,13},{5,9},{9,5},{13,1},{2,14},{6,10},... | collective-permute-start | bytes 98312 | tf_op jit(solution)/shard_map/ppermute | solution.py:17
  29.2 3.3 %collective-permute-start.11 = (bf16[4,4096]{1,0:T(4,128)(2,1)S(1)}, bf16[4,4096]{1,0:T(4,128)(2,1)S(1)}, u32[]{:S(2)}, u32[]{:S(2)}) collective-permute-start(bf16[4,4096]{1,0:T(4,128)(2,1)S(1)} %get-tuple-element.36), channel_id=1, source_target_pairs={{0,4},{4,0},{8,12},{12,8},{1,5},{5,1},{9,13},{13,9},{2,6},{6,2},{1... | collective-permute-start | bytes 98312 | tf_op jit(solution)/shard_map/ppermute | solution.py:17

commit v10 on v9

--- a/solution.py
+++ b/solution.py
@@ -21,8 +21,8 @@
     return list(range(2, count)) + [1]
 
 
-def query_order(count):
-    return [count - 1, 1] + list(range(2, count - 1))
+def far_first(count):
+    return list(range(count - 1, 0, -1))
 
 
 def in_hbm(x):
@@ -235,7 +235,7 @@
 
 
 def other_kernel(n_req, n_tp, *refs):
-    q_of = dict(zip(query_order(n_req), refs[: n_req - 1]))
+    q_of = dict(zip(far_first(n_req), refs[: n_req - 1]))
     q_refs = [q_of[d] for d in range(1, n_req)]
     acc_ref, log_ref, limit_ref, pages_ref = refs[n_req - 1 : n_req + 3]
     out_refs = refs[n_req + 3 : n_req + 3 + n_tp]
@@ -380,7 +380,7 @@
         attention[:, at] = functools.reduce(jnp.add, terms).astype(jnp.bfloat16)
 
     def put(product, at):
-        for i, d in enumerate([0] + near_last(n_tp)):
+        for i, d in enumerate([0] + far_first(n_tp)):
             out_refs[d][:, at] = product[i * n_req : (i + 1) * n_req].astype(out_refs[d].dtype)
 
     tile = columns // pl.cdiv(columns, 2048)
@@ -424,20 +424,20 @@
     n_req = lax.axis_size("req")
     n_tp = lax.axis_size("tp")
     pool = cache_pool[0, 0]
-    q_list = [swap(queries, "req", d) for d in query_order(n_req)]
+    q_list = [swap(queries, "req", d) for d in far_first(n_req)]
     own = own_attention(queries, new_kv, page_slot, page_owner, context_len, pool, n_req)
     pieces = other_attention(q_list, own, n_req, n_tp)
     depth, columns = out_weight.shape
     early = depth // 4
     columns -= min(512, columns // 2)
-    swapped = [swap(pieces[d], "tp", d) for d in near_last(n_tp)]
+    swapped = [swap(pieces[d], "tp", d) for d in far_first(n_tp)]
     first, mine = load_weight(pieces[0], out_weight, 0, early, columns)
     arrived = jnp.concatenate([mine] + swapped, axis=0)
     parts = [swap(arrived, "req", d) for d in reversed(near_last(n_req))]
     second, mine = load_weight(arrived, out_weight, early, depth - early, columns)
     sums = project([mine] + parts, (first, second), out_weight, n_req, n_tp)
     total = sums[0]
-    for d in near_last(n_tp):
+    for d in far_first(n_tp):
         total = total + swap(sums[d], "tp", d).astype(jnp.float32)
     return total.astype(jnp.bfloat16)
 

time: 33.4 us -> 32.1 us (0.961)
  waiting for transfers between devices: 6.73 us -> 5.98 us
  starting transfers between devices: 13.6 us -> 13 us
    ppermute x12, waiting for transfers between devices: 6.73 us -> 5.98 us  [swap(): return lax.ppermute(x, axis, [(i, i ^ offset) for i in range(count)])]
    ppermute x12, starting transfers between devices: 13.6 us -> 13 us  [swap(): return lax.ppermute(x, axis, [(i, i ^ offset) for i in range(count)])]
  transfers between devices with their start and end apart: 12 -> 12, of which waited for: 7 -> 5; matrix products, arithmetic and copies ran while one was open for 0% -> 0% of each run, Pallas kernels for 26% -> 27%
where the time goes in v10:
time: 32.1 us; the launch traced here: 31.9 us
  starting transfers between devices  13 us (40%)
  Pallas kernels  12.1 us (38%)
  waiting for transfers between devices  5.98 us (19%)
  other arithmetic  0.7 us (2%)
    ppermute x12, starting transfers between devices, swap(): return lax.ppermute(x, axis, [(i, i ^ offset) for i in range(count)])  13 us
    pallas_call x2, Pallas kernels, load_weight(): pl.pallas_call(functools.partial(load_kernel, first), out_shape=[jax.Shap...  6.29 us
    ppermute x12, waiting for transfers between devices, swap(): return lax.ppermute(x, axis, [(i, i ^ offset) for i in range(count)])  5.98 us
    pallas_call x1, Pallas kernels, project(): pl.pallas_call(functools.partial(project_kernel, n_req, n_tp), out_shape=...  2.61 us
    pallas_call x1, Pallas kernels, own_attention(): pl.pallas_call(functools.partial(own_kernel, n_req, own_pages), out_shape...  2.39 us
    pallas_call x1, Pallas kernels, other_attention(): pl.pallas_call(functools.partial(other_kernel, n_req, n_tp), out_shape=[j...  0.84 us
    convert_element_type x1, other arithmetic, on_device(): return total.astype(jnp.bfloat16)  0.65 us
  transfers between devices with their start and end apart: 12, of which 5 were waited for; matrix products, arithmetic and copies ran while one was open for 0% of the time, Pallas kernels for 27%

profile of v10, /device:TPU:0, one launch (start us, length us, event | category | flops | bytes accessed | tf_op | source)
XLA Modules:
  0.0 31.9 jit_solution(11091946033318320504)
XLA Ops:
  0.0 4.0 %collective-permute-start.1 = (bf16[1,8192]{1,0:T(2,128)(2,1)}, bf16[1,8192]{1,0:T(2,128)(2,1)S(1)}, u32[]{:S(2)}, u32[]{:S(2)}) collective-permute-start(bf16[1,8192]{1,0:T(2,128)(2,1)} %refs_0_.1), channel_id=1, source_target_pairs={{0,2},{1,3},{2,0},{3,1},{4,6},{5,7},{6,4},{7,5},{8,10},{9,11},{10,... | collective-permute-start | bytes 49160 | tf_op jit(solution)/shard_map/ppermute | solution.py:17
  4.0 1.3 %collective-permute-start = (bf16[1,8192]{1,0:T(2,128)(2,1)}, bf16[1,8192]{1,0:T(2,128)(2,1)S(1)}, u32[]{:S(2)}, u32[]{:S(2)}) collective-permute-start(bf16[1,8192]{1,0:T(2,128)(2,1)} %refs_0_.1), channel_id=1, source_target_pairs={{0,3},{1,2},{2,1},{3,0},{4,7},{5,6},{6,5},{7,4},{8,11},{9,10},{10,... | collective-permute-start | bytes 49160 | tf_op jit(solution)/shard_map/ppermute | solution.py:17
  5.4 0.2 collective-permute-start.2
  5.6 2.4 %own_attention.1 = (f32[64,128]{1,0:T(8,128)S(1)}, f32[8,128]{1,0:T(8,128)S(1)}, s32[8,128]{1,0:T(8,128)S(1)}, bf16[3,4,128,256]{3,2,1,0:T(8,128)(2,1)S(1)}) custom-call(bf16[1,8192]{1,0:T(2,128)(2,1)} %refs_0_.1, bf16[1,1024]{1,0:T(2,128)(2,1)} %refs_1_.1, s32[1,4,7]{2,1,0:T(4,128)} %refs_2_.1, s32[1,4,7]{2,1,0:T(4,128)} %refs_3_.1, s32[1,4]{1,0:T(1,128)} %refs_4_.1, ...), custom_call_target="tpu_custom_call" | custom-call | flops 25165824 | bytes 4718592 | tf_op jit(solution)/shard_map/own_attention/pallas_call | solution.py:205
  8.0 0.0 collective-permute-done.1.refs_1_
  8.0 1.9 %collective-permute-done.refs_0_ = bf16[1,8192]{1,0:T(2,128)(2,1)S(1)} collective-permute-done((bf16[1,8192]{1,0:T(2,128)(2,1)}, bf16[1,8192]{1,0:T(2,128)(2,1)S(1)}, u32[]{:S(2)}, u32[]{:S(2)}) %collective-permute-start) | collective-permute-done | bytes 16416 | tf_op jit(solution)/shard_map/ppermute | solution.py:17
  10.0 0.0 collective-permute-done.2.refs_2_
  10.0 0.8 %other_attention.1 = (bf16[4,2176]{1,0:T(4,128)(2,1)S(1)}, bf16[4,2176]{1,0:T(4,128)(2,1)S(1)}, bf16[4,2176]{1,0:T(4,128)(2,1)S(1)}, bf16[4,2176]{1,0:T(4,128)(2,1)S(1)}) custom-call(bf16[1,8192]{1,0:T(2,128)(2,1)S(1)} %collective-permute-done.refs_0_, bf16[1,8192]{1,0:T(2,128)(2,1)S(1)} %collective-permute-done.1.refs_1_, ...), custom_call_target="tpu_custom_call" | custom-call | flops 12582912 | bytes 786432 | tf_op jit(solution)/shard_map/other_attention/pallas_call | solution.py:304
  10.8 0.1 collective-permute-start.3
  10.9 1.6 %collective-permute-start.4 = (bf16[4,2176]{1,0:T(4,128)(2,1)S(1)}, bf16[4,2176]{1,0:T(4,128)(2,1)S(1)}, u32[]{:S(2)}, u32[]{:S(2)}) collective-permute-start(bf16[4,2176]{1,0:T(4,128)(2,1)S(1)} %get-tuple-element.28), channel_id=1, source_target_pairs={{0,8},{4,12},{8,0},{12,4},{1,9},{5,13},{9,1},{13,5},{2,10},{6,14},... | collective-permute-start | bytes 52232 | tf_op jit(solution)/shard_map/ppermute | solution.py:17
  12.5 0.3 collective-permute-start.5
  12.7 2.0 %load_weight.2 = (bf16[512,3584]{1,0:T(8,128)(2,1)S(1)}, bf16[4,2176]{1,0:T(4,128)(2,1)S(1)}) custom-call(bf16[4,2176]{1,0:T(4,128)(2,1)S(1)} %get-tuple-element.25.piece_ref, bf16[2048,4096]{1,0:T(8,128)(2,1)} %refs_6_.1), custom_call_target="tpu_custom_call" | custom-call | bytes 7340032 | tf_op jit(solution)/shard_map/load_weight/pallas_call | solution.py:343
  14.8 0.0 collective-permute-done.3
  14.8 0.0 collective-permute-done.4
  14.8 0.0 collective-permute-done.5
  14.9 1.3 %collective-permute-start.8 = (bf16[16,2176]{1,0:T(8,128)(2,1)S(1)}, bf16[16,2176]{1,0:T(8,128)(2,1)S(1)}, u32[]{:S(2)}, u32[]{:S(2)}) collective-permute-start(bf16[16,2176]{1,0:T(8,128)(2,1)S(1)} %pad_maximum_fusion.piece_ref), channel_id=1, source_target_pairs={{0,2},{1,3},{2,0},{3,1},{4,6},{5,7},{6,4},{7,5},{8,10},{9,11},{10,... | collective-permute-start | bytes 208904 | tf_op jit(solution)/shard_map/ppermute | solution.py:17
  16.2 1.0 %collective-permute-start.7 = (bf16[16,2176]{1,0:T(8,128)(2,1)S(1)}, bf16[16,2176]{1,0:T(8,128)(2,1)S(1)}, u32[]{:S(2)}, u32[]{:S(2)}) collective-permute-start(bf16[16,2176]{1,0:T(8,128)(2,1)S(1)} %pad_maximum_fusion.piece_ref), channel_id=1, source_target_pairs={{0,3},{1,2},{2,1},{3,0},{4,7},{5,6},{6,5},{7,4},{8,11},{9,10},{10,... | collective-permute-start | bytes 208904 | tf_op jit(solution)/shard_map/ppermute | solution.py:17
  17.2 1.2 %collective-permute-start.6 = (bf16[16,2176]{1,0:T(8,128)(2,1)S(1)}, bf16[16,2176]{1,0:T(8,128)(2,1)S(1)}, u32[]{:S(2)}, u32[]{:S(2)}) collective-permute-start(bf16[16,2176]{1,0:T(8,128)(2,1)S(1)} %pad_maximum_fusion.piece_ref), channel_id=1, source_target_pairs={{0,1},{1,0},{2,3},{3,2},{4,5},{5,4},{6,7},{7,6},{8,9},{9,8},{10,11... | collective-permute-start | bytes 208904 | tf_op jit(solution)/shard_map/ppermute | solution.py:17
  18.4 4.2 %load_weight.3 = (bf16[1536,3584]{1,0:T(8,128)(2,1)S(1)}, bf16[16,2176]{1,0:T(8,128)(2,1)S(1)}) custom-call(bf16[16,2176]{1,0:T(8,128)(2,1)S(1)} %pad_maximum_fusion.piece_ref, bf16[2048,4096]{1,0:T(8,128)(2,1)} %refs_6_.1), custom_call_target="tpu_custom_call" | custom-call | bytes 22020096 | tf_op jit(solution)/shard_map/load_weight/pallas_call | solution.py:343
  22.7 0.0 collective-permute-done.8.refs_3_
  22.7 0.1 collective-permute-done.7.refs_2_
  22.8 1.2 %collective-permute-done.6.refs_1_ = bf16[16,2176]{1,0:T(8,128)(2,1)S(1)} collective-permute-done((bf16[16,2176]{1,0:T(8,128)(2,1)S(1)}, bf16[16,2176]{1,0:T(8,128)(2,1)S(1)}, u32[]{:S(2)}, u32[]{:S(2)}) %collective-permute-start.6) | collective-permute-done | bytes 69664 | tf_op jit(solution)/shard_map/ppermute | solution.py:17
  24.0 2.6 %project.1 = (f32[4,4096]{1,0:T(4,128)S(1)}, bf16[4,4096]{1,0:T(4,128)(2,1)S(1)}, bf16[4,4096]{1,0:T(4,128)(2,1)S(1)}, bf16[4,4096]{1,0:T(4,128)(2,1)S(1)}) custom-call(bf16[16,2176]{1,0:T(8,128)(2,1)S(1)} %get-tuple-element.30.refs_0_, bf16[16,2176]{1,0:T(8,128)(2,1)S(1)} %collective-permute-done.6.refs_1_, ...), custom_call_target="tpu_custom_call" | custom-call | flops 268435456 | bytes 16777216 | tf_op jit(solution)/shard_map/project/pallas_call | solution.py:405
  26.6 0.7 %collective-permute-start.9 = (bf16[4,4096]{1,0:T(4,128)(2,1)S(1)}, bf16[4,4096]{1,0:T(4,128)(2,1)S(1)}, u32[]{:S(2)}, u32[]{:S(2)}) collective-permute-start(bf16[4,4096]{1,0:T(4,128)(2,1)S(1)} %get-tuple-element.34), channel_id=1, source_target_pairs={{0,12},{4,8},{8,4},{12,0},{1,13},{5,9},{9,5},{13,1},{2,14},{6,10},... | collective-permute-start | bytes 98312 | tf_op jit(solution)/shard_map/ppermute | solution.py:17
  27.3 1.0 %collective-permute-start.10 = (bf16[4,4096]{1,0:T(4,128)(2,1)S(1)}, bf16[4,4096]{1,0:T(4,128)(2,1)S(1)}, u32[]{:S(2)}, u32[]{:S(2)}) collective-permute-start(bf16[4,4096]{1,0:T(4,128)(2,1)S(1)} %get-tuple-element.35), channel_id=1, source_target_pairs={{0,8},{4,12},{8,0},{12,4},{1,9},{5,13},{9,1},{13,5},{2,10},{6,14},... | collective-permute-start | bytes 98312 | tf_op jit(solution)/shard_map/ppermute | solution.py:17
  28.3 0.3 collective-permute-start.11
  28.6 1.7 %collective-permute-done.9 = bf16[4,4096]{1,0:T(4,128)(2,1)S(1)} collective-permute-done((bf16[4,4096]{1,0:T(4,128)(2,1)S(1)}, bf16[4,4096]{1,0:T(4,128)(2,1)S(1)}, u32[]{:S(2)}, u32[]{:S(2)}) %collective-permute-start.9) | collective-permute-done | bytes 32800 | tf_op jit(solution)/shard_map/ppermute | solution.py:17
  30.2 1.0 %collective-permute-done.10 = bf16[4,4096]{1,0:T(4,128)(2,1)S(1)} collective-permute-done((bf16[4,4096]{1,0:T(4,128)(2,1)S(1)}, bf16[4,4096]{1,0:T(4,128)(2,1)S(1)}, u32[]{:S(2)}, u32[]{:S(2)}) %collective-permute-start.10) | collective-permute-done | bytes 32800 | tf_op jit(solution)/shard_map/ppermute | solution.py:17
  31.3 0.0 collective-permute-done.11
  31.3 0.7 %add_convert_fusion = bf16[4,4096]{1,0:T(4,128)(2,1)} fusion(bf16[4,4096]{1,0:T(4,128)(2,1)S(1)} %collective-permute-done.11, bf16[4,4096]{1,0:T(4,128)(2,1)S(1)} %collective-permute-done.10, f32[4,4096]{1,0:T(4,128)S(1)} %get-tuple-element.33, bf16[4,4096]{1,0:T(4,128)(2,1)S(1)} %collective-permute-done.9), kind=kLoop, calls=%fused_computation.1 | loop fusion | flops 114688 | bytes 196608 | tf_op jit(solution)/shard_map/convert_element_type | solution.py:442
  (1 shorter events, 0.0 us)
Async XLA Ops:
  0.0 8.0 %collective-permute-start.1 = (bf16[1,8192]{1,0:T(2,128)(2,1)}, bf16[1,8192]{1,0:T(2,128)(2,1)S(1)}, u32[]{:S(2)}, u32[]{:S(2)}) collective-permute-start(bf16[1,8192]{1,0:T(2,128)(2,1)} %refs_0_.1), channel_id=1, source_target_pairs={{0,2},{1,3},{2,0},{3,1},{4,6},{5,7},{6,4},{7,5},{8,10},{9,11},{10,... | collective-permute-start | bytes 49160 | tf_op jit(solution)/shard_map/ppermute | solution.py:17
  4.0 5.9 %collective-permute-start = (bf16[1,8192]{1,0:T(2,128)(2,1)}, bf16[1,8192]{1,0:T(2,128)(2,1)S(1)}, u32[]{:S(2)}, u32[]{:S(2)}) collective-permute-start(bf16[1,8192]{1,0:T(2,128)(2,1)} %refs_0_.1), channel_id=1, source_target_pairs={{0,3},{1,2},{2,1},{3,0},{4,7},{5,6},{6,5},{7,4},{8,11},{9,10},{10,... | collective-permute-start | bytes 49160 | tf_op jit(solution)/shard_map/ppermute | solution.py:17
  5.4 4.6 %collective-permute-start.2 = (bf16[1,8192]{1,0:T(2,128)(2,1)}, bf16[1,8192]{1,0:T(2,128)(2,1)S(1)}, u32[]{:S(2)}, u32[]{:S(2)}) collective-permute-start(bf16[1,8192]{1,0:T(2,128)(2,1)} %refs_0_.1), channel_id=1, source_target_pairs={{0,1},{1,0},{2,3},{3,2},{4,5},{5,4},{6,7},{7,6},{8,9},{9,8},{10,11... | collective-permute-start | bytes 49160 | tf_op jit(solution)/shard_map/ppermute | solution.py:17
  10.8 4.0 %collective-permute-start.3 = (bf16[4,2176]{1,0:T(4,128)(2,1)S(1)}, bf16[4,2176]{1,0:T(4,128)(2,1)S(1)}, u32[]{:S(2)}, u32[]{:S(2)}) collective-permute-start(bf16[4,2176]{1,0:T(4,128)(2,1)S(1)} %get-tuple-element.27), channel_id=1, source_target_pairs={{0,12},{4,8},{8,4},{12,0},{1,13},{5,9},{9,5},{13,1},{2,14},{6,10},... | collective-permute-start | bytes 52232 | tf_op jit(solution)/shard_map/ppermute | solution.py:17
  10.9 3.9 %collective-permute-start.4 = (bf16[4,2176]{1,0:T(4,128)(2,1)S(1)}, bf16[4,2176]{1,0:T(4,128)(2,1)S(1)}, u32[]{:S(2)}, u32[]{:S(2)}) collective-permute-start(bf16[4,2176]{1,0:T(4,128)(2,1)S(1)} %get-tuple-element.28), channel_id=1, source_target_pairs={{0,8},{4,12},{8,0},{12,4},{1,9},{5,13},{9,1},{13,5},{2,10},{6,14},... | collective-permute-start | bytes 52232 | tf_op jit(solution)/shard_map/ppermute | solution.py:17
  12.5 2.4 %collective-permute-start.5 = (bf16[4,2176]{1,0:T(4,128)(2,1)S(1)}, bf16[4,2176]{1,0:T(4,128)(2,1)S(1)}, u32[]{:S(2)}, u32[]{:S(2)}) collective-permute-start(bf16[4,2176]{1,0:T(4,128)(2,1)S(1)} %get-tuple-element.29), channel_id=1, source_target_pairs={{0,4},{4,0},{8,12},{12,8},{1,5},{5,1},{9,13},{13,9},{2,6},{6,2},{1... | collective-permute-start | bytes 52232 | tf_op jit(solution)/shard_map/ppermute | solution.py:17
  14.9 7.8 %collective-permute-start.8 = (bf16[16,2176]{1,0:T(8,128)(2,1)S(1)}, bf16[16,2176]{1,0:T(8,128)(2,1)S(1)}, u32[]{:S(2)}, u32[]{:S(2)}) collective-permute-start(bf16[16,2176]{1,0:T(8,128)(2,1)S(1)} %pad_maximum_fusion.piece_ref), channel_id=1, source_target_pairs={{0,2},{1,3},{2,0},{3,1},{4,6},{5,7},{6,4},{7,5},{8,10},{9,11},{10,... | collective-permute-start | bytes 208904 | tf_op jit(solution)/shard_map/ppermute | solution.py:17
  16.2 6.6 %collective-permute-start.7 = (bf16[16,2176]{1,0:T(8,128)(2,1)S(1)}, bf16[16,2176]{1,0:T(8,128)(2,1)S(1)}, u32[]{:S(2)}, u32[]{:S(2)}) collective-permute-start(bf16[16,2176]{1,0:T(8,128)(2,1)S(1)} %pad_maximum_fusion.piece_ref), channel_id=1, source_target_pairs={{0,3},{1,2},{2,1},{3,0},{4,7},{5,6},{6,5},{7,4},{8,11},{9,10},{10,... | collective-permute-start | bytes 208904 | tf_op jit(solution)/shard_map/ppermute | solution.py:17
  17.2 6.8 %collective-permute-start.6 = (bf16[16,2176]{1,0:T(8,128)(2,1)S(1)}, bf16[16,2176]{1,0:T(8,128)(2,1)S(1)}, u32[]{:S(2)}, u32[]{:S(2)}) collective-permute-start(bf16[16,2176]{1,0:T(8,128)(2,1)S(1)} %pad_maximum_fusion.piece_ref), channel_id=1, source_target_pairs={{0,1},{1,0},{2,3},{3,2},{4,5},{5,4},{6,7},{7,6},{8,9},{9,8},{10,11... | collective-permute-start | bytes 208904 | tf_op jit(solution)/shard_map/ppermute | solution.py:17
  26.6 3.6 %collective-permute-start.9 = (bf16[4,4096]{1,0:T(4,128)(2,1)S(1)}, bf16[4,4096]{1,0:T(4,128)(2,1)S(1)}, u32[]{:S(2)}, u32[]{:S(2)}) collective-permute-start(bf16[4,4096]{1,0:T(4,128)(2,1)S(1)} %get-tuple-element.34), channel_id=1, source_target_pairs={{0,12},{4,8},{8,4},{12,0},{1,13},{5,9},{9,5},{13,1},{2,14},{6,10},... | collective-permute-start | bytes 98312 | tf_op jit(solution)/shard_map/ppermute | solution.py:17
  27.3 3.9 %collective-permute-start.10 = (bf16[4,4096]{1,0:T(4,128)(2,1)S(1)}, bf16[4,4096]{1,0:T(4,128)(2,1)S(1)}, u32[]{:S(2)}, u32[]{:S(2)}) collective-permute-start(bf16[4,4096]{1,0:T(4,128)(2,1)S(1)} %get-tuple-element.35), channel_id=1, source_target_pairs={{0,8},{4,12},{8,0},{12,4},{1,9},{5,13},{9,1},{13,5},{2,10},{6,14},... | collective-permute-start | bytes 98312 | tf_op jit(solution)/shard_map/ppermute | solution.py:17
  28.3 3.0 %collective-permute-start.11 = (bf16[4,4096]{1,0:T(4,128)(2,1)S(1)}, bf16[4,4096]{1,0:T(4,128)(2,1)S(1)}, u32[]{:S(2)}, u32[]{:S(2)}) collective-permute-start(bf16[4,4096]{1,0:T(4,128)(2,1)S(1)} %get-tuple-element.36), channel_id=1, source_target_pairs={{0,4},{4,0},{8,12},{12,8},{1,5},{5,1},{9,13},{13,9},{2,6},{6,2},{1... | collective-permute-start | bytes 98312 | tf_op jit(solution)/shard_map/ppermute | solution.py:17

commit v11 on v10

--- a/solution.py
+++ b/solution.py
@@ -60,6 +60,8 @@
     total = None
     for h in range(len(tiles)):
         for a, page in enumerate((page_a, page_b)):
+            if page is None:
+                continue
             part = jnp.dot(page[h, :, :head_dim], tiles[h][a], preferred_element_type=jnp.float32)
             total = part if total is None else total + part
     return total
@@ -80,6 +82,9 @@
     group = 64 // kv_heads
     blocks = []
     for a, page in enumerate((page_a, page_b)):
+        if page is None:
+            blocks.append(jnp.zeros((64, head_dim), jnp.float32))
+            continue
         for h in range(kv_heads):
             at = a * 64 + h * group
             blocks.append(
@@ -257,17 +262,19 @@
     logs[...] = jnp.zeros_like(logs)
     scores, members = [], []
     for p in range(pairs):
-        a, b = 2 * p, min(2 * p + 1, others - 1)
-        members.append((a, b))
+        a, b = 2 * p, 2 * p + 1
         lay_rows(q_heads.at[p], 0, q_refs[a])
-        lay_rows(q_heads.at[p], 64, q_refs[b])
+        if b < others:
+            lay_rows(q_heads.at[p], 64, q_refs[b])
+        else:
+            q_heads[p, 64:] = jnp.zeros_like(q_heads[p, 64:])
+        members.append((pages_ref.at[a], pages_ref.at[b] if b < others else None))
         tiles = query_tiles(q_heads[p], kv_heads)
-        scores.append(pair_scores(pages_ref.at[a], pages_ref.at[b], tiles, head_dim) * scale)
+        scores.append(pair_scores(*members[p], tiles, head_dim) * scale)
     sums, inverse, log_rows = [], [], []
     for p in range(pairs):
-        a, b = members[p]
         top, total, weights = pair_softmax(scores[p], limit_ref[p : p + 1])
-        sums.append(pair_values(weights, pages_ref.at[a], pages_ref.at[b], head_dim))
+        sums.append(pair_values(weights, *members[p], head_dim))
         total = jnp.where(total > 0.0, total, 1.0)
         inverse.append(1.0 / total)
         log_rows.append(top + jnp.log(total))
@@ -317,20 +324,20 @@
     )(*q_list, *own)
 
 
-def row_copies(source, first, column, target, sems):
+def row_copies(source, column, target, sems):
     parts = sems.shape[0]
     step = target.shape[0] // parts
     columns = pl.ds(column, target.shape[1])
     return [
         pltpu.make_async_copy(
-            source.at[pl.ds(first + i * step, step), columns], target.at[pl.ds(i * step, step)], sems.at[i]
+            source.at[pl.ds(i * step, step), columns], target.at[pl.ds(i * step, step)], sems.at[i]
         )
         for i in range(parts)
     ]
 
 
-def load_kernel(first, piece_ref, weight_hbm, out_ref, same_ref, sems):
-    copies = row_copies(weight_hbm, first, 0, out_ref, sems)
+def load_kernel(piece_ref, weight_hbm, out_ref, same_ref, sems):
+    copies = row_copies(weight_hbm, 0, out_ref, sems)
     for copy in copies:
         copy.start()
     same_ref[...] = piece_ref[...]
@@ -338,30 +345,31 @@
         copy.wait()
 
 
-def load_weight(piece, out_weight, first, rows, columns):
+def load_weight(piece, out_weight, columns):
+    depth = out_weight.shape[0]
     vmem = pl.BlockSpec(memory_space=pltpu.VMEM)
     return pl.pallas_call(
-        functools.partial(load_kernel, first),
+        load_kernel,
         out_shape=[
-            jax.ShapeDtypeStruct((rows, columns), out_weight.dtype),
+            jax.ShapeDtypeStruct((depth, columns), out_weight.dtype),
             jax.ShapeDtypeStruct(piece.shape, piece.dtype),
         ],
         in_specs=[vmem, pl.BlockSpec(memory_space=pltpu.HBM)],
         out_specs=[vmem] * 2,
         scratch_shapes=[pltpu.SemaphoreType.DMA((4,))],
         compiler_params=pltpu.CompilerParams(vmem_limit_bytes=20 * MIB),
-        cost_estimate=pl.CostEstimate(flops=0, bytes_accessed=rows * columns * 4, transcendentals=0),
+        cost_estimate=pl.CostEstimate(flops=0, bytes_accessed=depth * columns * 4, transcendentals=0),
         name="load_weight",
     )(piece, in_hbm(out_weight))
 
 
 def project_kernel(n_req, n_tp, *refs):
     part_refs = refs[:n_req]
-    upper, lower, weight_hbm = refs[n_req : n_req + 3]
-    out_refs = refs[n_req + 3 : n_req + 3 + n_tp]
-    attention, last, sems = refs[n_req + 3 + n_tp :]
-    split, columns = upper.shape
-    copies = row_copies(weight_hbm, 0, columns, last, sems)
+    weight, weight_hbm = refs[n_req : n_req + 2]
+    out_refs = refs[n_req + 2 : n_req + 2 + n_tp]
+    attention, last, sems = refs[n_req + 2 + n_tp :]
+    columns = weight.shape[1]
+    copies = row_copies(weight_hbm, columns, last, sems)
     for copy in copies:
         copy.start()
     depth = attention.shape[1]
@@ -383,21 +391,19 @@
         for i, d in enumerate([0] + far_first(n_tp)):
             out_refs[d][:, at] = product[i * n_req : (i + 1) * n_req].astype(out_refs[d].dtype)
 
-    tile = columns // pl.cdiv(columns, 2048)
+    tile = round_up(pl.cdiv(columns, pl.cdiv(columns, 2048)), 256)
     for t in range(0, columns, tile):
-        at = slice(t, t + tile)
-        product = jnp.dot(attention[:, :split], upper[:, at], preferred_element_type=jnp.float32)
-        product += jnp.dot(attention[:, split:], lower[:, at], preferred_element_type=jnp.float32)
-        put(product, at)
+        at = slice(t, min(t + tile, columns))
+        put(jnp.dot(attention[...], weight[:, at], preferred_element_type=jnp.float32), at)
     for copy in copies:
         copy.wait()
     product = jnp.dot(attention[...], last[...], preferred_element_type=jnp.float32)
     put(product, slice(columns, columns + last.shape[1]))
 
 
-def project(parts, weights, out_weight, n_req, n_tp):
+def project(parts, weight, out_weight, n_req, n_tp):
     depth, columns = out_weight.shape
-    last = columns - weights[0].shape[1]
+    last = columns - weight.shape[1]
     vmem = pl.BlockSpec(memory_space=pltpu.VMEM)
     own = jax.ShapeDtypeStruct((n_req, columns), jnp.float32)
     sent = jax.ShapeDtypeStruct((n_req, columns), jnp.bfloat16)
@@ -405,7 +411,7 @@
     return pl.pallas_call(
         functools.partial(project_kernel, n_req, n_tp),
         out_shape=[own] + [sent] * (n_tp - 1),
-        in_specs=[vmem] * (n_req + 2) + [pl.BlockSpec(memory_space=pltpu.HBM)],
+        in_specs=[vmem] * (n_req + 1) + [pl.BlockSpec(memory_space=pltpu.HBM)],
         out_specs=[vmem] * n_tp,
         scratch_shapes=[
             pltpu.VMEM((rows, depth), jnp.bfloat16),
@@ -417,7 +423,7 @@
             flops=2 * rows * depth * columns, bytes_accessed=depth * columns * 2, transcendentals=0
         ),
         name="project",
-    )(*parts, *weights, in_hbm(out_weight))
+    )(*parts, weight, in_hbm(out_weight))
 
 
 def on_device(queries, new_kv, cache_pool, page_slot, page_owner, context_len, out_weight):
@@ -427,15 +433,13 @@
     q_list = [swap(queries, "req", d) for d in far_first(n_req)]
     own = own_attention(queries, new_kv, page_slot, page_owner, context_len, pool, n_req)
     pieces = other_attention(q_list, own, n_req, n_tp)
-    depth, columns = out_weight.shape
-    early = depth // 4
-    columns -= min(512, columns // 2)
+    columns = out_weight.shape[1]
+    columns -= min(768, columns // 2)
     swapped = [swap(pieces[d], "tp", d) for d in far_first(n_tp)]
-    first, mine = load_weight(pieces[0], out_weight, 0, early, columns)
-    arrived = jnp.concatenate([mine] + swapped, axis=0)
+    arrived = jnp.concatenate([pieces[0]] + swapped, axis=0)
     parts = [swap(arrived, "req", d) for d in reversed(near_last(n_req))]
-    second, mine = load_weight(arrived, out_weight, early, depth - early, columns)
-    sums = project([mine] + parts, (first, second), out_weight, n_req, n_tp)
+    weight, mine = load_weight(arrived, out_weight, columns)
+    sums = project([mine] + parts, weight, out_weight, n_req, n_tp)
     total = sums[0]
     for d in far_first(n_tp):
         total = total + swap(sums[d], "tp", d).astype(jnp.float32)

time: 32.1 us -> 33.4 us (1.040)
  waiting for transfers between devices: 5.98 us -> 7.12 us
    pallas_call x1, Pallas kernels: 2.61 us -> 4.14 us  [project(): pl.pallas_call(functools.partial(project_kernel, n_req, n_tp), out_shape=...]
    pallas_call x2 -> x1, Pallas kernels: 6.29 us -> 4.98 us  [load_weight(): pl.pallas_call(load_kernel, out_shape=[jax.ShapeDtypeStruct((depth, colum...]
    ppermute x12, waiting for transfers between devices: 5.98 us -> 7.12 us  [swap(): return lax.ppermute(x, axis, [(i, i ^ offset) for i in range(count)])]
  transfers between devices with their start and end apart: 12 -> 12, of which waited for: 5 -> 6; matrix products, arithmetic and copies ran while one was open for 0% -> 0% of each run, Pallas kernels for 27% -> 22%
where the time goes in v11:
time: 33.4 us; the launch traced here: 33.3 us
  starting transfers between devices  13 us (39%)
  Pallas kernels  12.3 us (37%)
  waiting for transfers between devices  7.12 us (21%)
  other arithmetic  0.7 us (2%)
    ppermute x12, starting transfers between devices, swap(): return lax.ppermute(x, axis, [(i, i ^ offset) for i in range(count)])  13 us
    ppermute x12, waiting for transfers between devices, swap(): return lax.ppermute(x, axis, [(i, i ^ offset) for i in range(count)])  7.12 us
    pallas_call x1, Pallas kernels, load_weight(): pl.pallas_call(load_kernel, out_shape=[jax.ShapeDtypeStruct((depth, colum...  4.98 us
    pallas_call x1, Pallas kernels, project(): pl.pallas_call(functools.partial(project_kernel, n_req, n_tp), out_shape=...  4.14 us
    pallas_call x1, Pallas kernels, own_attention(): pl.pallas_call(functools.partial(own_kernel, n_req, own_pages), out_shape...  2.39 us
    pallas_call x1, Pallas kernels, other_attention(): pl.pallas_call(functools.partial(other_kernel, n_req, n_tp), out_shape=[j...  0.84 us
  transfers between devices with their start and end apart: 12, of which 6 were waited for; matrix products, arithmetic and copies ran while one was open for 0% of the time, Pallas kernels for 22%

profile of v11, /device:TPU:0, one launch (start us, length us, event | category | flops | bytes accessed | tf_op | source)
XLA Modules:
  0.0 33.3 jit_solution(18296813866305489178)
XLA Ops:
  0.0 4.0 %collective-permute-start.1 = (bf16[1,8192]{1,0:T(2,128)(2,1)}, bf16[1,8192]{1,0:T(2,128)(2,1)S(1)}, u32[]{:S(2)}, u32[]{:S(2)}) collective-permute-start(bf16[1,8192]{1,0:T(2,128)(2,1)} %refs_0_.1), channel_id=1, source_target_pairs={{0,2},{1,3},{2,0},{3,1},{4,6},{5,7},{6,4},{7,5},{8,10},{9,11},{10,... | collective-permute-start | bytes 49160 | tf_op jit(solution)/shard_map/ppermute | solution.py:17
  4.0 1.3 %collective-permute-start = (bf16[1,8192]{1,0:T(2,128)(2,1)}, bf16[1,8192]{1,0:T(2,128)(2,1)S(1)}, u32[]{:S(2)}, u32[]{:S(2)}) collective-permute-start(bf16[1,8192]{1,0:T(2,128)(2,1)} %refs_0_.1), channel_id=1, source_target_pairs={{0,3},{1,2},{2,1},{3,0},{4,7},{5,6},{6,5},{7,4},{8,11},{9,10},{10,... | collective-permute-start | bytes 49160 | tf_op jit(solution)/shard_map/ppermute | solution.py:17
  5.4 0.2 collective-permute-start.2
  5.6 2.4 %own_attention.1 = (f32[64,128]{1,0:T(8,128)S(1)}, f32[8,128]{1,0:T(8,128)S(1)}, s32[8,128]{1,0:T(8,128)S(1)}, bf16[3,4,128,256]{3,2,1,0:T(8,128)(2,1)S(1)}) custom-call(bf16[1,8192]{1,0:T(2,128)(2,1)} %refs_0_.1, bf16[1,1024]{1,0:T(2,128)(2,1)} %refs_1_.1, s32[1,4,7]{2,1,0:T(4,128)} %refs_2_.1, s32[1,4,7]{2,1,0:T(4,128)} %refs_3_.1, s32[1,4]{1,0:T(1,128)} %refs_4_.1, ...), custom_call_target="tpu_custom_call" | custom-call | flops 25165824 | bytes 4718592 | tf_op jit(solution)/shard_map/own_attention/pallas_call | solution.py:210
  8.0 0.0 collective-permute-done.1.refs_1_
  8.0 1.9 %collective-permute-done.refs_0_ = bf16[1,8192]{1,0:T(2,128)(2,1)S(1)} collective-permute-done((bf16[1,8192]{1,0:T(2,128)(2,1)}, bf16[1,8192]{1,0:T(2,128)(2,1)S(1)}, u32[]{:S(2)}, u32[]{:S(2)}) %collective-permute-start) | collective-permute-done | bytes 16416 | tf_op jit(solution)/shard_map/ppermute | solution.py:17
  10.0 0.0 collective-permute-done.2.refs_2_
  10.0 0.8 %other_attention.1 = (bf16[4,2176]{1,0:T(4,128)(2,1)S(1)}, bf16[4,2176]{1,0:T(4,128)(2,1)S(1)}, bf16[4,2176]{1,0:T(4,128)(2,1)S(1)}, bf16[4,2176]{1,0:T(4,128)(2,1)S(1)}) custom-call(bf16[1,8192]{1,0:T(2,128)(2,1)S(1)} %collective-permute-done.refs_0_, bf16[1,8192]{1,0:T(2,128)(2,1)S(1)} %collective-permute-done.1.refs_1_, ...), custom_call_target="tpu_custom_call" | custom-call | flops 12582912 | bytes 786432 | tf_op jit(solution)/shard_map/other_attention/pallas_call | solution.py:311
  10.8 0.1 collective-permute-start.3
  10.9 1.6 %collective-permute-start.4 = (bf16[4,2176]{1,0:T(4,128)(2,1)S(1)}, bf16[4,2176]{1,0:T(4,128)(2,1)S(1)}, u32[]{:S(2)}, u32[]{:S(2)}) collective-permute-start(bf16[4,2176]{1,0:T(4,128)(2,1)S(1)} %get-tuple-element.25), channel_id=1, source_target_pairs={{0,8},{4,12},{8,0},{12,4},{1,9},{5,13},{9,1},{13,5},{2,10},{6,14},... | collective-permute-start | bytes 52232 | tf_op jit(solution)/shard_map/ppermute | solution.py:17
  12.4 0.3 collective-permute-start.5
  12.7 1.5 %collective-permute-done.3 = bf16[4,2176]{1,0:T(4,128)(2,1)S(1)} collective-permute-done((bf16[4,2176]{1,0:T(4,128)(2,1)S(1)}, bf16[4,2176]{1,0:T(4,128)(2,1)S(1)}, u32[]{:S(2)}, u32[]{:S(2)}) %collective-permute-start.3) | collective-permute-done | bytes 17440 | tf_op jit(solution)/shard_map/ppermute | solution.py:17
  14.2 0.5 %collective-permute-done.4 = bf16[4,2176]{1,0:T(4,128)(2,1)S(1)} collective-permute-done((bf16[4,2176]{1,0:T(4,128)(2,1)S(1)}, bf16[4,2176]{1,0:T(4,128)(2,1)S(1)}, u32[]{:S(2)}, u32[]{:S(2)}) %collective-permute-start.4) | collective-permute-done | bytes 17440 | tf_op jit(solution)/shard_map/ppermute | solution.py:17
  14.7 0.0 collective-permute-done.5
  14.8 1.3 %collective-permute-start.8 = (bf16[16,2176]{1,0:T(8,128)(2,1)S(1)}, bf16[16,2176]{1,0:T(8,128)(2,1)S(1)}, u32[]{:S(2)}, u32[]{:S(2)}) collective-permute-start(bf16[16,2176]{1,0:T(8,128)(2,1)S(1)} %pad_maximum_fusion.piece_ref), channel_id=1, source_target_pairs={{0,2},{1,3},{2,0},{3,1},{4,6},{5,7},{6,4},{7,5},{8,10},{9,11},{10,... | collective-permute-start | bytes 208904 | tf_op jit(solution)/shard_map/ppermute | solution.py:17
  16.1 1.0 %collective-permute-start.7 = (bf16[16,2176]{1,0:T(8,128)(2,1)S(1)}, bf16[16,2176]{1,0:T(8,128)(2,1)S(1)}, u32[]{:S(2)}, u32[]{:S(2)}) collective-permute-start(bf16[16,2176]{1,0:T(8,128)(2,1)S(1)} %pad_maximum_fusion.piece_ref), channel_id=1, source_target_pairs={{0,3},{1,2},{2,1},{3,0},{4,7},{5,6},{6,5},{7,4},{8,11},{9,10},{10,... | collective-permute-start | bytes 208904 | tf_op jit(solution)/shard_map/ppermute | solution.py:17
  17.1 1.2 %collective-permute-start.6 = (bf16[16,2176]{1,0:T(8,128)(2,1)S(1)}, bf16[16,2176]{1,0:T(8,128)(2,1)S(1)}, u32[]{:S(2)}, u32[]{:S(2)}) collective-permute-start(bf16[16,2176]{1,0:T(8,128)(2,1)S(1)} %pad_maximum_fusion.piece_ref), channel_id=1, source_target_pairs={{0,1},{1,0},{2,3},{3,2},{4,5},{5,4},{6,7},{7,6},{8,9},{9,8},{10,11... | collective-permute-start | bytes 208904 | tf_op jit(solution)/shard_map/ppermute | solution.py:17
  18.3 5.0 %load_weight.1 = (bf16[2048,3328]{1,0:T(8,128)(2,1)S(1)}, bf16[16,2176]{1,0:T(8,128)(2,1)S(1)}) custom-call(bf16[16,2176]{1,0:T(8,128)(2,1)S(1)} %pad_maximum_fusion.piece_ref, bf16[2048,4096]{1,0:T(8,128)(2,1)} %refs_5_.1), custom_call_target="tpu_custom_call" | custom-call | bytes 27262976 | tf_op jit(solution)/shard_map/load_weight/pallas_call | solution.py:351
  23.3 0.0 collective-permute-done.8.refs_3_
  23.3 0.0 collective-permute-done.7.refs_2_
  23.3 0.7 %collective-permute-done.6.refs_1_ = bf16[16,2176]{1,0:T(8,128)(2,1)S(1)} collective-permute-done((bf16[16,2176]{1,0:T(8,128)(2,1)S(1)}, bf16[16,2176]{1,0:T(8,128)(2,1)S(1)}, u32[]{:S(2)}, u32[]{:S(2)}) %collective-permute-start.6) | collective-permute-done | bytes 69664 | tf_op jit(solution)/shard_map/ppermute | solution.py:17
  24.0 4.1 %project.1 = (f32[4,4096]{1,0:T(4,128)S(1)}, bf16[4,4096]{1,0:T(4,128)(2,1)S(1)}, bf16[4,4096]{1,0:T(4,128)(2,1)S(1)}, bf16[4,4096]{1,0:T(4,128)(2,1)S(1)}) custom-call(bf16[16,2176]{1,0:T(8,128)(2,1)S(1)} %get-tuple-element.27.refs_0_, bf16[16,2176]{1,0:T(8,128)(2,1)S(1)} %collective-permute-done.6.refs_1_, ...), custom_call_target="tpu_custom_call" | custom-call | flops 268435456 | bytes 16777216 | tf_op jit(solution)/shard_map/project/pallas_call | solution.py:411
  28.1 0.1 collective-permute-start.9
  28.2 1.6 %collective-permute-start.10 = (bf16[4,4096]{1,0:T(4,128)(2,1)S(1)}, bf16[4,4096]{1,0:T(4,128)(2,1)S(1)}, u32[]{:S(2)}, u32[]{:S(2)}) collective-permute-start(bf16[4,4096]{1,0:T(4,128)(2,1)S(1)} %get-tuple-element.31), channel_id=1, source_target_pairs={{0,8},{4,12},{8,0},{12,4},{1,9},{5,13},{9,1},{13,5},{2,10},{6,14},... | collective-permute-start | bytes 98312 | tf_op jit(solution)/shard_map/ppermute | solution.py:17
  29.8 0.3 collective-permute-start.11
  30.1 1.7 %collective-permute-done.9 = bf16[4,4096]{1,0:T(4,128)(2,1)S(1)} collective-permute-done((bf16[4,4096]{1,0:T(4,128)(2,1)S(1)}, bf16[4,4096]{1,0:T(4,128)(2,1)S(1)}, u32[]{:S(2)}, u32[]{:S(2)}) %collective-permute-start.9) | collective-permute-done | bytes 32800 | tf_op jit(solution)/shard_map/ppermute | solution.py:17
  31.8 0.9 %collective-permute-done.10 = bf16[4,4096]{1,0:T(4,128)(2,1)S(1)} collective-permute-done((bf16[4,4096]{1,0:T(4,128)(2,1)S(1)}, bf16[4,4096]{1,0:T(4,128)(2,1)S(1)}, u32[]{:S(2)}, u32[]{:S(2)}) %collective-permute-start.10) | collective-permute-done | bytes 32800 | tf_op jit(solution)/shard_map/ppermute | solution.py:17
  32.6 0.0 collective-permute-done.11
  32.6 0.7 %add_convert_fusion = bf16[4,4096]{1,0:T(4,128)(2,1)} fusion(bf16[4,4096]{1,0:T(4,128)(2,1)S(1)} %collective-permute-done.11, bf16[4,4096]{1,0:T(4,128)(2,1)S(1)} %collective-permute-done.10, f32[4,4096]{1,0:T(4,128)S(1)} %get-tuple-element.29, bf16[4,4096]{1,0:T(4,128)(2,1)S(1)} %collective-permute-done.9), kind=kLoop, calls=%fused_computation.1 | loop fusion | flops 114688 | bytes 196608 | tf_op jit(solution)/shard_map/convert_element_type | solution.py:446
  (1 shorter events, 0.0 us)
Async XLA Ops:
  0.0 8.0 %collective-permute-start.1 = (bf16[1,8192]{1,0:T(2,128)(2,1)}, bf16[1,8192]{1,0:T(2,128)(2,1)S(1)}, u32[]{:S(2)}, u32[]{:S(2)}) collective-permute-start(bf16[1,8192]{1,0:T(2,128)(2,1)} %refs_0_.1), channel_id=1, source_target_pairs={{0,2},{1,3},{2,0},{3,1},{4,6},{5,7},{6,4},{7,5},{8,10},{9,11},{10,... | collective-permute-start | bytes 49160 | tf_op jit(solution)/shard_map/ppermute | solution.py:17
  4.0 5.9 %collective-permute-start = (bf16[1,8192]{1,0:T(2,128)(2,1)}, bf16[1,8192]{1,0:T(2,128)(2,1)S(1)}, u32[]{:S(2)}, u32[]{:S(2)}) collective-permute-start(bf16[1,8192]{1,0:T(2,128)(2,1)} %refs_0_.1), channel_id=1, source_target_pairs={{0,3},{1,2},{2,1},{3,0},{4,7},{5,6},{6,5},{7,4},{8,11},{9,10},{10,... | collective-permute-start | bytes 49160 | tf_op jit(solution)/shard_map/ppermute | solution.py:17
  5.4 4.6 %collective-permute-start.2 = (bf16[1,8192]{1,0:T(2,128)(2,1)}, bf16[1,8192]{1,0:T(2,128)(2,1)S(1)}, u32[]{:S(2)}, u32[]{:S(2)}) collective-permute-start(bf16[1,8192]{1,0:T(2,128)(2,1)} %refs_0_.1), channel_id=1, source_target_pairs={{0,1},{1,0},{2,3},{3,2},{4,5},{5,4},{6,7},{7,6},{8,9},{9,8},{10,11... | collective-permute-start | bytes 49160 | tf_op jit(solution)/shard_map/ppermute | solution.py:17
  10.8 3.4 %collective-permute-start.3 = (bf16[4,2176]{1,0:T(4,128)(2,1)S(1)}, bf16[4,2176]{1,0:T(4,128)(2,1)S(1)}, u32[]{:S(2)}, u32[]{:S(2)}) collective-permute-start(bf16[4,2176]{1,0:T(4,128)(2,1)S(1)} %get-tuple-element.24), channel_id=1, source_target_pairs={{0,12},{4,8},{8,4},{12,0},{1,13},{5,9},{9,5},{13,1},{2,14},{6,10},... | collective-permute-start | bytes 52232 | tf_op jit(solution)/shard_map/ppermute | solution.py:17
  10.9 3.8 %collective-permute-start.4 = (bf16[4,2176]{1,0:T(4,128)(2,1)S(1)}, bf16[4,2176]{1,0:T(4,128)(2,1)S(1)}, u32[]{:S(2)}, u32[]{:S(2)}) collective-permute-start(bf16[4,2176]{1,0:T(4,128)(2,1)S(1)} %get-tuple-element.25), channel_id=1, source_target_pairs={{0,8},{4,12},{8,0},{12,4},{1,9},{5,13},{9,1},{13,5},{2,10},{6,14},... | collective-permute-start | bytes 52232 | tf_op jit(solution)/shard_map/ppermute | solution.py:17
  12.4 2.3 %collective-permute-start.5 = (bf16[4,2176]{1,0:T(4,128)(2,1)S(1)}, bf16[4,2176]{1,0:T(4,128)(2,1)S(1)}, u32[]{:S(2)}, u32[]{:S(2)}) collective-permute-start(bf16[4,2176]{1,0:T(4,128)(2,1)S(1)} %get-tuple-element.26), channel_id=1, source_target_pairs={{0,4},{4,0},{8,12},{12,8},{1,5},{5,1},{9,13},{13,9},{2,6},{6,2},{1... | collective-permute-start | bytes 52232 | tf_op jit(solution)/shard_map/ppermute | solution.py:17
  14.8 8.6 %collective-permute-start.8 = (bf16[16,2176]{1,0:T(8,128)(2,1)S(1)}, bf16[16,2176]{1,0:T(8,128)(2,1)S(1)}, u32[]{:S(2)}, u32[]{:S(2)}) collective-permute-start(bf16[16,2176]{1,0:T(8,128)(2,1)S(1)} %pad_maximum_fusion.piece_ref), channel_id=1, source_target_pairs={{0,2},{1,3},{2,0},{3,1},{4,6},{5,7},{6,4},{7,5},{8,10},{9,11},{10,... | collective-permute-start | bytes 208904 | tf_op jit(solution)/shard_map/ppermute | solution.py:17
  16.1 7.2 %collective-permute-start.7 = (bf16[16,2176]{1,0:T(8,128)(2,1)S(1)}, bf16[16,2176]{1,0:T(8,128)(2,1)S(1)}, u32[]{:S(2)}, u32[]{:S(2)}) collective-permute-start(bf16[16,2176]{1,0:T(8,128)(2,1)S(1)} %pad_maximum_fusion.piece_ref), channel_id=1, source_target_pairs={{0,3},{1,2},{2,1},{3,0},{4,7},{5,6},{6,5},{7,4},{8,11},{9,10},{10,... | collective-permute-start | bytes 208904 | tf_op jit(solution)/shard_map/ppermute | solution.py:17
  17.1 6.9 %collective-permute-start.6 = (bf16[16,2176]{1,0:T(8,128)(2,1)S(1)}, bf16[16,2176]{1,0:T(8,128)(2,1)S(1)}, u32[]{:S(2)}, u32[]{:S(2)}) collective-permute-start(bf16[16,2176]{1,0:T(8,128)(2,1)S(1)} %pad_maximum_fusion.piece_ref), channel_id=1, source_target_pairs={{0,1},{1,0},{2,3},{3,2},{4,5},{5,4},{6,7},{7,6},{8,9},{9,8},{10,11... | collective-permute-start | bytes 208904 | tf_op jit(solution)/shard_map/ppermute | solution.py:17
  28.1 3.6 %collective-permute-start.9 = (bf16[4,4096]{1,0:T(4,128)(2,1)S(1)}, bf16[4,4096]{1,0:T(4,128)(2,1)S(1)}, u32[]{:S(2)}, u32[]{:S(2)}) collective-permute-start(bf16[4,4096]{1,0:T(4,128)(2,1)S(1)} %get-tuple-element.30), channel_id=1, source_target_pairs={{0,12},{4,8},{8,4},{12,0},{1,13},{5,9},{9,5},{13,1},{2,14},{6,10},... | collective-permute-start | bytes 98312 | tf_op jit(solution)/shard_map/ppermute | solution.py:17
  28.2 4.4 %collective-permute-start.10 = (bf16[4,4096]{1,0:T(4,128)(2,1)S(1)}, bf16[4,4096]{1,0:T(4,128)(2,1)S(1)}, u32[]{:S(2)}, u32[]{:S(2)}) collective-permute-start(bf16[4,4096]{1,0:T(4,128)(2,1)S(1)} %get-tuple-element.31), channel_id=1, source_target_pairs={{0,8},{4,12},{8,0},{12,4},{1,9},{5,13},{9,1},{13,5},{2,10},{6,14},... | collective-permute-start | bytes 98312 | tf_op jit(solution)/shard_map/ppermute | solution.py:17
  29.8 2.8 %collective-permute-start.11 = (bf16[4,4096]{1,0:T(4,128)(2,1)S(1)}, bf16[4,4096]{1,0:T(4,128)(2,1)S(1)}, u32[]{:S(2)}, u32[]{:S(2)}) collective-permute-start(bf16[4,4096]{1,0:T(4,128)(2,1)S(1)} %get-tuple-element.32), channel_id=1, source_target_pairs={{0,4},{4,0},{8,12},{12,8},{1,5},{5,1},{9,13},{13,9},{2,6},{6,2},{1... | collective-permute-start | bytes 98312 | tf_op jit(solution)/shard_map/ppermute | solution.py:17

commit v12 on v10

--- a/solution.py
+++ b/solution.py
@@ -15,10 +15,6 @@
 def swap(x, axis, offset):
     count = lax.axis_size(axis)
     return lax.ppermute(x, axis, [(i, i ^ offset) for i in range(count)])
-
-
-def near_last(count):
-    return list(range(2, count)) + [1]
 
 
 def far_first(count):
@@ -348,7 +344,7 @@
         ],
         in_specs=[vmem, pl.BlockSpec(memory_space=pltpu.HBM)],
         out_specs=[vmem] * 2,
-        scratch_shapes=[pltpu.SemaphoreType.DMA((4,))],
+        scratch_shapes=[pltpu.SemaphoreType.DMA((8,))],
         compiler_params=pltpu.CompilerParams(vmem_limit_bytes=20 * MIB),
         cost_estimate=pl.CostEstimate(flops=0, bytes_accessed=rows * columns * 4, transcendentals=0),
         name="load_weight",
@@ -410,7 +406,7 @@
         scratch_shapes=[
             pltpu.VMEM((rows, depth), jnp.bfloat16),
             pltpu.VMEM((depth, last), jnp.bfloat16),
-            pltpu.SemaphoreType.DMA((2,)),
+            pltpu.SemaphoreType.DMA((8,)),
         ],
         compiler_params=pltpu.CompilerParams(vmem_limit_bytes=16 * MIB),
         cost_estimate=pl.CostEstimate(
@@ -433,7 +429,7 @@
     swapped = [swap(pieces[d], "tp", d) for d in far_first(n_tp)]
     first, mine = load_weight(pieces[0], out_weight, 0, early, columns)
     arrived = jnp.concatenate([mine] + swapped, axis=0)
-    parts = [swap(arrived, "req", d) for d in reversed(near_last(n_req))]
+    parts = [swap(arrived, "req", d) for d in range(1, n_req)]
     second, mine = load_weight(arrived, out_weight, early, depth - early, columns)
     sums = project([mine] + parts, (first, second), out_weight, n_req, n_tp)
     total = sums[0]

time: 32.1 us -> 33.6 us (1.047)
  Pallas kernels: 12.1 us -> 13.4 us
  starting transfers between devices: 13 us -> 13.9 us
  waiting for transfers between devices: 5.98 us -> 5.36 us
    pallas_call x1, Pallas kernels: 2.61 us -> 3.87 us  [project(): pl.pallas_call(functools.partial(project_kernel, n_req, n_tp), out_shape=...]
    ppermute x12, starting transfers between devices: 13 us -> 13.9 us  [swap(): return lax.ppermute(x, axis, [(i, i ^ offset) for i in range(count)])]
    ppermute x12, waiting for transfers between devices: 5.98 us -> 5.36 us  [swap(): return lax.ppermute(x, axis, [(i, i ^ offset) for i in range(count)])]
  transfers between devices with their start and end apart: 12 -> 12, of which waited for: 5 -> 4; matrix products, arithmetic and copies ran while one was open for 0% -> 0% of each run, Pallas kernels for 27% -> 26%
where the time goes in v12:
time: 33.6 us; the launch traced here: 33.5 us
  starting transfers between devices  13.9 us (41%)
  Pallas kernels  13.4 us (40%)
  waiting for transfers between devices  5.36 us (16%)
  other arithmetic  0.7 us (2%)
    ppermute x12, starting transfers between devices, swap(): return lax.ppermute(x, axis, [(i, i ^ offset) for i in range(count)])  13.9 us
    pallas_call x2, Pallas kernels, load_weight(): pl.pallas_call(functools.partial(load_kernel, first), out_shape=[jax.Shap...  6.29 us
    ppermute x12, waiting for transfers between devices, swap(): return lax.ppermute(x, axis, [(i, i ^ offset) for i in range(count)])  5.36 us
    pallas_call x1, Pallas kernels, project(): pl.pallas_call(functools.partial(project_kernel, n_req, n_tp), out_shape=...  3.87 us
    pallas_call x1, Pallas kernels, own_attention(): pl.pallas_call(functools.partial(own_kernel, n_req, own_pages), out_shape...  2.39 us
    pallas_call x1, Pallas kernels, other_attention(): pl.pallas_call(functools.partial(other_kernel, n_req, n_tp), out_shape=[j...  0.84 us
  transfers between devices with their start and end apart: 12, of which 4 were waited for; matrix products, arithmetic and copies ran while one was open for 0% of the time, Pallas kernels for 26%

profile of v12, /device:TPU:0, one launch (start us, length us, event | category | flops | bytes accessed | tf_op | source)
XLA Modules:
  0.0 33.5 jit_solution(3106110683403048193)
XLA Ops:
  0.0 4.0 %collective-permute-start.1 = (bf16[1,8192]{1,0:T(2,128)(2,1)}, bf16[1,8192]{1,0:T(2,128)(2,1)S(1)}, u32[]{:S(2)}, u32[]{:S(2)}) collective-permute-start(bf16[1,8192]{1,0:T(2,128)(2,1)} %refs_0_.1), channel_id=1, source_target_pairs={{0,2},{1,3},{2,0},{3,1},{4,6},{5,7},{6,4},{7,5},{8,10},{9,11},{10,... | collective-permute-start | bytes 49160 | tf_op jit(solution)/shard_map/ppermute | solution.py:17
  4.0 1.3 %collective-permute-start = (bf16[1,8192]{1,0:T(2,128)(2,1)}, bf16[1,8192]{1,0:T(2,128)(2,1)S(1)}, u32[]{:S(2)}, u32[]{:S(2)}) collective-permute-start(bf16[1,8192]{1,0:T(2,128)(2,1)} %refs_0_.1), channel_id=1, source_target_pairs={{0,3},{1,2},{2,1},{3,0},{4,7},{5,6},{6,5},{7,4},{8,11},{9,10},{10,... | collective-permute-start | bytes 49160 | tf_op jit(solution)/shard_map/ppermute | solution.py:17
  5.4 0.2 collective-permute-start.2
  5.6 2.4 %own_attention.1 = (f32[64,128]{1,0:T(8,128)S(1)}, f32[8,128]{1,0:T(8,128)S(1)}, s32[8,128]{1,0:T(8,128)S(1)}, bf16[3,4,128,256]{3,2,1,0:T(8,128)(2,1)S(1)}) custom-call(bf16[1,8192]{1,0:T(2,128)(2,1)} %refs_0_.1, bf16[1,1024]{1,0:T(2,128)(2,1)} %refs_1_.1, s32[1,4,7]{2,1,0:T(4,128)} %refs_2_.1, s32[1,4,7]{2,1,0:T(4,128)} %refs_3_.1, s32[1,4]{1,0:T(1,128)} %refs_4_.1, ...), custom_call_target="tpu_custom_call" | custom-call | flops 25165824 | bytes 4718592 | tf_op jit(solution)/shard_map/own_attention/pallas_call | solution.py:201
  8.0 0.0 collective-permute-done.1.refs_1_
  8.0 1.9 %collective-permute-done.refs_0_ = bf16[1,8192]{1,0:T(2,128)(2,1)S(1)} collective-permute-done((bf16[1,8192]{1,0:T(2,128)(2,1)}, bf16[1,8192]{1,0:T(2,128)(2,1)S(1)}, u32[]{:S(2)}, u32[]{:S(2)}) %collective-permute-start) | collective-permute-done | bytes 16416 | tf_op jit(solution)/shard_map/ppermute | solution.py:17
  10.0 0.0 collective-permute-done.2.refs_2_
  10.0 0.8 %other_attention.1 = (bf16[4,2176]{1,0:T(4,128)(2,1)S(1)}, bf16[4,2176]{1,0:T(4,128)(2,1)S(1)}, bf16[4,2176]{1,0:T(4,128)(2,1)S(1)}, bf16[4,2176]{1,0:T(4,128)(2,1)S(1)}) custom-call(bf16[1,8192]{1,0:T(2,128)(2,1)S(1)} %collective-permute-done.refs_0_, bf16[1,8192]{1,0:T(2,128)(2,1)S(1)} %collective-permute-done.1.refs_1_, ...), custom_call_target="tpu_custom_call" | custom-call | flops 12582912 | bytes 786432 | tf_op jit(solution)/shard_map/other_attention/pallas_call | solution.py:300
  10.8 0.1 collective-permute-start.3
  10.9 1.6 %collective-permute-start.4 = (bf16[4,2176]{1,0:T(4,128)(2,1)S(1)}, bf16[4,2176]{1,0:T(4,128)(2,1)S(1)}, u32[]{:S(2)}, u32[]{:S(2)}) collective-permute-start(bf16[4,2176]{1,0:T(4,128)(2,1)S(1)} %get-tuple-element.28), channel_id=1, source_target_pairs={{0,8},{4,12},{8,0},{12,4},{1,9},{5,13},{9,1},{13,5},{2,10},{6,14},... | collective-permute-start | bytes 52232 | tf_op jit(solution)/shard_map/ppermute | solution.py:17
  12.5 0.3 collective-permute-start.5
  12.7 2.1 %load_weight.2 = (bf16[512,3584]{1,0:T(8,128)(2,1)S(1)}, bf16[4,2176]{1,0:T(4,128)(2,1)S(1)}) custom-call(bf16[4,2176]{1,0:T(4,128)(2,1)S(1)} %get-tuple-element.25.piece_ref, bf16[2048,4096]{1,0:T(8,128)(2,1)} %refs_6_.1), custom_call_target="tpu_custom_call" | custom-call | bytes 7340032 | tf_op jit(solution)/shard_map/load_weight/pallas_call | solution.py:339
  14.8 0.0 collective-permute-done.3
  14.8 0.0 collective-permute-done.4
  14.8 0.0 collective-permute-done.5
  14.9 2.1 %collective-permute-start.8 = (bf16[16,2176]{1,0:T(8,128)(2,1)S(1)}, bf16[16,2176]{1,0:T(8,128)(2,1)S(1)}, u32[]{:S(2)}, u32[]{:S(2)}) collective-permute-start(bf16[16,2176]{1,0:T(8,128)(2,1)S(1)} %pad_maximum_fusion.piece_ref), channel_id=1, source_target_pairs={{0,3},{1,2},{2,1},{3,0},{4,7},{5,6},{6,5},{7,4},{8,11},{9,10},{10,... | collective-permute-start | bytes 208904 | tf_op jit(solution)/shard_map/ppermute | solution.py:17
  17.0 0.0 collective-permute-start.7
  17.0 2.4 %collective-permute-start.6 = (bf16[16,2176]{1,0:T(8,128)(2,1)S(1)}, bf16[16,2176]{1,0:T(8,128)(2,1)S(1)}, u32[]{:S(2)}, u32[]{:S(2)}) collective-permute-start(bf16[16,2176]{1,0:T(8,128)(2,1)S(1)} %pad_maximum_fusion.piece_ref), channel_id=1, source_target_pairs={{0,1},{1,0},{2,3},{3,2},{4,5},{5,4},{6,7},{7,6},{8,9},{9,8},{10,11... | collective-permute-start | bytes 208904 | tf_op jit(solution)/shard_map/ppermute | solution.py:17
  19.3 4.2 %load_weight.3 = (bf16[1536,3584]{1,0:T(8,128)(2,1)S(1)}, bf16[16,2176]{1,0:T(8,128)(2,1)S(1)}) custom-call(bf16[16,2176]{1,0:T(8,128)(2,1)S(1)} %pad_maximum_fusion.piece_ref, bf16[2048,4096]{1,0:T(8,128)(2,1)} %refs_6_.1), custom_call_target="tpu_custom_call" | custom-call | bytes 22020096 | tf_op jit(solution)/shard_map/load_weight/pallas_call | solution.py:339
  23.6 0.0 collective-permute-done.8.refs_3_
  23.6 0.5 %collective-permute-done.7.refs_2_ = bf16[16,2176]{1,0:T(8,128)(2,1)S(1)} collective-permute-done((bf16[16,2176]{1,0:T(8,128)(2,1)S(1)}, bf16[16,2176]{1,0:T(8,128)(2,1)S(1)}, u32[]{:S(2)}, u32[]{:S(2)}) %collective-permute-start.7) | collective-permute-done | bytes 69664 | tf_op jit(solution)/shard_map/ppermute | solution.py:17
  24.1 0.0 collective-permute-done.6.refs_1_
  24.1 3.9 %project.1 = (f32[4,4096]{1,0:T(4,128)S(1)}, bf16[4,4096]{1,0:T(4,128)(2,1)S(1)}, bf16[4,4096]{1,0:T(4,128)(2,1)S(1)}, bf16[4,4096]{1,0:T(4,128)(2,1)S(1)}) custom-call(bf16[16,2176]{1,0:T(8,128)(2,1)S(1)} %get-tuple-element.30.refs_0_, bf16[16,2176]{1,0:T(8,128)(2,1)S(1)} %collective-permute-done.6.refs_1_, ...), custom_call_target="tpu_custom_call" | custom-call | flops 268435456 | bytes 16777216 | tf_op jit(solution)/shard_map/project/pallas_call | solution.py:401
  28.0 0.9 %collective-permute-start.9 = (bf16[4,4096]{1,0:T(4,128)(2,1)S(1)}, bf16[4,4096]{1,0:T(4,128)(2,1)S(1)}, u32[]{:S(2)}, u32[]{:S(2)}) collective-permute-start(bf16[4,4096]{1,0:T(4,128)(2,1)S(1)} %get-tuple-element.34), channel_id=1, source_target_pairs={{0,12},{4,8},{8,4},{12,0},{1,13},{5,9},{9,5},{13,1},{2,14},{6,10},... | collective-permute-start | bytes 98312 | tf_op jit(solution)/shard_map/ppermute | solution.py:17
  28.9 0.8 %collective-permute-start.10 = (bf16[4,4096]{1,0:T(4,128)(2,1)S(1)}, bf16[4,4096]{1,0:T(4,128)(2,1)S(1)}, u32[]{:S(2)}, u32[]{:S(2)}) collective-permute-start(bf16[4,4096]{1,0:T(4,128)(2,1)S(1)} %get-tuple-element.35), channel_id=1, source_target_pairs={{0,8},{4,12},{8,0},{12,4},{1,9},{5,13},{9,1},{13,5},{2,10},{6,14},... | collective-permute-start | bytes 98312 | tf_op jit(solution)/shard_map/ppermute | solution.py:17
  29.7 0.2 collective-permute-start.11
  29.9 1.6 %collective-permute-done.9 = bf16[4,4096]{1,0:T(4,128)(2,1)S(1)} collective-permute-done((bf16[4,4096]{1,0:T(4,128)(2,1)S(1)}, bf16[4,4096]{1,0:T(4,128)(2,1)S(1)}, u32[]{:S(2)}, u32[]{:S(2)}) %collective-permute-start.9) | collective-permute-done | bytes 32800 | tf_op jit(solution)/shard_map/ppermute | solution.py:17
  31.5 1.3 %collective-permute-done.10 = bf16[4,4096]{1,0:T(4,128)(2,1)S(1)} collective-permute-done((bf16[4,4096]{1,0:T(4,128)(2,1)S(1)}, bf16[4,4096]{1,0:T(4,128)(2,1)S(1)}, u32[]{:S(2)}, u32[]{:S(2)}) %collective-permute-start.10) | collective-permute-done | bytes 32800 | tf_op jit(solution)/shard_map/ppermute | solution.py:17
  32.8 0.0 collective-permute-done.11
  32.8 0.7 %add_convert_fusion = bf16[4,4096]{1,0:T(4,128)(2,1)} fusion(bf16[4,4096]{1,0:T(4,128)(2,1)S(1)} %collective-permute-done.11, bf16[4,4096]{1,0:T(4,128)(2,1)S(1)} %collective-permute-done.10, f32[4,4096]{1,0:T(4,128)S(1)} %get-tuple-element.33, bf16[4,4096]{1,0:T(4,128)(2,1)S(1)} %collective-permute-done.9), kind=kLoop, calls=%fused_computation.1 | loop fusion | flops 114688 | bytes 196608 | tf_op jit(solution)/shard_map/convert_element_type | solution.py:438
  (1 shorter events, 0.0 us)
Async XLA Ops:
  0.0 8.0 %collective-permute-start.1 = (bf16[1,8192]{1,0:T(2,128)(2,1)}, bf16[1,8192]{1,0:T(2,128)(2,1)S(1)}, u32[]{:S(2)}, u32[]{:S(2)}) collective-permute-start(bf16[1,8192]{1,0:T(2,128)(2,1)} %refs_0_.1), channel_id=1, source_target_pairs={{0,2},{1,3},{2,0},{3,1},{4,6},{5,7},{6,4},{7,5},{8,10},{9,11},{10,... | collective-permute-start | bytes 49160 | tf_op jit(solution)/shard_map/ppermute | solution.py:17
  4.0 5.9 %collective-permute-start = (bf16[1,8192]{1,0:T(2,128)(2,1)}, bf16[1,8192]{1,0:T(2,128)(2,1)S(1)}, u32[]{:S(2)}, u32[]{:S(2)}) collective-permute-start(bf16[1,8192]{1,0:T(2,128)(2,1)} %refs_0_.1), channel_id=1, source_target_pairs={{0,3},{1,2},{2,1},{3,0},{4,7},{5,6},{6,5},{7,4},{8,11},{9,10},{10,... | collective-permute-start | bytes 49160 | tf_op jit(solution)/shard_map/ppermute | solution.py:17
  5.4 4.6 %collective-permute-start.2 = (bf16[1,8192]{1,0:T(2,128)(2,1)}, bf16[1,8192]{1,0:T(2,128)(2,1)S(1)}, u32[]{:S(2)}, u32[]{:S(2)}) collective-permute-start(bf16[1,8192]{1,0:T(2,128)(2,1)} %refs_0_.1), channel_id=1, source_target_pairs={{0,1},{1,0},{2,3},{3,2},{4,5},{5,4},{6,7},{7,6},{8,9},{9,8},{10,11... | collective-permute-start | bytes 49160 | tf_op jit(solution)/shard_map/ppermute | solution.py:17
  10.8 4.0 %collective-permute-start.3 = (bf16[4,2176]{1,0:T(4,128)(2,1)S(1)}, bf16[4,2176]{1,0:T(4,128)(2,1)S(1)}, u32[]{:S(2)}, u32[]{:S(2)}) collective-permute-start(bf16[4,2176]{1,0:T(4,128)(2,1)S(1)} %get-tuple-element.27), channel_id=1, source_target_pairs={{0,12},{4,8},{8,4},{12,0},{1,13},{5,9},{9,5},{13,1},{2,14},{6,10},... | collective-permute-start | bytes 52232 | tf_op jit(solution)/shard_map/ppermute | solution.py:17
  10.9 3.9 %collective-permute-start.4 = (bf16[4,2176]{1,0:T(4,128)(2,1)S(1)}, bf16[4,2176]{1,0:T(4,128)(2,1)S(1)}, u32[]{:S(2)}, u32[]{:S(2)}) collective-permute-start(bf16[4,2176]{1,0:T(4,128)(2,1)S(1)} %get-tuple-element.28), channel_id=1, source_target_pairs={{0,8},{4,12},{8,0},{12,4},{1,9},{5,13},{9,1},{13,5},{2,10},{6,14},... | collective-permute-start | bytes 52232 | tf_op jit(solution)/shard_map/ppermute | solution.py:17
  12.5 2.4 %collective-permute-start.5 = (bf16[4,2176]{1,0:T(4,128)(2,1)S(1)}, bf16[4,2176]{1,0:T(4,128)(2,1)S(1)}, u32[]{:S(2)}, u32[]{:S(2)}) collective-permute-start(bf16[4,2176]{1,0:T(4,128)(2,1)S(1)} %get-tuple-element.29), channel_id=1, source_target_pairs={{0,4},{4,0},{8,12},{12,8},{1,5},{5,1},{9,13},{13,9},{2,6},{6,2},{1... | collective-permute-start | bytes 52232 | tf_op jit(solution)/shard_map/ppermute | solution.py:17
  14.9 8.7 %collective-permute-start.8 = (bf16[16,2176]{1,0:T(8,128)(2,1)S(1)}, bf16[16,2176]{1,0:T(8,128)(2,1)S(1)}, u32[]{:S(2)}, u32[]{:S(2)}) collective-permute-start(bf16[16,2176]{1,0:T(8,128)(2,1)S(1)} %pad_maximum_fusion.piece_ref), channel_id=1, source_target_pairs={{0,3},{1,2},{2,1},{3,0},{4,7},{5,6},{6,5},{7,4},{8,11},{9,10},{10,... | collective-permute-start | bytes 208904 | tf_op jit(solution)/shard_map/ppermute | solution.py:17
  17.0 7.1 %collective-permute-start.7 = (bf16[16,2176]{1,0:T(8,128)(2,1)S(1)}, bf16[16,2176]{1,0:T(8,128)(2,1)S(1)}, u32[]{:S(2)}, u32[]{:S(2)}) collective-permute-start(bf16[16,2176]{1,0:T(8,128)(2,1)S(1)} %pad_maximum_fusion.piece_ref), channel_id=1, source_target_pairs={{0,2},{1,3},{2,0},{3,1},{4,6},{5,7},{6,4},{7,5},{8,10},{9,11},{10,... | collective-permute-start | bytes 208904 | tf_op jit(solution)/shard_map/ppermute | solution.py:17
  17.0 7.1 %collective-permute-start.6 = (bf16[16,2176]{1,0:T(8,128)(2,1)S(1)}, bf16[16,2176]{1,0:T(8,128)(2,1)S(1)}, u32[]{:S(2)}, u32[]{:S(2)}) collective-permute-start(bf16[16,2176]{1,0:T(8,128)(2,1)S(1)} %pad_maximum_fusion.piece_ref), channel_id=1, source_target_pairs={{0,1},{1,0},{2,3},{3,2},{4,5},{5,4},{6,7},{7,6},{8,9},{9,8},{10,11... | collective-permute-start | bytes 208904 | tf_op jit(solution)/shard_map/ppermute | solution.py:17
  28.0 3.6 %collective-permute-start.9 = (bf16[4,4096]{1,0:T(4,128)(2,1)S(1)}, bf16[4,4096]{1,0:T(4,128)(2,1)S(1)}, u32[]{:S(2)}, u32[]{:S(2)}) collective-permute-start(bf16[4,4096]{1,0:T(4,128)(2,1)S(1)} %get-tuple-element.34), channel_id=1, source_target_pairs={{0,12},{4,8},{8,4},{12,0},{1,13},{5,9},{9,5},{13,1},{2,14},{6,10},... | collective-permute-start | bytes 98312 | tf_op jit(solution)/shard_map/ppermute | solution.py:17
  28.9 3.9 %collective-permute-start.10 = (bf16[4,4096]{1,0:T(4,128)(2,1)S(1)}, bf16[4,4096]{1,0:T(4,128)(2,1)S(1)}, u32[]{:S(2)}, u32[]{:S(2)}) collective-permute-start(bf16[4,4096]{1,0:T(4,128)(2,1)S(1)} %get-tuple-element.35), channel_id=1, source_target_pairs={{0,8},{4,12},{8,0},{12,4},{1,9},{5,13},{9,1},{13,5},{2,10},{6,14},... | collective-permute-start | bytes 98312 | tf_op jit(solution)/shard_map/ppermute | solution.py:17
  29.7 3.1 %collective-permute-start.11 = (bf16[4,4096]{1,0:T(4,128)(2,1)S(1)}, bf16[4,4096]{1,0:T(4,128)(2,1)S(1)}, u32[]{:S(2)}, u32[]{:S(2)}) collective-permute-start(bf16[4,4096]{1,0:T(4,128)(2,1)S(1)} %get-tuple-element.36), channel_id=1, source_target_pairs={{0,4},{4,0},{8,12},{12,8},{1,5},{5,1},{9,13},{13,9},{2,6},{6,2},{1... | collective-permute-start | bytes 98312 | tf_op jit(solution)/shard_map/ppermute | solution.py:17

commit v13 on v10

--- a/solution.py
+++ b/solution.py
@@ -357,13 +357,10 @@
 
 def project_kernel(n_req, n_tp, *refs):
     part_refs = refs[:n_req]
-    upper, lower, weight_hbm = refs[n_req : n_req + 3]
-    out_refs = refs[n_req + 3 : n_req + 3 + n_tp]
-    attention, last, sems = refs[n_req + 3 + n_tp :]
+    upper, lower = refs[n_req : n_req + 2]
+    out_refs = refs[n_req + 2 : n_req + 2 + n_tp]
+    attention = refs[n_req + 2 + n_tp]
     split, columns = upper.shape
-    copies = row_copies(weight_hbm, 0, columns, last, sems)
-    for copy in copies:
-        copy.start()
     depth = attention.shape[1]
     chunk = depth // 128
     values = []
@@ -389,15 +386,11 @@
         product = jnp.dot(attention[:, :split], upper[:, at], preferred_element_type=jnp.float32)
         product += jnp.dot(attention[:, split:], lower[:, at], preferred_element_type=jnp.float32)
         put(product, at)
-    for copy in copies:
-        copy.wait()
-    product = jnp.dot(attention[...], last[...], preferred_element_type=jnp.float32)
-    put(product, slice(columns, columns + last.shape[1]))
-
-
-def project(parts, weights, out_weight, n_req, n_tp):
-    depth, columns = out_weight.shape
-    last = columns - weights[0].shape[1]
+
+
+def project(parts, weights, n_req, n_tp):
+    depth = sum(w.shape[0] for w in weights)
+    columns = weights[0].shape[1]
     vmem = pl.BlockSpec(memory_space=pltpu.VMEM)
     own = jax.ShapeDtypeStruct((n_req, columns), jnp.float32)
     sent = jax.ShapeDtypeStruct((n_req, columns), jnp.bfloat16)
@@ -405,19 +398,15 @@
     return pl.pallas_call(
         functools.partial(project_kernel, n_req, n_tp),
         out_shape=[own] + [sent] * (n_tp - 1),
-        in_specs=[vmem] * (n_req + 2) + [pl.BlockSpec(memory_space=pltpu.HBM)],
+        in_specs=[vmem] * (n_req + 2),
         out_specs=[vmem] * n_tp,
-        scratch_shapes=[
-            pltpu.VMEM((rows, depth), jnp.bfloat16),
-            pltpu.VMEM((depth, last), jnp.bfloat16),
-            pltpu.SemaphoreType.DMA((2,)),
-        ],
+        scratch_shapes=[pltpu.VMEM((rows, depth), jnp.bfloat16)],
         compiler_params=pltpu.CompilerParams(vmem_limit_bytes=16 * MIB),
         cost_estimate=pl.CostEstimate(
             flops=2 * rows * depth * columns, bytes_accessed=depth * columns * 2, transcendentals=0
         ),
         name="project",
-    )(*parts, *weights, in_hbm(out_weight))
+    )(*parts, *weights)
 
 
 def on_device(queries, new_kv, cache_pool, page_slot, page_owner, context_len, out_weight):
@@ -429,13 +418,12 @@
     pieces = other_attention(q_list, own, n_req, n_tp)
     depth, columns = out_weight.shape
     early = depth // 4
-    columns -= min(512, columns // 2)
     swapped = [swap(pieces[d], "tp", d) for d in far_first(n_tp)]
     first, mine = load_weight(pieces[0], out_weight, 0, early, columns)
     arrived = jnp.concatenate([mine] + swapped, axis=0)
     parts = [swap(arrived, "req", d) for d in reversed(near_last(n_req))]
     second, mine = load_weight(arrived, out_weight, early, depth - early, columns)
-    sums = project([mine] + parts, (first, second), out_weight, n_req, n_tp)
+    sums = project([mine] + parts, (first, second), n_req, n_tp)
     total = sums[0]
     for d in far_first(n_tp):
         total = total + swap(sums[d], "tp", d).astype(jnp.float32)

time: 32.1 us -> 32 us (level)
  Pallas kernels: 12.1 us -> 12.6 us
  waiting for transfers between devices: 5.98 us -> 5.53 us
    pallas_call x2, Pallas kernels: 6.29 us -> 6.89 us  [load_weight(): pl.pallas_call(functools.partial(load_kernel, first), out_shape=[jax.Shap...]
    ppermute x12, waiting for transfers between devices: 5.98 us -> 5.53 us  [swap(): return lax.ppermute(x, axis, [(i, i ^ offset) for i in range(count)])]
  transfers between devices with their start and end apart: 12 -> 12, of which waited for: 5 -> 4; matrix products, arithmetic and copies ran while one was open for 0% -> 0% of each run, Pallas kernels for 27% -> 29%
where the time goes in v13:
time: 32 us; the launch traced here: 31.9 us
  starting transfers between devices  13 us (41%)
  Pallas kernels  12.6 us (39%)
  waiting for transfers between devices  5.53 us (17%)
  other arithmetic  0.7 us (2%)
    ppermute x12, starting transfers between devices, swap(): return lax.ppermute(x, axis, [(i, i ^ offset) for i in range(count)])  13 us
    pallas_call x2, Pallas kernels, load_weight(): pl.pallas_call(functools.partial(load_kernel, first), out_shape=[jax.Shap...  6.89 us
    ppermute x12, waiting for transfers between devices, swap(): return lax.ppermute(x, axis, [(i, i ^ offset) for i in range(count)])  5.53 us
    pallas_call x1, Pallas kernels, project(): pl.pallas_call(functools.partial(project_kernel, n_req, n_tp), out_shape=...  2.46 us
    pallas_call x1, Pallas kernels, own_attention(): pl.pallas_call(functools.partial(own_kernel, n_req, own_pages), out_shape...  2.39 us
    pallas_call x1, Pallas kernels, other_attention(): pl.pallas_call(functools.partial(other_kernel, n_req, n_tp), out_shape=[j...  0.84 us
    convert_element_type x1, other arithmetic, on_device(): return total.astype(jnp.bfloat16)  0.65 us
  transfers between devices with their start and end apart: 12, of which 4 were waited for; matrix products, arithmetic and copies ran while one was open for 0% of the time, Pallas kernels for 29%

profile of v13, /device:TPU:0, one launch (start us, length us, event | category | flops | bytes accessed | tf_op | source)
XLA Modules:
  0.0 31.9 jit_solution(318318781227852074)
XLA Ops:
  0.0 4.0 %collective-permute-start.1 = (bf16[1,8192]{1,0:T(2,128)(2,1)}, bf16[1,8192]{1,0:T(2,128)(2,1)S(1)}, u32[]{:S(2)}, u32[]{:S(2)}) collective-permute-start(bf16[1,8192]{1,0:T(2,128)(2,1)} %refs_0_.1), channel_id=1, source_target_pairs={{0,2},{1,3},{2,0},{3,1},{4,6},{5,7},{6,4},{7,5},{8,10},{9,11},{10,... | collective-permute-start | bytes 49160 | tf_op jit(solution)/shard_map/ppermute | solution.py:17
  4.0 1.3 %collective-permute-start = (bf16[1,8192]{1,0:T(2,128)(2,1)}, bf16[1,8192]{1,0:T(2,128)(2,1)S(1)}, u32[]{:S(2)}, u32[]{:S(2)}) collective-permute-start(bf16[1,8192]{1,0:T(2,128)(2,1)} %refs_0_.1), channel_id=1, source_target_pairs={{0,3},{1,2},{2,1},{3,0},{4,7},{5,6},{6,5},{7,4},{8,11},{9,10},{10,... | collective-permute-start | bytes 49160 | tf_op jit(solution)/shard_map/ppermute | solution.py:17
  5.4 0.2 collective-permute-start.2
  5.6 2.4 %own_attention.1 = (f32[64,128]{1,0:T(8,128)S(1)}, f32[8,128]{1,0:T(8,128)S(1)}, s32[8,128]{1,0:T(8,128)S(1)}, bf16[3,4,128,256]{3,2,1,0:T(8,128)(2,1)S(1)}) custom-call(bf16[1,8192]{1,0:T(2,128)(2,1)} %refs_0_.1, bf16[1,1024]{1,0:T(2,128)(2,1)} %refs_1_.1, s32[1,4,7]{2,1,0:T(4,128)} %refs_2_.1, s32[1,4,7]{2,1,0:T(4,128)} %refs_3_.1, s32[1,4]{1,0:T(1,128)} %refs_4_.1, ...), custom_call_target="tpu_custom_call" | custom-call | flops 25165824 | bytes 4718592 | tf_op jit(solution)/shard_map/own_attention/pallas_call | solution.py:205
  8.0 0.0 collective-permute-done.1.refs_1_
  8.0 1.9 %collective-permute-done.refs_0_ = bf16[1,8192]{1,0:T(2,128)(2,1)S(1)} collective-permute-done((bf16[1,8192]{1,0:T(2,128)(2,1)}, bf16[1,8192]{1,0:T(2,128)(2,1)S(1)}, u32[]{:S(2)}, u32[]{:S(2)}) %collective-permute-start) | collective-permute-done | bytes 16416 | tf_op jit(solution)/shard_map/ppermute | solution.py:17
  10.0 0.0 collective-permute-done.2.refs_2_
  10.0 0.8 %other_attention.1 = (bf16[4,2176]{1,0:T(4,128)(2,1)S(1)}, bf16[4,2176]{1,0:T(4,128)(2,1)S(1)}, bf16[4,2176]{1,0:T(4,128)(2,1)S(1)}, bf16[4,2176]{1,0:T(4,128)(2,1)S(1)}) custom-call(bf16[1,8192]{1,0:T(2,128)(2,1)S(1)} %collective-permute-done.refs_0_, bf16[1,8192]{1,0:T(2,128)(2,1)S(1)} %collective-permute-done.1.refs_1_, ...), custom_call_target="tpu_custom_call" | custom-call | flops 12582912 | bytes 786432 | tf_op jit(solution)/shard_map/other_attention/pallas_call | solution.py:304
  10.8 0.1 collective-permute-start.3
  10.9 1.6 %collective-permute-start.4 = (bf16[4,2176]{1,0:T(4,128)(2,1)S(1)}, bf16[4,2176]{1,0:T(4,128)(2,1)S(1)}, u32[]{:S(2)}, u32[]{:S(2)}) collective-permute-start(bf16[4,2176]{1,0:T(4,128)(2,1)S(1)} %get-tuple-element.28), channel_id=1, source_target_pairs={{0,8},{4,12},{8,0},{12,4},{1,9},{5,13},{9,1},{13,5},{2,10},{6,14},... | collective-permute-start | bytes 52232 | tf_op jit(solution)/shard_map/ppermute | solution.py:17
  12.5 0.3 collective-permute-start.5
  12.7 2.2 %load_weight.2 = (bf16[512,4096]{1,0:T(8,128)(2,1)S(1)}, bf16[4,2176]{1,0:T(4,128)(2,1)S(1)}) custom-call(bf16[4,2176]{1,0:T(4,128)(2,1)S(1)} %get-tuple-element.25.piece_ref, bf16[2048,4096]{1,0:T(8,128)(2,1)} %weight_hbm.3), custom_call_target="tpu_custom_call" | custom-call | bytes 8388608 | tf_op jit(solution)/shard_map/load_weight/pallas_call | solution.py:343
  14.9 0.0 collective-permute-done.3
  15.0 0.0 collective-permute-done.4
  15.0 0.0 collective-permute-done.5
  15.0 1.3 %collective-permute-start.8 = (bf16[16,2176]{1,0:T(8,128)(2,1)S(1)}, bf16[16,2176]{1,0:T(8,128)(2,1)S(1)}, u32[]{:S(2)}, u32[]{:S(2)}) collective-permute-start(bf16[16,2176]{1,0:T(8,128)(2,1)S(1)} %pad_maximum_fusion.piece_ref), channel_id=1, source_target_pairs={{0,2},{1,3},{2,0},{3,1},{4,6},{5,7},{6,4},{7,5},{8,10},{9,11},{10,... | collective-permute-start | bytes 208904 | tf_op jit(solution)/shard_map/ppermute | solution.py:17
  16.3 1.0 %collective-permute-start.7 = (bf16[16,2176]{1,0:T(8,128)(2,1)S(1)}, bf16[16,2176]{1,0:T(8,128)(2,1)S(1)}, u32[]{:S(2)}, u32[]{:S(2)}) collective-permute-start(bf16[16,2176]{1,0:T(8,128)(2,1)S(1)} %pad_maximum_fusion.piece_ref), channel_id=1, source_target_pairs={{0,3},{1,2},{2,1},{3,0},{4,7},{5,6},{6,5},{7,4},{8,11},{9,10},{10,... | collective-permute-start | bytes 208904 | tf_op jit(solution)/shard_map/ppermute | solution.py:17
  17.4 1.2 %collective-permute-start.6 = (bf16[16,2176]{1,0:T(8,128)(2,1)S(1)}, bf16[16,2176]{1,0:T(8,128)(2,1)S(1)}, u32[]{:S(2)}, u32[]{:S(2)}) collective-permute-start(bf16[16,2176]{1,0:T(8,128)(2,1)S(1)} %pad_maximum_fusion.piece_ref), channel_id=1, source_target_pairs={{0,1},{1,0},{2,3},{3,2},{4,5},{5,4},{6,7},{7,6},{8,9},{9,8},{10,11... | collective-permute-start | bytes 208904 | tf_op jit(solution)/shard_map/ppermute | solution.py:17
  18.6 4.7 %load_weight.3 = (bf16[1536,4096]{1,0:T(8,128)(2,1)S(1)}, bf16[16,2176]{1,0:T(8,128)(2,1)S(1)}) custom-call(bf16[16,2176]{1,0:T(8,128)(2,1)S(1)} %pad_maximum_fusion.piece_ref, bf16[2048,4096]{1,0:T(8,128)(2,1)} %weight_hbm.3), custom_call_target="tpu_custom_call" | custom-call | bytes 25165824 | tf_op jit(solution)/shard_map/load_weight/pallas_call | solution.py:343
  23.3 0.0 collective-permute-done.8.refs_3_
  23.3 0.0 collective-permute-done.7.refs_2_
  23.3 0.8 %collective-permute-done.6.refs_1_ = bf16[16,2176]{1,0:T(8,128)(2,1)S(1)} collective-permute-done((bf16[16,2176]{1,0:T(8,128)(2,1)S(1)}, bf16[16,2176]{1,0:T(8,128)(2,1)S(1)}, u32[]{:S(2)}, u32[]{:S(2)}) %collective-permute-start.6) | collective-permute-done | bytes 69664 | tf_op jit(solution)/shard_map/ppermute | solution.py:17
  24.1 2.5 %project.1 = (f32[4,4096]{1,0:T(4,128)S(1)}, bf16[4,4096]{1,0:T(4,128)(2,1)S(1)}, bf16[4,4096]{1,0:T(4,128)(2,1)S(1)}, bf16[4,4096]{1,0:T(4,128)(2,1)S(1)}) custom-call(bf16[16,2176]{1,0:T(8,128)(2,1)S(1)} %get-tuple-element.30.refs_0_, bf16[16,2176]{1,0:T(8,128)(2,1)S(1)} %collective-permute-done.6.refs_1_, ...), custom_call_target="tpu_custom_call" | custom-call | flops 268435456 | bytes 16777216 | tf_op jit(solution)/shard_map/project/pallas_call | solution.py:398
  26.6 0.7 %collective-permute-start.9 = (bf16[4,4096]{1,0:T(4,128)(2,1)S(1)}, bf16[4,4096]{1,0:T(4,128)(2,1)S(1)}, u32[]{:S(2)}, u32[]{:S(2)}) collective-permute-start(bf16[4,4096]{1,0:T(4,128)(2,1)S(1)} %get-tuple-element.34), channel_id=1, source_target_pairs={{0,12},{4,8},{8,4},{12,0},{1,13},{5,9},{9,5},{13,1},{2,14},{6,10},... | collective-permute-start | bytes 98312 | tf_op jit(solution)/shard_map/ppermute | solution.py:17
  27.3 0.9 %collective-permute-start.10 = (bf16[4,4096]{1,0:T(4,128)(2,1)S(1)}, bf16[4,4096]{1,0:T(4,128)(2,1)S(1)}, u32[]{:S(2)}, u32[]{:S(2)}) collective-permute-start(bf16[4,4096]{1,0:T(4,128)(2,1)S(1)} %get-tuple-element.35), channel_id=1, source_target_pairs={{0,8},{4,12},{8,0},{12,4},{1,9},{5,13},{9,1},{13,5},{2,10},{6,14},... | collective-permute-start | bytes 98312 | tf_op jit(solution)/shard_map/ppermute | solution.py:17
  28.2 0.3 collective-permute-start.11
  28.5 1.7 %collective-permute-done.9 = bf16[4,4096]{1,0:T(4,128)(2,1)S(1)} collective-permute-done((bf16[4,4096]{1,0:T(4,128)(2,1)S(1)}, bf16[4,4096]{1,0:T(4,128)(2,1)S(1)}, u32[]{:S(2)}, u32[]{:S(2)}) %collective-permute-start.9) | collective-permute-done | bytes 32800 | tf_op jit(solution)/shard_map/ppermute | solution.py:17
  30.1 1.1 %collective-permute-done.10 = bf16[4,4096]{1,0:T(4,128)(2,1)S(1)} collective-permute-done((bf16[4,4096]{1,0:T(4,128)(2,1)S(1)}, bf16[4,4096]{1,0:T(4,128)(2,1)S(1)}, u32[]{:S(2)}, u32[]{:S(2)}) %collective-permute-start.10) | collective-permute-done | bytes 32800 | tf_op jit(solution)/shard_map/ppermute | solution.py:17
  31.2 0.0 collective-permute-done.11
  31.2 0.7 %add_convert_fusion = bf16[4,4096]{1,0:T(4,128)(2,1)} fusion(bf16[4,4096]{1,0:T(4,128)(2,1)S(1)} %collective-permute-done.11, bf16[4,4096]{1,0:T(4,128)(2,1)S(1)} %collective-permute-done.10, f32[4,4096]{1,0:T(4,128)S(1)} %get-tuple-element.33, bf16[4,4096]{1,0:T(4,128)(2,1)S(1)} %collective-permute-done.9), kind=kLoop, calls=%fused_computation.1 | loop fusion | flops 114688 | bytes 196608 | tf_op jit(solution)/shard_map/convert_element_type | solution.py:430
  (1 shorter events, 0.0 us)
Async XLA Ops:
  0.0 8.0 %collective-permute-start.1 = (bf16[1,8192]{1,0:T(2,128)(2,1)}, bf16[1,8192]{1,0:T(2,128)(2,1)S(1)}, u32[]{:S(2)}, u32[]{:S(2)}) collective-permute-start(bf16[1,8192]{1,0:T(2,128)(2,1)} %refs_0_.1), channel_id=1, source_target_pairs={{0,2},{1,3},{2,0},{3,1},{4,6},{5,7},{6,4},{7,5},{8,10},{9,11},{10,... | collective-permute-start | bytes 49160 | tf_op jit(solution)/shard_map/ppermute | solution.py:17
  4.0 5.9 %collective-permute-start = (bf16[1,8192]{1,0:T(2,128)(2,1)}, bf16[1,8192]{1,0:T(2,128)(2,1)S(1)}, u32[]{:S(2)}, u32[]{:S(2)}) collective-permute-start(bf16[1,8192]{1,0:T(2,128)(2,1)} %refs_0_.1), channel_id=1, source_target_pairs={{0,3},{1,2},{2,1},{3,0},{4,7},{5,6},{6,5},{7,4},{8,11},{9,10},{10,... | collective-permute-start | bytes 49160 | tf_op jit(solution)/shard_map/ppermute | solution.py:17
  5.4 4.6 %collective-permute-start.2 = (bf16[1,8192]{1,0:T(2,128)(2,1)}, bf16[1,8192]{1,0:T(2,128)(2,1)S(1)}, u32[]{:S(2)}, u32[]{:S(2)}) collective-permute-start(bf16[1,8192]{1,0:T(2,128)(2,1)} %refs_0_.1), channel_id=1, source_target_pairs={{0,1},{1,0},{2,3},{3,2},{4,5},{5,4},{6,7},{7,6},{8,9},{9,8},{10,11... | collective-permute-start | bytes 49160 | tf_op jit(solution)/shard_map/ppermute | solution.py:17
  10.8 4.1 %collective-permute-start.3 = (bf16[4,2176]{1,0:T(4,128)(2,1)S(1)}, bf16[4,2176]{1,0:T(4,128)(2,1)S(1)}, u32[]{:S(2)}, u32[]{:S(2)}) collective-permute-start(bf16[4,2176]{1,0:T(4,128)(2,1)S(1)} %get-tuple-element.27), channel_id=1, source_target_pairs={{0,12},{4,8},{8,4},{12,0},{1,13},{5,9},{9,5},{13,1},{2,14},{6,10},... | collective-permute-start | bytes 52232 | tf_op jit(solution)/shard_map/ppermute | solution.py:17
  10.9 4.1 %collective-permute-start.4 = (bf16[4,2176]{1,0:T(4,128)(2,1)S(1)}, bf16[4,2176]{1,0:T(4,128)(2,1)S(1)}, u32[]{:S(2)}, u32[]{:S(2)}) collective-permute-start(bf16[4,2176]{1,0:T(4,128)(2,1)S(1)} %get-tuple-element.28), channel_id=1, source_target_pairs={{0,8},{4,12},{8,0},{12,4},{1,9},{5,13},{9,1},{13,5},{2,10},{6,14},... | collective-permute-start | bytes 52232 | tf_op jit(solution)/shard_map/ppermute | solution.py:17
  12.5 2.5 %collective-permute-start.5 = (bf16[4,2176]{1,0:T(4,128)(2,1)S(1)}, bf16[4,2176]{1,0:T(4,128)(2,1)S(1)}, u32[]{:S(2)}, u32[]{:S(2)}) collective-permute-start(bf16[4,2176]{1,0:T(4,128)(2,1)S(1)} %get-tuple-element.29), channel_id=1, source_target_pairs={{0,4},{4,0},{8,12},{12,8},{1,5},{5,1},{9,13},{13,9},{2,6},{6,2},{1... | collective-permute-start | bytes 52232 | tf_op jit(solution)/shard_map/ppermute | solution.py:17
  15.0 8.3 %collective-permute-start.8 = (bf16[16,2176]{1,0:T(8,128)(2,1)S(1)}, bf16[16,2176]{1,0:T(8,128)(2,1)S(1)}, u32[]{:S(2)}, u32[]{:S(2)}) collective-permute-start(bf16[16,2176]{1,0:T(8,128)(2,1)S(1)} %pad_maximum_fusion.piece_ref), channel_id=1, source_target_pairs={{0,2},{1,3},{2,0},{3,1},{4,6},{5,7},{6,4},{7,5},{8,10},{9,11},{10,... | collective-permute-start | bytes 208904 | tf_op jit(solution)/shard_map/ppermute | solution.py:17
  16.3 7.0 %collective-permute-start.7 = (bf16[16,2176]{1,0:T(8,128)(2,1)S(1)}, bf16[16,2176]{1,0:T(8,128)(2,1)S(1)}, u32[]{:S(2)}, u32[]{:S(2)}) collective-permute-start(bf16[16,2176]{1,0:T(8,128)(2,1)S(1)} %pad_maximum_fusion.piece_ref), channel_id=1, source_target_pairs={{0,3},{1,2},{2,1},{3,0},{4,7},{5,6},{6,5},{7,4},{8,11},{9,10},{10,... | collective-permute-start | bytes 208904 | tf_op jit(solution)/shard_map/ppermute | solution.py:17
  17.4 6.8 %collective-permute-start.6 = (bf16[16,2176]{1,0:T(8,128)(2,1)S(1)}, bf16[16,2176]{1,0:T(8,128)(2,1)S(1)}, u32[]{:S(2)}, u32[]{:S(2)}) collective-permute-start(bf16[16,2176]{1,0:T(8,128)(2,1)S(1)} %pad_maximum_fusion.piece_ref), channel_id=1, source_target_pairs={{0,1},{1,0},{2,3},{3,2},{4,5},{5,4},{6,7},{7,6},{8,9},{9,8},{10,11... | collective-permute-start | bytes 208904 | tf_op jit(solution)/shard_map/ppermute | solution.py:17
  26.6 3.6 %collective-permute-start.9 = (bf16[4,4096]{1,0:T(4,128)(2,1)S(1)}, bf16[4,4096]{1,0:T(4,128)(2,1)S(1)}, u32[]{:S(2)}, u32[]{:S(2)}) collective-permute-start(bf16[4,4096]{1,0:T(4,128)(2,1)S(1)} %get-tuple-element.34), channel_id=1, source_target_pairs={{0,12},{4,8},{8,4},{12,0},{1,13},{5,9},{9,5},{13,1},{2,14},{6,10},... | collective-permute-start | bytes 98312 | tf_op jit(solution)/shard_map/ppermute | solution.py:17
  27.3 3.9 %collective-permute-start.10 = (bf16[4,4096]{1,0:T(4,128)(2,1)S(1)}, bf16[4,4096]{1,0:T(4,128)(2,1)S(1)}, u32[]{:S(2)}, u32[]{:S(2)}) collective-permute-start(bf16[4,4096]{1,0:T(4,128)(2,1)S(1)} %get-tuple-element.35), channel_id=1, source_target_pairs={{0,8},{4,12},{8,0},{12,4},{1,9},{5,13},{9,1},{13,5},{2,10},{6,14},... | collective-permute-start | bytes 98312 | tf_op jit(solution)/shard_map/ppermute | solution.py:17
  28.2 3.0 %collective-permute-start.11 = (bf16[4,4096]{1,0:T(4,128)(2,1)S(1)}, bf16[4,4096]{1,0:T(4,128)(2,1)S(1)}, u32[]{:S(2)}, u32[]{:S(2)}) collective-permute-start(bf16[4,4096]{1,0:T(4,128)(2,1)S(1)} %get-tuple-element.36), channel_id=1, source_target_pairs={{0,4},{4,0},{8,12},{12,8},{1,5},{5,1},{9,13},{13,9},{2,6},{6,2},{1... | collective-permute-start | bytes 98312 | tf_op jit(solution)/shard_map/ppermute | solution.py:17

commit v14 on v13

--- a/solution.py
+++ b/solution.py
@@ -15,10 +15,6 @@
 def swap(x, axis, offset):
     count = lax.axis_size(axis)
     return lax.ppermute(x, axis, [(i, i ^ offset) for i in range(count)])
-
-
-def near_last(count):
-    return list(range(2, count)) + [1]
 
 
 def far_first(count):
@@ -417,11 +413,11 @@
     own = own_attention(queries, new_kv, page_slot, page_owner, context_len, pool, n_req)
     pieces = other_attention(q_list, own, n_req, n_tp)
     depth, columns = out_weight.shape
-    early = depth // 4
+    early = depth // 8
     swapped = [swap(pieces[d], "tp", d) for d in far_first(n_tp)]
     first, mine = load_weight(pieces[0], out_weight, 0, early, columns)
     arrived = jnp.concatenate([mine] + swapped, axis=0)
-    parts = [swap(arrived, "req", d) for d in reversed(near_last(n_req))]
+    parts = [swap(arrived, "req", d) for d in range(1, n_req)]
     second, mine = load_weight(arrived, out_weight, early, depth - early, columns)
     sums = project([mine] + parts, (first, second), n_req, n_tp)
     total = sums[0]

time: 32 us -> 31.9 us (level)
  waiting for transfers between devices: 5.53 us -> 4.54 us
  starting transfers between devices: 13 us -> 13.9 us
    ppermute x12, waiting for transfers between devices: 5.53 us -> 4.54 us  [swap(): return lax.ppermute(x, axis, [(i, i ^ offset) for i in range(count)])]
    ppermute x12, starting transfers between devices: 13 us -> 13.9 us  [swap(): return lax.ppermute(x, axis, [(i, i ^ offset) for i in range(count)])]
where the time goes in v14:
time: 31.9 us; the launch traced here: 31.8 us
  starting transfers between devices  13.9 us (44%)
  Pallas kernels  12.5 us (39%)
  waiting for transfers between devices  4.54 us (14%)
  other arithmetic  0.7 us (2%)
    ppermute x12, starting transfers between devices, swap(): return lax.ppermute(x, axis, [(i, i ^ offset) for i in range(count)])  13.9 us
    pallas_call x2, Pallas kernels, load_weight(): pl.pallas_call(functools.partial(load_kernel, first), out_shape=[jax.Shap...  6.83 us
    ppermute x12, waiting for transfers between devices, swap(): return lax.ppermute(x, axis, [(i, i ^ offset) for i in range(count)])  4.54 us
    pallas_call x1, Pallas kernels, project(): pl.pallas_call(functools.partial(project_kernel, n_req, n_tp), out_shape=...  2.46 us
    pallas_call x1, Pallas kernels, own_attention(): pl.pallas_call(functools.partial(own_kernel, n_req, own_pages), out_shape...  2.39 us
    pallas_call x1, Pallas kernels, other_attention(): pl.pallas_call(functools.partial(other_kernel, n_req, n_tp), out_shape=[j...  0.84 us
    convert_element_type x1, other arithmetic, on_device(): return total.astype(jnp.bfloat16)  0.65 us
  transfers between devices with their start and end apart: 12, of which 4 were waited for; matrix products, arithmetic and copies ran while one was open for 0% of the time, Pallas kernels for 29%

profile of v14, /device:TPU:0, one launch (start us, length us, event | category | flops | bytes accessed | tf_op | source)
XLA Modules:
  0.0 31.8 jit_solution(15080760205438031995)
XLA Ops:
  0.0 4.0 %collective-permute-start.1 = (bf16[1,8192]{1,0:T(2,128)(2,1)}, bf16[1,8192]{1,0:T(2,128)(2,1)S(1)}, u32[]{:S(2)}, u32[]{:S(2)}) collective-permute-start(bf16[1,8192]{1,0:T(2,128)(2,1)} %refs_0_.1), channel_id=1, source_target_pairs={{0,2},{1,3},{2,0},{3,1},{4,6},{5,7},{6,4},{7,5},{8,10},{9,11},{10,... | collective-permute-start | bytes 49160 | tf_op jit(solution)/shard_map/ppermute | solution.py:17
  4.0 1.3 %collective-permute-start = (bf16[1,8192]{1,0:T(2,128)(2,1)}, bf16[1,8192]{1,0:T(2,128)(2,1)S(1)}, u32[]{:S(2)}, u32[]{:S(2)}) collective-permute-start(bf16[1,8192]{1,0:T(2,128)(2,1)} %refs_0_.1), channel_id=1, source_target_pairs={{0,3},{1,2},{2,1},{3,0},{4,7},{5,6},{6,5},{7,4},{8,11},{9,10},{10,... | collective-permute-start | bytes 49160 | tf_op jit(solution)/shard_map/ppermute | solution.py:17
  5.4 0.2 collective-permute-start.2
  5.6 2.4 %own_attention.1 = (f32[64,128]{1,0:T(8,128)S(1)}, f32[8,128]{1,0:T(8,128)S(1)}, s32[8,128]{1,0:T(8,128)S(1)}, bf16[3,4,128,256]{3,2,1,0:T(8,128)(2,1)S(1)}) custom-call(bf16[1,8192]{1,0:T(2,128)(2,1)} %refs_0_.1, bf16[1,1024]{1,0:T(2,128)(2,1)} %refs_1_.1, s32[1,4,7]{2,1,0:T(4,128)} %refs_2_.1, s32[1,4,7]{2,1,0:T(4,128)} %refs_3_.1, s32[1,4]{1,0:T(1,128)} %refs_4_.1, ...), custom_call_target="tpu_custom_call" | custom-call | flops 25165824 | bytes 4718592 | tf_op jit(solution)/shard_map/own_attention/pallas_call | solution.py:201
  8.0 0.0 collective-permute-done.1.refs_1_
  8.0 1.9 %collective-permute-done.refs_0_ = bf16[1,8192]{1,0:T(2,128)(2,1)S(1)} collective-permute-done((bf16[1,8192]{1,0:T(2,128)(2,1)}, bf16[1,8192]{1,0:T(2,128)(2,1)S(1)}, u32[]{:S(2)}, u32[]{:S(2)}) %collective-permute-start) | collective-permute-done | bytes 16416 | tf_op jit(solution)/shard_map/ppermute | solution.py:17
  10.0 0.0 collective-permute-done.2.refs_2_
  10.0 0.8 %other_attention.1 = (bf16[4,2176]{1,0:T(4,128)(2,1)S(1)}, bf16[4,2176]{1,0:T(4,128)(2,1)S(1)}, bf16[4,2176]{1,0:T(4,128)(2,1)S(1)}, bf16[4,2176]{1,0:T(4,128)(2,1)S(1)}) custom-call(bf16[1,8192]{1,0:T(2,128)(2,1)S(1)} %collective-permute-done.refs_0_, bf16[1,8192]{1,0:T(2,128)(2,1)S(1)} %collective-permute-done.1.refs_1_, ...), custom_call_target="tpu_custom_call" | custom-call | flops 12582912 | bytes 786432 | tf_op jit(solution)/shard_map/other_attention/pallas_call | solution.py:300
  10.8 0.1 collective-permute-start.3
  10.9 1.6 %collective-permute-start.4 = (bf16[4,2176]{1,0:T(4,128)(2,1)S(1)}, bf16[4,2176]{1,0:T(4,128)(2,1)S(1)}, u32[]{:S(2)}, u32[]{:S(2)}) collective-permute-start(bf16[4,2176]{1,0:T(4,128)(2,1)S(1)} %get-tuple-element.28), channel_id=1, source_target_pairs={{0,8},{4,12},{8,0},{12,4},{1,9},{5,13},{9,1},{13,5},{2,10},{6,14},... | collective-permute-start | bytes 52232 | tf_op jit(solution)/shard_map/ppermute | solution.py:17
  12.5 0.3 collective-permute-start.5
  12.7 1.5 %load_weight.2 = (bf16[256,4096]{1,0:T(8,128)(2,1)S(1)}, bf16[4,2176]{1,0:T(4,128)(2,1)S(1)}) custom-call(bf16[4,2176]{1,0:T(4,128)(2,1)S(1)} %get-tuple-element.25.piece_ref, bf16[2048,4096]{1,0:T(8,128)(2,1)} %weight_hbm.3), custom_call_target="tpu_custom_call" | custom-call | bytes 4194304 | tf_op jit(solution)/shard_map/load_weight/pallas_call | solution.py:339
  14.3 0.0 collective-permute-done.3
  14.3 0.4 %collective-permute-done.4 = bf16[4,2176]{1,0:T(4,128)(2,1)S(1)} collective-permute-done((bf16[4,2176]{1,0:T(4,128)(2,1)S(1)}, bf16[4,2176]{1,0:T(4,128)(2,1)S(1)}, u32[]{:S(2)}, u32[]{:S(2)}) %collective-permute-start.4) | collective-permute-done | bytes 17440 | tf_op jit(solution)/shard_map/ppermute | solution.py:17
  14.7 0.0 collective-permute-done.5
  14.8 2.1 %collective-permute-start.8 = (bf16[16,2176]{1,0:T(8,128)(2,1)S(1)}, bf16[16,2176]{1,0:T(8,128)(2,1)S(1)}, u32[]{:S(2)}, u32[]{:S(2)}) collective-permute-start(bf16[16,2176]{1,0:T(8,128)(2,1)S(1)} %pad_maximum_fusion.piece_ref), channel_id=1, source_target_pairs={{0,3},{1,2},{2,1},{3,0},{4,7},{5,6},{6,5},{7,4},{8,11},{9,10},{10,... | collective-permute-start | bytes 208904 | tf_op jit(solution)/shard_map/ppermute | solution.py:17
  16.9 0.0 collective-permute-start.7
  16.9 2.4 %collective-permute-start.6 = (bf16[16,2176]{1,0:T(8,128)(2,1)S(1)}, bf16[16,2176]{1,0:T(8,128)(2,1)S(1)}, u32[]{:S(2)}, u32[]{:S(2)}) collective-permute-start(bf16[16,2176]{1,0:T(8,128)(2,1)S(1)} %pad_maximum_fusion.piece_ref), channel_id=1, source_target_pairs={{0,1},{1,0},{2,3},{3,2},{4,5},{5,4},{6,7},{7,6},{8,9},{9,8},{10,11... | collective-permute-start | bytes 208904 | tf_op jit(solution)/shard_map/ppermute | solution.py:17
  19.2 5.3 %load_weight.3 = (bf16[1792,4096]{1,0:T(8,128)(2,1)S(1)}, bf16[16,2176]{1,0:T(8,128)(2,1)S(1)}) custom-call(bf16[16,2176]{1,0:T(8,128)(2,1)S(1)} %pad_maximum_fusion.piece_ref, bf16[2048,4096]{1,0:T(8,128)(2,1)} %weight_hbm.3), custom_call_target="tpu_custom_call" | custom-call | bytes 29360128 | tf_op jit(solution)/shard_map/load_weight/pallas_call | solution.py:339
  24.5 0.0 collective-permute-done.8.refs_3_
  24.5 0.0 collective-permute-done.7.refs_2_
  24.5 0.0 collective-permute-done.6.refs_1_
  24.6 2.5 %project.1 = (f32[4,4096]{1,0:T(4,128)S(1)}, bf16[4,4096]{1,0:T(4,128)(2,1)S(1)}, bf16[4,4096]{1,0:T(4,128)(2,1)S(1)}, bf16[4,4096]{1,0:T(4,128)(2,1)S(1)}) custom-call(bf16[16,2176]{1,0:T(8,128)(2,1)S(1)} %get-tuple-element.30.refs_0_, bf16[16,2176]{1,0:T(8,128)(2,1)S(1)} %collective-permute-done.6.refs_1_, ...), custom_call_target="tpu_custom_call" | custom-call | flops 268435456 | bytes 16777216 | tf_op jit(solution)/shard_map/project/pallas_call | solution.py:394
  27.0 0.1 collective-permute-start.9
  27.1 1.5 %collective-permute-start.10 = (bf16[4,4096]{1,0:T(4,128)(2,1)S(1)}, bf16[4,4096]{1,0:T(4,128)(2,1)S(1)}, u32[]{:S(2)}, u32[]{:S(2)}) collective-permute-start(bf16[4,4096]{1,0:T(4,128)(2,1)S(1)} %get-tuple-element.35), channel_id=1, source_target_pairs={{0,8},{4,12},{8,0},{12,4},{1,9},{5,13},{9,1},{13,5},{2,10},{6,14},... | collective-permute-start | bytes 98312 | tf_op jit(solution)/shard_map/ppermute | solution.py:17
  28.6 0.3 collective-permute-start.11
  28.9 1.8 %collective-permute-done.9 = bf16[4,4096]{1,0:T(4,128)(2,1)S(1)} collective-permute-done((bf16[4,4096]{1,0:T(4,128)(2,1)S(1)}, bf16[4,4096]{1,0:T(4,128)(2,1)S(1)}, u32[]{:S(2)}, u32[]{:S(2)}) %collective-permute-start.9) | collective-permute-done | bytes 32800 | tf_op jit(solution)/shard_map/ppermute | solution.py:17
  30.7 0.4 %collective-permute-done.10 = bf16[4,4096]{1,0:T(4,128)(2,1)S(1)} collective-permute-done((bf16[4,4096]{1,0:T(4,128)(2,1)S(1)}, bf16[4,4096]{1,0:T(4,128)(2,1)S(1)}, u32[]{:S(2)}, u32[]{:S(2)}) %collective-permute-start.10) | collective-permute-done | bytes 32800 | tf_op jit(solution)/shard_map/ppermute | solution.py:17
  31.1 0.0 collective-permute-done.11
  31.1 0.7 %add_convert_fusion = bf16[4,4096]{1,0:T(4,128)(2,1)} fusion(bf16[4,4096]{1,0:T(4,128)(2,1)S(1)} %collective-permute-done.11, bf16[4,4096]{1,0:T(4,128)(2,1)S(1)} %collective-permute-done.10, f32[4,4096]{1,0:T(4,128)S(1)} %get-tuple-element.33, bf16[4,4096]{1,0:T(4,128)(2,1)S(1)} %collective-permute-done.9), kind=kLoop, calls=%fused_computation.1 | loop fusion | flops 114688 | bytes 196608 | tf_op jit(solution)/shard_map/convert_element_type | solution.py:426
  (1 shorter events, 0.0 us)
Async XLA Ops:
  0.0 8.0 %collective-permute-start.1 = (bf16[1,8192]{1,0:T(2,128)(2,1)}, bf16[1,8192]{1,0:T(2,128)(2,1)S(1)}, u32[]{:S(2)}, u32[]{:S(2)}) collective-permute-start(bf16[1,8192]{1,0:T(2,128)(2,1)} %refs_0_.1), channel_id=1, source_target_pairs={{0,2},{1,3},{2,0},{3,1},{4,6},{5,7},{6,4},{7,5},{8,10},{9,11},{10,... | collective-permute-start | bytes 49160 | tf_op jit(solution)/shard_map/ppermute | solution.py:17
  4.0 5.9 %collective-permute-start = (bf16[1,8192]{1,0:T(2,128)(2,1)}, bf16[1,8192]{1,0:T(2,128)(2,1)S(1)}, u32[]{:S(2)}, u32[]{:S(2)}) collective-permute-start(bf16[1,8192]{1,0:T(2,128)(2,1)} %refs_0_.1), channel_id=1, source_target_pairs={{0,3},{1,2},{2,1},{3,0},{4,7},{5,6},{6,5},{7,4},{8,11},{9,10},{10,... | collective-permute-start | bytes 49160 | tf_op jit(solution)/shard_map/ppermute | solution.py:17
  5.4 4.6 %collective-permute-start.2 = (bf16[1,8192]{1,0:T(2,128)(2,1)}, bf16[1,8192]{1,0:T(2,128)(2,1)S(1)}, u32[]{:S(2)}, u32[]{:S(2)}) collective-permute-start(bf16[1,8192]{1,0:T(2,128)(2,1)} %refs_0_.1), channel_id=1, source_target_pairs={{0,1},{1,0},{2,3},{3,2},{4,5},{5,4},{6,7},{7,6},{8,9},{9,8},{10,11... | collective-permute-start | bytes 49160 | tf_op jit(solution)/shard_map/ppermute | solution.py:17
  10.8 3.5 %collective-permute-start.3 = (bf16[4,2176]{1,0:T(4,128)(2,1)S(1)}, bf16[4,2176]{1,0:T(4,128)(2,1)S(1)}, u32[]{:S(2)}, u32[]{:S(2)}) collective-permute-start(bf16[4,2176]{1,0:T(4,128)(2,1)S(1)} %get-tuple-element.27), channel_id=1, source_target_pairs={{0,12},{4,8},{8,4},{12,0},{1,13},{5,9},{9,5},{13,1},{2,14},{6,10},... | collective-permute-start | bytes 52232 | tf_op jit(solution)/shard_map/ppermute | solution.py:17
  10.9 3.8 %collective-permute-start.4 = (bf16[4,2176]{1,0:T(4,128)(2,1)S(1)}, bf16[4,2176]{1,0:T(4,128)(2,1)S(1)}, u32[]{:S(2)}, u32[]{:S(2)}) collective-permute-start(bf16[4,2176]{1,0:T(4,128)(2,1)S(1)} %get-tuple-element.28), channel_id=1, source_target_pairs={{0,8},{4,12},{8,0},{12,4},{1,9},{5,13},{9,1},{13,5},{2,10},{6,14},... | collective-permute-start | bytes 52232 | tf_op jit(solution)/shard_map/ppermute | solution.py:17
  12.5 2.3 %collective-permute-start.5 = (bf16[4,2176]{1,0:T(4,128)(2,1)S(1)}, bf16[4,2176]{1,0:T(4,128)(2,1)S(1)}, u32[]{:S(2)}, u32[]{:S(2)}) collective-permute-start(bf16[4,2176]{1,0:T(4,128)(2,1)S(1)} %get-tuple-element.29), channel_id=1, source_target_pairs={{0,4},{4,0},{8,12},{12,8},{1,5},{5,1},{9,13},{13,9},{2,6},{6,2},{1... | collective-permute-start | bytes 52232 | tf_op jit(solution)/shard_map/ppermute | solution.py:17
  14.8 9.8 %collective-permute-start.8 = (bf16[16,2176]{1,0:T(8,128)(2,1)S(1)}, bf16[16,2176]{1,0:T(8,128)(2,1)S(1)}, u32[]{:S(2)}, u32[]{:S(2)}) collective-permute-start(bf16[16,2176]{1,0:T(8,128)(2,1)S(1)} %pad_maximum_fusion.piece_ref), channel_id=1, source_target_pairs={{0,3},{1,2},{2,1},{3,0},{4,7},{5,6},{6,5},{7,4},{8,11},{9,10},{10,... | collective-permute-start | bytes 208904 | tf_op jit(solution)/shard_map/ppermute | solution.py:17
  16.9 7.7 %collective-permute-start.7 = (bf16[16,2176]{1,0:T(8,128)(2,1)S(1)}, bf16[16,2176]{1,0:T(8,128)(2,1)S(1)}, u32[]{:S(2)}, u32[]{:S(2)}) collective-permute-start(bf16[16,2176]{1,0:T(8,128)(2,1)S(1)} %pad_maximum_fusion.piece_ref), channel_id=1, source_target_pairs={{0,2},{1,3},{2,0},{3,1},{4,6},{5,7},{6,4},{7,5},{8,10},{9,11},{10,... | collective-permute-start | bytes 208904 | tf_op jit(solution)/shard_map/ppermute | solution.py:17
  16.9 7.7 %collective-permute-start.6 = (bf16[16,2176]{1,0:T(8,128)(2,1)S(1)}, bf16[16,2176]{1,0:T(8,128)(2,1)S(1)}, u32[]{:S(2)}, u32[]{:S(2)}) collective-permute-start(bf16[16,2176]{1,0:T(8,128)(2,1)S(1)} %pad_maximum_fusion.piece_ref), channel_id=1, source_target_pairs={{0,1},{1,0},{2,3},{3,2},{4,5},{5,4},{6,7},{7,6},{8,9},{9,8},{10,11... | collective-permute-start | bytes 208904 | tf_op jit(solution)/shard_map/ppermute | solution.py:17
  27.0 3.7 %collective-permute-start.9 = (bf16[4,4096]{1,0:T(4,128)(2,1)S(1)}, bf16[4,4096]{1,0:T(4,128)(2,1)S(1)}, u32[]{:S(2)}, u32[]{:S(2)}) collective-permute-start(bf16[4,4096]{1,0:T(4,128)(2,1)S(1)} %get-tuple-element.34), channel_id=1, source_target_pairs={{0,12},{4,8},{8,4},{12,0},{1,13},{5,9},{9,5},{13,1},{2,14},{6,10},... | collective-permute-start | bytes 98312 | tf_op jit(solution)/shard_map/ppermute | solution.py:17
  27.1 4.0 %collective-permute-start.10 = (bf16[4,4096]{1,0:T(4,128)(2,1)S(1)}, bf16[4,4096]{1,0:T(4,128)(2,1)S(1)}, u32[]{:S(2)}, u32[]{:S(2)}) collective-permute-start(bf16[4,4096]{1,0:T(4,128)(2,1)S(1)} %get-tuple-element.35), channel_id=1, source_target_pairs={{0,8},{4,12},{8,0},{12,4},{1,9},{5,13},{9,1},{13,5},{2,10},{6,14},... | collective-permute-start | bytes 98312 | tf_op jit(solution)/shard_map/ppermute | solution.py:17
  28.6 2.5 %collective-permute-start.11 = (bf16[4,4096]{1,0:T(4,128)(2,1)S(1)}, bf16[4,4096]{1,0:T(4,128)(2,1)S(1)}, u32[]{:S(2)}, u32[]{:S(2)}) collective-permute-start(bf16[4,4096]{1,0:T(4,128)(2,1)S(1)} %get-tuple-element.36), channel_id=1, source_target_pairs={{0,4},{4,0},{8,12},{12,8},{1,5},{5,1},{9,13},{13,9},{2,6},{6,2},{1... | collective-permute-start | bytes 98312 | tf_op jit(solution)/shard_map/ppermute | solution.py:17

commit v15 on v14

--- a/solution.py
+++ b/solution.py
@@ -413,7 +413,7 @@
     own = own_attention(queries, new_kv, page_slot, page_owner, context_len, pool, n_req)
     pieces = other_attention(q_list, own, n_req, n_tp)
     depth, columns = out_weight.shape
-    early = depth // 8
+    early = depth // 4
     swapped = [swap(pieces[d], "tp", d) for d in far_first(n_tp)]
     first, mine = load_weight(pieces[0], out_weight, 0, early, columns)
     arrived = jnp.concatenate([mine] + swapped, axis=0)

time: 31.9 us -> 32.4 us (1.016)
  waiting for transfers between devices: 4.54 us -> 5.01 us
    ppermute x12, waiting for transfers between devices: 4.54 us -> 5.01 us  [swap(): return lax.ppermute(x, axis, [(i, i ^ offset) for i in range(count)])]
  transfers between devices with their start and end apart: 12 -> 12, of which waited for: 4 -> 3; matrix products, arithmetic and copies ran while one was open for 0% -> 0% of each run, Pallas kernels for 29% -> 29%
where the time goes in v15:
time: 32.4 us; the launch traced here: 32.3 us
  starting transfers between devices  13.9 us (43%)
  Pallas kernels  12.6 us (39%)
  waiting for transfers between devices  5.01 us (15%)
  other arithmetic  0.7 us (2%)
    ppermute x12, starting transfers between devices, swap(): return lax.ppermute(x, axis, [(i, i ^ offset) for i in range(count)])  13.9 us
    pallas_call x2, Pallas kernels, load_weight(): pl.pallas_call(functools.partial(load_kernel, first), out_shape=[jax.Shap...  6.89 us
    ppermute x12, waiting for transfers between devices, swap(): return lax.ppermute(x, axis, [(i, i ^ offset) for i in range(count)])  5.01 us
    pallas_call x1, Pallas kernels, project(): pl.pallas_call(functools.partial(project_kernel, n_req, n_tp), out_shape=...  2.46 us
    pallas_call x1, Pallas kernels, own_attention(): pl.pallas_call(functools.partial(own_kernel, n_req, own_pages), out_shape...  2.39 us
    pallas_call x1, Pallas kernels, other_attention(): pl.pallas_call(functools.partial(other_kernel, n_req, n_tp), out_shape=[j...  0.84 us
    convert_element_type x1, other arithmetic, on_device(): return total.astype(jnp.bfloat16)  0.65 us
  transfers between devices with their start and end apart: 12, of which 3 were waited for; matrix products, arithmetic and copies ran while one was open for 0% of the time, Pallas kernels for 29%

profile of v15, /device:TPU:0, one launch (start us, length us, event | category | flops | bytes accessed | tf_op | source)
XLA Modules:
  0.0 32.3 jit_solution(9576030083663943181)
XLA Ops:
  0.0 4.0 %collective-permute-start.1 = (bf16[1,8192]{1,0:T(2,128)(2,1)}, bf16[1,8192]{1,0:T(2,128)(2,1)S(1)}, u32[]{:S(2)}, u32[]{:S(2)}) collective-permute-start(bf16[1,8192]{1,0:T(2,128)(2,1)} %refs_0_.1), channel_id=1, source_target_pairs={{0,2},{1,3},{2,0},{3,1},{4,6},{5,7},{6,4},{7,5},{8,10},{9,11},{10,... | collective-permute-start | bytes 49160 | tf_op jit(solution)/shard_map/ppermute | solution.py:17
  4.0 1.3 %collective-permute-start = (bf16[1,8192]{1,0:T(2,128)(2,1)}, bf16[1,8192]{1,0:T(2,128)(2,1)S(1)}, u32[]{:S(2)}, u32[]{:S(2)}) collective-permute-start(bf16[1,8192]{1,0:T(2,128)(2,1)} %refs_0_.1), channel_id=1, source_target_pairs={{0,3},{1,2},{2,1},{3,0},{4,7},{5,6},{6,5},{7,4},{8,11},{9,10},{10,... | collective-permute-start | bytes 49160 | tf_op jit(solution)/shard_map/ppermute | solution.py:17
  5.4 0.2 collective-permute-start.2
  5.6 2.4 %own_attention.1 = (f32[64,128]{1,0:T(8,128)S(1)}, f32[8,128]{1,0:T(8,128)S(1)}, s32[8,128]{1,0:T(8,128)S(1)}, bf16[3,4,128,256]{3,2,1,0:T(8,128)(2,1)S(1)}) custom-call(bf16[1,8192]{1,0:T(2,128)(2,1)} %refs_0_.1, bf16[1,1024]{1,0:T(2,128)(2,1)} %refs_1_.1, s32[1,4,7]{2,1,0:T(4,128)} %refs_2_.1, s32[1,4,7]{2,1,0:T(4,128)} %refs_3_.1, s32[1,4]{1,0:T(1,128)} %refs_4_.1, ...), custom_call_target="tpu_custom_call" | custom-call | flops 25165824 | bytes 4718592 | tf_op jit(solution)/shard_map/own_attention/pallas_call | solution.py:201
  8.0 0.0 collective-permute-done.1.refs_1_
  8.0 1.9 %collective-permute-done.refs_0_ = bf16[1,8192]{1,0:T(2,128)(2,1)S(1)} collective-permute-done((bf16[1,8192]{1,0:T(2,128)(2,1)}, bf16[1,8192]{1,0:T(2,128)(2,1)S(1)}, u32[]{:S(2)}, u32[]{:S(2)}) %collective-permute-start) | collective-permute-done | bytes 16416 | tf_op jit(solution)/shard_map/ppermute | solution.py:17
  10.0 0.0 collective-permute-done.2.refs_2_
  10.0 0.8 %other_attention.1 = (bf16[4,2176]{1,0:T(4,128)(2,1)S(1)}, bf16[4,2176]{1,0:T(4,128)(2,1)S(1)}, bf16[4,2176]{1,0:T(4,128)(2,1)S(1)}, bf16[4,2176]{1,0:T(4,128)(2,1)S(1)}) custom-call(bf16[1,8192]{1,0:T(2,128)(2,1)S(1)} %collective-permute-done.refs_0_, bf16[1,8192]{1,0:T(2,128)(2,1)S(1)} %collective-permute-done.1.refs_1_, ...), custom_call_target="tpu_custom_call" | custom-call | flops 12582912 | bytes 786432 | tf_op jit(solution)/shard_map/other_attention/pallas_call | solution.py:300
  10.8 0.1 collective-permute-start.3
  10.9 1.6 %collective-permute-start.4 = (bf16[4,2176]{1,0:T(4,128)(2,1)S(1)}, bf16[4,2176]{1,0:T(4,128)(2,1)S(1)}, u32[]{:S(2)}, u32[]{:S(2)}) collective-permute-start(bf16[4,2176]{1,0:T(4,128)(2,1)S(1)} %get-tuple-element.28), channel_id=1, source_target_pairs={{0,8},{4,12},{8,0},{12,4},{1,9},{5,13},{9,1},{13,5},{2,10},{6,14},... | collective-permute-start | bytes 52232 | tf_op jit(solution)/shard_map/ppermute | solution.py:17
  12.5 0.3 collective-permute-start.5
  12.7 2.2 %load_weight.2 = (bf16[512,4096]{1,0:T(8,128)(2,1)S(1)}, bf16[4,2176]{1,0:T(4,128)(2,1)S(1)}) custom-call(bf16[4,2176]{1,0:T(4,128)(2,1)S(1)} %get-tuple-element.25.piece_ref, bf16[2048,4096]{1,0:T(8,128)(2,1)} %weight_hbm.3), custom_call_target="tpu_custom_call" | custom-call | bytes 8388608 | tf_op jit(solution)/shard_map/load_weight/pallas_call | solution.py:339
  14.9 0.0 collective-permute-done.3
  15.0 0.0 collective-permute-done.4
  15.0 0.0 collective-permute-done.5
  15.0 2.1 %collective-permute-start.8 = (bf16[16,2176]{1,0:T(8,128)(2,1)S(1)}, bf16[16,2176]{1,0:T(8,128)(2,1)S(1)}, u32[]{:S(2)}, u32[]{:S(2)}) collective-permute-start(bf16[16,2176]{1,0:T(8,128)(2,1)S(1)} %pad_maximum_fusion.piece_ref), channel_id=1, source_target_pairs={{0,3},{1,2},{2,1},{3,0},{4,7},{5,6},{6,5},{7,4},{8,11},{9,10},{10,... | collective-permute-start | bytes 208904 | tf_op jit(solution)/shard_map/ppermute | solution.py:17
  17.1 0.0 collective-permute-start.7
  17.1 2.4 %collective-permute-start.6 = (bf16[16,2176]{1,0:T(8,128)(2,1)S(1)}, bf16[16,2176]{1,0:T(8,128)(2,1)S(1)}, u32[]{:S(2)}, u32[]{:S(2)}) collective-permute-start(bf16[16,2176]{1,0:T(8,128)(2,1)S(1)} %pad_maximum_fusion.piece_ref), channel_id=1, source_target_pairs={{0,1},{1,0},{2,3},{3,2},{4,5},{5,4},{6,7},{7,6},{8,9},{9,8},{10,11... | collective-permute-start | bytes 208904 | tf_op jit(solution)/shard_map/ppermute | solution.py:17
  19.5 4.7 %load_weight.3 = (bf16[1536,4096]{1,0:T(8,128)(2,1)S(1)}, bf16[16,2176]{1,0:T(8,128)(2,1)S(1)}) custom-call(bf16[16,2176]{1,0:T(8,128)(2,1)S(1)} %pad_maximum_fusion.piece_ref, bf16[2048,4096]{1,0:T(8,128)(2,1)} %weight_hbm.3), custom_call_target="tpu_custom_call" | custom-call | bytes 25165824 | tf_op jit(solution)/shard_map/load_weight/pallas_call | solution.py:339
  24.2 0.0 collective-permute-done.8.refs_3_
  24.2 0.0 collective-permute-done.7.refs_2_
  24.2 0.0 collective-permute-done.6.refs_1_
  24.2 2.5 %project.1 = (f32[4,4096]{1,0:T(4,128)S(1)}, bf16[4,4096]{1,0:T(4,128)(2,1)S(1)}, bf16[4,4096]{1,0:T(4,128)(2,1)S(1)}, bf16[4,4096]{1,0:T(4,128)(2,1)S(1)}) custom-call(bf16[16,2176]{1,0:T(8,128)(2,1)S(1)} %get-tuple-element.30.refs_0_, bf16[16,2176]{1,0:T(8,128)(2,1)S(1)} %collective-permute-done.6.refs_1_, ...), custom_call_target="tpu_custom_call" | custom-call | flops 268435456 | bytes 16777216 | tf_op jit(solution)/shard_map/project/pallas_call | solution.py:394
  26.7 0.9 %collective-permute-start.9 = (bf16[4,4096]{1,0:T(4,128)(2,1)S(1)}, bf16[4,4096]{1,0:T(4,128)(2,1)S(1)}, u32[]{:S(2)}, u32[]{:S(2)}) collective-permute-start(bf16[4,4096]{1,0:T(4,128)(2,1)S(1)} %get-tuple-element.34), channel_id=1, source_target_pairs={{0,12},{4,8},{8,4},{12,0},{1,13},{5,9},{9,5},{13,1},{2,14},{6,10},... | collective-permute-start | bytes 98312 | tf_op jit(solution)/shard_map/ppermute | solution.py:17
  27.6 0.8 %collective-permute-start.10 = (bf16[4,4096]{1,0:T(4,128)(2,1)S(1)}, bf16[4,4096]{1,0:T(4,128)(2,1)S(1)}, u32[]{:S(2)}, u32[]{:S(2)}) collective-permute-start(bf16[4,4096]{1,0:T(4,128)(2,1)S(1)} %get-tuple-element.35), channel_id=1, source_target_pairs={{0,8},{4,12},{8,0},{12,4},{1,9},{5,13},{9,1},{13,5},{2,10},{6,14},... | collective-permute-start | bytes 98312 | tf_op jit(solution)/shard_map/ppermute | solution.py:17
  28.3 0.2 collective-permute-start.11
  28.6 1.6 %collective-permute-done.9 = bf16[4,4096]{1,0:T(4,128)(2,1)S(1)} collective-permute-done((bf16[4,4096]{1,0:T(4,128)(2,1)S(1)}, bf16[4,4096]{1,0:T(4,128)(2,1)S(1)}, u32[]{:S(2)}, u32[]{:S(2)}) %collective-permute-start.9) | collective-permute-done | bytes 32800 | tf_op jit(solution)/shard_map/ppermute | solution.py:17
  30.2 1.4 %collective-permute-done.10 = bf16[4,4096]{1,0:T(4,128)(2,1)S(1)} collective-permute-done((bf16[4,4096]{1,0:T(4,128)(2,1)S(1)}, bf16[4,4096]{1,0:T(4,128)(2,1)S(1)}, u32[]{:S(2)}, u32[]{:S(2)}) %collective-permute-start.10) | collective-permute-done | bytes 32800 | tf_op jit(solution)/shard_map/ppermute | solution.py:17
  31.6 0.0 collective-permute-done.11
  31.6 0.7 %add_convert_fusion = bf16[4,4096]{1,0:T(4,128)(2,1)} fusion(bf16[4,4096]{1,0:T(4,128)(2,1)S(1)} %collective-permute-done.11, bf16[4,4096]{1,0:T(4,128)(2,1)S(1)} %collective-permute-done.10, f32[4,4096]{1,0:T(4,128)S(1)} %get-tuple-element.33, bf16[4,4096]{1,0:T(4,128)(2,1)S(1)} %collective-permute-done.9), kind=kLoop, calls=%fused_computation.1 | loop fusion | flops 114688 | bytes 196608 | tf_op jit(solution)/shard_map/convert_element_type | solution.py:426
  (1 shorter events, 0.0 us)
Async XLA Ops:
  0.0 8.0 %collective-permute-start.1 = (bf16[1,8192]{1,0:T(2,128)(2,1)}, bf16[1,8192]{1,0:T(2,128)(2,1)S(1)}, u32[]{:S(2)}, u32[]{:S(2)}) collective-permute-start(bf16[1,8192]{1,0:T(2,128)(2,1)} %refs_0_.1), channel_id=1, source_target_pairs={{0,2},{1,3},{2,0},{3,1},{4,6},{5,7},{6,4},{7,5},{8,10},{9,11},{10,... | collective-permute-start | bytes 49160 | tf_op jit(solution)/shard_map/ppermute | solution.py:17
  4.0 5.9 %collective-permute-start = (bf16[1,8192]{1,0:T(2,128)(2,1)}, bf16[1,8192]{1,0:T(2,128)(2,1)S(1)}, u32[]{:S(2)}, u32[]{:S(2)}) collective-permute-start(bf16[1,8192]{1,0:T(2,128)(2,1)} %refs_0_.1), channel_id=1, source_target_pairs={{0,3},{1,2},{2,1},{3,0},{4,7},{5,6},{6,5},{7,4},{8,11},{9,10},{10,... | collective-permute-start | bytes 49160 | tf_op jit(solution)/shard_map/ppermute | solution.py:17
  5.4 4.6 %collective-permute-start.2 = (bf16[1,8192]{1,0:T(2,128)(2,1)}, bf16[1,8192]{1,0:T(2,128)(2,1)S(1)}, u32[]{:S(2)}, u32[]{:S(2)}) collective-permute-start(bf16[1,8192]{1,0:T(2,128)(2,1)} %refs_0_.1), channel_id=1, source_target_pairs={{0,1},{1,0},{2,3},{3,2},{4,5},{5,4},{6,7},{7,6},{8,9},{9,8},{10,11... | collective-permute-start | bytes 49160 | tf_op jit(solution)/shard_map/ppermute | solution.py:17
  10.8 4.1 %collective-permute-start.3 = (bf16[4,2176]{1,0:T(4,128)(2,1)S(1)}, bf16[4,2176]{1,0:T(4,128)(2,1)S(1)}, u32[]{:S(2)}, u32[]{:S(2)}) collective-permute-start(bf16[4,2176]{1,0:T(4,128)(2,1)S(1)} %get-tuple-element.27), channel_id=1, source_target_pairs={{0,12},{4,8},{8,4},{12,0},{1,13},{5,9},{9,5},{13,1},{2,14},{6,10},... | collective-permute-start | bytes 52232 | tf_op jit(solution)/shard_map/ppermute | solution.py:17
  10.9 4.1 %collective-permute-start.4 = (bf16[4,2176]{1,0:T(4,128)(2,1)S(1)}, bf16[4,2176]{1,0:T(4,128)(2,1)S(1)}, u32[]{:S(2)}, u32[]{:S(2)}) collective-permute-start(bf16[4,2176]{1,0:T(4,128)(2,1)S(1)} %get-tuple-element.28), channel_id=1, source_target_pairs={{0,8},{4,12},{8,0},{12,4},{1,9},{5,13},{9,1},{13,5},{2,10},{6,14},... | collective-permute-start | bytes 52232 | tf_op jit(solution)/shard_map/ppermute | solution.py:17
  12.5 2.5 %collective-permute-start.5 = (bf16[4,2176]{1,0:T(4,128)(2,1)S(1)}, bf16[4,2176]{1,0:T(4,128)(2,1)S(1)}, u32[]{:S(2)}, u32[]{:S(2)}) collective-permute-start(bf16[4,2176]{1,0:T(4,128)(2,1)S(1)} %get-tuple-element.29), channel_id=1, source_target_pairs={{0,4},{4,0},{8,12},{12,8},{1,5},{5,1},{9,13},{13,9},{2,6},{6,2},{1... | collective-permute-start | bytes 52232 | tf_op jit(solution)/shard_map/ppermute | solution.py:17
  15.0 9.2 %collective-permute-start.8 = (bf16[16,2176]{1,0:T(8,128)(2,1)S(1)}, bf16[16,2176]{1,0:T(8,128)(2,1)S(1)}, u32[]{:S(2)}, u32[]{:S(2)}) collective-permute-start(bf16[16,2176]{1,0:T(8,128)(2,1)S(1)} %pad_maximum_fusion.piece_ref), channel_id=1, source_target_pairs={{0,3},{1,2},{2,1},{3,0},{4,7},{5,6},{6,5},{7,4},{8,11},{9,10},{10,... | collective-permute-start | bytes 208904 | tf_op jit(solution)/shard_map/ppermute | solution.py:17
  17.1 7.1 %collective-permute-start.7 = (bf16[16,2176]{1,0:T(8,128)(2,1)S(1)}, bf16[16,2176]{1,0:T(8,128)(2,1)S(1)}, u32[]{:S(2)}, u32[]{:S(2)}) collective-permute-start(bf16[16,2176]{1,0:T(8,128)(2,1)S(1)} %pad_maximum_fusion.piece_ref), channel_id=1, source_target_pairs={{0,2},{1,3},{2,0},{3,1},{4,6},{5,7},{6,4},{7,5},{8,10},{9,11},{10,... | collective-permute-start | bytes 208904 | tf_op jit(solution)/shard_map/ppermute | solution.py:17
  17.1 7.1 %collective-permute-start.6 = (bf16[16,2176]{1,0:T(8,128)(2,1)S(1)}, bf16[16,2176]{1,0:T(8,128)(2,1)S(1)}, u32[]{:S(2)}, u32[]{:S(2)}) collective-permute-start(bf16[16,2176]{1,0:T(8,128)(2,1)S(1)} %pad_maximum_fusion.piece_ref), channel_id=1, source_target_pairs={{0,1},{1,0},{2,3},{3,2},{4,5},{5,4},{6,7},{7,6},{8,9},{9,8},{10,11... | collective-permute-start | bytes 208904 | tf_op jit(solution)/shard_map/ppermute | solution.py:17
  26.7 3.5 %collective-permute-start.9 = (bf16[4,4096]{1,0:T(4,128)(2,1)S(1)}, bf16[4,4096]{1,0:T(4,128)(2,1)S(1)}, u32[]{:S(2)}, u32[]{:S(2)}) collective-permute-start(bf16[4,4096]{1,0:T(4,128)(2,1)S(1)} %get-tuple-element.34), channel_id=1, source_target_pairs={{0,12},{4,8},{8,4},{12,0},{1,13},{5,9},{9,5},{13,1},{2,14},{6,10},... | collective-permute-start | bytes 98312 | tf_op jit(solution)/shard_map/ppermute | solution.py:17
  27.6 4.0 %collective-permute-start.10 = (bf16[4,4096]{1,0:T(4,128)(2,1)S(1)}, bf16[4,4096]{1,0:T(4,128)(2,1)S(1)}, u32[]{:S(2)}, u32[]{:S(2)}) collective-permute-start(bf16[4,4096]{1,0:T(4,128)(2,1)S(1)} %get-tuple-element.35), channel_id=1, source_target_pairs={{0,8},{4,12},{8,0},{12,4},{1,9},{5,13},{9,1},{13,5},{2,10},{6,14},... | collective-permute-start | bytes 98312 | tf_op jit(solution)/shard_map/ppermute | solution.py:17
  28.3 3.3 %collective-permute-start.11 = (bf16[4,4096]{1,0:T(4,128)(2,1)S(1)}, bf16[4,4096]{1,0:T(4,128)(2,1)S(1)}, u32[]{:S(2)}, u32[]{:S(2)}) collective-permute-start(bf16[4,4096]{1,0:T(4,128)(2,1)S(1)} %get-tuple-element.36), channel_id=1, source_target_pairs={{0,4},{4,0},{8,12},{12,8},{1,5},{5,1},{9,13},{13,9},{2,6},{6,2},{1... | collective-permute-start | bytes 98312 | tf_op jit(solution)/shard_map/ppermute | solution.py:17
